TPU v7x, 32 devices: a whole 2x2x4 slice. The times are simulated.
32 devices in a mesh: ctx: 8 (over z, x), head: 4 (over y, core).
Axes of the slice: x: 2, y: 2, z: 4, core: 2. Of those that a mesh axis runs over, the one named last changes fastest.
Arguments:
- queries: bfloat16 [1, 2048, 2048], P(None, 'ctx', 'head'), may hold values from -128 to 128
- key_rows: bfloat16 [1, 2048, 128], P(None, ('ctx', 'head')), may hold values from -4.5 to 4.5
- value_rows: bfloat16 [1, 2048, 128], P(None, ('ctx', 'head')), may hold values from -5 to 5
- document_lengths: int32 [1, 4], replicated, may hold values from 1 to 1536, 2048 in all within a row
Outputs:
- attended: bfloat16 [1, 2048, 2048], P(None, 'ctx', 'head')
All inputs are finite; a program needn't handle non-finite values.
Results may differ from a plain program's by a relative error of at most 0.0045.
Values may be sent and summed in bfloat16 or wider, within the bound.
No kernel may reach another device: no remote copies, remote signals or barrier semaphores. Data moves between devices by JAX's collectives and lax.ppermute only.
A program may use at most 64 MiB of HBM per device.

v0:
```python
import math

import jax
import jax.numpy as jnp
from jax import lax
from jax.sharding import PartitionSpec as P

NEG = -1e30


def document_ids(positions, ends):
    return jnp.sum((positions[None, :, None] >= ends[:, None, :]).astype(jnp.int32), axis=2)


def body(queries, key_rows, value_rows, document_lengths):
    device = lax.axis_index("ctx")
    seqs, rows, width = queries.shape
    head_size = key_rows.shape[2]
    heads = width // head_size
    scale = 1.0 / math.sqrt(head_size)
    ends = jnp.cumsum(document_lengths, axis=1)
    query_pos = device * rows + jnp.arange(rows, dtype=jnp.int32)
    query_docs = document_ids(query_pos, ends)
    query_heads = queries.reshape(seqs, rows, heads, head_size)

    def update(state, key_block, value_block, valid):
        running_max, running_total, accum = state
        scores = (
            jnp.einsum("sqhd,skd->sqhk", query_heads, key_block, preferred_element_type=jnp.float32)
            * scale
        )
        scores = jnp.where(valid[:, :, None, :], scores, NEG)
        new_max = jnp.maximum(running_max, jnp.max(scores, axis=3))
        factor = jnp.exp(running_max - new_max)
        weights = jnp.where(valid[:, :, None, :], jnp.exp(scores - new_max[..., None]), 0.0)
        running_total = running_total * factor + jnp.sum(weights, axis=3)
        accum = accum * factor[..., None] + jnp.einsum(
            "sqhk,skd->sqhd",
            weights.astype(jnp.bfloat16),
            value_block,
            preferred_element_type=jnp.float32,
        )
        return (new_max, running_total, accum)

    initial = (
        jnp.full((seqs, rows, heads), NEG, jnp.float32),
        jnp.zeros((seqs, rows, heads), jnp.float32),
        jnp.zeros((seqs, rows, heads, head_size), jnp.float32),
    )
    key_piece = lax.all_gather(key_rows, ("ctx", "head"), axis=1, tiled=True)
    value_piece = lax.all_gather(value_rows, ("ctx", "head"), axis=1, tiled=True)
    key_count = key_piece.shape[1]
    block_rows = math.gcd(key_count, 256)

    def one_block(block_index, inner):
        offset = block_index * block_rows
        key_block = lax.dynamic_slice_in_dim(key_piece, offset, block_rows, 1)
        value_block = lax.dynamic_slice_in_dim(value_piece, offset, block_rows, 1)
        key_pos = offset + jnp.arange(block_rows, dtype=jnp.int32)
        key_docs = document_ids(key_pos, ends)
        valid = (
            (key_pos[None, None, :] <= query_pos[None, :, None])
            & (key_pos[None, None, :] >= 0)
            & (key_docs[:, None, :] == query_docs[:, :, None])
        )
        return update(inner, key_block, value_block, valid)

    result = lax.fori_loop(0, key_count // block_rows, one_block, initial)
    running_max, running_total, accum = result
    attended = (accum / running_total[..., None]).astype(jnp.bfloat16).reshape(seqs, rows, width)
    return attended


def solution(mesh):
    in_specs = (
        P(None, "ctx", "head"),
        P(None, ("ctx", "head"), None),
        P(None, ("ctx", "head"), None),
        P(),
    )
    out_specs = P(None, "ctx", "head")
    return jax.shard_map(body, mesh=mesh, in_specs=in_specs, out_specs=out_specs, check_vma=False)
```

profile of v0, /device:TPU:0, one launch (start us, length us, event | category | flops | bytes accessed | tf_op | source)
XLA Modules:
  0.0 96.4 jit_solution(17494557329379299280)
XLA Ops:
  0.0 0.8 reduce_window_sum.11
  0.8 0.1 convert_reduce_fusion.1
  0.9 44.8 %all_gather.6 = bf16[1,2048,128]{2,1,0:T(8,128)(2,1)S(1)} all-gather(bf16[1,64,128]{2,1,0:T(8,128)(2,1)S(1)} %copy-done.1), channel_id=1, replica_groups=mesh['ctx'=8,'head'=4] {'ctx','head'}, dimensions={1}, use_global_device_ids=true | all-gather | bytes 540672 | tf_op jit(solution)/shard_map/all_gather | solution.py:50
  45.7 38.2 %all_gather.7 = bf16[1,2048,128]{2,1,0:T(8,128)(2,1)S(1)} all-gather(bf16[1,64,128]{2,1,0:T(8,128)(2,1)S(1)} %copy-done.2), channel_id=1, replica_groups=mesh['ctx'=8,'head'=4] {'ctx','head'}, dimensions={1}, use_global_device_ids=true | all-gather | bytes 540672 | tf_op jit(solution)/shard_map/all_gather | solution.py:51
  83.9 0.1 copy.12
  84.0 0.2 copy.13
  84.2 11.3 %while.18 = (s32[]{:T(128)}, f32[1,256,4]{1,2,0:T(4,128)S(1)}, f32[1,256,4]{1,2,0:T(4,128)S(1)}, f32[1,256,4,128]{3,1,2,0:T(8,128)S(1)}, s32[1,4]{1,0:T(1,128)S(...) while((s32[]{:T(128)}, f32[1,256,4]{1,2,0:T(4,128)S(1)}, ...), condition=%wide.region_6.7_spmd.clone, body=%wide.region_2.6_spmd.clone.sunk | while | flops 137242368 | bytes 4924131 | solution.py:68
  84.2 0.1 convert_reduce_fusion.3
  84.3 0.2 compare_and_fusion.2
  84.5 0.3 fusion.31
  84.9 0.5 fusion.34
  85.4 0.2 fusion.33
  85.6 0.1 convert_reduce_fusion.3
  85.7 0.2 compare_and_fusion.2
  85.9 0.3 fusion.31
  86.3 0.5 fusion.34
  86.8 0.2 fusion.33
  87.1 0.1 convert_reduce_fusion.3
  87.2 0.2 compare_and_fusion.2
  87.3 0.3 fusion.31
  87.7 0.5 fusion.34
  88.2 0.2 fusion.33
  88.5 0.1 convert_reduce_fusion.3
  88.6 0.2 compare_and_fusion.2
  88.8 0.3 fusion.31
  89.1 0.5 fusion.34
  89.6 0.2 fusion.33
  89.9 0.1 convert_reduce_fusion.3
  90.0 0.2 compare_and_fusion.2
  90.2 0.3 fusion.31
  90.5 0.5 fusion.34
  91.0 0.2 fusion.33
  91.3 0.1 convert_reduce_fusion.3
  91.4 0.2 compare_and_fusion.2
  91.6 0.3 fusion.31
  91.9 0.5 fusion.34
  92.4 0.2 fusion.33
  92.7 0.1 convert_reduce_fusion.3
  92.8 0.2 compare_and_fusion.2
  93.0 0.3 fusion.31
  93.3 0.5 fusion.34
  93.8 0.2 fusion.33
  94.1 0.1 convert_reduce_fusion.3
  94.2 0.2 compare_and_fusion.2
  94.4 0.3 fusion.31
  94.7 0.5 fusion.34
  95.3 0.2 fusion.33
  95.5 0.9 copy_bitcast_fusion
  (50 shorter events, 0.4 us)
Async XLA Ops:
  0.0 0.9 copy-start.1
  0.9 44.8 %copy-start.2 = (bf16[1,64,128]{2,1,0:T(8,128)(2,1)S(1)}, bf16[1,64,128]{2,1,0:T(8,128)(2,1)}, u32[]{:S(2)}) copy-start(bf16[1,64,128]{2,1,0:T(8,128)(2,1)} %param.8) | copy-start | bytes 49156
  45.7 38.2 %copy-start = (bf16[1,256,512]{2,1,0:T(8,128)(2,1)S(1)}, bf16[1,256,512]{2,1,0:T(8,128)(2,1)}, u32[]{:S(2)}) copy-start(bf16[1,256,512]{2,1,0:T(8,128)(2,1)} %param.6) | copy-start | bytes 786436
where the time goes:
time: 96.6 us; the launch traced here: 96.4 us
  blocking collectives  82.9 us (86%)
  matrix products  6.65 us (7%)
  other arithmetic  5.88 us (6%)
    all_gather x1, blocking collectives, body(): key_piece = lax.all_gather(key_rows, ('ctx', 'head'), axis=1, tiled=True)  44.8 us
    all_gather x1, blocking collectives, body(): lax.all_gather(value_rows, ('ctx', 'head'), axis=1, tiled=True)  38.2 us
    dot_general x8, matrix products, update(): jnp.einsum('sqhk,skd->sqhd', weights.astype(jnp.bfloat16), value_block, p...  4.04 us
    dot_general x8, matrix products, update(): jnp.einsum('sqhd,skd->sqhk', query_heads, key_block, preferred_element_ty...  2.6 us

commit v1 on v0

v1 whole, which is shorter than its diff:
```python
import functools
import math

import jax
import jax.numpy as jnp
from jax import lax
from jax.experimental import pallas as pl
from jax.experimental.pallas import tpu as pltpu
from jax.sharding import PartitionSpec as P

NEG = -1e30


def attention_kernel(head_size, lengths_ref, queries_ref, kv_ref, out_ref, accum_ref):
    own = lax.axis_index("ctx")
    rows, width = queries_ref.shape
    heads = width // head_size
    pieces, _, piece_rows, _ = kv_ref.shape
    block_rows = pieces * piece_rows
    slope = math.log2(math.e) / math.sqrt(head_size)

    query_pos = own * rows + lax.broadcasted_iota(jnp.int32, (1, rows), 1)
    starts = jnp.zeros((1, rows), jnp.int32)
    first = jnp.int32(0)
    end = jnp.int32(0)
    for document in range(lengths_ref.shape[1]):
        end = end + lengths_ref[0, document]
        starts = jnp.where(query_pos >= end, end, starts)
        first = jnp.where(own * rows >= end, end, first)

    def block_step(block, state, fresh):
        kv = kv_ref[:, pl.ds(block, 1)].reshape(block_rows, 2 * head_size)
        keys, values = kv[:, :head_size], kv[:, head_size:]
        key_pos = block * block_rows + lax.broadcasted_iota(jnp.int32, (block_rows, rows), 0)
        valid = (key_pos >= starts) & (key_pos <= query_pos)
        new_state = []
        for head in range(heads):
            query = queries_ref[:, head * head_size : (head + 1) * head_size]
            scores = lax.dot_general(keys, query, (((1,), (1,)), ((), ())), preferred_element_type=jnp.float32)
            scores = jnp.where(valid, scores, NEG)
            block_top = jnp.max(scores, axis=0, keepdims=True)
            if fresh:
                top = block_top
            else:
                top = jnp.maximum(state[2 * head], block_top)
            weights = jnp.exp2((scores - top) * slope)
            total = jnp.sum(weights, axis=0, keepdims=True)
            mixed = lax.dot_general(
                values, weights.astype(jnp.bfloat16), (((0,), (0,)), ((), ())), preferred_element_type=jnp.float32
            )
            if fresh:
                accum_ref[head] = mixed
            else:
                factor = jnp.exp2((state[2 * head] - top) * slope)
                total = state[2 * head + 1] * factor + total
                accum_ref[head] = accum_ref[head] * factor + mixed
            new_state += [top, total]
        return tuple(new_state)

    state = block_step(own, None, True)
    state = lax.fori_loop(
        first // block_rows, own, lambda block, inner: block_step(block, inner, False), state
    )
    for head in range(heads):
        mixed = accum_ref[head] / state[2 * head + 1]
        out_ref[:, head * head_size : (head + 1) * head_size] = mixed.T.astype(out_ref.dtype)


def attend(queries, kv, lengths, head_size):
    rows, width = queries.shape
    heads = width // head_size
    keys = kv.shape[0] * kv.shape[1] * kv.shape[2]
    whole = pl.BlockSpec(memory_space=pltpu.VMEM)
    return pl.pallas_call(
        functools.partial(attention_kernel, head_size),
        out_shape=jax.ShapeDtypeStruct((rows, width), queries.dtype),
        in_specs=[pl.BlockSpec(memory_space=pltpu.SMEM), whole, whole],
        out_specs=whole,
        scratch_shapes=[pltpu.VMEM((heads, head_size, rows), jnp.float32)],
        compiler_params=pltpu.CompilerParams(vmem_limit_bytes=48 * 1024 * 1024),
        cost_estimate=pl.CostEstimate(
            flops=4 * rows * width * keys, bytes_accessed=4 * rows * width + 4 * keys * head_size,
            transcendentals=rows * heads * keys,
        ),
    )(lengths, queries, kv)


def body(queries, key_rows, value_rows, document_lengths):
    seqs, rows, width = queries.shape
    piece_rows, head_size = key_rows.shape[1:]
    results = []
    for seq in range(seqs):
        kv = jnp.concatenate([key_rows[seq], value_rows[seq]], axis=1)
        kv = lax.all_gather(kv, "ctx", axis=0)
        kv = lax.all_gather(kv, "head", axis=0)
        lengths = document_lengths[seq : seq + 1]
        results.append(attend(queries[seq], kv, lengths, head_size))
    return jnp.stack(results)


def solution(mesh):
    in_specs = (
        P(None, "ctx", "head"),
        P(None, ("ctx", "head"), None),
        P(None, ("ctx", "head"), None),
        P(),
    )
    out_specs = P(None, "ctx", "head")
    return jax.shard_map(body, mesh=mesh, in_specs=in_specs, out_specs=out_specs, check_vma=False)
```

time: 96.6 us -> 78 us (0.81)
  the two profiles are of different devices: /device:TPU:0 before, /device:TPU:25 now
where the time goes in v1:
time: 78 us; the launch traced here: 77.7 us
  waiting for transfers between devices  27.3 us (35%)
  blocking collectives  23.8 us (31%)
  between operations  13.4 us (17%)
  Pallas kernels  10.5 us (13%)
  local copies, waits for them, and re-layouts  1.88 us (2%)
    all_gather x1, waiting for transfers between devices, body(): kv = lax.all_gather(kv, 'head', axis=0)  27.3 us
    all_gather x1, blocking collectives, body(): kv = lax.all_gather(kv, 'ctx', axis=0)  23.8 us
    pallas_call x1, Pallas kernels, attend(): pl.pallas_call(functools.partial(attention_kernel, head_size), out_shape=...  10.5 us
    unnamed x6, local copies, waits for them, and re-layouts  1.88 us
  transfers between devices with their start and end apart: 1, of which 1 were waited for; matrix products, arithmetic and copies ran while one was open for 0% of the time, Pallas kernels for 0%

profile of v1, /device:TPU:25, one launch (start us, length us, event | category | flops | bytes accessed | tf_op | source)
XLA Modules:
  0.0 77.7 jit_solution(2419728783760863679)
XLA Ops:
  6.5 0.0 all-gather.4.cloned.1.call-start
  6.5 0.7 pad_maximum_fusion
  7.3 0.0 copy-start.1
  7.3 23.8 %all-gather = bf16[512,256]{1,0:T(8,128)(2,1)} all-gather(bf16[64,256]{1,0:T(8,128)(2,1)S(1)} %pad_maximum_fusion), channel_id=2, replica_groups=mesh['ctx'=8,'head'=4] {'ctx'}, dimensions={0}, use_global_device_ids=true | all-gather | bytes 294912 | tf_op jit(solution)/shard_map/all_gather | solution.py:94
  31.1 0.0 all-gather.4.cloned.1.call-update
  31.1 27.3 %all-gather.4.cloned.1.call-done = bf16[32,64,256]{2,1,0:T(8,128)(2,1)} async-done(((bf16[8,64,256]{2,1,0:T(8,128)(2,1)}), bf16[32,64,256]{2,1,0:T(8,128)(2,1)}) %all-gather.4.cloned.1.call-update) | async-done | bytes 1048592 | tf_op jit(solution)/shard_map/all_gather | solution.py:95
  58.4 0.0 copy-start.2
  58.4 0.0 copy-done.1
  58.4 0.7 copy-done.2
  59.1 0.0 copy-start
  59.1 1.2 %copy-done = bf16[32,64,256]{2,1,0:T(8,128)(2,1)S(1)} copy-done((bf16[32,64,256]{2,1,0:T(8,128)(2,1)S(1)}, bf16[32,64,256]{2,1,0:T(8,128)(2,1)}, u32[]{:S(2)}) %copy-start) | copy-done | bytes 1048600
  60.3 10.5 %shard_map.46 = bf16[256,512]{1,0:T(8,128)(2,1)} custom-call(s32[1,4]{1,0:T(1,128)S(1)} %copy-done.2, bf16[256,512]{1,0:T(8,128)(2,1)S(1)} %bitcast.7, bf16[4,8,64,256]{3,2,1,0:T(8,128)(2,1)S(1)} %bitcast.6), custom_call_target="tpu_custom_call" | custom-call | flops 1073741824 | bytes 1572864 | tf_op jit(solution)/shard_map/pallas_call | solution.py:74
Async XLA Ops:
  6.5 51.9 %all-gather.4.cloned.1.call-start = ((), (), s32[]{:S(2)}) async-start(), calls=%async_computation | async-start | bytes 1310720 | tf_op jit(solution)/shard_map/all_gather | solution.py:95
  7.3 51.1 %copy-start.1 = (bf16[1,256,512]{2,1,0:T(8,128)(2,1)S(1)}, bf16[1,256,512]{2,1,0:T(8,128)(2,1)}, u32[]{:S(2)}) copy-start(bf16[1,256,512]{2,1,0:T(8,128)(2,1)} %param.4) | copy-start | bytes 786436
  58.4 0.7 copy-start.2
  59.1 1.2 %copy-start = (bf16[32,64,256]{2,1,0:T(8,128)(2,1)S(1)}, bf16[32,64,256]{2,1,0:T(8,128)(2,1)}, u32[]{:S(2)}) copy-start(bf16[32,64,256]{2,1,0:T(8,128)(2,1)} %all-gather.4.cloned.1.call-done) | copy-start | bytes 3145732
Sparse Core Ops, SparseCore 0:
  31.2 27.1 all-gather.3

commit v2 on v1

--- a/solution.py
+++ b/solution.py
@@ -11,11 +11,13 @@
 NEG = -1e30
 
 
-def attention_kernel(head_size, lengths_ref, queries_ref, kv_ref, out_ref, accum_ref):
-    own = lax.axis_index("ctx")
+def attention_kernel(head_size, lengths_ref, queries_ref, *refs):
+    *kv_refs, out_ref, accum_ref = refs
+    own, piece = lax.axis_index("ctx"), lax.axis_index("head")
     rows, width = queries_ref.shape
     heads = width // head_size
-    pieces, _, piece_rows, _ = kv_ref.shape
+    pieces = len(kv_refs)
+    piece_rows = kv_refs[0].shape[1]
     block_rows = pieces * piece_rows
     slope = math.log2(math.e) / math.sqrt(head_size)
 
@@ -27,11 +29,13 @@
         end = end + lengths_ref[0, document]
         starts = jnp.where(query_pos >= end, end, starts)
         first = jnp.where(own * rows >= end, end, first)
+    in_piece = lax.broadcasted_iota(jnp.int32, (piece_rows, rows), 0)
+    in_block = jnp.concatenate([in_piece + lax.rem(piece + pieces - i, pieces) * piece_rows for i in range(pieces)], axis=0)
 
-    def block_step(block, state, fresh):
-        kv = kv_ref[:, pl.ds(block, 1)].reshape(block_rows, 2 * head_size)
+    def block_step(back, state, fresh):
+        kv = jnp.concatenate([kv_ref[back] for kv_ref in kv_refs], axis=0)
         keys, values = kv[:, :head_size], kv[:, head_size:]
-        key_pos = block * block_rows + lax.broadcasted_iota(jnp.int32, (block_rows, rows), 0)
+        key_pos = (own - back) * block_rows + in_block
         valid = (key_pos >= starts) & (key_pos <= query_pos)
         new_state = []
         for head in range(heads):
@@ -57,24 +61,24 @@
             new_state += [top, total]
         return tuple(new_state)
 
-    state = block_step(own, None, True)
+    state = block_step(0, None, True)
     state = lax.fori_loop(
-        first // block_rows, own, lambda block, inner: block_step(block, inner, False), state
+        1, own - first // block_rows + 1, lambda back, inner: block_step(back, inner, False), state
     )
     for head in range(heads):
         mixed = accum_ref[head] / state[2 * head + 1]
         out_ref[:, head * head_size : (head + 1) * head_size] = mixed.T.astype(out_ref.dtype)
 
 
-def attend(queries, kv, lengths, head_size):
+def attend(queries, kvs, lengths, head_size):
     rows, width = queries.shape
     heads = width // head_size
-    keys = kv.shape[0] * kv.shape[1] * kv.shape[2]
+    keys = sum(kv.shape[0] * kv.shape[1] for kv in kvs)
     whole = pl.BlockSpec(memory_space=pltpu.VMEM)
     return pl.pallas_call(
         functools.partial(attention_kernel, head_size),
         out_shape=jax.ShapeDtypeStruct((rows, width), queries.dtype),
-        in_specs=[pl.BlockSpec(memory_space=pltpu.SMEM), whole, whole],
+        in_specs=[pl.BlockSpec(memory_space=pltpu.SMEM)] + [whole] * (1 + len(kvs)),
         out_specs=whole,
         scratch_shapes=[pltpu.VMEM((heads, head_size, rows), jnp.float32)],
         compiler_params=pltpu.CompilerParams(vmem_limit_bytes=48 * 1024 * 1024),
@@ -82,19 +86,39 @@
             flops=4 * rows * width * keys, bytes_accessed=4 * rows * width + 4 * keys * head_size,
             transcendentals=rows * heads * keys,
         ),
-    )(lengths, queries, kv)
+    )(lengths, queries, *kvs)
+
+
+RADIX = 8
+
+
+def earlier_blocks(block, axis):
+    size = lax.axis_size(axis)
+    held = block[None]
+    while held.shape[0] < size:
+        count = held.shape[0]
+        moved = [held]
+        for step in range(1, RADIX):
+            shift = step * count
+            if shift < size:
+                moved.append(lax.ppermute(held, axis, [(i, i + shift) for i in range(size - shift)]))
+        held = jnp.concatenate(moved, axis=0)
+    return held[:size]
 
 
 def body(queries, key_rows, value_rows, document_lengths):
     seqs, rows, width = queries.shape
     piece_rows, head_size = key_rows.shape[1:]
+    pieces = lax.axis_size("head")
     results = []
     for seq in range(seqs):
         kv = jnp.concatenate([key_rows[seq], value_rows[seq]], axis=1)
-        kv = lax.all_gather(kv, "ctx", axis=0)
-        kv = lax.all_gather(kv, "head", axis=0)
+        kv = earlier_blocks(kv, "ctx")
+        kvs = [kv]
+        for shift in range(1, pieces):
+            kvs.append(lax.ppermute(kv, "head", [(i, (i + shift) % pieces) for i in range(pieces)]))
         lengths = document_lengths[seq : seq + 1]
-        results.append(attend(queries[seq], kv, lengths, head_size))
+        results.append(attend(queries[seq], kvs, lengths, head_size))
     return jnp.stack(results)
 
 

time: 78 us -> 50.5 us (0.65)
  the two profiles are of different devices: /device:TPU:25 before, /device:TPU:16 now
where the time goes in v2:
time: 50.5 us; the launch traced here: 51.2 us
  waiting for transfers between devices  29.2 us (58%)
  starting transfers between devices  13.1 us (26%)
  Pallas kernels  7.96 us (16%)
  other arithmetic  0.8 us (2%)
    ppermute x7, waiting for transfers between devices, earlier_blocks(): lax.ppermute(held, axis, [(i, i + shift) for i in range(size - shift)])  16.6 us
    ppermute x3, waiting for transfers between devices, body(): lax.ppermute(kv, 'head', [(i, (i + shift) % pieces) for i in range(pieces)])  12.5 us
    ppermute x7, starting transfers between devices, earlier_blocks(): lax.ppermute(held, axis, [(i, i + shift) for i in range(size - shift)])  11.3 us
    pallas_call x1, Pallas kernels, attend(): pl.pallas_call(functools.partial(attention_kernel, head_size), out_shape=...  7.96 us
    ppermute x3, starting transfers between devices, body(): lax.ppermute(kv, 'head', [(i, (i + shift) % pieces) for i in range(pieces)])  1.81 us
  transfers between devices with their start and end apart: 10, of which 6 were waited for; matrix products, arithmetic and copies ran while one was open for 0% of the time, Pallas kernels for 0%

profile of v2, /device:TPU:16, one launch (start us, length us, event | category | flops | bytes accessed | tf_op | source)
XLA Modules:
  0.0 51.2 jit_solution(9186739537293866962)
XLA Ops:
  0.0 0.0 copy-start.2
  0.0 0.0 copy-start.3
  0.0 0.8 %maximum_bitcast_fusion = bf16[1,64,256]{2,1,0:T(8,128)(2,1)S(1)} fusion(bf16[64,128]{1,0:T(8,128)(2,1)} %bitcast.9, bf16[64,128]{1,0:T(8,128)(2,1)} %bitcast.11), kind=kLoop, calls=%fused_computation | loop fusion | flops 65536 | bytes 65536 | tf_op jit(solution)/shard_map/broadcast_in_dim | solution.py:97
  0.8 0.0 copy-start
  0.8 0.8 %collective-permute-start.6 = (bf16[1,64,256]{2,1,0:T(8,128)(2,1)S(1)}, bf16[1,64,256]{2,1,0:T(8,128)(2,1)S(1)}, u32[]{:S(2)}, u32[]{:S(2)}) collective-permute-start(bf16[1,64,256]{2,1,0:T(8,128)(2,1)S(1)} %maximum_bitcast_fusion), channel_id=1, source_target_pairs={{0,28},{1,29},{2,30},{3,31}} | collective-permute-start | bytes 98312 | tf_op jit(solution)/shard_map/ppermute | solution.py:104
  1.6 0.7 %collective-permute-start.5 = (bf16[1,64,256]{2,1,0:T(8,128)(2,1)S(1)}, bf16[1,64,256]{2,1,0:T(8,128)(2,1)S(1)}, u32[]{:S(2)}, u32[]{:S(2)}) collective-permute-start(bf16[1,64,256]{2,1,0:T(8,128)(2,1)S(1)} %maximum_bitcast_fusion), channel_id=1, source_target_pairs={{0,24},{4,28},{1,25},{5,29},{2,26},{6,30},{3,27},{7,31}} | collective-permute-start | bytes 98312 | tf_op jit(solution)/shard_map/ppermute | solution.py:104
  2.3 0.7 %collective-permute-start.4 = (bf16[1,64,256]{2,1,0:T(8,128)(2,1)S(1)}, bf16[1,64,256]{2,1,0:T(8,128)(2,1)S(1)}, u32[]{:S(2)}, u32[]{:S(2)}) collective-permute-start(bf16[1,64,256]{2,1,0:T(8,128)(2,1)S(1)} %maximum_bitcast_fusion), channel_id=1, source_target_pairs={{0,20},{4,24},{8,28},{1,21},{5,25},{9,29},{2,22},{6,26},{10,30},{3... | collective-permute-start | bytes 98312 | tf_op jit(solution)/shard_map/ppermute | solution.py:104
  2.9 1.3 %collective-permute-start.3 = (bf16[1,64,256]{2,1,0:T(8,128)(2,1)S(1)}, bf16[1,64,256]{2,1,0:T(8,128)(2,1)S(1)}, u32[]{:S(2)}, u32[]{:S(2)}) collective-permute-start(bf16[1,64,256]{2,1,0:T(8,128)(2,1)S(1)} %maximum_bitcast_fusion), channel_id=1, source_target_pairs={{0,16},{4,20},{8,24},{12,28},{1,17},{5,21},{9,25},{13,29},{2,18},{... | collective-permute-start | bytes 98312 | tf_op jit(solution)/shard_map/ppermute | solution.py:104
  4.2 4.0 %collective-permute-start = (bf16[1,64,256]{2,1,0:T(8,128)(2,1)S(1)}, bf16[1,64,256]{2,1,0:T(8,128)(2,1)S(1)}, u32[]{:S(2)}, u32[]{:S(2)}) collective-permute-start(bf16[1,64,256]{2,1,0:T(8,128)(2,1)S(1)} %maximum_bitcast_fusion), channel_id=1, source_target_pairs={{0,4},{4,8},{8,12},{12,16},{16,20},{20,24},{24,28},{1,5},{5,9},{9,... | collective-permute-start | bytes 98312 | tf_op jit(solution)/shard_map/ppermute | solution.py:104
  8.3 0.0 copy-done.2
  8.3 0.0 copy-done.3
  8.3 6.2 %collective-permute-done = bf16[1,64,256]{2,1,0:T(8,128)(2,1)S(1)} collective-permute-done((bf16[1,64,256]{2,1,0:T(8,128)(2,1)S(1)}, bf16[1,64,256]{2,1,0:T(8,128)(2,1)S(1)}, u32[]{:S(2)}, u32[]{:S(2)}) %collective-permute-start) | collective-permute-done | bytes 32800 | tf_op jit(solution)/shard_map/ppermute | solution.py:104
  14.5 1.9 %collective-permute-start.1 = (bf16[1,64,256]{2,1,0:T(8,128)(2,1)S(1)}, bf16[1,64,256]{2,1,0:T(8,128)(2,1)S(1)}, u32[]{:S(2)}, u32[]{:S(2)}) collective-permute-start(bf16[1,64,256]{2,1,0:T(8,128)(2,1)S(1)} %maximum_bitcast_fusion), channel_id=1, source_target_pairs={{0,8},{4,12},{8,16},{12,20},{16,24},{20,28},{1,9},{5,13},{9,17},{1... | collective-permute-start | bytes 98312 | tf_op jit(solution)/shard_map/ppermute | solution.py:104
  16.4 4.8 %collective-permute-done.1 = bf16[1,64,256]{2,1,0:T(8,128)(2,1)S(1)} collective-permute-done((bf16[1,64,256]{2,1,0:T(8,128)(2,1)S(1)}, bf16[1,64,256]{2,1,0:T(8,128)(2,1)S(1)}, u32[]{:S(2)}, u32[]{:S(2)}) %collective-permute-start.1) | collective-permute-done | bytes 32800 | tf_op jit(solution)/shard_map/ppermute | solution.py:104
  21.2 1.9 %collective-permute-start.2 = (bf16[1,64,256]{2,1,0:T(8,128)(2,1)S(1)}, bf16[1,64,256]{2,1,0:T(8,128)(2,1)S(1)}, u32[]{:S(2)}, u32[]{:S(2)}) collective-permute-start(bf16[1,64,256]{2,1,0:T(8,128)(2,1)S(1)} %maximum_bitcast_fusion), channel_id=1, source_target_pairs={{0,12},{4,16},{8,20},{12,24},{16,28},{1,13},{5,17},{9,21},{13,25},... | collective-permute-start | bytes 98312 | tf_op jit(solution)/shard_map/ppermute | solution.py:104
  23.1 5.7 %collective-permute-done.2 = bf16[1,64,256]{2,1,0:T(8,128)(2,1)S(1)} collective-permute-done((bf16[1,64,256]{2,1,0:T(8,128)(2,1)S(1)}, bf16[1,64,256]{2,1,0:T(8,128)(2,1)S(1)}, u32[]{:S(2)}, u32[]{:S(2)}) %collective-permute-start.2) | collective-permute-done | bytes 32800 | tf_op jit(solution)/shard_map/ppermute | solution.py:104
  28.8 0.0 collective-permute-done.3
  28.8 0.0 collective-permute-done.4
  28.8 0.0 collective-permute-done.5
  28.9 0.0 collective-permute-done.6
  28.9 0.0 copy-start.1
  28.9 0.1 collective-permute-start.9
  29.0 1.6 %collective-permute-start.8 = (bf16[8,64,256]{2,1,0:T(8,128)(2,1)S(1)}, bf16[8,64,256]{2,1,0:T(8,128)(2,1)S(1)}, u32[]{:S(2)}, u32[]{:S(2)}) collective-permute-start(bf16[8,64,256]{2,1,0:T(8,128)(2,1)S(1)} %constant_dynamic-update-slice_fusion.refs_0_), channel_id=1, source_target_pairs={{0,2},{1,3},{2,0},{3,1},{4,6},{5,7},{6,4},{7,5},{8,10},{9,11},{10,... | collective-permute-start | bytes 786440 | tf_op jit(solution)/shard_map/ppermute | solution.py:119
  30.5 0.2 collective-permute-start.7
  30.7 3.9 %collective-permute-done.9.refs_3_ = bf16[8,64,256]{2,1,0:T(8,128)(2,1)S(1)} collective-permute-done((bf16[8,64,256]{2,1,0:T(8,128)(2,1)S(1)}, bf16[8,64,256]{2,1,0:T(8,128)(2,1)S(1)}, u32[]{:S(2)}, u32[]{:S(2)}) %collective-permute-start.9) | collective-permute-done | bytes 262176 | tf_op jit(solution)/shard_map/ppermute | solution.py:119
  34.6 8.6 %collective-permute-done.8.refs_2_ = bf16[8,64,256]{2,1,0:T(8,128)(2,1)S(1)} collective-permute-done((bf16[8,64,256]{2,1,0:T(8,128)(2,1)S(1)}, bf16[8,64,256]{2,1,0:T(8,128)(2,1)S(1)}, u32[]{:S(2)}, u32[]{:S(2)}) %collective-permute-start.8) | collective-permute-done | bytes 262176 | tf_op jit(solution)/shard_map/ppermute | solution.py:119
  43.2 0.1 collective-permute-done.7.refs_1_
  43.2 0.0 copy-done
  43.2 0.0 copy-done.1
  43.2 8.0 %shard_map.46 = bf16[256,512]{1,0:T(8,128)(2,1)} custom-call(s32[1,4]{1,0:T(1,128)S(1)} %copy-done.1, bf16[256,512]{1,0:T(8,128)(2,1)S(1)} %bitcast.8, bf16[8,64,256]{2,1,0:T(8,128)(2,1)S(1)} %constant_dynamic-update-slice_fusion.refs_0_, bf16[8,64,256]{2,1,0:T(8,128)(2,1)S(1)} %collective-permute-done.7.refs_1_, ...), custom_call_target="tpu_custom_call" | custom-call | flops 1073741824 | bytes 1572864 | tf_op jit(solution)/shard_map/pallas_call | solution.py:78
  (8 shorter events, 0.0 us)
Async XLA Ops:
  0.0 8.3 %copy-start.2 = (bf16[1,64,128]{2,1,0:T(8,128)(2,1)S(1)}, bf16[1,64,128]{2,1,0:T(8,128)(2,1)}, u32[]{:S(2)}) copy-start(bf16[1,64,128]{2,1,0:T(8,128)(2,1)} %param.6) | copy-start | bytes 49156
  0.0 8.3 %copy-start.3 = (bf16[1,64,128]{2,1,0:T(8,128)(2,1)S(1)}, bf16[1,64,128]{2,1,0:T(8,128)(2,1)}, u32[]{:S(2)}) copy-start(bf16[1,64,128]{2,1,0:T(8,128)(2,1)} %param.5) | copy-start | bytes 49156
  0.8 42.4 %copy-start = (bf16[1,256,512]{2,1,0:T(8,128)(2,1)S(1)}, bf16[1,256,512]{2,1,0:T(8,128)(2,1)}, u32[]{:S(2)}) copy-start(bf16[1,256,512]{2,1,0:T(8,128)(2,1)} %param.4) | copy-start | bytes 786436
  0.8 28.1 %collective-permute-start.6 = (bf16[1,64,256]{2,1,0:T(8,128)(2,1)S(1)}, bf16[1,64,256]{2,1,0:T(8,128)(2,1)S(1)}, u32[]{:S(2)}, u32[]{:S(2)}) collective-permute-start(bf16[1,64,256]{2,1,0:T(8,128)(2,1)S(1)} %maximum_bitcast_fusion), channel_id=1, source_target_pairs={{0,28},{1,29},{2,30},{3,31}} | collective-permute-start | bytes 98312 | tf_op jit(solution)/shard_map/ppermute | solution.py:104
  1.6 27.2 %collective-permute-start.5 = (bf16[1,64,256]{2,1,0:T(8,128)(2,1)S(1)}, bf16[1,64,256]{2,1,0:T(8,128)(2,1)S(1)}, u32[]{:S(2)}, u32[]{:S(2)}) collective-permute-start(bf16[1,64,256]{2,1,0:T(8,128)(2,1)S(1)} %maximum_bitcast_fusion), channel_id=1, source_target_pairs={{0,24},{4,28},{1,25},{5,29},{2,26},{6,30},{3,27},{7,31}} | collective-permute-start | bytes 98312 | tf_op jit(solution)/shard_map/ppermute | solution.py:104
  2.3 26.5 %collective-permute-start.4 = (bf16[1,64,256]{2,1,0:T(8,128)(2,1)S(1)}, bf16[1,64,256]{2,1,0:T(8,128)(2,1)S(1)}, u32[]{:S(2)}, u32[]{:S(2)}) collective-permute-start(bf16[1,64,256]{2,1,0:T(8,128)(2,1)S(1)} %maximum_bitcast_fusion), channel_id=1, source_target_pairs={{0,20},{4,24},{8,28},{1,21},{5,25},{9,29},{2,22},{6,26},{10,30},{3... | collective-permute-start | bytes 98312 | tf_op jit(solution)/shard_map/ppermute | solution.py:104
  2.9 25.9 %collective-permute-start.3 = (bf16[1,64,256]{2,1,0:T(8,128)(2,1)S(1)}, bf16[1,64,256]{2,1,0:T(8,128)(2,1)S(1)}, u32[]{:S(2)}, u32[]{:S(2)}) collective-permute-start(bf16[1,64,256]{2,1,0:T(8,128)(2,1)S(1)} %maximum_bitcast_fusion), channel_id=1, source_target_pairs={{0,16},{4,20},{8,24},{12,28},{1,17},{5,21},{9,25},{13,29},{2,18},{... | collective-permute-start | bytes 98312 | tf_op jit(solution)/shard_map/ppermute | solution.py:104
  4.2 10.3 %collective-permute-start = (bf16[1,64,256]{2,1,0:T(8,128)(2,1)S(1)}, bf16[1,64,256]{2,1,0:T(8,128)(2,1)S(1)}, u32[]{:S(2)}, u32[]{:S(2)}) collective-permute-start(bf16[1,64,256]{2,1,0:T(8,128)(2,1)S(1)} %maximum_bitcast_fusion), channel_id=1, source_target_pairs={{0,4},{4,8},{8,12},{12,16},{16,20},{20,24},{24,28},{1,5},{5,9},{9,... | collective-permute-start | bytes 98312 | tf_op jit(solution)/shard_map/ppermute | solution.py:104
  14.5 6.7 %collective-permute-start.1 = (bf16[1,64,256]{2,1,0:T(8,128)(2,1)S(1)}, bf16[1,64,256]{2,1,0:T(8,128)(2,1)S(1)}, u32[]{:S(2)}, u32[]{:S(2)}) collective-permute-start(bf16[1,64,256]{2,1,0:T(8,128)(2,1)S(1)} %maximum_bitcast_fusion), channel_id=1, source_target_pairs={{0,8},{4,12},{8,16},{12,20},{16,24},{20,28},{1,9},{5,13},{9,17},{1... | collective-permute-start | bytes 98312 | tf_op jit(solution)/shard_map/ppermute | solution.py:104
  21.2 7.6 %collective-permute-start.2 = (bf16[1,64,256]{2,1,0:T(8,128)(2,1)S(1)}, bf16[1,64,256]{2,1,0:T(8,128)(2,1)S(1)}, u32[]{:S(2)}, u32[]{:S(2)}) collective-permute-start(bf16[1,64,256]{2,1,0:T(8,128)(2,1)S(1)} %maximum_bitcast_fusion), channel_id=1, source_target_pairs={{0,12},{4,16},{8,20},{12,24},{16,28},{1,13},{5,17},{9,21},{13,25},... | collective-permute-start | bytes 98312 | tf_op jit(solution)/shard_map/ppermute | solution.py:104
  28.9 14.4 %copy-start.1 = (s32[1,4]{1,0:T(1,128)S(1)}, s32[1,4]{1,0:T(1,128)}, u32[]{:S(2)}) copy-start(s32[1,4]{1,0:T(1,128)} %lengths_ref.1) | copy-start | bytes 52
  28.9 5.7 %collective-permute-start.9 = (bf16[8,64,256]{2,1,0:T(8,128)(2,1)S(1)}, bf16[8,64,256]{2,1,0:T(8,128)(2,1)S(1)}, u32[]{:S(2)}, u32[]{:S(2)}) collective-permute-start(bf16[8,64,256]{2,1,0:T(8,128)(2,1)S(1)} %constant_dynamic-update-slice_fusion.refs_0_), channel_id=1, source_target_pairs={{0,3},{1,0},{2,1},{3,2},{4,7},{5,4},{6,5},{7,6},{8,11},{9,8},{10,9... | collective-permute-start | bytes 786440 | tf_op jit(solution)/shard_map/ppermute | solution.py:119
  29.0 14.2 %collective-permute-start.8 = (bf16[8,64,256]{2,1,0:T(8,128)(2,1)S(1)}, bf16[8,64,256]{2,1,0:T(8,128)(2,1)S(1)}, u32[]{:S(2)}, u32[]{:S(2)}) collective-permute-start(bf16[8,64,256]{2,1,0:T(8,128)(2,1)S(1)} %constant_dynamic-update-slice_fusion.refs_0_), channel_id=1, source_target_pairs={{0,2},{1,3},{2,0},{3,1},{4,6},{5,7},{6,4},{7,5},{8,10},{9,11},{10,... | collective-permute-start | bytes 786440 | tf_op jit(solution)/shard_map/ppermute | solution.py:119
  30.5 12.7 %collective-permute-start.7 = (bf16[8,64,256]{2,1,0:T(8,128)(2,1)S(1)}, bf16[8,64,256]{2,1,0:T(8,128)(2,1)S(1)}, u32[]{:S(2)}, u32[]{:S(2)}) collective-permute-start(bf16[8,64,256]{2,1,0:T(8,128)(2,1)S(1)} %constant_dynamic-update-slice_fusion.refs_0_), channel_id=1, source_target_pairs={{0,1},{1,2},{2,3},{3,0},{4,5},{5,6},{6,7},{7,4},{8,9},{9,10},{10,1... | collective-permute-start | bytes 786440 | tf_op jit(solution)/shard_map/ppermute | solution.py:119

commit v3 on v1

--- a/solution.py
+++ b/solution.py
@@ -11,12 +11,13 @@
 NEG = -1e30
 
 
-def attention_kernel(head_size, lengths_ref, queries_ref, kv_ref, out_ref, accum_ref):
-    own = lax.axis_index("ctx")
+def attention_kernel(head_size, order, lengths_ref, queries_ref, *refs):
+    *kv_refs, out_ref, accum_ref = refs
+    own, piece = lax.axis_index("ctx"), lax.axis_index("head")
     rows, width = queries_ref.shape
     heads = width // head_size
-    pieces, _, piece_rows, _ = kv_ref.shape
-    block_rows = pieces * piece_rows
+    piece_rows = kv_refs[0].shape[2]
+    block_rows = len(order) * piece_rows
     slope = math.log2(math.e) / math.sqrt(head_size)
 
     query_pos = own * rows + lax.broadcasted_iota(jnp.int32, (1, rows), 1)
@@ -27,11 +28,13 @@
         end = end + lengths_ref[0, document]
         starts = jnp.where(query_pos >= end, end, starts)
         first = jnp.where(own * rows >= end, end, first)
+    in_piece = lax.broadcasted_iota(jnp.int32, (piece_rows, rows), 0)
+    in_block = jnp.concatenate([in_piece + (piece ^ i) * piece_rows for i in order], axis=0)
 
     def block_step(block, state, fresh):
-        kv = kv_ref[:, pl.ds(block, 1)].reshape(block_rows, 2 * head_size)
+        kv = jnp.concatenate([kv_ref[i, block] for kv_ref in kv_refs for i in range(kv_ref.shape[0])], axis=0)
         keys, values = kv[:, :head_size], kv[:, head_size:]
-        key_pos = block * block_rows + lax.broadcasted_iota(jnp.int32, (block_rows, rows), 0)
+        key_pos = block * block_rows + in_block
         valid = (key_pos >= starts) & (key_pos <= query_pos)
         new_state = []
         for head in range(heads):
@@ -66,15 +69,15 @@
         out_ref[:, head * head_size : (head + 1) * head_size] = mixed.T.astype(out_ref.dtype)
 
 
-def attend(queries, kv, lengths, head_size):
+def attend(queries, kvs, order, lengths, head_size):
     rows, width = queries.shape
     heads = width // head_size
-    keys = kv.shape[0] * kv.shape[1] * kv.shape[2]
+    keys = sum(math.prod(kv.shape[:3]) for kv in kvs)
     whole = pl.BlockSpec(memory_space=pltpu.VMEM)
     return pl.pallas_call(
-        functools.partial(attention_kernel, head_size),
+        functools.partial(attention_kernel, head_size, order),
         out_shape=jax.ShapeDtypeStruct((rows, width), queries.dtype),
-        in_specs=[pl.BlockSpec(memory_space=pltpu.SMEM), whole, whole],
+        in_specs=[pl.BlockSpec(memory_space=pltpu.SMEM)] + [whole] * (1 + len(kvs)),
         out_specs=whole,
         scratch_shapes=[pltpu.VMEM((heads, head_size, rows), jnp.float32)],
         compiler_params=pltpu.CompilerParams(vmem_limit_bytes=48 * 1024 * 1024),
@@ -82,7 +85,23 @@
             flops=4 * rows * width * keys, bytes_accessed=4 * rows * width + 4 * keys * head_size,
             transcendentals=rows * heads * keys,
         ),
-    )(lengths, queries, kv)
+    )(lengths, queries, *kvs)
+
+
+def all_blocks(block, axis):
+    size = lax.axis_size(axis)
+    return lax.all_to_all(jnp.broadcast_to(block, (size,) + block.shape), axis, 0, 0)
+
+
+def exchanged(piece, axis):
+    size = lax.axis_size(axis)
+    held, order = [piece[None]], [0]
+    bit = size // 2
+    while bit:
+        held.append(lax.ppermute(jnp.concatenate(held), axis, [(i, i ^ bit) for i in range(size)]))
+        order = order + [i ^ bit for i in order]
+        bit //= 2
+    return held, order
 
 
 def body(queries, key_rows, value_rows, document_lengths):
@@ -91,10 +110,9 @@
     results = []
     for seq in range(seqs):
         kv = jnp.concatenate([key_rows[seq], value_rows[seq]], axis=1)
-        kv = lax.all_gather(kv, "ctx", axis=0)
-        kv = lax.all_gather(kv, "head", axis=0)
+        kvs, order = exchanged(all_blocks(kv, "ctx"), "head")
         lengths = document_lengths[seq : seq + 1]
-        results.append(attend(queries[seq], kv, lengths, head_size))
+        results.append(attend(queries[seq], kvs, order, lengths, head_size))
     return jnp.stack(results)
 
 

time: 78 us -> 34 us (0.44)
  the two profiles are of different devices: /device:TPU:25 before, /device:TPU:27 now
where the time goes in v3:
time: 34 us; the launch traced here: 33.7 us
  blocking collectives  12 us (35%)
  Pallas kernels  10.6 us (31%)
  waiting for transfers between devices  7.07 us (21%)
  starting transfers between devices  3.25 us (10%)
  other arithmetic  0.79 us (2%)
    all_to_all x1, blocking collectives, all_blocks(): lax.all_to_all(jnp.broadcast_to(block, (size,) + block.shape), axis, 0, 0)  12 us
    pallas_call x1, Pallas kernels, attend(): pl.pallas_call(functools.partial(attention_kernel, head_size, order), out...  10.6 us
    ppermute x2, waiting for transfers between devices, exchanged(): lax.ppermute(jnp.concatenate(held), axis, [(i, i ^ bit) for i in range(si...  7.07 us
    ppermute x2, starting transfers between devices, exchanged(): lax.ppermute(jnp.concatenate(held), axis, [(i, i ^ bit) for i in range(si...  3.25 us
    concatenate x1, other arithmetic, body(): kv = jnp.concatenate([key_rows[seq], value_rows[seq]], axis=1)  0.74 us
  transfers between devices with their start and end apart: 2, of which 2 were waited for; matrix products, arithmetic and copies ran while one was open for 0% of the time, Pallas kernels for 0%

profile of v3, /device:TPU:27, one launch (start us, length us, event | category | flops | bytes accessed | tf_op | source)
XLA Modules:
  0.0 33.7 jit_solution(18224386656274506118)
XLA Ops:
  0.0 0.7 %pad_maximum_fusion.1 = bf16[64,256]{1,0:T(8,128)(2,1)S(1)} fusion(bf16[64,128]{1,0:T(8,128)(2,1)} %bitcast.9, bf16[64,128]{1,0:T(8,128)(2,1)} %bitcast.10), kind=kLoop, calls=%fused_computation.1 | loop fusion | flops 65536 | bytes 65536 | tf_op jit(solution)/shard_map/concatenate | solution.py:112
  0.8 12.0 %all_to_all.5 = bf16[8,64,256]{2,1,0:T(8,128)(2,1)S(1)} all-to-all(bf16[8,64,256]{2,1,0:T(8,128)(2,1)S(1)} %broadcast_in_dim.6), channel_id=1, replica_groups=mesh['ctx'=8,'head'=4] {'ctx'}, dimensions={0} | all-to-all | bytes 524288 | tf_op jit(solution)/shard_map/all_to_all | solution.py:93
  12.7 0.0 copy-start
  12.7 1.2 %collective-permute-start = (bf16[1,8,64,256]{3,2,1,0:T(8,128)(2,1)S(1)}, bf16[1,8,64,256]{3,2,1,0:T(8,128)(2,1)S(1)}, u32[]{:S(2)}, u32[]{:S(2)}) collective-permute-start(bf16[1,8,64,256]{3,2,1,0:T(8,128)(2,1)S(1)} %bitcast.5), channel_id=1, source_target_pairs={{0,2},{1,3},{2,0},{3,1},{4,6},{5,7},{6,4},{7,5},{8,10},{9,11},{10,... | collective-permute-start | bytes 786440 | tf_op jit(solution)/shard_map/ppermute | solution.py:101
  14.0 5.5 %collective-permute-done.refs_1_ = bf16[1,8,64,256]{3,2,1,0:T(8,128)(2,1)S(1)} collective-permute-done((bf16[1,8,64,256]{3,2,1,0:T(8,128)(2,1)S(1)}, bf16[1,8,64,256]{3,2,1,0:T(8,128)(2,1)S(1)}, u32[]{:S(2)}, u32[]{:S(2)}) %collective-permute-start) | collective-permute-done | bytes 262176 | tf_op jit(solution)/shard_map/ppermute | solution.py:101
  19.5 0.1 pad_maximum_fusion
  19.5 0.0 copy-start.1
  19.6 2.0 %collective-permute-start.1 = (bf16[2,8,64,256]{3,2,1,0:T(8,128)(2,1)S(1)}, bf16[2,8,64,256]{3,2,1,0:T(8,128)(2,1)S(1)}, u32[]{:S(2)}, u32[]{:S(2)}) collective-permute-start(bf16[2,8,64,256]{3,2,1,0:T(8,128)(2,1)S(1)} %pad_maximum_fusion), channel_id=1, source_target_pairs={{0,1},{1,0},{2,3},{3,2},{4,5},{5,4},{6,7},{7,6},{8,9},{9,8},{10,11... | collective-permute-start | bytes 1572872 | tf_op jit(solution)/shard_map/ppermute | solution.py:101
  21.6 1.5 %collective-permute-done.1.refs_2_ = bf16[2,8,64,256]{3,2,1,0:T(8,128)(2,1)S(1)} collective-permute-done((bf16[2,8,64,256]{3,2,1,0:T(8,128)(2,1)S(1)}, bf16[2,8,64,256]{3,2,1,0:T(8,128)(2,1)S(1)}, u32[]{:S(2)}, u32[]{:S(2)}) %collective-permute-start.1) | collective-permute-done | bytes 524320 | tf_op jit(solution)/shard_map/ppermute | solution.py:101
  23.1 0.0 copy-done
  23.1 0.0 copy-done.1
  23.1 10.6 %shard_map.46 = bf16[256,512]{1,0:T(8,128)(2,1)} custom-call(s32[1,4]{1,0:T(1,128)S(1)} %copy-done.1, bf16[256,512]{1,0:T(8,128)(2,1)S(1)} %bitcast.8, bf16[1,8,64,256]{3,2,1,0:T(8,128)(2,1)S(1)} %bitcast.7, bf16[1,8,64,256]{3,2,1,0:T(8,128)(2,1)S(1)} %collective-permute-done.refs_1_, bf16[2,8,64,256]{3,2,1,0:T(8,128)(2,1)S(1)} %collective-permute-done.1.refs_2_), custom_call_target="tpu_custom_call" | custom-call | flops 1073741824 | bytes 1572864 | tf_op jit(solution)/shard_map/pallas_call | solution.py:77
  (1 shorter events, 0.0 us)
Async XLA Ops:
  12.7 10.4 %copy-start = (bf16[1,256,512]{2,1,0:T(8,128)(2,1)S(1)}, bf16[1,256,512]{2,1,0:T(8,128)(2,1)}, u32[]{:S(2)}) copy-start(bf16[1,256,512]{2,1,0:T(8,128)(2,1)} %param.4) | copy-start | bytes 786436
  12.7 6.8 %collective-permute-start = (bf16[1,8,64,256]{3,2,1,0:T(8,128)(2,1)S(1)}, bf16[1,8,64,256]{3,2,1,0:T(8,128)(2,1)S(1)}, u32[]{:S(2)}, u32[]{:S(2)}) collective-permute-start(bf16[1,8,64,256]{3,2,1,0:T(8,128)(2,1)S(1)} %bitcast.5), channel_id=1, source_target_pairs={{0,2},{1,3},{2,0},{3,1},{4,6},{5,7},{6,4},{7,5},{8,10},{9,11},{10,... | collective-permute-start | bytes 786440 | tf_op jit(solution)/shard_map/ppermute | solution.py:101
  19.5 3.6 %copy-start.1 = (s32[1,4]{1,0:T(1,128)S(1)}, s32[1,4]{1,0:T(1,128)}, u32[]{:S(2)}) copy-start(s32[1,4]{1,0:T(1,128)} %lengths_ref.1) | copy-start | bytes 52
  19.6 3.5 %collective-permute-start.1 = (bf16[2,8,64,256]{3,2,1,0:T(8,128)(2,1)S(1)}, bf16[2,8,64,256]{3,2,1,0:T(8,128)(2,1)S(1)}, u32[]{:S(2)}, u32[]{:S(2)}) collective-permute-start(bf16[2,8,64,256]{3,2,1,0:T(8,128)(2,1)S(1)} %pad_maximum_fusion), channel_id=1, source_target_pairs={{0,1},{1,0},{2,3},{3,2},{4,5},{5,4},{6,7},{7,6},{8,9},{9,8},{10,11... | collective-permute-start | bytes 1572872 | tf_op jit(solution)/shard_map/ppermute | solution.py:101

commit v4 on v1

v4 whole, which is shorter than its diff:
```python
import functools
import math

import jax
import jax.numpy as jnp
from jax import lax
from jax.experimental import pallas as pl
from jax.experimental.pallas import tpu as pltpu
from jax.sharding import PartitionSpec as P

NEG = -1e30
STEP_BLOCKS = 8


def attention_kernel(head_size, place, first, last, lengths_ref, queries_ref, kv_ref, *refs):
    if first:
        old_stats_ref = old_sums_ref = None
    else:
        old_stats_ref, old_sums_ref, *refs = refs
    if last:
        out_ref, stats_ref, sums_ref = refs
    elif first:
        stats_ref, sums_ref, turned_ref = refs
    else:
        stats_ref, sums_ref = refs
    own, piece = lax.axis_index("ctx"), lax.axis_index("head") ^ place
    heads, _, rows = sums_ref.shape
    blocks, piece_rows, _ = kv_ref.shape
    slope = math.log2(math.e) / math.sqrt(head_size)
    step_blocks = math.gcd(blocks, STEP_BLOCKS)
    keys_a_step = step_blocks * piece_rows

    query_pos = own * rows + lax.broadcasted_iota(jnp.int32, (1, rows), 1)
    starts = jnp.zeros((1, rows), jnp.int32)
    first_key = jnp.int32(0)
    end = jnp.int32(0)
    for document in range(lengths_ref.shape[1]):
        end = end + lengths_ref[0, document]
        starts = jnp.where(query_pos >= end, end, starts)
        first_key = jnp.where(own * rows >= end, end, first_key)

    if first:
        for head in range(heads):
            turned_ref[head] = queries_ref[:, head * head_size : (head + 1) * head_size].T
        queries_ref = turned_ref
    in_block = piece * piece_rows + lax.broadcasted_iota(jnp.int32, (piece_rows, rows), 0)

    def step(start, old):
        kv = kv_ref[pl.ds(start, step_blocks)].reshape(keys_a_step, 2 * head_size)
        keys, values = kv[:, :head_size], kv[:, head_size:].T
        key_pos = jnp.concatenate([(start + i) * rows + in_block for i in range(step_blocks)], axis=0)
        valid = (key_pos >= starts) & (key_pos <= query_pos)
        scores = [
            jnp.where(valid, jnp.dot(keys, queries_ref[head], preferred_element_type=jnp.float32), NEG)
            for head in range(heads)
        ]
        tops, totals, sums = [], [], []
        for head in range(heads):
            top = jnp.max(scores[head], axis=0, keepdims=True)
            if old is not None:
                top = jnp.maximum(old[0][head], top)
            weights = jnp.exp2((scores[head] - top) * slope)
            total = jnp.sum(weights, axis=0, keepdims=True)
            mixed = jnp.dot(values, weights.astype(jnp.bfloat16), preferred_element_type=jnp.float32)
            if old is not None:
                factor = jnp.exp2((old[0][head] - top) * slope)
                total = old[1][head] * factor + total
                mixed = old[2][head] * factor + mixed
            tops.append(top)
            totals.append(total)
            sums.append(mixed)
        return tops, totals, sums

    def load(stats, sums):
        return (
            [stats[head : head + 1] for head in range(heads)],
            [stats[heads + head : heads + head + 1] for head in range(heads)],
            [sums[head] for head in range(heads)],
        )

    def store(state):
        tops, totals, sums = state
        stats_ref[...] = jnp.concatenate(tops + totals, axis=0)
        for head in range(heads):
            sums_ref[head] = sums[head]

    if blocks == step_blocks:
        state = step(0, None if first else load(old_stats_ref[...], old_sums_ref))
        if not last:
            store(state)
    else:
        if first:
            stats_ref[...] = jnp.concatenate([jnp.full((heads, rows), NEG), jnp.zeros((heads, rows))], axis=0)
            sums_ref[...] = jnp.zeros_like(sums_ref)
        else:
            stats_ref[...] = old_stats_ref[...]
            sums_ref[...] = old_sums_ref[...]

        @pl.loop(first_key // rows // step_blocks, own // step_blocks + 1)
        def _(index):
            store(step(index * step_blocks, load(stats_ref[...], sums_ref)))

        state = load(stats_ref[...], sums_ref)
    if last:
        _, totals, sums = state
        for head in range(heads):
            out_ref[:, head * head_size : (head + 1) * head_size] = (sums[head] / totals[head]).T.astype(out_ref.dtype)


def attend(place, first, last, lengths, queries, kv, state, heads):
    head_size = kv.shape[2] // 2
    rows = queries.shape[0] if first else queries.shape[2]
    keys = kv.shape[0] * kv.shape[1]
    stats = jax.ShapeDtypeStruct((2 * heads, rows), jnp.float32)
    sums = jax.ShapeDtypeStruct((heads, head_size, rows), jnp.float32)
    turned = jax.ShapeDtypeStruct((heads, head_size, rows), queries.dtype)
    whole = pl.BlockSpec(memory_space=pltpu.VMEM)
    scratch = []
    if last:
        out_shape = jax.ShapeDtypeStruct((rows, heads * head_size), queries.dtype)
        scratch = [pltpu.VMEM(stats.shape, stats.dtype), pltpu.VMEM(sums.shape, sums.dtype)]
    elif first:
        out_shape = (stats, sums, turned)
    else:
        out_shape = (stats, sums)
    return pl.pallas_call(
        functools.partial(attention_kernel, head_size, place, first, last),
        out_shape=out_shape,
        in_specs=[pl.BlockSpec(memory_space=pltpu.SMEM)] + [whole] * (2 + len(state)),
        out_specs=jax.tree.map(lambda _: whole, out_shape),
        scratch_shapes=scratch,
        compiler_params=pltpu.CompilerParams(vmem_limit_bytes=32 * 1024 * 1024),
        cost_estimate=pl.CostEstimate(
            flops=4 * rows * heads * head_size * keys,
            bytes_accessed=4 * keys * head_size + 16 * rows * heads * head_size,
            transcendentals=rows * heads * keys,
        ),
    )(lengths, queries, kv, *state)


def all_blocks(block, axis):
    size = lax.axis_size(axis)
    return lax.all_to_all(jnp.broadcast_to(block, (size,) + block.shape), axis, 0, 0)


def exchange(piece, axis, bit):
    return lax.ppermute(piece, axis, [(i, i ^ bit) for i in range(lax.axis_size(axis))])


def body(queries, key_rows, value_rows, document_lengths):
    seqs, rows, width = queries.shape
    heads = width // key_rows.shape[2]
    places = lax.axis_size("head")
    assert places in (1, 2, 4)
    results = []
    for seq in range(seqs):
        kv = jnp.concatenate([key_rows[seq], value_rows[seq]], axis=1)
        lengths = document_lengths[seq : seq + 1]
        state, turned = (), queries[seq]
        near = {0: all_blocks(kv, "ctx")}
        bit, left = 2, places
        while near:
            far = {place ^ bit: exchange(piece, "head", bit) for place, piece in near.items() if bit < places}
            near |= {place ^ 1: exchange(piece, "head", 1) for place, piece in near.items() if places > 1}
            for place, piece in near.items():
                first, last = left == places, left == 1
                result = attend(place, first, last, lengths, turned, piece, state, heads)
                left -= 1
                if last:
                    results.append(result)
                elif first:
                    *state, turned = result
                else:
                    state = result
            if far:
                far, state = lax.optimization_barrier((far, state))
            near = far
            bit *= 2
    return jnp.stack(results)


def solution(mesh):
    in_specs = (
        P(None, "ctx", "head"),
        P(None, ("ctx", "head"), None),
        P(None, ("ctx", "head"), None),
        P(),
    )
    out_specs = P(None, "ctx", "head")
    return jax.shard_map(body, mesh=mesh, in_specs=in_specs, out_specs=out_specs, check_vma=False)
```

time: 78 us -> 30.1 us (0.39)
  the two profiles are of different devices: /device:TPU:25 before, /device:TPU:0 now
where the time goes in v4:
time: 30.1 us; the launch traced here: 29.7 us
  blocking collectives  16.1 us (53%)
  Pallas kernels  7.36 us (24%)
  waiting for transfers between devices  3.89 us (13%)
  starting transfers between devices  1.53 us (5%)
  other arithmetic  0.74 us (2%)
    all_to_all x1, blocking collectives, all_blocks(): lax.all_to_all(jnp.broadcast_to(block, (size,) + block.shape), axis, 0, 0)  16.1 us
    pallas_call x4, Pallas kernels, attend(): pl.pallas_call(functools.partial(attention_kernel, head_size, place, firs...  7.36 us
    ppermute x3, waiting for transfers between devices, exchange(): lax.ppermute(piece, axis, [(i, i ^ bit) for i in range(lax.axis_size(axis...  3.89 us
    ppermute x3, starting transfers between devices, exchange(): lax.ppermute(piece, axis, [(i, i ^ bit) for i in range(lax.axis_size(axis...  1.53 us
    concatenate x1, other arithmetic, body(): kv = jnp.concatenate([key_rows[seq], value_rows[seq]], axis=1)  0.74 us
  transfers between devices with their start and end apart: 3, of which 1 were waited for; matrix products, arithmetic and copies ran while one was open for 0% of the time, Pallas kernels for 17%

profile of v4, /device:TPU:0, one launch (start us, length us, event | category | flops | bytes accessed | tf_op | source)
XLA Modules:
  0.0 29.7 jit_solution(8014216726494983443)
XLA Ops:
  0.0 0.7 %pad_maximum_fusion = bf16[64,256]{1,0:T(8,128)(2,1)S(1)} fusion(bf16[64,128]{1,0:T(8,128)(2,1)} %bitcast.5, bf16[64,128]{1,0:T(8,128)(2,1)} %bitcast.6), kind=kLoop, calls=%fused_computation | loop fusion | flops 65536 | bytes 65536 | tf_op jit(solution)/shard_map/concatenate | solution.py:157
  0.8 0.0 copy-start.1
  0.8 16.1 %all_to_all.5.kv_ref = bf16[8,64,256]{2,1,0:T(8,128)(2,1)S(1)} all-to-all(bf16[8,64,256]{2,1,0:T(8,128)(2,1)S(1)} %broadcast_in_dim.3), channel_id=1, replica_groups=mesh['ctx'=8,'head'=4] {'ctx'}, dimensions={0} | all-to-all | bytes 524288 | tf_op jit(solution)/shard_map/all_to_all | solution.py:143
  16.9 0.0 copy-start
  16.9 0.0 collective-permute-start.1
  16.9 1.5 %collective-permute-start = (bf16[8,64,256]{2,1,0:T(8,128)(2,1)S(1)}, bf16[8,64,256]{2,1,0:T(8,128)(2,1)S(1)}, u32[]{:S(2)}, u32[]{:S(2)}) collective-permute-start(bf16[8,64,256]{2,1,0:T(8,128)(2,1)S(1)} %all_to_all.5.kv_ref), channel_id=1, source_target_pairs={{0,2},{1,3},{2,0},{3,1},{4,6},{5,7},{6,4},{7,5},{8,10},{9,11},{10,... | collective-permute-start | bytes 786440 | tf_op jit(solution)/shard_map/ppermute | solution.py:147
  18.4 0.0 copy-done.1
  18.4 0.0 copy-done
  18.4 1.6 %shard_map.46 = (f32[8,256]{1,0:T(8,128)S(1)}, f32[4,128,256]{2,1,0:T(8,128)S(1)}, bf16[4,128,256]{2,1,0:T(8,128)(2,1)S(1)}) custom-call(s32[1,4]{1,0:T(1,128)S(1)} %copy-done, bf16[256,512]{1,0:T(8,128)(2,1)S(1)} %bitcast.4, bf16[8,64,256]{2,1,0:T(8,128)(2,1)S(1)} %all_to_all.5.kv_ref), custom_call_target="tpu_custom_call" | custom-call | flops 268435456 | bytes 2359296 | tf_op jit(solution)/shard_map/pallas_call | solution.py:126
  20.1 0.0 collective-permute-done.1.kv_ref
  20.1 1.6 %shard_map.47 = (f32[8,256]{1,0:T(8,128)S(1)}, f32[4,128,256]{2,1,0:T(8,128)S(1)}) custom-call(s32[1,4]{1,0:T(1,128)S(1)} %copy-done, bf16[4,128,256]{2,1,0:T(8,128)(2,1)S(1)} %get-tuple-element.15.queries_ref, bf16[8,64,256]{2,1,0:T(8,128)(2,1)S(1)} %collective-permute-done.1.kv_ref, f32[8,256]{1,0:T(8,128)S(1)} %get-tuple-element.16.refs_0_, ...), custom_call_target="tpu_custom_call" | custom-call | flops 268435456 | bytes 2359296 | tf_op jit(solution)/shard_map/pallas_call | solution.py:126
  21.7 3.9 %collective-permute-done.kv_ref = bf16[8,64,256]{2,1,0:T(8,128)(2,1)S(1)} collective-permute-done((bf16[8,64,256]{2,1,0:T(8,128)(2,1)S(1)}, bf16[8,64,256]{2,1,0:T(8,128)(2,1)S(1)}, u32[]{:S(2)}, u32[]{:S(2)}) %collective-permute-start) | collective-permute-done | bytes 262176 | tf_op jit(solution)/shard_map/ppermute | solution.py:147
  25.6 0.0 collective-permute-start.2
  25.6 1.6 %shard_map.48 = (f32[8,256]{1,0:T(8,128)S(1)}, f32[4,128,256]{2,1,0:T(8,128)S(1)}) custom-call(s32[1,4]{1,0:T(1,128)S(1)} %copy-done, bf16[4,128,256]{2,1,0:T(8,128)(2,1)S(1)} %get-tuple-element.15.queries_ref, bf16[8,64,256]{2,1,0:T(8,128)(2,1)S(1)} %collective-permute-done.kv_ref, f32[8,256]{1,0:T(8,128)S(1)} %get-tuple-element.21.refs_0_, ...), custom_call_target="tpu_custom_call" | custom-call | flops 268435456 | bytes 2359296 | tf_op jit(solution)/shard_map/pallas_call | solution.py:126
  27.3 0.0 collective-permute-done.2.kv_ref
  27.3 2.4 %shard_map.49 = bf16[256,512]{1,0:T(8,128)(2,1)} custom-call(s32[1,4]{1,0:T(1,128)S(1)} %copy-done, bf16[4,128,256]{2,1,0:T(8,128)(2,1)S(1)} %get-tuple-element.15.queries_ref, bf16[8,64,256]{2,1,0:T(8,128)(2,1)S(1)} %collective-permute-done.2.kv_ref, f32[8,256]{1,0:T(8,128)S(1)} %get-tuple-element.23.refs_0_, f32[4,128,256]{2,1,0:T(8,128)S(1)} %get-tuple-element.24.refs_1_), custom_call_target="tpu_custom_call" | custom-call | flops 268435456 | bytes 2359296 | tf_op jit(solution)/shard_map/pallas_call | solution.py:126
  (1 shorter events, 0.0 us)
Async XLA Ops:
  0.8 17.6 %copy-start.1 = (bf16[1,256,512]{2,1,0:T(8,128)(2,1)S(1)}, bf16[1,256,512]{2,1,0:T(8,128)(2,1)}, u32[]{:S(2)}) copy-start(bf16[1,256,512]{2,1,0:T(8,128)(2,1)} %param.4) | copy-start | bytes 786436
  16.9 1.5 %copy-start = (s32[1,4]{1,0:T(1,128)S(1)}, s32[1,4]{1,0:T(1,128)}, u32[]{:S(2)}) copy-start(s32[1,4]{1,0:T(1,128)} %lengths_ref.7) | copy-start | bytes 52
  16.9 3.2 %collective-permute-start.1 = (bf16[8,64,256]{2,1,0:T(8,128)(2,1)S(1)}, bf16[8,64,256]{2,1,0:T(8,128)(2,1)S(1)}, u32[]{:S(2)}, u32[]{:S(2)}) collective-permute-start(bf16[8,64,256]{2,1,0:T(8,128)(2,1)S(1)} %all_to_all.5.kv_ref), channel_id=1, source_target_pairs={{0,1},{1,0},{2,3},{3,2},{4,5},{5,4},{6,7},{7,6},{8,9},{9,8},{10,11... | collective-permute-start | bytes 786440 | tf_op jit(solution)/shard_map/ppermute | solution.py:147
  16.9 8.7 %collective-permute-start = (bf16[8,64,256]{2,1,0:T(8,128)(2,1)S(1)}, bf16[8,64,256]{2,1,0:T(8,128)(2,1)S(1)}, u32[]{:S(2)}, u32[]{:S(2)}) collective-permute-start(bf16[8,64,256]{2,1,0:T(8,128)(2,1)S(1)} %all_to_all.5.kv_ref), channel_id=1, source_target_pairs={{0,2},{1,3},{2,0},{3,1},{4,6},{5,7},{6,4},{7,5},{8,10},{9,11},{10,... | collective-permute-start | bytes 786440 | tf_op jit(solution)/shard_map/ppermute | solution.py:147
  25.6 1.7 %collective-permute-start.2 = (bf16[8,64,256]{2,1,0:T(8,128)(2,1)S(1)}, bf16[8,64,256]{2,1,0:T(8,128)(2,1)S(1)}, u32[]{:S(2)}, u32[]{:S(2)}) collective-permute-start(bf16[8,64,256]{2,1,0:T(8,128)(2,1)S(1)} %collective-permute-done.kv_ref), channel_id=1, source_target_pairs={{0,1},{1,0},{2,3},{3,2},{4,5},{5,4},{6,7},{7,6},{8,9},{9,8},{10,11... | collective-permute-start | bytes 786440 | tf_op jit(solution)/shard_map/ppermute | solution.py:147

commit v5 on v4

v5 whole, which is shorter than its diff:
```python
import functools
import math

import jax
import jax.numpy as jnp
from jax import lax
from jax.experimental import pallas as pl
from jax.experimental.pallas import tpu as pltpu
from jax.sharding import PartitionSpec as P

NEG = -1e30
DIGIT = 8


def attention_kernel(head_size, parts, step_blocks, first, last, lengths_ref, queries_ref, *refs):
    kv_refs, refs = refs[: len(parts)], refs[len(parts) :]
    if first:
        stats_ref, sums_ref, turned_ref = refs
        old_stats_ref, old_sums_ref = stats_ref, sums_ref
    elif last:
        old_stats_ref, old_sums_ref, out_ref = refs
    else:
        old_stats_ref, old_sums_ref, stats_ref, sums_ref = refs
    own = lax.axis_index("ctx")
    heads, _, rows = old_sums_ref.shape
    entries, piece_rows, _ = kv_refs[0].shape
    slope = math.log2(math.e) / math.sqrt(head_size)

    query_pos = own * rows + lax.broadcasted_iota(jnp.int32, (1, rows), 1)
    starts = jnp.zeros((1, rows), jnp.int32)
    first_key = jnp.int32(0)
    end = jnp.int32(0)
    for document in range(lengths_ref.shape[1]):
        end = end + lengths_ref[0, document]
        starts = jnp.where(query_pos >= end, end, starts)
        first_key = jnp.where(own * rows >= end, end, first_key)

    if first:
        for head in range(heads):
            turned_ref[head] = queries_ref[:, head * head_size : (head + 1) * head_size].T
        queries_ref = turned_ref
    in_piece = lax.broadcasted_iota(jnp.int32, (piece_rows, rows), 0)

    def step(index, old):
        kv, key_pos = [], []
        for kv_ref, (place, start) in zip(kv_refs, parts):
            in_block = (lax.axis_index("head") ^ place) * piece_rows + in_piece
            kv.append(kv_ref[pl.ds(index * step_blocks, step_blocks)].reshape(step_blocks * piece_rows, 2 * head_size))
            key_pos += [(own ^ (start + index * step_blocks + i)) * rows + in_block for i in range(step_blocks)]
        kv = jnp.concatenate(kv, axis=0)
        key_pos = jnp.concatenate(key_pos, axis=0)
        keys, values = kv[:, :head_size], kv[:, head_size:].T
        valid = (key_pos >= starts) & (key_pos <= query_pos)
        scores = [
            jnp.where(valid, jnp.dot(keys, queries_ref[head], preferred_element_type=jnp.float32), NEG)
            for head in range(heads)
        ]
        tops, totals, sums = [], [], []
        for head in range(heads):
            top = jnp.max(scores[head], axis=0, keepdims=True)
            if old is not None:
                top = jnp.maximum(old[0][head], top)
            weights = jnp.exp2((scores[head] - top) * slope)
            total = jnp.sum(weights, axis=0, keepdims=True)
            mixed = jnp.dot(values, weights.astype(jnp.bfloat16), preferred_element_type=jnp.float32)
            if old is not None:
                factor = jnp.exp2((old[0][head] - top) * slope)
                total = old[1][head] * factor + total
                mixed = old[2][head] * factor + mixed
            tops.append(top)
            totals.append(total)
            sums.append(mixed)
        return tops, totals, sums

    def load(stats, sums):
        return (
            [stats[head : head + 1] for head in range(heads)],
            [stats[heads + head : heads + head + 1] for head in range(heads)],
            [sums[head] for head in range(heads)],
        )

    def store(state):
        tops, totals, sums = state
        if last:
            for head in range(heads):
                result = (sums[head] * (1.0 / totals[head])).astype(out_ref.dtype)
                out_ref[:, head * head_size : (head + 1) * head_size] = result.T
        else:
            stats_ref[...] = jnp.concatenate(tops + totals, axis=0)
            for head in range(heads):
                sums_ref[head] = sums[head]

    def needed(index):
        group = (own ^ (parts[0][1] + index * step_blocks)) // step_blocks
        return (group <= own // step_blocks) & (group >= first_key // rows // step_blocks)

    def step_or_skip(index, state):
        return lax.cond(needed(index), lambda: step(index, state), lambda: state)

    steps = entries // step_blocks
    if first:
        state = step(0, None)
    else:
        state = load(old_stats_ref[...], old_sums_ref)
        state = step_or_skip(0, state)
    if steps == 2:
        state = step_or_skip(1, state)
    elif steps > 2:
        state = lax.fori_loop(1, steps, step_or_skip, state)
    store(state)


def attend(parts, step_blocks, first, last, lengths, queries, kvs, state, heads):
    head_size = kvs[0].shape[2] // 2
    rows = queries.shape[0] if first else queries.shape[2]
    keys = sum(kv.shape[0] * kv.shape[1] for kv in kvs)
    stats = jax.ShapeDtypeStruct((2 * heads, rows), jnp.float32)
    sums = jax.ShapeDtypeStruct((heads, head_size, rows), jnp.float32)
    turned = jax.ShapeDtypeStruct((heads, head_size, rows), queries.dtype)
    whole = pl.BlockSpec(memory_space=pltpu.VMEM)
    if last:
        out_shape = jax.ShapeDtypeStruct((rows, heads * head_size), queries.dtype)
    elif first:
        out_shape = (stats, sums, turned)
    else:
        out_shape = (stats, sums)
    return pl.pallas_call(
        functools.partial(attention_kernel, head_size, parts, step_blocks, first, last),
        out_shape=out_shape,
        in_specs=[pl.BlockSpec(memory_space=pltpu.SMEM)] + [whole] * (1 + len(kvs) + len(state)),
        out_specs=jax.tree.map(lambda _: whole, out_shape),
        compiler_params=pltpu.CompilerParams(vmem_limit_bytes=32 * 1024 * 1024),
        cost_estimate=pl.CostEstimate(
            flops=4 * rows * heads * head_size * keys,
            bytes_accessed=4 * keys * head_size + 16 * rows * heads * head_size,
            transcendentals=rows * heads * keys,
        ),
    )(lengths, queries, *kvs, *state)


def exchange(piece, axis, bits):
    return lax.ppermute(piece, axis, [(i, i ^ bits) for i in range(lax.axis_size(axis))])


def all_blocks(block, axis):
    held = block[None]
    while (count := held.shape[0]) < lax.axis_size(axis):
        held = jnp.concatenate([held] + [exchange(held, axis, digit * count) for digit in range(1, DIGIT)])
    return held


def body(queries, key_rows, value_rows, document_lengths):
    seqs, rows, width = queries.shape
    heads = width // key_rows.shape[2]
    assert lax.axis_size("head") == 4
    results = []
    for seq in range(seqs):
        lengths = document_lengths[seq : seq + 1]
        piece_0 = all_blocks(jnp.concatenate([key_rows[seq], value_rows[seq]], axis=1), "ctx")
        whole, half = DIGIT, DIGIT // 2
        piece_2 = exchange(piece_0, "head", 2)
        piece_1 = exchange(piece_0, "head", 1)
        *state, turned = attend([(0, 0)], whole, True, False, lengths, queries[seq], [piece_0], (), heads)
        state = attend([(1, 0)], whole, False, False, lengths, turned, [piece_1], state, heads)
        piece_2, state = lax.optimization_barrier((piece_2, state))
        piece_3 = exchange(piece_2, "head", 1)
        state = attend([(2, 0)], whole, False, False, lengths, turned, [piece_2], state, heads)
        results.append(attend([(3, 0)], half, False, True, lengths, turned, [piece_3], state, heads))
    return jnp.stack(results)


def solution(mesh):
    in_specs = (
        P(None, "ctx", "head"),
        P(None, ("ctx", "head"), None),
        P(None, ("ctx", "head"), None),
        P(),
    )
    out_specs = P(None, "ctx", "head")
    return jax.shard_map(body, mesh=mesh, in_specs=in_specs, out_specs=out_specs, check_vma=False)
```

time: 30.1 us -> 35.8 us (1.19)
  blocking collectives: 16.1 us -> 0 us
  starting transfers between devices: 1.53 us -> 16.4 us
  waiting for transfers between devices: 3.89 us -> 10.6 us
    all_to_all x1 -> x0, blocking collectives: 16.1 us -> none  [all_blocks(): lax.all_to_all(jnp.broadcast_to(block, (size,) + block.shape), axis, 0, 0)]
    ppermute x3 -> x10, starting transfers between devices: 1.53 us -> 16.4 us  [exchange(): lax.ppermute(piece, axis, [(i, i ^ bits) for i in range(lax.axis_size(axi...]
    ppermute x3 -> x10, waiting for transfers between devices: 3.89 us -> 10.6 us  [exchange(): lax.ppermute(piece, axis, [(i, i ^ bits) for i in range(lax.axis_size(axi...]
    broadcast_in_dim x0 -> x1, other arithmetic: none -> 0.79 us  [all_blocks(): held = block[None]]
    concatenate x1 -> x0, other arithmetic: 0.74 us -> none  [body(): kv = jnp.concatenate([key_rows[seq], value_rows[seq]], axis=1)]
  transfers between devices with their start and end apart: 3 -> 10, of which waited for: 1 -> 4; matrix products, arithmetic and copies ran while one was open for 0% -> 0% of each run, Pallas kernels for 17% -> 15%
where the time goes in v5:
time: 35.8 us; the launch traced here: 35.5 us
  starting transfers between devices  16.4 us (46%)
  waiting for transfers between devices  10.6 us (30%)
  Pallas kernels  7.6 us (21%)
  other arithmetic  0.8 us (2%)
    ppermute x10, starting transfers between devices, exchange(): lax.ppermute(piece, axis, [(i, i ^ bits) for i in range(lax.axis_size(axi...  16.4 us
    ppermute x10, waiting for transfers between devices, exchange(): lax.ppermute(piece, axis, [(i, i ^ bits) for i in range(lax.axis_size(axi...  10.6 us
    pallas_call x4, Pallas kernels, attend(): pl.pallas_call(functools.partial(attention_kernel, head_size, parts, step...  7.6 us
    broadcast_in_dim x1, other arithmetic, all_blocks(): held = block[None]  0.79 us
  transfers between devices with their start and end apart: 10, of which 4 were waited for; matrix products, arithmetic and copies ran while one was open for 0% of the time, Pallas kernels for 15%

profile of v5, /device:TPU:0, one launch (start us, length us, event | category | flops | bytes accessed | tf_op | source)
XLA Modules:
  0.0 35.5 jit_solution(1525573000589104173)
XLA Ops:
  0.0 0.0 copy-start.2
  0.0 0.0 copy-start.3
  0.0 0.8 %maximum_bitcast_fusion = bf16[1,64,256]{2,1,0:T(8,128)(2,1)S(1)} fusion(bf16[64,128]{1,0:T(8,128)(2,1)} %bitcast.9, bf16[64,128]{1,0:T(8,128)(2,1)} %bitcast.11), kind=kLoop, calls=%fused_computation | loop fusion | flops 65536 | bytes 65536 | tf_op jit(solution)/shard_map/broadcast_in_dim | solution.py:146
  0.8 0.0 copy-start.1
  0.8 6.0 %collective-permute-start.6 = (bf16[1,64,256]{2,1,0:T(8,128)(2,1)S(1)}, bf16[1,64,256]{2,1,0:T(8,128)(2,1)S(1)}, u32[]{:S(2)}, u32[]{:S(2)}) collective-permute-start(bf16[1,64,256]{2,1,0:T(8,128)(2,1)S(1)} %maximum_bitcast_fusion), channel_id=1, source_target_pairs={{0,28},{4,24},{8,20},{12,16},{16,12},{20,8},{24,4},{28,0},{1,29},{... | collective-permute-start | bytes 98312 | tf_op jit(solution)/shard_map/ppermute | solution.py:142
  6.8 0.2 collective-permute-start.5
  7.1 0.8 %collective-permute-start.4 = (bf16[1,64,256]{2,1,0:T(8,128)(2,1)S(1)}, bf16[1,64,256]{2,1,0:T(8,128)(2,1)S(1)}, u32[]{:S(2)}, u32[]{:S(2)}) collective-permute-start(bf16[1,64,256]{2,1,0:T(8,128)(2,1)S(1)} %maximum_bitcast_fusion), channel_id=1, source_target_pairs={{0,20},{4,16},{8,28},{12,24},{16,4},{20,0},{24,12},{28,8},{1,21},{... | collective-permute-start | bytes 98312 | tf_op jit(solution)/shard_map/ppermute | solution.py:142
  7.8 2.0 %collective-permute-start.3 = (bf16[1,64,256]{2,1,0:T(8,128)(2,1)S(1)}, bf16[1,64,256]{2,1,0:T(8,128)(2,1)S(1)}, u32[]{:S(2)}, u32[]{:S(2)}) collective-permute-start(bf16[1,64,256]{2,1,0:T(8,128)(2,1)S(1)} %maximum_bitcast_fusion), channel_id=1, source_target_pairs={{0,16},{4,20},{8,24},{12,28},{16,0},{20,4},{24,8},{28,12},{1,17},{... | collective-permute-start | bytes 98312 | tf_op jit(solution)/shard_map/ppermute | solution.py:142
  9.8 1.6 %collective-permute-start = (bf16[1,64,256]{2,1,0:T(8,128)(2,1)S(1)}, bf16[1,64,256]{2,1,0:T(8,128)(2,1)S(1)}, u32[]{:S(2)}, u32[]{:S(2)}) collective-permute-start(bf16[1,64,256]{2,1,0:T(8,128)(2,1)S(1)} %maximum_bitcast_fusion), channel_id=1, source_target_pairs={{0,4},{4,0},{8,12},{12,8},{16,20},{20,16},{24,28},{28,24},{1,5},{5... | collective-permute-start | bytes 98312 | tf_op jit(solution)/shard_map/ppermute | solution.py:142
  11.4 0.0 copy-done.2
  11.5 0.0 copy-done.3
  11.5 2.3 %collective-permute-done = bf16[1,64,256]{2,1,0:T(8,128)(2,1)S(1)} collective-permute-done((bf16[1,64,256]{2,1,0:T(8,128)(2,1)S(1)}, bf16[1,64,256]{2,1,0:T(8,128)(2,1)S(1)}, u32[]{:S(2)}, u32[]{:S(2)}) %collective-permute-start) | collective-permute-done | bytes 32800 | tf_op jit(solution)/shard_map/ppermute | solution.py:142
  13.8 1.4 %collective-permute-start.1 = (bf16[1,64,256]{2,1,0:T(8,128)(2,1)S(1)}, bf16[1,64,256]{2,1,0:T(8,128)(2,1)S(1)}, u32[]{:S(2)}, u32[]{:S(2)}) collective-permute-start(bf16[1,64,256]{2,1,0:T(8,128)(2,1)S(1)} %maximum_bitcast_fusion), channel_id=1, source_target_pairs={{0,8},{4,12},{8,0},{12,4},{16,24},{20,28},{24,16},{28,20},{1,9},{5... | collective-permute-start | bytes 98312 | tf_op jit(solution)/shard_map/ppermute | solution.py:142
  15.1 2.5 %collective-permute-done.1 = bf16[1,64,256]{2,1,0:T(8,128)(2,1)S(1)} collective-permute-done((bf16[1,64,256]{2,1,0:T(8,128)(2,1)S(1)}, bf16[1,64,256]{2,1,0:T(8,128)(2,1)S(1)}, u32[]{:S(2)}, u32[]{:S(2)}) %collective-permute-start.1) | collective-permute-done | bytes 32800 | tf_op jit(solution)/shard_map/ppermute | solution.py:142
  17.7 2.6 %collective-permute-start.2 = (bf16[1,64,256]{2,1,0:T(8,128)(2,1)S(1)}, bf16[1,64,256]{2,1,0:T(8,128)(2,1)S(1)}, u32[]{:S(2)}, u32[]{:S(2)}) collective-permute-start(bf16[1,64,256]{2,1,0:T(8,128)(2,1)S(1)} %maximum_bitcast_fusion), channel_id=1, source_target_pairs={{0,12},{4,8},{8,4},{12,0},{16,28},{20,24},{24,20},{28,16},{1,13},{... | collective-permute-start | bytes 98312 | tf_op jit(solution)/shard_map/ppermute | solution.py:142
  20.3 2.2 %collective-permute-done.2 = bf16[1,64,256]{2,1,0:T(8,128)(2,1)S(1)} collective-permute-done((bf16[1,64,256]{2,1,0:T(8,128)(2,1)S(1)}, bf16[1,64,256]{2,1,0:T(8,128)(2,1)S(1)}, u32[]{:S(2)}, u32[]{:S(2)}) %collective-permute-start.2) | collective-permute-done | bytes 32800 | tf_op jit(solution)/shard_map/ppermute | solution.py:142
  22.5 0.0 collective-permute-done.3
  22.5 0.0 collective-permute-done.4
  22.5 0.0 collective-permute-done.5
  22.5 0.0 collective-permute-done.6
  22.6 0.0 copy-start
  22.6 0.1 collective-permute-start.8
  22.7 1.7 %collective-permute-start.7 = (bf16[8,64,256]{2,1,0:T(8,128)(2,1)S(1)}, bf16[8,64,256]{2,1,0:T(8,128)(2,1)S(1)}, u32[]{:S(2)}, u32[]{:S(2)}) collective-permute-start(bf16[8,64,256]{2,1,0:T(8,128)(2,1)S(1)} %constant_dynamic-update-slice_fusion.refs_0_), channel_id=1, source_target_pairs={{0,2},{1,3},{2,0},{3,1},{4,6},{5,7},{6,4},{7,5},{8,10},{9,11},{10,... | collective-permute-start | bytes 786440 | tf_op jit(solution)/shard_map/ppermute | solution.py:142
  24.4 0.0 copy-done.1
  24.4 0.0 copy-done
  24.4 1.6 %shard_map.46 = (f32[8,256]{1,0:T(8,128)S(1)}, f32[4,128,256]{2,1,0:T(8,128)S(1)}, bf16[4,128,256]{2,1,0:T(8,128)(2,1)S(1)}) custom-call(s32[1,4]{1,0:T(1,128)S(1)} %copy-done, bf16[256,512]{1,0:T(8,128)(2,1)S(1)} %bitcast.8, bf16[8,64,256]{2,1,0:T(8,128)(2,1)S(1)} %constant_dynamic-update-slice_fusion.refs_0_), custom_call_target="tpu_custom_call" | custom-call | flops 268435456 | bytes 2359296 | tf_op jit(solution)/shard_map/pallas_call | solution.py:127
  26.0 0.0 collective-permute-done.8.refs_0_
  26.0 1.8 %shard_map.47 = (f32[8,256]{1,0:T(8,128)S(1)}, f32[4,128,256]{2,1,0:T(8,128)S(1)}) custom-call(s32[1,4]{1,0:T(1,128)S(1)} %copy-done, bf16[4,128,256]{2,1,0:T(8,128)(2,1)S(1)} %get-tuple-element.15.queries_ref, bf16[8,64,256]{2,1,0:T(8,128)(2,1)S(1)} %collective-permute-done.8.refs_0_, f32[8,256]{1,0:T(8,128)S(1)} %get-tuple-element.16.refs_1_, ...), custom_call_target="tpu_custom_call" | custom-call | flops 268435456 | bytes 2359296 | tf_op jit(solution)/shard_map/pallas_call | solution.py:127
  27.9 3.5 %collective-permute-done.7.refs_0_ = bf16[8,64,256]{2,1,0:T(8,128)(2,1)S(1)} collective-permute-done((bf16[8,64,256]{2,1,0:T(8,128)(2,1)S(1)}, bf16[8,64,256]{2,1,0:T(8,128)(2,1)S(1)}, u32[]{:S(2)}, u32[]{:S(2)}) %collective-permute-start.7) | collective-permute-done | bytes 262176 | tf_op jit(solution)/shard_map/ppermute | solution.py:142
  31.4 0.0 collective-permute-start.9
  31.4 1.8 %shard_map.48 = (f32[8,256]{1,0:T(8,128)S(1)}, f32[4,128,256]{2,1,0:T(8,128)S(1)}) custom-call(s32[1,4]{1,0:T(1,128)S(1)} %copy-done, bf16[4,128,256]{2,1,0:T(8,128)(2,1)S(1)} %get-tuple-element.15.queries_ref, bf16[8,64,256]{2,1,0:T(8,128)(2,1)S(1)} %collective-permute-done.7.refs_0_, f32[8,256]{1,0:T(8,128)S(1)} %get-tuple-element.21.refs_1_, ...), custom_call_target="tpu_custom_call" | custom-call | flops 268435456 | bytes 2359296 | tf_op jit(solution)/shard_map/pallas_call | solution.py:127
  33.2 0.0 collective-permute-done.9.refs_0_
  33.2 2.3 %shard_map.49 = bf16[256,512]{1,0:T(8,128)(2,1)} custom-call(s32[1,4]{1,0:T(1,128)S(1)} %copy-done, bf16[4,128,256]{2,1,0:T(8,128)(2,1)S(1)} %get-tuple-element.15.queries_ref, bf16[8,64,256]{2,1,0:T(8,128)(2,1)S(1)} %collective-permute-done.9.refs_0_, f32[8,256]{1,0:T(8,128)S(1)} %get-tuple-element.23.refs_1_, f32[4,128,256]{2,1,0:T(8,128)S(1)} %get-tuple-element.24.refs_2_), custom_call_target="tpu_custom_call" | custom-call | flops 268435456 | bytes 2359296 | tf_op jit(solution)/shard_map/pallas_call | solution.py:127
  (8 shorter events, 0.0 us)
Async XLA Ops:
  0.0 11.5 %copy-start.2 = (bf16[1,64,128]{2,1,0:T(8,128)(2,1)S(1)}, bf16[1,64,128]{2,1,0:T(8,128)(2,1)}, u32[]{:S(2)}) copy-start(bf16[1,64,128]{2,1,0:T(8,128)(2,1)} %param.6) | copy-start | bytes 49156
  0.0 11.5 %copy-start.3 = (bf16[1,64,128]{2,1,0:T(8,128)(2,1)S(1)}, bf16[1,64,128]{2,1,0:T(8,128)(2,1)}, u32[]{:S(2)}) copy-start(bf16[1,64,128]{2,1,0:T(8,128)(2,1)} %param.5) | copy-start | bytes 49156
  0.8 23.6 %copy-start.1 = (bf16[1,256,512]{2,1,0:T(8,128)(2,1)S(1)}, bf16[1,256,512]{2,1,0:T(8,128)(2,1)}, u32[]{:S(2)}) copy-start(bf16[1,256,512]{2,1,0:T(8,128)(2,1)} %param.4) | copy-start | bytes 786436
  0.8 21.7 %collective-permute-start.6 = (bf16[1,64,256]{2,1,0:T(8,128)(2,1)S(1)}, bf16[1,64,256]{2,1,0:T(8,128)(2,1)S(1)}, u32[]{:S(2)}, u32[]{:S(2)}) collective-permute-start(bf16[1,64,256]{2,1,0:T(8,128)(2,1)S(1)} %maximum_bitcast_fusion), channel_id=1, source_target_pairs={{0,28},{4,24},{8,20},{12,16},{16,12},{20,8},{24,4},{28,0},{1,29},{... | collective-permute-start | bytes 98312 | tf_op jit(solution)/shard_map/ppermute | solution.py:142
  6.8 15.7 %collective-permute-start.5 = (bf16[1,64,256]{2,1,0:T(8,128)(2,1)S(1)}, bf16[1,64,256]{2,1,0:T(8,128)(2,1)S(1)}, u32[]{:S(2)}, u32[]{:S(2)}) collective-permute-start(bf16[1,64,256]{2,1,0:T(8,128)(2,1)S(1)} %maximum_bitcast_fusion), channel_id=1, source_target_pairs={{0,24},{4,28},{8,16},{12,20},{16,8},{20,12},{24,0},{28,4},{1,25},{... | collective-permute-start | bytes 98312 | tf_op jit(solution)/shard_map/ppermute | solution.py:142
  7.1 15.4 %collective-permute-start.4 = (bf16[1,64,256]{2,1,0:T(8,128)(2,1)S(1)}, bf16[1,64,256]{2,1,0:T(8,128)(2,1)S(1)}, u32[]{:S(2)}, u32[]{:S(2)}) collective-permute-start(bf16[1,64,256]{2,1,0:T(8,128)(2,1)S(1)} %maximum_bitcast_fusion), channel_id=1, source_target_pairs={{0,20},{4,16},{8,28},{12,24},{16,4},{20,0},{24,12},{28,8},{1,21},{... | collective-permute-start | bytes 98312 | tf_op jit(solution)/shard_map/ppermute | solution.py:142
  7.8 14.7 %collective-permute-start.3 = (bf16[1,64,256]{2,1,0:T(8,128)(2,1)S(1)}, bf16[1,64,256]{2,1,0:T(8,128)(2,1)S(1)}, u32[]{:S(2)}, u32[]{:S(2)}) collective-permute-start(bf16[1,64,256]{2,1,0:T(8,128)(2,1)S(1)} %maximum_bitcast_fusion), channel_id=1, source_target_pairs={{0,16},{4,20},{8,24},{12,28},{16,0},{20,4},{24,8},{28,12},{1,17},{... | collective-permute-start | bytes 98312 | tf_op jit(solution)/shard_map/ppermute | solution.py:142
  9.8 3.9 %collective-permute-start = (bf16[1,64,256]{2,1,0:T(8,128)(2,1)S(1)}, bf16[1,64,256]{2,1,0:T(8,128)(2,1)S(1)}, u32[]{:S(2)}, u32[]{:S(2)}) collective-permute-start(bf16[1,64,256]{2,1,0:T(8,128)(2,1)S(1)} %maximum_bitcast_fusion), channel_id=1, source_target_pairs={{0,4},{4,0},{8,12},{12,8},{16,20},{20,16},{24,28},{28,24},{1,5},{5... | collective-permute-start | bytes 98312 | tf_op jit(solution)/shard_map/ppermute | solution.py:142
  13.8 3.9 %collective-permute-start.1 = (bf16[1,64,256]{2,1,0:T(8,128)(2,1)S(1)}, bf16[1,64,256]{2,1,0:T(8,128)(2,1)S(1)}, u32[]{:S(2)}, u32[]{:S(2)}) collective-permute-start(bf16[1,64,256]{2,1,0:T(8,128)(2,1)S(1)} %maximum_bitcast_fusion), channel_id=1, source_target_pairs={{0,8},{4,12},{8,0},{12,4},{16,24},{20,28},{24,16},{28,20},{1,9},{5... | collective-permute-start | bytes 98312 | tf_op jit(solution)/shard_map/ppermute | solution.py:142
  17.7 4.8 %collective-permute-start.2 = (bf16[1,64,256]{2,1,0:T(8,128)(2,1)S(1)}, bf16[1,64,256]{2,1,0:T(8,128)(2,1)S(1)}, u32[]{:S(2)}, u32[]{:S(2)}) collective-permute-start(bf16[1,64,256]{2,1,0:T(8,128)(2,1)S(1)} %maximum_bitcast_fusion), channel_id=1, source_target_pairs={{0,12},{4,8},{8,4},{12,0},{16,28},{20,24},{24,20},{28,16},{1,13},{... | collective-permute-start | bytes 98312 | tf_op jit(solution)/shard_map/ppermute | solution.py:142
  22.6 1.8 %copy-start = (s32[1,4]{1,0:T(1,128)S(1)}, s32[1,4]{1,0:T(1,128)}, u32[]{:S(2)}) copy-start(s32[1,4]{1,0:T(1,128)} %lengths_ref.7) | copy-start | bytes 52
  22.6 3.4 %collective-permute-start.8 = (bf16[8,64,256]{2,1,0:T(8,128)(2,1)S(1)}, bf16[8,64,256]{2,1,0:T(8,128)(2,1)S(1)}, u32[]{:S(2)}, u32[]{:S(2)}) collective-permute-start(bf16[8,64,256]{2,1,0:T(8,128)(2,1)S(1)} %constant_dynamic-update-slice_fusion.refs_0_), channel_id=1, source_target_pairs={{0,1},{1,0},{2,3},{3,2},{4,5},{5,4},{6,7},{7,6},{8,9},{9,8},{10,11... | collective-permute-start | bytes 786440 | tf_op jit(solution)/shard_map/ppermute | solution.py:142
  22.7 8.7 %collective-permute-start.7 = (bf16[8,64,256]{2,1,0:T(8,128)(2,1)S(1)}, bf16[8,64,256]{2,1,0:T(8,128)(2,1)S(1)}, u32[]{:S(2)}, u32[]{:S(2)}) collective-permute-start(bf16[8,64,256]{2,1,0:T(8,128)(2,1)S(1)} %constant_dynamic-update-slice_fusion.refs_0_), channel_id=1, source_target_pairs={{0,2},{1,3},{2,0},{3,1},{4,6},{5,7},{6,4},{7,5},{8,10},{9,11},{10,... | collective-permute-start | bytes 786440 | tf_op jit(solution)/shard_map/ppermute | solution.py:142
  31.4 1.8 %collective-permute-start.9 = (bf16[8,64,256]{2,1,0:T(8,128)(2,1)S(1)}, bf16[8,64,256]{2,1,0:T(8,128)(2,1)S(1)}, u32[]{:S(2)}, u32[]{:S(2)}) collective-permute-start(bf16[8,64,256]{2,1,0:T(8,128)(2,1)S(1)} %collective-permute-done.7.refs_0_), channel_id=1, source_target_pairs={{0,1},{1,0},{2,3},{3,2},{4,5},{5,4},{6,7},{7,6},{8,9},{9,8},{10,11... | collective-permute-start | bytes 786440 | tf_op jit(solution)/shard_map/ppermute | solution.py:142

commit v6 on v5

--- a/solution.py
+++ b/solution.py
@@ -9,7 +9,7 @@
 from jax.sharding import PartitionSpec as P
 
 NEG = -1e30
-DIGIT = 8
+STEP_BLOCKS = 8
 
 
 def attention_kernel(head_size, parts, step_blocks, first, last, lengths_ref, queries_ref, *refs):
@@ -46,21 +46,25 @@
         for kv_ref, (place, start) in zip(kv_refs, parts):
             in_block = (lax.axis_index("head") ^ place) * piece_rows + in_piece
             kv.append(kv_ref[pl.ds(index * step_blocks, step_blocks)].reshape(step_blocks * piece_rows, 2 * head_size))
-            key_pos += [(own ^ (start + index * step_blocks + i)) * rows + in_block for i in range(step_blocks)]
+            key_pos += [(start + index * step_blocks + i) * rows + in_block for i in range(step_blocks)]
         kv = jnp.concatenate(kv, axis=0)
         key_pos = jnp.concatenate(key_pos, axis=0)
         keys, values = kv[:, :head_size], kv[:, head_size:].T
-        valid = (key_pos >= starts) & (key_pos <= query_pos)
-        scores = [
-            jnp.where(valid, jnp.dot(keys, queries_ref[head], preferred_element_type=jnp.float32), NEG)
-            for head in range(heads)
-        ]
+        bias = jnp.where((key_pos >= starts) & (key_pos <= query_pos), 0.0, NEG)
+
+        def scores_of(head):
+            return jnp.dot(keys, queries_ref[head], preferred_element_type=jnp.float32) + bias
+
         tops, totals, sums = [], [], []
+        ahead = scores_of(0)
         for head in range(heads):
-            top = jnp.max(scores[head], axis=0, keepdims=True)
+            scores = ahead
+            if head + 1 < heads:
+                ahead = scores_of(head + 1)
+            top = jnp.max(scores, axis=0, keepdims=True)
             if old is not None:
                 top = jnp.maximum(old[0][head], top)
-            weights = jnp.exp2((scores[head] - top) * slope)
+            weights = jnp.exp2((scores - top) * slope)
             total = jnp.sum(weights, axis=0, keepdims=True)
             mixed = jnp.dot(values, weights.astype(jnp.bfloat16), preferred_element_type=jnp.float32)
             if old is not None:
@@ -90,28 +94,30 @@
             for head in range(heads):
                 sums_ref[head] = sums[head]
 
-    def needed(index):
-        group = (own ^ (parts[0][1] + index * step_blocks)) // step_blocks
-        return (group <= own // step_blocks) & (group >= first_key // rows // step_blocks)
+    start = parts[0][1]
+    steps = entries // step_blocks
+    low = jnp.maximum(first_key // rows - start, 0) // step_blocks
+    high = jnp.minimum(own + step_blocks - start, entries) // step_blocks
 
-    def step_or_skip(index, state):
-        return lax.cond(needed(index), lambda: step(index, state), lambda: state)
+    def old_state():
+        return load(old_stats_ref[...], old_sums_ref)
 
-    steps = entries // step_blocks
     if first:
         state = step(0, None)
+        if steps > 1:
+            state = lax.fori_loop(jnp.maximum(low, 1), high, step, state)
+        store(state)
+    elif steps > 1:
+        store(lax.fori_loop(low, high, step, old_state()))
     else:
-        state = load(old_stats_ref[...], old_sums_ref)
-        state = step_or_skip(0, state)
-    if steps == 2:
-        state = step_or_skip(1, state)
-    elif steps > 2:
-        state = lax.fori_loop(1, steps, step_or_skip, state)
-    store(state)
+        needed = (low < 1) & (high > 0)
+        pl.when(needed)(lambda: store(step(0, old_state())))
+        pl.when(jnp.logical_not(needed))(lambda: store(old_state()))
 
 
-def attend(parts, step_blocks, first, last, lengths, queries, kvs, state, heads):
+def attend(parts, first, last, lengths, queries, kvs, state, heads):
     head_size = kvs[0].shape[2] // 2
+    step_blocks = math.gcd(kvs[0].shape[0], STEP_BLOCKS)
     rows = queries.shape[0] if first else queries.shape[2]
     keys = sum(kv.shape[0] * kv.shape[1] for kv in kvs)
     stats = jax.ShapeDtypeStruct((2 * heads, rows), jnp.float32)
@@ -143,10 +149,12 @@
 
 
 def all_blocks(block, axis):
-    held = block[None]
-    while (count := held.shape[0]) < lax.axis_size(axis):
-        held = jnp.concatenate([held] + [exchange(held, axis, digit * count) for digit in range(1, DIGIT)])
-    return held
+    size = lax.axis_size(axis)
+    return lax.all_to_all(jnp.broadcast_to(block, (size,) + block.shape), axis, 0, 0)
+
+
+def exchange(piece, axis, bits):
+    return lax.ppermute(piece, axis, [(i, i ^ bits) for i in range(lax.axis_size(axis))])
 
 
 def body(queries, key_rows, value_rows, document_lengths):
@@ -157,15 +165,19 @@
     for seq in range(seqs):
         lengths = document_lengths[seq : seq + 1]
         piece_0 = all_blocks(jnp.concatenate([key_rows[seq], value_rows[seq]], axis=1), "ctx")
-        whole, half = DIGIT, DIGIT // 2
-        piece_2 = exchange(piece_0, "head", 2)
+        half = piece_0.shape[0] // 2
+        piece_2a = exchange(piece_0[:half], "head", 2)
+        piece_2b = exchange(piece_0[half:], "head", 2)
         piece_1 = exchange(piece_0, "head", 1)
-        *state, turned = attend([(0, 0)], whole, True, False, lengths, queries[seq], [piece_0], (), heads)
-        state = attend([(1, 0)], whole, False, False, lengths, turned, [piece_1], state, heads)
-        piece_2, state = lax.optimization_barrier((piece_2, state))
-        piece_3 = exchange(piece_2, "head", 1)
-        state = attend([(2, 0)], whole, False, False, lengths, turned, [piece_2], state, heads)
-        results.append(attend([(3, 0)], half, False, True, lengths, turned, [piece_3], state, heads))
+        *state, turned = attend([(0, 0)], True, False, lengths, queries[seq], [piece_0], (), heads)
+        state = attend([(1, 0)], False, False, lengths, turned, [piece_1], state, heads)
+        piece_2a, state = lax.optimization_barrier((piece_2a, state))
+        piece_3a = exchange(piece_2a, "head", 1)
+        state = attend([(2, 0), (3, 0)], False, False, lengths, turned, [piece_2a, piece_3a], state, heads)
+        piece_2b, state = lax.optimization_barrier((piece_2b, state))
+        piece_3b = exchange(piece_2b, "head", 1)
+        state = attend([(2, half)], False, False, lengths, turned, [piece_2b], state, heads)
+        results.append(attend([(3, half)], False, True, lengths, turned, [piece_3b], state, heads))
     return jnp.stack(results)
 
 

time: 35.8 us -> 31.8 us (0.89)
  blocking collectives: 0 us -> 16 us
  starting transfers between devices: 16.4 us -> 3.11 us
  waiting for transfers between devices: 10.6 us -> 4.3 us
  Pallas kernels: 7.6 us -> 7.18 us
    all_to_all x0 -> x1, blocking collectives: none -> 16 us  [all_blocks(): lax.all_to_all(jnp.broadcast_to(block, (size,) + block.shape), axis, 0, 0)]
    ppermute x10 -> x5, starting transfers between devices: 16.4 us -> 3.11 us  [exchange(): lax.ppermute(piece, axis, [(i, i ^ bits) for i in range(lax.axis_size(axi...]
    ppermute x10 -> x5, waiting for transfers between devices: 10.6 us -> 4.3 us  [exchange(): lax.ppermute(piece, axis, [(i, i ^ bits) for i in range(lax.axis_size(axi...]
    broadcast_in_dim x1 -> x0, other arithmetic: 0.79 us -> none  [all_blocks(): held = block[None]]
    concatenate x0 -> x1, other arithmetic: none -> 0.74 us  [body(): jnp.concatenate([key_rows[seq], value_rows[seq]], axis=1)]
    pallas_call x4 -> x5, Pallas kernels: 7.6 us -> 7.18 us  [attend(): pl.pallas_call(functools.partial(attention_kernel, head_size, parts, step...]
  transfers between devices with their start and end apart: 10 -> 5, of which waited for: 4 -> 3; matrix products, arithmetic and copies ran while one was open for 0% -> 0% of each run, Pallas kernels for 15% -> 18%
where the time goes in v6:
time: 31.8 us; the launch traced here: 31.4 us
  blocking collectives  16 us (50%)
  Pallas kernels  7.18 us (23%)
  waiting for transfers between devices  4.3 us (14%)
  starting transfers between devices  3.11 us (10%)
  other arithmetic  0.74 us (2%)
    all_to_all x1, blocking collectives, all_blocks(): lax.all_to_all(jnp.broadcast_to(block, (size,) + block.shape), axis, 0, 0)  16 us
    pallas_call x5, Pallas kernels, attend(): pl.pallas_call(functools.partial(attention_kernel, head_size, parts, step...  7.18 us
    ppermute x5, waiting for transfers between devices, exchange(): lax.ppermute(piece, axis, [(i, i ^ bits) for i in range(lax.axis_size(axi...  4.3 us
    ppermute x5, starting transfers between devices, exchange(): lax.ppermute(piece, axis, [(i, i ^ bits) for i in range(lax.axis_size(axi...  3.11 us
    concatenate x1, other arithmetic, body(): jnp.concatenate([key_rows[seq], value_rows[seq]], axis=1)  0.74 us
  transfers between devices with their start and end apart: 5, of which 3 were waited for; matrix products, arithmetic and copies ran while one was open for 0% of the time, Pallas kernels for 18%

profile of v6, /device:TPU:0, one launch (start us, length us, event | category | flops | bytes accessed | tf_op | source)
XLA Modules:
  0.0 31.4 jit_solution(13381441690922406216)
XLA Ops:
  0.0 0.7 %pad_maximum_fusion = bf16[64,256]{1,0:T(8,128)(2,1)S(1)} fusion(bf16[64,128]{1,0:T(8,128)(2,1)} %bitcast.5, bf16[64,128]{1,0:T(8,128)(2,1)} %bitcast.6), kind=kLoop, calls=%fused_computation | loop fusion | flops 65536 | bytes 65536 | tf_op jit(solution)/shard_map/concatenate | solution.py:167
  0.8 16.0 %all_to_all.5.refs_0_ = bf16[8,64,256]{2,1,0:T(8,128)(2,1)S(1)} all-to-all(bf16[8,64,256]{2,1,0:T(8,128)(2,1)S(1)} %broadcast_in_dim.3), channel_id=1, replica_groups=mesh['ctx'=8,'head'=4] {'ctx'}, dimensions={0} | all-to-all | bytes 524288 | tf_op jit(solution)/shard_map/all_to_all | solution.py:153
  16.7 0.0 copy-start.1
  16.7 0.0 collective-permute-start.2
  16.8 0.0 copy-start
  16.8 1.6 %collective-permute-start.1 = (bf16[4,64,256]{2,1,0:T(8,128)(2,1)S(1)}, bf16[4,64,256]{2,1,0:T(8,128)(2,1)S(1)}, u32[]{:S(2)}, u32[]{:S(2)}) collective-permute-start(bf16[4,64,256]{2,1,0:T(8,128)(2,1)S(1)} %get-tuple-element.35), channel_id=1, source_target_pairs={{0,2},{1,3},{2,0},{3,1},{4,6},{5,7},{6,4},{7,5},{8,10},{9,11},{10,... | collective-permute-start | bytes 393224 | tf_op jit(solution)/shard_map/ppermute | solution.py:157
  18.4 0.0 copy-done.1
  18.4 0.0 copy-done
  18.4 1.7 %shard_map.46 = (f32[8,256]{1,0:T(8,128)S(1)}, f32[4,128,256]{2,1,0:T(8,128)S(1)}, bf16[4,128,256]{2,1,0:T(8,128)(2,1)S(1)}) custom-call(s32[1,4]{1,0:T(1,128)S(1)} %copy-done, bf16[256,512]{1,0:T(8,128)(2,1)S(1)} %bitcast.4, bf16[8,64,256]{2,1,0:T(8,128)(2,1)S(1)} %all_to_all.5.refs_0_), custom_call_target="tpu_custom_call" | custom-call | flops 268435456 | bytes 2359296 | tf_op jit(solution)/shard_map/pallas_call | solution.py:133
  20.1 0.0 collective-permute-done.2.refs_0_
  20.1 1.7 %shard_map.47 = (f32[8,256]{1,0:T(8,128)S(1)}, f32[4,128,256]{2,1,0:T(8,128)S(1)}) custom-call(s32[1,4]{1,0:T(1,128)S(1)} %copy-done, bf16[4,128,256]{2,1,0:T(8,128)(2,1)S(1)} %get-tuple-element.20.queries_ref, bf16[8,64,256]{2,1,0:T(8,128)(2,1)S(1)} %collective-permute-done.2.refs_0_, f32[8,256]{1,0:T(8,128)S(1)} %get-tuple-element.21.refs_1_, ...), custom_call_target="tpu_custom_call" | custom-call | flops 268435456 | bytes 2359296 | tf_op jit(solution)/shard_map/pallas_call | solution.py:133
  21.8 0.9 %collective-permute-done.1.refs_0_ = bf16[4,64,256]{2,1,0:T(8,128)(2,1)S(1)} collective-permute-done((bf16[4,64,256]{2,1,0:T(8,128)(2,1)S(1)}, bf16[4,64,256]{2,1,0:T(8,128)(2,1)S(1)}, u32[]{:S(2)}, u32[]{:S(2)}) %collective-permute-start.1) | collective-permute-done | bytes 131104 | tf_op jit(solution)/shard_map/ppermute | solution.py:157
  22.7 0.0 collective-permute-start.3
  22.7 1.5 %collective-permute-start = (bf16[4,64,256]{2,1,0:T(8,128)(2,1)S(1)}, bf16[4,64,256]{2,1,0:T(8,128)(2,1)S(1)}, u32[]{:S(2)}, u32[]{:S(2)}) collective-permute-start(bf16[4,64,256]{2,1,0:T(8,128)(2,1)S(1)} %get-tuple-element.36), channel_id=1, source_target_pairs={{0,2},{1,3},{2,0},{3,1},{4,6},{5,7},{6,4},{7,5},{8,10},{9,11},{10,... | collective-permute-start | bytes 393224 | tf_op jit(solution)/shard_map/ppermute | solution.py:157
  24.3 0.0 collective-permute-done.3.refs_1_
  24.3 1.7 %shard_map.48 = (f32[8,256]{1,0:T(8,128)S(1)}, f32[4,128,256]{2,1,0:T(8,128)S(1)}) custom-call(s32[1,4]{1,0:T(1,128)S(1)} %copy-done, bf16[4,128,256]{2,1,0:T(8,128)(2,1)S(1)} %get-tuple-element.20.queries_ref, bf16[4,64,256]{2,1,0:T(8,128)(2,1)S(1)} %collective-permute-done.1.refs_0_, bf16[4,64,256]{2,1,0:T(8,128)(2,1)S(1)} %collective-permute-done.3.refs_1_, ...), custom_call_target="tpu_custom_call" | custom-call | flops 268435456 | bytes 2359296 | tf_op jit(solution)/shard_map/pallas_call | solution.py:133
  26.0 2.7 %collective-permute-done.refs_0_ = bf16[4,64,256]{2,1,0:T(8,128)(2,1)S(1)} collective-permute-done((bf16[4,64,256]{2,1,0:T(8,128)(2,1)S(1)}, bf16[4,64,256]{2,1,0:T(8,128)(2,1)S(1)}, u32[]{:S(2)}, u32[]{:S(2)}) %collective-permute-start) | collective-permute-done | bytes 131104 | tf_op jit(solution)/shard_map/ppermute | solution.py:157
  28.7 0.0 collective-permute-start.4
  28.7 0.6 %shard_map.49 = (f32[8,256]{1,0:T(8,128)S(1)}, f32[4,128,256]{2,1,0:T(8,128)S(1)}) custom-call(s32[1,4]{1,0:T(1,128)S(1)} %copy-done, bf16[4,128,256]{2,1,0:T(8,128)(2,1)S(1)} %get-tuple-element.20.queries_ref, bf16[4,64,256]{2,1,0:T(8,128)(2,1)S(1)} %collective-permute-done.refs_0_, f32[8,256]{1,0:T(8,128)S(1)} %get-tuple-element.31.refs_1_, ...), custom_call_target="tpu_custom_call" | custom-call | flops 134217728 | bytes 2228224 | tf_op jit(solution)/shard_map/pallas_call | solution.py:133
  29.3 0.7 %collective-permute-done.4.refs_0_ = bf16[4,64,256]{2,1,0:T(8,128)(2,1)S(1)} collective-permute-done((bf16[4,64,256]{2,1,0:T(8,128)(2,1)S(1)}, bf16[4,64,256]{2,1,0:T(8,128)(2,1)S(1)}, u32[]{:S(2)}, u32[]{:S(2)}) %collective-permute-start.4) | collective-permute-done | bytes 131104 | tf_op jit(solution)/shard_map/ppermute | solution.py:157
  30.0 1.4 %shard_map.50 = bf16[256,512]{1,0:T(8,128)(2,1)} custom-call(s32[1,4]{1,0:T(1,128)S(1)} %copy-done, bf16[4,128,256]{2,1,0:T(8,128)(2,1)S(1)} %get-tuple-element.20.queries_ref, bf16[4,64,256]{2,1,0:T(8,128)(2,1)S(1)} %collective-permute-done.4.refs_0_, f32[8,256]{1,0:T(8,128)S(1)} %get-tuple-element.33.refs_1_, f32[4,128,256]{2,1,0:T(8,128)S(1)} %get-tuple-element.34.refs_2_), custom_call_target="tpu_custom_call" | custom-call | flops 134217728 | bytes 2228224 | tf_op jit(solution)/shard_map/pallas_call | solution.py:133
  (2 shorter events, 0.0 us)
Async XLA Ops:
  16.7 1.6 %copy-start.1 = (bf16[1,256,512]{2,1,0:T(8,128)(2,1)S(1)}, bf16[1,256,512]{2,1,0:T(8,128)(2,1)}, u32[]{:S(2)}) copy-start(bf16[1,256,512]{2,1,0:T(8,128)(2,1)} %param.4) | copy-start | bytes 786436
  16.7 3.4 %collective-permute-start.2 = (bf16[8,64,256]{2,1,0:T(8,128)(2,1)S(1)}, bf16[8,64,256]{2,1,0:T(8,128)(2,1)S(1)}, u32[]{:S(2)}, u32[]{:S(2)}) collective-permute-start(bf16[8,64,256]{2,1,0:T(8,128)(2,1)S(1)} %all_to_all.5.refs_0_), channel_id=1, source_target_pairs={{0,1},{1,0},{2,3},{3,2},{4,5},{5,4},{6,7},{7,6},{8,9},{9,8},{10,11... | collective-permute-start | bytes 786440 | tf_op jit(solution)/shard_map/ppermute | solution.py:157
  16.8 1.6 %copy-start = (s32[1,4]{1,0:T(1,128)S(1)}, s32[1,4]{1,0:T(1,128)}, u32[]{:S(2)}) copy-start(s32[1,4]{1,0:T(1,128)} %lengths_ref.9) | copy-start | bytes 52
  16.8 6.0 %collective-permute-start.1 = (bf16[4,64,256]{2,1,0:T(8,128)(2,1)S(1)}, bf16[4,64,256]{2,1,0:T(8,128)(2,1)S(1)}, u32[]{:S(2)}, u32[]{:S(2)}) collective-permute-start(bf16[4,64,256]{2,1,0:T(8,128)(2,1)S(1)} %get-tuple-element.35), channel_id=1, source_target_pairs={{0,2},{1,3},{2,0},{3,1},{4,6},{5,7},{6,4},{7,5},{8,10},{9,11},{10,... | collective-permute-start | bytes 393224 | tf_op jit(solution)/shard_map/ppermute | solution.py:157
  22.7 1.5 %collective-permute-start.3 = (bf16[4,64,256]{2,1,0:T(8,128)(2,1)S(1)}, bf16[4,64,256]{2,1,0:T(8,128)(2,1)S(1)}, u32[]{:S(2)}, u32[]{:S(2)}) collective-permute-start(bf16[4,64,256]{2,1,0:T(8,128)(2,1)S(1)} %collective-permute-done.1.refs_0_), channel_id=1, source_target_pairs={{0,1},{1,0},{2,3},{3,2},{4,5},{5,4},{6,7},{7,6},{8,9},{9,8},{10,11... | collective-permute-start | bytes 393224 | tf_op jit(solution)/shard_map/ppermute | solution.py:157
  22.7 5.9 %collective-permute-start = (bf16[4,64,256]{2,1,0:T(8,128)(2,1)S(1)}, bf16[4,64,256]{2,1,0:T(8,128)(2,1)S(1)}, u32[]{:S(2)}, u32[]{:S(2)}) collective-permute-start(bf16[4,64,256]{2,1,0:T(8,128)(2,1)S(1)} %get-tuple-element.36), channel_id=1, source_target_pairs={{0,2},{1,3},{2,0},{3,1},{4,6},{5,7},{6,4},{7,5},{8,10},{9,11},{10,... | collective-permute-start | bytes 393224 | tf_op jit(solution)/shard_map/ppermute | solution.py:157
  28.7 1.3 %collective-permute-start.4 = (bf16[4,64,256]{2,1,0:T(8,128)(2,1)S(1)}, bf16[4,64,256]{2,1,0:T(8,128)(2,1)S(1)}, u32[]{:S(2)}, u32[]{:S(2)}) collective-permute-start(bf16[4,64,256]{2,1,0:T(8,128)(2,1)S(1)} %collective-permute-done.refs_0_), channel_id=1, source_target_pairs={{0,1},{1,0},{2,3},{3,2},{4,5},{5,4},{6,7},{7,6},{8,9},{9,8},{10,11... | collective-permute-start | bytes 393224 | tf_op jit(solution)/shard_map/ppermute | solution.py:157

commit v7 on v4

v7 whole, which is shorter than its diff:
```python
import functools
import math

import jax
import jax.numpy as jnp
from jax import lax
from jax.experimental import pallas as pl
from jax.experimental.pallas import tpu as pltpu
from jax.sharding import PartitionSpec as P

NEG = -1e30
STEP_BLOCKS = 8


def attention_kernel(head_size, place, first, tail, last, lengths_ref, queries_ref, kv_ref, *refs):
    if first:
        stats_ref, sums_ref, turned_ref = refs
        old_stats_ref, old_sums_ref = stats_ref, sums_ref
    elif last:
        old_stats_ref, old_sums_ref, out_ref, result_ref, sent = refs
    else:
        old_stats_ref, old_sums_ref, stats_ref, sums_ref = refs
    own, piece = lax.axis_index("ctx"), lax.axis_index("head") ^ place
    heads, _, rows = old_sums_ref.shape
    blocks, _, piece_rows, _ = kv_ref.shape
    slope = math.log2(math.e) / math.sqrt(head_size)
    step_blocks = math.gcd(blocks, STEP_BLOCKS)

    query_pos = own * rows + lax.broadcasted_iota(jnp.int32, (1, rows), 1)
    starts = jnp.zeros((1, rows), jnp.int32)
    first_key = jnp.int32(0)
    end = jnp.int32(0)
    for document in range(lengths_ref.shape[1]):
        end = end + lengths_ref[0, document]
        starts = jnp.where(query_pos >= end, end, starts)
        first_key = jnp.where(own * rows >= end, end, first_key)

    if first:
        for head in range(heads):
            turned_ref[head] = queries_ref[:, head * head_size : (head + 1) * head_size].T
        queries_ref = turned_ref
    in_block = piece * piece_rows + lax.broadcasted_iota(jnp.int32, (piece_rows, rows), 0)

    def step(index, count, old, emit):
        start = index * step_blocks
        keys = kv_ref[pl.ds(start, count), 0].reshape(count * piece_rows, head_size)
        values = kv_ref[pl.ds(start, count), 1].reshape(count * piece_rows, head_size).T
        key_pos = jnp.concatenate([(start + i) * rows + in_block for i in range(count)], axis=0)
        valid = (key_pos >= starts) & (key_pos <= query_pos)
        scores = [
            jnp.where(valid, jnp.dot(keys, queries_ref[head], preferred_element_type=jnp.float32), NEG)
            for head in range(heads)
        ]
        for head in range(heads):
            top = jnp.max(scores[head], axis=0, keepdims=True)
            if old is not None:
                old_top, old_total, old_sums = old(head)
                top = jnp.maximum(old_top, top)
            weights = jnp.exp2((scores[head] - top) * slope)
            total = jnp.sum(weights, axis=0, keepdims=True)
            sums = jnp.dot(values, weights.astype(jnp.bfloat16), preferred_element_type=jnp.float32)
            if old is not None:
                factor = jnp.exp2((old_top - top) * slope)
                total = old_total * factor + total
                sums = old_sums * factor + sums
            emit(head, top, total, sums)

    def old_state(head):
        return old_stats_ref[head : head + 1], old_stats_ref[heads + head : heads + head + 1], old_sums_ref[head]

    def keep(head, top, total, sums):
        stats_ref[head : head + 1] = top
        stats_ref[heads + head : heads + head + 1] = total
        sums_ref[head] = sums

    def send(head):
        columns = pl.ds(head * head_size, head_size)
        return pltpu.make_async_copy(result_ref.at[:, columns], out_ref.at[:, columns], sent.at[head])

    def finish(head, top, total, sums):
        del top
        result_ref[:, head * head_size : (head + 1) * head_size] = (sums * (1.0 / total)).astype(result_ref.dtype).T
        send(head).start()

    if blocks == step_blocks:
        if first or not tail:
            step(0, blocks, None if first else old_state, keep)
        else:
            emit = finish if last else keep
            reach = 0
            for count in sorted({max(blocks // 4, 1), max(blocks // 2, 1), blocks}):
                pl.when((own >= reach) & (own < count))(functools.partial(step, 0, count, old_state, emit))
                reach = count
    else:
        if first:
            stats_ref[...] = jnp.concatenate([jnp.full((heads, rows), NEG), jnp.zeros((heads, rows))], axis=0)
            sums_ref[...] = jnp.zeros_like(sums_ref)

        def keep_old(head, top, total, sums):
            old_stats_ref[head : head + 1] = top
            old_stats_ref[heads + head : heads + head + 1] = total
            old_sums_ref[head] = sums

        @pl.loop(first_key // rows // step_blocks, own // step_blocks + 1)
        def _(index):
            step(index, step_blocks, old_state, keep_old)

        for head in range(heads):
            if not first:
                (finish if last else keep)(head, *old_state(head))
    if last:
        for head in range(heads):
            send(head).wait()


def attend(place, first, tail, last, lengths, queries, kv, state, heads):
    blocks, _, piece_rows, head_size = kv.shape
    rows = queries.shape[0] if first else queries.shape[2]
    keys = blocks * piece_rows
    stats = jax.ShapeDtypeStruct((2 * heads, rows), jnp.float32)
    sums = jax.ShapeDtypeStruct((heads, head_size, rows), jnp.float32)
    turned = jax.ShapeDtypeStruct((heads, head_size, rows), queries.dtype)
    whole = pl.BlockSpec(memory_space=pltpu.VMEM)
    scratch = []
    if last:
        out_shape = jax.ShapeDtypeStruct((rows, heads * head_size), queries.dtype)
        out_specs = pl.BlockSpec(memory_space=pl.ANY)
        scratch = [pltpu.VMEM(out_shape.shape, out_shape.dtype), pltpu.SemaphoreType.DMA((heads,))]
    else:
        out_shape = (stats, sums, turned) if first else (stats, sums)
        out_specs = (whole,) * len(out_shape)
    return pl.pallas_call(
        functools.partial(attention_kernel, head_size, place, first, tail, last),
        out_shape=out_shape,
        in_specs=[pl.BlockSpec(memory_space=pltpu.SMEM)] + [whole] * (2 + len(state)),
        out_specs=out_specs,
        scratch_shapes=scratch,
        compiler_params=pltpu.CompilerParams(vmem_limit_bytes=32 * 1024 * 1024),
        cost_estimate=pl.CostEstimate(
            flops=4 * rows * heads * head_size * keys,
            bytes_accessed=4 * keys * head_size + 16 * rows * heads * head_size,
            transcendentals=rows * heads * keys,
        ),
    )(lengths, queries, kv, *state)


def all_blocks(block, axis):
    size = lax.axis_size(axis)
    return lax.all_to_all(jnp.broadcast_to(block, (size,) + block.shape), axis, 0, 0)


def exchange(piece, axis, bits):
    return lax.ppermute(piece, axis, [(i, i ^ bits) for i in range(lax.axis_size(axis))])


def body(queries, key_rows, value_rows, document_lengths):
    seqs, rows, width = queries.shape
    heads = width // key_rows.shape[2]
    assert lax.axis_size("head") == 4
    results = []
    for seq in range(seqs):
        lengths = document_lengths[seq : seq + 1]
        piece_0 = all_blocks(jnp.stack([key_rows[seq], value_rows[seq]]), "ctx")
        piece_2 = exchange(piece_0, "head", 2)
        piece_1 = exchange(piece_0, "head", 1)
        *state, turned = attend(0, True, False, False, lengths, queries[seq], piece_0, (), heads)
        state = attend(1, False, False, False, lengths, turned, piece_1, state, heads)
        piece_2, state = lax.optimization_barrier((piece_2, state))
        piece_3 = exchange(piece_2, "head", 1)
        state = attend(2, False, True, False, lengths, turned, piece_2, state, heads)
        results.append(attend(3, False, True, True, lengths, turned, piece_3, state, heads))
    return jnp.stack(results)


def solution(mesh):
    in_specs = (
        P(None, "ctx", "head"),
        P(None, ("ctx", "head"), None),
        P(None, ("ctx", "head"), None),
        P(),
    )
    out_specs = P(None, "ctx", "head")
    return jax.shard_map(body, mesh=mesh, in_specs=in_specs, out_specs=out_specs, check_vma=False)
```

time: 30.1 us -> 29.3 us (0.973)
  Pallas kernels: 7.36 us -> 6.12 us
  waiting for transfers between devices: 3.89 us -> 4.36 us
    pallas_call x4, Pallas kernels: 7.36 us -> 6.12 us  [attend(): pl.pallas_call(functools.partial(attention_kernel, head_size, place, firs...]
    concatenate x1 -> x0, other arithmetic: 0.74 us -> none  [body(): kv = jnp.concatenate([key_rows[seq], value_rows[seq]], axis=1)]
    another operation x0 -> x1, other arithmetic: none -> 0.74 us  [body(): piece_0 = all_blocks(jnp.stack([key_rows[seq], value_rows[seq]]), 'ctx')]
    ppermute x3, waiting for transfers between devices: 3.89 us -> 4.36 us  [exchange(): lax.ppermute(piece, axis, [(i, i ^ bits) for i in range(lax.axis_size(axi...]
  transfers between devices with their start and end apart: 3 -> 3, of which waited for: 1 -> 2; matrix products, arithmetic and copies ran while one was open for 0% -> 0% of each run, Pallas kernels for 17% -> 15%
where the time goes in v7:
time: 29.3 us; the launch traced here: 28.9 us
  blocking collectives  16.1 us (55%)
  Pallas kernels  6.12 us (21%)
  waiting for transfers between devices  4.36 us (15%)
  starting transfers between devices  1.53 us (5%)
  other arithmetic  0.74 us (3%)
    all_to_all x1, blocking collectives, all_blocks(): lax.all_to_all(jnp.broadcast_to(block, (size,) + block.shape), axis, 0, 0)  16.1 us
    pallas_call x4, Pallas kernels, attend(): pl.pallas_call(functools.partial(attention_kernel, head_size, place, firs...  6.12 us
    ppermute x3, waiting for transfers between devices, exchange(): lax.ppermute(piece, axis, [(i, i ^ bits) for i in range(lax.axis_size(axi...  4.36 us
    ppermute x3, starting transfers between devices, exchange(): lax.ppermute(piece, axis, [(i, i ^ bits) for i in range(lax.axis_size(axi...  1.53 us
    another operation x1, other arithmetic, body(): piece_0 = all_blocks(jnp.stack([key_rows[seq], value_rows[seq]]), 'ctx')  0.74 us
  transfers between devices with their start and end apart: 3, of which 2 were waited for; matrix products, arithmetic and copies ran while one was open for 0% of the time, Pallas kernels for 15%

profile of v7, /device:TPU:0, one launch (start us, length us, event | category | flops | bytes accessed | tf_op | source)
XLA Modules:
  0.0 28.9 jit_solution(14396382005128685320)
XLA Ops:
  0.0 0.7 %pad_maximum_fusion = bf16[2,64,128]{2,1,0:T(8,128)(2,1)S(1)} fusion(bf16[1,64,128]{2,1,0:T(8,128)(2,1)} %param.6, bf16[1,64,128]{2,1,0:T(8,128)(2,1)} %param.5), kind=kLoop, calls=%fused_computation | loop fusion | flops 16384 | bytes 65536 | tf_op jit(solution)/shard_map/stack | solution.py:163
  0.8 0.0 copy-start.1
  0.8 16.1 %all_to_all.5.kv_ref = bf16[8,2,64,128]{3,2,1,0:T(8,128)(2,1)S(1)} all-to-all(bf16[8,2,64,128]{3,2,1,0:T(8,128)(2,1)S(1)} %broadcast_in_dim.3), channel_id=1, replica_groups=mesh['ctx'=8,'head'=4] {'ctx'}, dimensions={0} | all-to-all | bytes 524288 | tf_op jit(solution)/shard_map/all_to_all | solution.py:149
  16.9 0.0 copy-start
  16.9 0.0 collective-permute-start.1
  16.9 1.5 %collective-permute-start = (bf16[8,2,64,128]{3,2,1,0:T(8,128)(2,1)S(1)}, bf16[8,2,64,128]{3,2,1,0:T(8,128)(2,1)S(1)}, u32[]{:S(2)}, u32[]{:S(2)}) collective-permute-start(bf16[8,2,64,128]{3,2,1,0:T(8,128)(2,1)S(1)} %all_to_all.5.kv_ref), channel_id=1, source_target_pairs={{0,2},{1,3},{2,0},{3,1},{4,6},{5,7},{6,4},{7,5},{8,10},{9,11},{10,... | collective-permute-start | bytes 786440 | tf_op jit(solution)/shard_map/ppermute | solution.py:153
  18.4 0.0 copy-done.1
  18.4 0.0 copy-done
  18.4 1.6 %shard_map.46 = (f32[8,256]{1,0:T(8,128)S(1)}, f32[4,128,256]{2,1,0:T(8,128)S(1)}, bf16[4,128,256]{2,1,0:T(8,128)(2,1)S(1)}) custom-call(s32[1,4]{1,0:T(1,128)S(1)} %copy-done, bf16[256,512]{1,0:T(8,128)(2,1)S(1)} %bitcast.2, bf16[8,2,64,128]{3,2,1,0:T(8,128)(2,1)S(1)} %all_to_all.5.kv_ref), custom_call_target="tpu_custom_call" | custom-call | flops 268435456 | bytes 2359296 | tf_op jit(solution)/shard_map/pallas_call | solution.py:132
  20.1 0.0 collective-permute-done.1.kv_ref
  20.1 1.7 %shard_map.47 = (f32[8,256]{1,0:T(8,128)S(1)}, f32[4,128,256]{2,1,0:T(8,128)S(1)}) custom-call(s32[1,4]{1,0:T(1,128)S(1)} %copy-done, bf16[4,128,256]{2,1,0:T(8,128)(2,1)S(1)} %get-tuple-element.15.queries_ref, bf16[8,2,64,128]{3,2,1,0:T(8,128)(2,1)S(1)} %collective-permute-done.1.kv_ref, f32[8,256]{1,0:T(8,128)S(1)} %get-tuple-element.16.refs_0_, ...), custom_call_target="tpu_custom_call" | custom-call | flops 268435456 | bytes 2359296 | tf_op jit(solution)/shard_map/pallas_call | solution.py:132
  21.8 3.9 %collective-permute-done.kv_ref = bf16[8,2,64,128]{3,2,1,0:T(8,128)(2,1)S(1)} collective-permute-done((bf16[8,2,64,128]{3,2,1,0:T(8,128)(2,1)S(1)}, bf16[8,2,64,128]{3,2,1,0:T(8,128)(2,1)S(1)}, u32[]{:S(2)}, u32[]{:S(2)}) %collective-permute-start) | collective-permute-done | bytes 262176 | tf_op jit(solution)/shard_map/ppermute | solution.py:153
  25.6 0.0 collective-permute-start.2
  25.6 1.0 %shard_map.48 = (f32[8,256]{1,0:T(8,128)S(1)}, f32[4,128,256]{2,1,0:T(8,128)S(1)}) custom-call(s32[1,4]{1,0:T(1,128)S(1)} %copy-done, bf16[4,128,256]{2,1,0:T(8,128)(2,1)S(1)} %get-tuple-element.15.queries_ref, bf16[8,2,64,128]{3,2,1,0:T(8,128)(2,1)S(1)} %collective-permute-done.kv_ref, f32[8,256]{1,0:T(8,128)S(1)} %get-tuple-element.21.refs_0_, ...), custom_call_target="tpu_custom_call" | custom-call | flops 268435456 | bytes 2359296 | tf_op jit(solution)/shard_map/pallas_call | solution.py:132
  26.7 0.5 %collective-permute-done.2.kv_ref = bf16[8,2,64,128]{3,2,1,0:T(8,128)(2,1)S(1)} collective-permute-done((bf16[8,2,64,128]{3,2,1,0:T(8,128)(2,1)S(1)}, bf16[8,2,64,128]{3,2,1,0:T(8,128)(2,1)S(1)}, u32[]{:S(2)}, u32[]{:S(2)}) %collective-permute-start.2) | collective-permute-done | bytes 262176 | tf_op jit(solution)/shard_map/ppermute | solution.py:153
  27.2 1.8 %shard_map.49 = bf16[256,512]{1,0:T(8,128)(2,1)} custom-call(s32[1,4]{1,0:T(1,128)S(1)} %copy-done, bf16[4,128,256]{2,1,0:T(8,128)(2,1)S(1)} %get-tuple-element.15.queries_ref, bf16[8,2,64,128]{3,2,1,0:T(8,128)(2,1)S(1)} %collective-permute-done.2.kv_ref, f32[8,256]{1,0:T(8,128)S(1)} %get-tuple-element.23.refs_0_, f32[4,128,256]{2,1,0:T(8,128)S(1)} %get-tuple-element.24.refs_1_), custom_call_target="tpu_custom_call" | custom-call | flops 268435456 | bytes 2359296 | tf_op jit(solution)/shard_map/pallas_call | solution.py:132
  (1 shorter events, 0.0 us)
Async XLA Ops:
  0.8 17.6 %copy-start.1 = (bf16[1,256,512]{2,1,0:T(8,128)(2,1)S(1)}, bf16[1,256,512]{2,1,0:T(8,128)(2,1)}, u32[]{:S(2)}) copy-start(bf16[1,256,512]{2,1,0:T(8,128)(2,1)} %param.4) | copy-start | bytes 786436
  16.9 1.5 %copy-start = (s32[1,4]{1,0:T(1,128)S(1)}, s32[1,4]{1,0:T(1,128)}, u32[]{:S(2)}) copy-start(s32[1,4]{1,0:T(1,128)} %lengths_ref.7) | copy-start | bytes 52
  16.9 3.2 %collective-permute-start.1 = (bf16[8,2,64,128]{3,2,1,0:T(8,128)(2,1)S(1)}, bf16[8,2,64,128]{3,2,1,0:T(8,128)(2,1)S(1)}, u32[]{:S(2)}, u32[]{:S(2)}) collective-permute-start(bf16[8,2,64,128]{3,2,1,0:T(8,128)(2,1)S(1)} %all_to_all.5.kv_ref), channel_id=1, source_target_pairs={{0,1},{1,0},{2,3},{3,2},{4,5},{5,4},{6,7},{7,6},{8,9},{9,8},{10,11... | collective-permute-start | bytes 786440 | tf_op jit(solution)/shard_map/ppermute | solution.py:153
  16.9 8.7 %collective-permute-start = (bf16[8,2,64,128]{3,2,1,0:T(8,128)(2,1)S(1)}, bf16[8,2,64,128]{3,2,1,0:T(8,128)(2,1)S(1)}, u32[]{:S(2)}, u32[]{:S(2)}) collective-permute-start(bf16[8,2,64,128]{3,2,1,0:T(8,128)(2,1)S(1)} %all_to_all.5.kv_ref), channel_id=1, source_target_pairs={{0,2},{1,3},{2,0},{3,1},{4,6},{5,7},{6,4},{7,5},{8,10},{9,11},{10,... | collective-permute-start | bytes 786440 | tf_op jit(solution)/shard_map/ppermute | solution.py:153
  25.6 1.5 %collective-permute-start.2 = (bf16[8,2,64,128]{3,2,1,0:T(8,128)(2,1)S(1)}, bf16[8,2,64,128]{3,2,1,0:T(8,128)(2,1)S(1)}, u32[]{:S(2)}, u32[]{:S(2)}) collective-permute-start(bf16[8,2,64,128]{3,2,1,0:T(8,128)(2,1)S(1)} %collective-permute-done.kv_ref), channel_id=1, source_target_pairs={{0,1},{1,0},{2,3},{3,2},{4,5},{5,4},{6,7},{7,6},{8,9},{9,8},{10,11... | collective-permute-start | bytes 786440 | tf_op jit(solution)/shard_map/ppermute | solution.py:153

commit v8 on v7

v8 whole, which is shorter than its diff:
```python
import functools
import math

import jax
import jax.numpy as jnp
from jax import lax
from jax.experimental import pallas as pl
from jax.experimental.pallas import tpu as pltpu
from jax.sharding import PartitionSpec as P

NEG = -1e30
STEP_BLOCKS = 8


def attention_kernel(head_size, place, first, tail, last, pieces, *refs):
    queries_ref, *refs = refs
    kv_refs, refs = refs[:pieces], refs[pieces:]
    blocks, _, piece_rows, _ = kv_refs[0].shape
    step_blocks = math.gcd(blocks, STEP_BLOCKS)
    lengths_ref = None
    if first or blocks > step_blocks:
        lengths_ref, *refs = refs
    if first:
        stats_ref, sums_ref, starts_ref, turned_ref = refs
        old_stats_ref, old_sums_ref = stats_ref, sums_ref
    elif last:
        old_stats_ref, old_sums_ref, starts_ref, out_ref, result_ref, sent = refs[:6]
    else:
        old_stats_ref, old_sums_ref, starts_ref, stats_ref, sums_ref = refs
    own, piece = lax.axis_index("ctx"), lax.axis_index("head") ^ place
    heads, _, rows = old_sums_ref.shape
    slope = math.log2(math.e) / math.sqrt(head_size)

    query_pos = own * rows + lax.broadcasted_iota(jnp.int32, (1, rows), 1)
    first_key = jnp.int32(0)
    if lengths_ref is not None:
        starts = jnp.zeros((1, rows), jnp.int32)
        end = jnp.int32(0)
        for document in range(lengths_ref.shape[1]):
            end = end + lengths_ref[0, document]
            starts = jnp.where(query_pos >= end, end, starts)
            first_key = jnp.where(own * rows >= end, end, first_key)
    else:
        starts = starts_ref[...]
    if first:
        starts_ref[...] = starts
        for head in range(heads):
            turned_ref[head] = queries_ref[:, head * head_size : (head + 1) * head_size].T
        queries_ref = turned_ref
    in_block = piece * piece_rows + lax.broadcasted_iota(jnp.int32, (piece_rows, rows), 0)

    def step(index, count, old, emit):
        start = index * step_blocks
        keys, values = (
            jnp.concatenate(
                [kv_ref[pl.ds(start, count), i].reshape(count * piece_rows, head_size) for kv_ref in kv_refs], axis=0
            )
            for i in range(2)
        )
        values = values.T
        key_pos = jnp.concatenate(
            [(i * blocks + start + j) * rows + in_block for i in range(pieces) for j in range(count)], axis=0
        )
        valid = (key_pos >= starts) & (key_pos <= query_pos)
        scores = [
            jnp.where(valid, jnp.dot(keys, queries_ref[head], preferred_element_type=jnp.float32), NEG)
            for head in range(heads)
        ]
        for head in range(heads):
            top = jnp.max(scores[head], axis=0, keepdims=True)
            if old is not None:
                old_top, old_total, old_sums = old(head)
                top = jnp.maximum(old_top, top)
            weights = jnp.exp2((scores[head] - top) * slope)
            total = jnp.sum(weights, axis=0, keepdims=True)
            sums = jnp.dot(values, weights.astype(jnp.bfloat16), preferred_element_type=jnp.float32)
            if old is not None:
                factor = jnp.exp2((old_top - top) * slope)
                total = old_total * factor + total
                sums = old_sums * factor + sums
            emit(head, top, total, sums)

    def old_state(head):
        return old_stats_ref[head : head + 1], old_stats_ref[heads + head : heads + head + 1], old_sums_ref[head]

    def keep(head, top, total, sums):
        stats_ref[head : head + 1] = top
        stats_ref[heads + head : heads + head + 1] = total
        sums_ref[head] = sums

    def send(head):
        columns = pl.ds(head * head_size, head_size)
        return pltpu.make_async_copy(result_ref.at[:, columns], out_ref.at[:, columns], sent.at[head])

    def finish(head, top, total, sums):
        del top
        result_ref[:, head * head_size : (head + 1) * head_size] = (sums * (1.0 / total)).astype(result_ref.dtype).T
        send(head).start()

    if blocks == step_blocks:
        if first or not tail:
            step(0, blocks, None if first else old_state, keep)
        else:
            emit = finish if last else keep
            reach = 0
            for count in sorted({max(blocks // 4, 1), max(blocks // 2, 1), blocks}):
                pl.when((own >= reach) & (own < count))(functools.partial(step, 0, count, old_state, emit))
                reach = count
    else:
        if last:
            stats_ref, sums_ref = refs[-2:]
        if first:
            stats_ref[...] = jnp.concatenate([jnp.full((heads, rows), NEG), jnp.zeros((heads, rows))], axis=0)
            sums_ref[...] = jnp.zeros_like(sums_ref)
        else:
            stats_ref[...] = old_stats_ref[...]
            sums_ref[...] = old_sums_ref[...]

        def new_state(head):
            return stats_ref[head : head + 1], stats_ref[heads + head : heads + head + 1], sums_ref[head]

        low = first_key // rows // step_blocks if pieces == 1 else 0
        high = jnp.minimum(own // step_blocks + 1, blocks // step_blocks)

        @pl.loop(low, high)
        def _(index):
            step(index, step_blocks, new_state, keep)

        if last:
            for head in range(heads):
                finish(head, *new_state(head))
    if last:
        for head in range(heads):
            send(head).wait()


def attend(place, first, tail, last, lengths, queries, kvs, state, heads):
    blocks, _, piece_rows, head_size = kvs[0].shape
    rows = queries.shape[0] if first else queries.shape[2]
    stats = jax.ShapeDtypeStruct((2 * heads, rows), jnp.float32)
    sums = jax.ShapeDtypeStruct((heads, head_size, rows), jnp.float32)
    starts = jax.ShapeDtypeStruct((1, rows), jnp.int32)
    turned = jax.ShapeDtypeStruct((heads, head_size, rows), queries.dtype)
    whole = pl.BlockSpec(memory_space=pltpu.VMEM)
    operands, in_specs = [queries, *kvs], [whole] * (1 + len(kvs))
    if first or blocks > math.gcd(blocks, STEP_BLOCKS):
        operands.append(lengths)
        in_specs.append(pl.BlockSpec(memory_space=pltpu.SMEM))
    scratch = []
    if last:
        out_shape = jax.ShapeDtypeStruct((rows, heads * head_size), queries.dtype)
        out_specs = pl.BlockSpec(memory_space=pl.ANY)
        scratch = [pltpu.VMEM(out_shape.shape, out_shape.dtype), pltpu.SemaphoreType.DMA((heads,))]
        if blocks > math.gcd(blocks, STEP_BLOCKS):
            scratch += [pltpu.VMEM(stats.shape, stats.dtype), pltpu.VMEM(sums.shape, sums.dtype)]
    else:
        out_shape = (stats, sums, starts, turned) if first else (stats, sums)
        out_specs = (whole,) * len(out_shape)
    return pl.pallas_call(
        functools.partial(attention_kernel, head_size, place, first, tail, last, len(kvs)),
        out_shape=out_shape,
        in_specs=in_specs + [whole] * len(state),
        out_specs=out_specs,
        scratch_shapes=scratch,
        compiler_params=pltpu.CompilerParams(vmem_limit_bytes=32 * 1024 * 1024),
        cost_estimate=pl.CostEstimate(flops=1, bytes_accessed=1, transcendentals=0),
    )(*operands, *state)


def all_blocks(block, axis):
    size = lax.axis_size(axis)
    return lax.all_to_all(jnp.broadcast_to(block, (size,) + block.shape), axis, 0, 0)


def exchange(piece, axis, bits):
    return lax.ppermute(piece, axis, [(i, i ^ bits) for i in range(lax.axis_size(axis))])


def body(queries, key_rows, value_rows, document_lengths):
    seqs, rows, width = queries.shape
    heads = width // key_rows.shape[2]
    assert lax.axis_size("head") == 4
    results = []
    for seq in range(seqs):
        lengths = document_lengths[seq : seq + 1]
        piece_0 = all_blocks(jnp.stack([key_rows[seq], value_rows[seq]]), "ctx")
        half = piece_0.shape[0] // 2
        piece_2 = exchange(piece_0, "head", 2)
        piece_1 = [exchange(piece_0[:half], "head", 1), exchange(piece_0[half:], "head", 1)]
        *state, starts, turned = attend(0, True, False, False, lengths, queries[seq], [piece_0], (), heads)
        state = attend(1, False, False, False, lengths, turned, piece_1, (*state, starts), heads)
        piece_2, state = lax.optimization_barrier((piece_2, state))
        piece_3 = exchange(piece_2, "head", 1)
        state = attend(2, False, True, False, lengths, turned, [piece_2], (*state, starts), heads)
        results.append(attend(3, False, True, True, lengths, turned, [piece_3], (*state, starts), heads))
    return jnp.stack(results)


def solution(mesh):
    in_specs = (
        P(None, "ctx", "head"),
        P(None, ("ctx", "head"), None),
        P(None, ("ctx", "head"), None),
        P(),
    )
    out_specs = P(None, "ctx", "head")
    return jax.shard_map(body, mesh=mesh, in_specs=in_specs, out_specs=out_specs, check_vma=False)
```

time: 29.3 us -> 26.2 us (0.89)
  waiting for transfers between devices: 4.36 us -> 2.34 us
  Pallas kernels: 6.12 us -> 4.47 us
  starting transfers between devices: 1.53 us -> 2.08 us
    ppermute x3 -> x4, waiting for transfers between devices: 4.36 us -> 2.34 us  [exchange(): lax.ppermute(piece, axis, [(i, i ^ bits) for i in range(lax.axis_size(axi...]
    pallas_call x4, Pallas kernels: 6.12 us -> 4.47 us  [attend(): pl.pallas_call(functools.partial(attention_kernel, head_size, place, firs...]
    ppermute x3 -> x4, starting transfers between devices: 1.53 us -> 2.08 us  [exchange(): lax.ppermute(piece, axis, [(i, i ^ bits) for i in range(lax.axis_size(axi...]
  transfers between devices with their start and end apart: 3 -> 4, of which waited for: 2 -> 2; matrix products, arithmetic and copies ran while one was open for 0% -> 0% of each run, Pallas kernels for 15% -> 13%
where the time goes in v8:
time: 26.2 us; the launch traced here: 25.9 us
  blocking collectives  16 us (61%)
  Pallas kernels  4.47 us (17%)
  waiting for transfers between devices  2.34 us (9%)
  starting transfers between devices  2.08 us (8%)
  other arithmetic  0.74 us (3%)
    all_to_all x1, blocking collectives, all_blocks(): lax.all_to_all(jnp.broadcast_to(block, (size,) + block.shape), axis, 0, 0)  16 us
    pallas_call x4, Pallas kernels, attend(): pl.pallas_call(functools.partial(attention_kernel, head_size, place, firs...  4.47 us
    ppermute x4, waiting for transfers between devices, exchange(): lax.ppermute(piece, axis, [(i, i ^ bits) for i in range(lax.axis_size(axi...  2.34 us
    ppermute x4, starting transfers between devices, exchange(): lax.ppermute(piece, axis, [(i, i ^ bits) for i in range(lax.axis_size(axi...  2.08 us
    another operation x1, other arithmetic, body(): piece_0 = all_blocks(jnp.stack([key_rows[seq], value_rows[seq]]), 'ctx')  0.74 us
  transfers between devices with their start and end apart: 4, of which 2 were waited for; matrix products, arithmetic and copies ran while one was open for 0% of the time, Pallas kernels for 13%

profile of v8, /device:TPU:0, one launch (start us, length us, event | category | flops | bytes accessed | tf_op | source)
XLA Modules:
  0.0 25.9 jit_solution(17318276432232014451)
XLA Ops:
  0.0 0.7 %pad_maximum_fusion = bf16[2,64,128]{2,1,0:T(8,128)(2,1)S(1)} fusion(bf16[1,64,128]{2,1,0:T(8,128)(2,1)} %param.6, bf16[1,64,128]{2,1,0:T(8,128)(2,1)} %param.5), kind=kLoop, calls=%fused_computation | loop fusion | flops 16384 | bytes 65536 | tf_op jit(solution)/shard_map/stack | solution.py:186
  0.8 16.0 %all_to_all.5.refs_1_ = bf16[8,2,64,128]{3,2,1,0:T(8,128)(2,1)S(1)} all-to-all(bf16[8,2,64,128]{3,2,1,0:T(8,128)(2,1)S(1)} %broadcast_in_dim.3), channel_id=1, replica_groups=mesh['ctx'=8,'head'=4] {'ctx'}, dimensions={0} | all-to-all | bytes 524288 | tf_op jit(solution)/shard_map/all_to_all | solution.py:172
  16.8 0.0 copy-start
  16.8 1.5 %collective-permute-start = (bf16[8,2,64,128]{3,2,1,0:T(8,128)(2,1)S(1)}, bf16[8,2,64,128]{3,2,1,0:T(8,128)(2,1)S(1)}, u32[]{:S(2)}, u32[]{:S(2)}) collective-permute-start(bf16[8,2,64,128]{3,2,1,0:T(8,128)(2,1)S(1)} %all_to_all.5.refs_1_), channel_id=1, source_target_pairs={{0,2},{1,3},{2,0},{3,1},{4,6},{5,7},{6,4},{7,5},{8,10},{9,11},{10,... | collective-permute-start | bytes 786440 | tf_op jit(solution)/shard_map/ppermute | solution.py:176
  18.3 0.1 collective-permute-start.2
  18.4 0.0 copy-start.1
  18.4 0.5 %collective-permute-start.1 = (bf16[4,2,64,128]{3,2,1,0:T(8,128)(2,1)S(1)}, bf16[4,2,64,128]{3,2,1,0:T(8,128)(2,1)S(1)}, u32[]{:S(2)}, u32[]{:S(2)}) collective-permute-start(bf16[4,2,64,128]{3,2,1,0:T(8,128)(2,1)S(1)} %get-tuple-element.28), channel_id=1, source_target_pairs={{0,1},{1,0},{2,3},{3,2},{4,5},{5,4},{6,7},{7,6},{8,9},{9,8},{10,11... | collective-permute-start | bytes 393224 | tf_op jit(solution)/shard_map/ppermute | solution.py:176
  18.9 0.0 copy-done
  18.9 0.2 copy-done.1
  19.0 1.7 %shard_map.46 = (f32[8,256]{1,0:T(8,128)S(1)}, f32[4,128,256]{2,1,0:T(8,128)S(1)}, s32[1,256]{1,0:T(1,128)S(1)}, bf16[4,128,256]{2,1,0:T(8,128)(2,1)S(1)}) custom-call(bf16[256,512]{1,0:T(8,128)(2,1)S(1)} %bitcast.2, bf16[8,2,64,128]{3,2,1,0:T(8,128)(2,1)S(1)} %all_to_all.5.refs_1_, s32[1,4]{1,0:T(1,128)S(1)} %copy-done.1), custom_call_target="tpu_custom_call" | custom-call | flops 1 | bytes 1 | tf_op jit(solution)/shard_map/pallas_call | solution.py:159
  20.7 0.0 collective-permute-done.2.refs_2_
  20.7 0.0 collective-permute-done.1.refs_1_
  20.7 1.1 %shard_map.47 = (f32[8,256]{1,0:T(8,128)S(1)}, f32[4,128,256]{2,1,0:T(8,128)S(1)}) custom-call(bf16[4,128,256]{2,1,0:T(8,128)(2,1)S(1)} %get-tuple-element.16.refs_0_, bf16[4,2,64,128]{3,2,1,0:T(8,128)(2,1)S(1)} %collective-permute-done.1.refs_1_, bf16[4,2,64,128]{3,2,1,0:T(8,128)(2,1)S(1)} %collective-permute-done.2.refs_2_, ...), custom_call_target="tpu_custom_call" | custom-call | flops 1 | bytes 1 | tf_op jit(solution)/shard_map/pallas_call | solution.py:159
  21.8 1.3 %collective-permute-done.refs_1_ = bf16[8,2,64,128]{3,2,1,0:T(8,128)(2,1)S(1)} collective-permute-done((bf16[8,2,64,128]{3,2,1,0:T(8,128)(2,1)S(1)}, bf16[8,2,64,128]{3,2,1,0:T(8,128)(2,1)S(1)}, u32[]{:S(2)}, u32[]{:S(2)}) %collective-permute-start) | collective-permute-done | bytes 262176 | tf_op jit(solution)/shard_map/ppermute | solution.py:176
  23.1 0.0 collective-permute-start.3
  23.1 0.5 %shard_map.48 = (f32[8,256]{1,0:T(8,128)S(1)}, f32[4,128,256]{2,1,0:T(8,128)S(1)}) custom-call(bf16[4,128,256]{2,1,0:T(8,128)(2,1)S(1)} %get-tuple-element.16.refs_0_, bf16[8,2,64,128]{3,2,1,0:T(8,128)(2,1)S(1)} %collective-permute-done.refs_1_, f32[8,256]{1,0:T(8,128)S(1)} %get-tuple-element.23.refs_2_, f32[4,128,256]{2,1,0:T(8,128)S(1)} %get-tuple-element.24.refs_3_, ...), custom_call_target="tpu_custom_call" | custom-call | flops 1 | bytes 1 | tf_op jit(solution)/shard_map/pallas_call | solution.py:159
  23.6 1.0 %collective-permute-done.3.refs_1_ = bf16[8,2,64,128]{3,2,1,0:T(8,128)(2,1)S(1)} collective-permute-done((bf16[8,2,64,128]{3,2,1,0:T(8,128)(2,1)S(1)}, bf16[8,2,64,128]{3,2,1,0:T(8,128)(2,1)S(1)}, u32[]{:S(2)}, u32[]{:S(2)}) %collective-permute-start.3) | collective-permute-done | bytes 262176 | tf_op jit(solution)/shard_map/ppermute | solution.py:176
  24.7 1.2 %shard_map.49 = bf16[256,512]{1,0:T(8,128)(2,1)} custom-call(bf16[4,128,256]{2,1,0:T(8,128)(2,1)S(1)} %get-tuple-element.16.refs_0_, bf16[8,2,64,128]{3,2,1,0:T(8,128)(2,1)S(1)} %collective-permute-done.3.refs_1_, f32[8,256]{1,0:T(8,128)S(1)} %get-tuple-element.25.refs_2_, f32[4,128,256]{2,1,0:T(8,128)S(1)} %get-tuple-element.26.refs_3_, ...), custom_call_target="tpu_custom_call" | custom-call | flops 1 | bytes 1 | tf_op jit(solution)/shard_map/pallas_call | solution.py:159
  (2 shorter events, 0.1 us)
Async XLA Ops:
  16.8 2.1 %copy-start = (bf16[1,256,512]{2,1,0:T(8,128)(2,1)S(1)}, bf16[1,256,512]{2,1,0:T(8,128)(2,1)}, u32[]{:S(2)}) copy-start(bf16[1,256,512]{2,1,0:T(8,128)(2,1)} %param.4) | copy-start | bytes 786436
  16.8 6.4 %collective-permute-start = (bf16[8,2,64,128]{3,2,1,0:T(8,128)(2,1)S(1)}, bf16[8,2,64,128]{3,2,1,0:T(8,128)(2,1)S(1)}, u32[]{:S(2)}, u32[]{:S(2)}) collective-permute-start(bf16[8,2,64,128]{3,2,1,0:T(8,128)(2,1)S(1)} %all_to_all.5.refs_1_), channel_id=1, source_target_pairs={{0,2},{1,3},{2,0},{3,1},{4,6},{5,7},{6,4},{7,5},{8,10},{9,11},{10,... | collective-permute-start | bytes 786440 | tf_op jit(solution)/shard_map/ppermute | solution.py:176
  18.3 2.4 %collective-permute-start.2 = (bf16[4,2,64,128]{3,2,1,0:T(8,128)(2,1)S(1)}, bf16[4,2,64,128]{3,2,1,0:T(8,128)(2,1)S(1)}, u32[]{:S(2)}, u32[]{:S(2)}) collective-permute-start(bf16[4,2,64,128]{3,2,1,0:T(8,128)(2,1)S(1)} %get-tuple-element.27), channel_id=1, source_target_pairs={{0,1},{1,0},{2,3},{3,2},{4,5},{5,4},{6,7},{7,6},{8,9},{9,8},{10,11... | collective-permute-start | bytes 393224 | tf_op jit(solution)/shard_map/ppermute | solution.py:176
  18.4 0.7 %copy-start.1 = (s32[1,4]{1,0:T(1,128)S(1)}, s32[1,4]{1,0:T(1,128)}, u32[]{:S(2)}) copy-start(s32[1,4]{1,0:T(1,128)} %refs_2_.1) | copy-start | bytes 52
  18.4 2.3 %collective-permute-start.1 = (bf16[4,2,64,128]{3,2,1,0:T(8,128)(2,1)S(1)}, bf16[4,2,64,128]{3,2,1,0:T(8,128)(2,1)S(1)}, u32[]{:S(2)}, u32[]{:S(2)}) collective-permute-start(bf16[4,2,64,128]{3,2,1,0:T(8,128)(2,1)S(1)} %get-tuple-element.28), channel_id=1, source_target_pairs={{0,1},{1,0},{2,3},{3,2},{4,5},{5,4},{6,7},{7,6},{8,9},{9,8},{10,11... | collective-permute-start | bytes 393224 | tf_op jit(solution)/shard_map/ppermute | solution.py:176
  23.1 1.5 %collective-permute-start.3 = (bf16[8,2,64,128]{3,2,1,0:T(8,128)(2,1)S(1)}, bf16[8,2,64,128]{3,2,1,0:T(8,128)(2,1)S(1)}, u32[]{:S(2)}, u32[]{:S(2)}) collective-permute-start(bf16[8,2,64,128]{3,2,1,0:T(8,128)(2,1)S(1)} %collective-permute-done.refs_1_), channel_id=1, source_target_pairs={{0,1},{1,0},{2,3},{3,2},{4,5},{5,4},{6,7},{7,6},{8,9},{9,8},{10,11... | collective-permute-start | bytes 786440 | tf_op jit(solution)/shard_map/ppermute | solution.py:176

commit v9 on v8

--- a/solution.py
+++ b/solution.py
@@ -12,10 +12,11 @@
 STEP_BLOCKS = 8
 
 
-def attention_kernel(head_size, place, first, tail, last, pieces, *refs):
+def attention_kernel(head_size, parts, kind, *refs):
+    first, last = kind == "first", kind == "last"
     queries_ref, *refs = refs
-    kv_refs, refs = refs[:pieces], refs[pieces:]
-    blocks, _, piece_rows, _ = kv_refs[0].shape
+    kv_refs, refs = refs[: len(parts)], refs[len(parts) :]
+    blocks = kv_refs[0].shape[0]
     step_blocks = math.gcd(blocks, STEP_BLOCKS)
     lengths_ref = None
     if first or blocks > step_blocks:
@@ -27,8 +28,9 @@
         old_stats_ref, old_sums_ref, starts_ref, out_ref, result_ref, sent = refs[:6]
     else:
         old_stats_ref, old_sums_ref, starts_ref, stats_ref, sums_ref = refs
-    own, piece = lax.axis_index("ctx"), lax.axis_index("head") ^ place
+    own, head_place = lax.axis_index("ctx"), lax.axis_index("head")
     heads, _, rows = old_sums_ref.shape
+    piece_rows = rows // lax.axis_size("head")
     slope = math.log2(math.e) / math.sqrt(head_size)
 
     query_pos = own * rows + lax.broadcasted_iota(jnp.int32, (1, rows), 1)
@@ -47,20 +49,21 @@
         for head in range(heads):
             turned_ref[head] = queries_ref[:, head * head_size : (head + 1) * head_size].T
         queries_ref = turned_ref
-    in_block = piece * piece_rows + lax.broadcasted_iota(jnp.int32, (piece_rows, rows), 0)
+    in_piece = lax.broadcasted_iota(jnp.int32, (piece_rows, rows), 0)
 
     def step(index, count, old, emit):
-        start = index * step_blocks
+        here = pl.ds(index * step_blocks, count)
         keys, values = (
-            jnp.concatenate(
-                [kv_ref[pl.ds(start, count), i].reshape(count * piece_rows, head_size) for kv_ref in kv_refs], axis=0
-            )
-            for i in range(2)
+            jnp.concatenate([kv_ref[here, i].reshape(-1, head_size) for kv_ref in kv_refs], axis=0) for i in range(2)
         )
         values = values.T
-        key_pos = jnp.concatenate(
-            [(i * blocks + start + j) * rows + in_block for i in range(pieces) for j in range(count)], axis=0
-        )
+        key_pos = []
+        for kv_ref, (flip, place, skip) in zip(kv_refs, parts):
+            for i in range(count):
+                block = 2 * (index * step_blocks + i) + (own ^ flip) % 2
+                start = block * rows + (head_place ^ place) * piece_rows + skip
+                key_pos.append(start + in_piece[: kv_ref.shape[2]])
+        key_pos = jnp.concatenate(key_pos, axis=0)
         valid = (key_pos >= starts) & (key_pos <= query_pos)
         scores = [
             jnp.where(valid, jnp.dot(keys, queries_ref[head], preferred_element_type=jnp.float32), NEG)
@@ -98,13 +101,13 @@
         send(head).start()
 
     if blocks == step_blocks:
-        if first or not tail:
-            step(0, blocks, None if first else old_state, keep)
+        if first:
+            step(0, blocks, None, keep)
         else:
             emit = finish if last else keep
             reach = 0
             for count in sorted({max(blocks // 4, 1), max(blocks // 2, 1), blocks}):
-                pl.when((own >= reach) & (own < count))(functools.partial(step, 0, count, old_state, emit))
+                pl.when((own // 2 >= reach) & (own // 2 < count))(functools.partial(step, 0, count, old_state, emit))
                 reach = count
     else:
         if last:
@@ -119,10 +122,7 @@
         def new_state(head):
             return stats_ref[head : head + 1], stats_ref[heads + head : heads + head + 1], sums_ref[head]
 
-        low = first_key // rows // step_blocks if pieces == 1 else 0
-        high = jnp.minimum(own // step_blocks + 1, blocks // step_blocks)
-
-        @pl.loop(low, high)
+        @pl.loop(first_key // rows // 2 // step_blocks, own // 2 // step_blocks + 1)
         def _(index):
             step(index, step_blocks, new_state, keep)
 
@@ -134,8 +134,9 @@
             send(head).wait()
 
 
-def attend(place, first, tail, last, lengths, queries, kvs, state, heads):
-    blocks, _, piece_rows, head_size = kvs[0].shape
+def attend(parts, kind, lengths, queries, kvs, state, heads):
+    first, last = kind == "first", kind == "last"
+    blocks, head_size = kvs[0].shape[0], kvs[0].shape[3]
     rows = queries.shape[0] if first else queries.shape[2]
     stats = jax.ShapeDtypeStruct((2 * heads, rows), jnp.float32)
     sums = jax.ShapeDtypeStruct((heads, head_size, rows), jnp.float32)
@@ -157,7 +158,7 @@
         out_shape = (stats, sums, starts, turned) if first else (stats, sums)
         out_specs = (whole,) * len(out_shape)
     return pl.pallas_call(
-        functools.partial(attention_kernel, head_size, place, first, tail, last, len(kvs)),
+        functools.partial(attention_kernel, head_size, parts, kind),
         out_shape=out_shape,
         in_specs=in_specs + [whole] * len(state),
         out_specs=out_specs,
@@ -167,9 +168,11 @@
     )(*operands, *state)
 
 
-def all_blocks(block, axis):
+def same_parity_blocks(block, axis):
     size = lax.axis_size(axis)
-    return lax.all_to_all(jnp.broadcast_to(block, (size,) + block.shape), axis, 0, 0)
+    groups = [list(range(parity, size, 2)) for parity in range(2)]
+    spread = jnp.broadcast_to(block, (size // 2,) + block.shape)
+    return lax.all_to_all(spread, axis, 0, 0, axis_index_groups=groups)
 
 
 def exchange(piece, axis, bits):
@@ -179,20 +182,30 @@
 def body(queries, key_rows, value_rows, document_lengths):
     seqs, rows, width = queries.shape
     heads = width // key_rows.shape[2]
-    assert lax.axis_size("head") == 4
+    assert lax.axis_size("head") == 4 and lax.axis_size("ctx") % 2 == 0
     results = []
     for seq in range(seqs):
-        lengths = document_lengths[seq : seq + 1]
-        piece_0 = all_blocks(jnp.stack([key_rows[seq], value_rows[seq]]), "ctx")
-        half = piece_0.shape[0] // 2
-        piece_2 = exchange(piece_0, "head", 2)
-        piece_1 = [exchange(piece_0[:half], "head", 1), exchange(piece_0[half:], "head", 1)]
-        *state, starts, turned = attend(0, True, False, False, lengths, queries[seq], [piece_0], (), heads)
-        state = attend(1, False, False, False, lengths, turned, piece_1, (*state, starts), heads)
-        piece_2, state = lax.optimization_barrier((piece_2, state))
-        piece_3 = exchange(piece_2, "head", 1)
-        state = attend(2, False, True, False, lengths, turned, [piece_2], (*state, starts), heads)
-        results.append(attend(3, False, True, True, lengths, turned, [piece_3], (*state, starts), heads))
+        run = functools.partial(attend, lengths=document_lengths[seq : seq + 1], heads=heads)
+        own = same_parity_blocks(jnp.stack([key_rows[seq], value_rows[seq]]), "ctx")
+        half = own.shape[2] // 2
+
+        across = exchange(own, "ctx", 1)
+        far = exchange(own, "head", 2)
+        near = [exchange(own[:, :, :half], "head", 1), exchange(own[:, :, half:], "head", 1)]
+        stats, sums, starts, turned = run([(0, 0, 0)], "first", queries=queries[seq], kvs=[own], state=())
+        run = functools.partial(run, queries=turned)
+        stats, sums = run([(0, 1, 0), (0, 1, half)], "middle", kvs=near, state=(stats, sums, starts))
+        across, far, stats, sums = lax.optimization_barrier((across, far, stats, sums))
+
+        corner = [exchange(across[:, :, :half], "head", 2), exchange(far[:, :, half:], "ctx", 1)]
+        near = [exchange(across, "head", 1), exchange(far, "head", 1)]
+        stats, sums = run([(1, 0, 0), (0, 2, 0)], "middle", kvs=[across, far], state=(stats, sums, starts))
+        stats, sums = run([(1, 1, 0), (0, 3, 0)], "middle", kvs=near, state=(stats, sums, starts))
+        *corner, stats, sums = lax.optimization_barrier((*corner, stats, sums))
+
+        near = [exchange(part, "head", 1) for part in corner]
+        stats, sums = run([(1, 2, 0), (1, 2, half)], "middle", kvs=corner, state=(stats, sums, starts))
+        results.append(run([(1, 3, 0), (1, 3, half)], "last", kvs=near, state=(stats, sums, starts)))
     return jnp.stack(results)
 
 

time: 26.2 us -> 28.9 us (1.10)
  starting transfers between devices: 2.08 us -> 6.65 us
  blocking collectives: 16 us -> 12.3 us
  waiting for transfers between devices: 2.34 us -> 4.2 us
    ppermute x4 -> x10, starting transfers between devices: 2.08 us -> 6.65 us  [exchange(): lax.ppermute(piece, axis, [(i, i ^ bits) for i in range(lax.axis_size(axi...]
    all_to_all x1, blocking collectives: 16 us -> 12.3 us  [same_parity_blocks(): return lax.all_to_all(spread, axis, 0, 0, axis_index_groups=groups)]
    ppermute x4 -> x10, waiting for transfers between devices: 2.34 us -> 4.2 us  [exchange(): lax.ppermute(piece, axis, [(i, i ^ bits) for i in range(lax.axis_size(axi...]
    pallas_call x4 -> x6, Pallas kernels: 4.47 us -> 4.29 us  [attend(): pl.pallas_call(functools.partial(attention_kernel, head_size, parts, kind...]
  transfers between devices with their start and end apart: 4 -> 10, of which waited for: 2 -> 5; matrix products, arithmetic and copies ran while one was open for 0% -> 0% of each run, Pallas kernels for 13% -> 11%
where the time goes in v9:
time: 28.9 us; the launch traced here: 28.5 us
  blocking collectives  12.3 us (43%)
  starting transfers between devices  6.65 us (23%)
  Pallas kernels  4.29 us (15%)
  waiting for transfers between devices  4.2 us (15%)
  other arithmetic  0.74 us (3%)
    all_to_all x1, blocking collectives, same_parity_blocks(): return lax.all_to_all(spread, axis, 0, 0, axis_index_groups=groups)  12.3 us
    ppermute x10, starting transfers between devices, exchange(): lax.ppermute(piece, axis, [(i, i ^ bits) for i in range(lax.axis_size(axi...  6.65 us
    pallas_call x6, Pallas kernels, attend(): pl.pallas_call(functools.partial(attention_kernel, head_size, parts, kind...  4.29 us
    ppermute x10, waiting for transfers between devices, exchange(): lax.ppermute(piece, axis, [(i, i ^ bits) for i in range(lax.axis_size(axi...  4.2 us
    another operation x1, other arithmetic, body(): own = same_parity_blocks(jnp.stack([key_rows[seq], value_rows[seq]]), 'ctx')  0.74 us
  transfers between devices with their start and end apart: 10, of which 5 were waited for; matrix products, arithmetic and copies ran while one was open for 0% of the time, Pallas kernels for 11%

profile of v9, /device:TPU:0, one launch (start us, length us, event | category | flops | bytes accessed | tf_op | source)
XLA Modules:
  0.0 28.5 jit_solution(13099900867212623495)
XLA Ops:
  0.0 0.7 %pad_maximum_fusion = bf16[2,64,128]{2,1,0:T(8,128)(2,1)S(1)} fusion(bf16[1,64,128]{2,1,0:T(8,128)(2,1)} %param.6, bf16[1,64,128]{2,1,0:T(8,128)(2,1)} %param.5), kind=kLoop, calls=%fused_computation | loop fusion | flops 16384 | bytes 65536 | tf_op jit(solution)/shard_map/stack | solution.py:189
  0.8 0.0 copy-start
  0.8 12.3 %all_to_all.5.refs_1_ = bf16[4,2,64,128]{3,2,1,0:T(8,128)(2,1)S(1)} all-to-all(bf16[4,2,64,128]{3,2,1,0:T(8,128)(2,1)S(1)} %broadcast_in_dim.3), channel_id=1, replica_groups={{0,8,16,24},{4,12,20,28},{1,9,17,25},{5,13,21,29},{2,10,18,26},{6,14,22..., dimensions={0} | all-to-all | bytes 262144 | tf_op jit(solution)/shard_map/all_to_all | solution.py:175
  13.1 1.5 %collective-permute-start.1 = (bf16[4,2,64,128]{3,2,1,0:T(8,128)(2,1)S(1)}, bf16[4,2,64,128]{3,2,1,0:T(8,128)(2,1)S(1)}, u32[]{:S(2)}, u32[]{:S(2)}) collective-permute-start(bf16[4,2,64,128]{3,2,1,0:T(8,128)(2,1)S(1)} %all_to_all.5.refs_1_), channel_id=1, source_target_pairs={{0,2},{1,3},{2,0},{3,1},{4,6},{5,7},{6,4},{7,5},{8,10},{9,11},{10,... | collective-permute-start | bytes 393224 | tf_op jit(solution)/shard_map/ppermute | solution.py:179
  14.6 1.5 %collective-permute-start = (bf16[4,2,64,128]{3,2,1,0:T(8,128)(2,1)S(1)}, bf16[4,2,64,128]{3,2,1,0:T(8,128)(2,1)S(1)}, u32[]{:S(2)}, u32[]{:S(2)}) collective-permute-start(bf16[4,2,64,128]{3,2,1,0:T(8,128)(2,1)S(1)} %all_to_all.5.refs_1_), channel_id=1, source_target_pairs={{0,4},{4,0},{8,12},{12,8},{16,20},{20,16},{24,28},{28,24},{1,5},{5... | collective-permute-start | bytes 393224 | tf_op jit(solution)/shard_map/ppermute | solution.py:179
  16.1 0.1 collective-permute-start.3
  16.2 0.0 copy-start.1
  16.2 0.5 %collective-permute-start.2 = (bf16[4,2,32,128]{3,2,1,0:T(8,128)(2,1)S(1)}, bf16[4,2,32,128]{3,2,1,0:T(8,128)(2,1)S(1)}, u32[]{:S(2)}, u32[]{:S(2)}) collective-permute-start(bf16[4,2,32,128]{3,2,1,0:T(8,128)(2,1)S(1)} %get-tuple-element.46), channel_id=1, source_target_pairs={{0,1},{1,0},{2,3},{3,2},{4,5},{5,4},{6,7},{7,6},{8,9},{9,8},{10,11... | collective-permute-start | bytes 196616 | tf_op jit(solution)/shard_map/ppermute | solution.py:179
  16.7 0.0 copy-done
  16.7 0.2 copy-done.1
  16.9 1.2 %shard_map.46 = (f32[8,256]{1,0:T(8,128)S(1)}, f32[4,128,256]{2,1,0:T(8,128)S(1)}, s32[1,256]{1,0:T(1,128)S(1)}, bf16[4,128,256]{2,1,0:T(8,128)(2,1)S(1)}) custom-call(bf16[256,512]{1,0:T(8,128)(2,1)S(1)} %bitcast.2, bf16[4,2,64,128]{3,2,1,0:T(8,128)(2,1)S(1)} %all_to_all.5.refs_1_, s32[1,4]{1,0:T(1,128)S(1)} %copy-done.1), custom_call_target="tpu_custom_call" | custom-call | flops 1 | bytes 1 | tf_op jit(solution)/shard_map/pallas_call | solution.py:160
  18.1 0.0 collective-permute-done.3.refs_2_
  18.1 0.0 collective-permute-done.2.refs_1_
  18.1 0.4 %shard_map.47 = (f32[8,256]{1,0:T(8,128)S(1)}, f32[4,128,256]{2,1,0:T(8,128)S(1)}) custom-call(bf16[4,128,256]{2,1,0:T(8,128)(2,1)S(1)} %get-tuple-element.25.refs_0_, bf16[4,2,32,128]{3,2,1,0:T(8,128)(2,1)S(1)} %collective-permute-done.2.refs_1_, bf16[4,2,32,128]{3,2,1,0:T(8,128)(2,1)S(1)} %collective-permute-done.3.refs_2_, ...), custom_call_target="tpu_custom_call" | custom-call | flops 1 | bytes 1 | tf_op jit(solution)/shard_map/pallas_call | solution.py:160
  18.6 0.0 collective-permute-done.1.refs_2_
  18.6 1.0 %collective-permute-done.refs_1_ = bf16[4,2,64,128]{3,2,1,0:T(8,128)(2,1)S(1)} collective-permute-done((bf16[4,2,64,128]{3,2,1,0:T(8,128)(2,1)S(1)}, bf16[4,2,64,128]{3,2,1,0:T(8,128)(2,1)S(1)}, u32[]{:S(2)}, u32[]{:S(2)}) %collective-permute-start) | collective-permute-done | bytes 131104 | tf_op jit(solution)/shard_map/ppermute | solution.py:179
  19.6 0.0 collective-permute-start.6
  19.6 0.5 %collective-permute-start.7 = (bf16[4,2,64,128]{3,2,1,0:T(8,128)(2,1)S(1)}, bf16[4,2,64,128]{3,2,1,0:T(8,128)(2,1)S(1)}, u32[]{:S(2)}, u32[]{:S(2)}) collective-permute-start(bf16[4,2,64,128]{3,2,1,0:T(8,128)(2,1)S(1)} %collective-permute-done.1.refs_2_), channel_id=1, source_target_pairs={{0,1},{1,0},{2,3},{3,2},{4,5},{5,4},{6,7},{7,6},{8,9},{9,8},{10,11... | collective-permute-start | bytes 393224 | tf_op jit(solution)/shard_map/ppermute | solution.py:179
  20.1 1.6 %collective-permute-start.5 = (bf16[4,2,32,128]{3,2,1,0:T(8,128)(2,1)S(1)}, bf16[4,2,32,128]{3,2,1,0:T(8,128)(2,1)S(1)}, u32[]{:S(2)}, u32[]{:S(2)}) collective-permute-start(bf16[4,2,32,128]{3,2,1,0:T(8,128)(2,1)S(1)} %slice.15), channel_id=1, source_target_pairs={{0,4},{4,0},{8,12},{12,8},{16,20},{20,16},{24,28},{28,24},{1,5},{5... | collective-permute-start | bytes 196616 | tf_op jit(solution)/shard_map/ppermute | solution.py:179
  21.7 0.5 %collective-permute-start.4 = (bf16[4,2,32,128]{3,2,1,0:T(8,128)(2,1)S(1)}, bf16[4,2,32,128]{3,2,1,0:T(8,128)(2,1)S(1)}, u32[]{:S(2)}, u32[]{:S(2)}) collective-permute-start(bf16[4,2,32,128]{3,2,1,0:T(8,128)(2,1)S(1)} %slice.14), channel_id=1, source_target_pairs={{0,2},{1,3},{2,0},{3,1},{4,6},{5,7},{6,4},{7,5},{8,10},{9,11},{10,... | collective-permute-start | bytes 196616 | tf_op jit(solution)/shard_map/ppermute | solution.py:179
  22.2 0.5 %shard_map.48 = (f32[8,256]{1,0:T(8,128)S(1)}, f32[4,128,256]{2,1,0:T(8,128)S(1)}) custom-call(bf16[4,128,256]{2,1,0:T(8,128)(2,1)S(1)} %get-tuple-element.25.refs_0_, bf16[4,2,64,128]{3,2,1,0:T(8,128)(2,1)S(1)} %collective-permute-done.refs_1_, bf16[4,2,64,128]{3,2,1,0:T(8,128)(2,1)S(1)} %collective-permute-done.1.refs_2_, ...), custom_call_target="tpu_custom_call" | custom-call | flops 1 | bytes 1 | tf_op jit(solution)/shard_map/pallas_call | solution.py:160
  22.7 0.0 collective-permute-done.6.refs_1_
  22.7 0.0 collective-permute-done.7.refs_2_
  22.7 0.5 %shard_map.49 = (f32[8,256]{1,0:T(8,128)S(1)}, f32[4,128,256]{2,1,0:T(8,128)S(1)}) custom-call(bf16[4,128,256]{2,1,0:T(8,128)(2,1)S(1)} %get-tuple-element.25.refs_0_, bf16[4,2,64,128]{3,2,1,0:T(8,128)(2,1)S(1)} %collective-permute-done.6.refs_1_, bf16[4,2,64,128]{3,2,1,0:T(8,128)(2,1)S(1)} %collective-permute-done.7.refs_2_, ...), custom_call_target="tpu_custom_call" | custom-call | flops 1 | bytes 1 | tf_op jit(solution)/shard_map/pallas_call | solution.py:160
  23.2 1.2 %collective-permute-done.5.refs_2_ = bf16[4,2,32,128]{3,2,1,0:T(8,128)(2,1)S(1)} collective-permute-done((bf16[4,2,32,128]{3,2,1,0:T(8,128)(2,1)S(1)}, bf16[4,2,32,128]{3,2,1,0:T(8,128)(2,1)S(1)}, u32[]{:S(2)}, u32[]{:S(2)}) %collective-permute-start.5) | collective-permute-done | bytes 65568 | tf_op jit(solution)/shard_map/ppermute | solution.py:179
  24.4 1.5 %collective-permute-done.4.refs_1_ = bf16[4,2,32,128]{3,2,1,0:T(8,128)(2,1)S(1)} collective-permute-done((bf16[4,2,32,128]{3,2,1,0:T(8,128)(2,1)S(1)}, bf16[4,2,32,128]{3,2,1,0:T(8,128)(2,1)S(1)}, u32[]{:S(2)}, u32[]{:S(2)}) %collective-permute-start.4) | collective-permute-done | bytes 65568 | tf_op jit(solution)/shard_map/ppermute | solution.py:179
  25.9 0.0 collective-permute-start.8
  25.9 0.5 %collective-permute-start.9 = (bf16[4,2,32,128]{3,2,1,0:T(8,128)(2,1)S(1)}, bf16[4,2,32,128]{3,2,1,0:T(8,128)(2,1)S(1)}, u32[]{:S(2)}, u32[]{:S(2)}) collective-permute-start(bf16[4,2,32,128]{3,2,1,0:T(8,128)(2,1)S(1)} %collective-permute-done.5.refs_2_), channel_id=1, source_target_pairs={{0,1},{1,0},{2,3},{3,2},{4,5},{5,4},{6,7},{7,6},{8,9},{9,8},{10,11... | collective-permute-start | bytes 196616 | tf_op jit(solution)/shard_map/ppermute | solution.py:179
  26.4 0.4 %shard_map.50 = (f32[8,256]{1,0:T(8,128)S(1)}, f32[4,128,256]{2,1,0:T(8,128)S(1)}) custom-call(bf16[4,128,256]{2,1,0:T(8,128)(2,1)S(1)} %get-tuple-element.25.refs_0_, bf16[4,2,32,128]{3,2,1,0:T(8,128)(2,1)S(1)} %collective-permute-done.4.refs_1_, bf16[4,2,32,128]{3,2,1,0:T(8,128)(2,1)S(1)} %collective-permute-done.5.refs_2_, ...), custom_call_target="tpu_custom_call" | custom-call | flops 1 | bytes 1 | tf_op jit(solution)/shard_map/pallas_call | solution.py:160
  26.9 0.3 %collective-permute-done.8.refs_1_ = bf16[4,2,32,128]{3,2,1,0:T(8,128)(2,1)S(1)} collective-permute-done((bf16[4,2,32,128]{3,2,1,0:T(8,128)(2,1)S(1)}, bf16[4,2,32,128]{3,2,1,0:T(8,128)(2,1)S(1)}, u32[]{:S(2)}, u32[]{:S(2)}) %collective-permute-start.8) | collective-permute-done | bytes 65568 | tf_op jit(solution)/shard_map/ppermute | solution.py:179
  27.2 0.2 collective-permute-done.9.refs_2_
  27.4 1.2 %shard_map.51 = bf16[256,512]{1,0:T(8,128)(2,1)} custom-call(bf16[4,128,256]{2,1,0:T(8,128)(2,1)S(1)} %get-tuple-element.25.refs_0_, bf16[4,2,32,128]{3,2,1,0:T(8,128)(2,1)S(1)} %collective-permute-done.8.refs_1_, bf16[4,2,32,128]{3,2,1,0:T(8,128)(2,1)S(1)} %collective-permute-done.9.refs_2_, f32[8,256]{1,0:T(8,128)S(1)} %get-tuple-element.43.refs_3_, ...), custom_call_target="tpu_custom_call" | custom-call | flops 1 | bytes 1 | tf_op jit(solution)/shard_map/pallas_call | solution.py:160
  (4 shorter events, 0.0 us)
Async XLA Ops:
  0.8 15.9 %copy-start = (bf16[1,256,512]{2,1,0:T(8,128)(2,1)S(1)}, bf16[1,256,512]{2,1,0:T(8,128)(2,1)}, u32[]{:S(2)}) copy-start(bf16[1,256,512]{2,1,0:T(8,128)(2,1)} %param.4) | copy-start | bytes 786436
  13.1 5.5 %collective-permute-start.1 = (bf16[4,2,64,128]{3,2,1,0:T(8,128)(2,1)S(1)}, bf16[4,2,64,128]{3,2,1,0:T(8,128)(2,1)S(1)}, u32[]{:S(2)}, u32[]{:S(2)}) collective-permute-start(bf16[4,2,64,128]{3,2,1,0:T(8,128)(2,1)S(1)} %all_to_all.5.refs_1_), channel_id=1, source_target_pairs={{0,2},{1,3},{2,0},{3,1},{4,6},{5,7},{6,4},{7,5},{8,10},{9,11},{10,... | collective-permute-start | bytes 393224 | tf_op jit(solution)/shard_map/ppermute | solution.py:179
  14.6 5.0 %collective-permute-start = (bf16[4,2,64,128]{3,2,1,0:T(8,128)(2,1)S(1)}, bf16[4,2,64,128]{3,2,1,0:T(8,128)(2,1)S(1)}, u32[]{:S(2)}, u32[]{:S(2)}) collective-permute-start(bf16[4,2,64,128]{3,2,1,0:T(8,128)(2,1)S(1)} %all_to_all.5.refs_1_), channel_id=1, source_target_pairs={{0,4},{4,0},{8,12},{12,8},{16,20},{20,16},{24,28},{28,24},{1,5},{5... | collective-permute-start | bytes 393224 | tf_op jit(solution)/shard_map/ppermute | solution.py:179
  16.1 2.0 %collective-permute-start.3 = (bf16[4,2,32,128]{3,2,1,0:T(8,128)(2,1)S(1)}, bf16[4,2,32,128]{3,2,1,0:T(8,128)(2,1)S(1)}, u32[]{:S(2)}, u32[]{:S(2)}) collective-permute-start(bf16[4,2,32,128]{3,2,1,0:T(8,128)(2,1)S(1)} %get-tuple-element.45), channel_id=1, source_target_pairs={{0,1},{1,0},{2,3},{3,2},{4,5},{5,4},{6,7},{7,6},{8,9},{9,8},{10,11... | collective-permute-start | bytes 196616 | tf_op jit(solution)/shard_map/ppermute | solution.py:179
  16.2 0.7 %copy-start.1 = (s32[1,4]{1,0:T(1,128)S(1)}, s32[1,4]{1,0:T(1,128)}, u32[]{:S(2)}) copy-start(s32[1,4]{1,0:T(1,128)} %refs_2_.1) | copy-start | bytes 52
  16.2 1.9 %collective-permute-start.2 = (bf16[4,2,32,128]{3,2,1,0:T(8,128)(2,1)S(1)}, bf16[4,2,32,128]{3,2,1,0:T(8,128)(2,1)S(1)}, u32[]{:S(2)}, u32[]{:S(2)}) collective-permute-start(bf16[4,2,32,128]{3,2,1,0:T(8,128)(2,1)S(1)} %get-tuple-element.46), channel_id=1, source_target_pairs={{0,1},{1,0},{2,3},{3,2},{4,5},{5,4},{6,7},{7,6},{8,9},{9,8},{10,11... | collective-permute-start | bytes 196616 | tf_op jit(solution)/shard_map/ppermute | solution.py:179
  19.6 3.1 %collective-permute-start.6 = (bf16[4,2,64,128]{3,2,1,0:T(8,128)(2,1)S(1)}, bf16[4,2,64,128]{3,2,1,0:T(8,128)(2,1)S(1)}, u32[]{:S(2)}, u32[]{:S(2)}) collective-permute-start(bf16[4,2,64,128]{3,2,1,0:T(8,128)(2,1)S(1)} %collective-permute-done.refs_1_), channel_id=1, source_target_pairs={{0,1},{1,0},{2,3},{3,2},{4,5},{5,4},{6,7},{7,6},{8,9},{9,8},{10,11... | collective-permute-start | bytes 393224 | tf_op jit(solution)/shard_map/ppermute | solution.py:179
  19.6 3.1 %collective-permute-start.7 = (bf16[4,2,64,128]{3,2,1,0:T(8,128)(2,1)S(1)}, bf16[4,2,64,128]{3,2,1,0:T(8,128)(2,1)S(1)}, u32[]{:S(2)}, u32[]{:S(2)}) collective-permute-start(bf16[4,2,64,128]{3,2,1,0:T(8,128)(2,1)S(1)} %collective-permute-done.1.refs_2_), channel_id=1, source_target_pairs={{0,1},{1,0},{2,3},{3,2},{4,5},{5,4},{6,7},{7,6},{8,9},{9,8},{10,11... | collective-permute-start | bytes 393224 | tf_op jit(solution)/shard_map/ppermute | solution.py:179
  20.1 4.3 %collective-permute-start.5 = (bf16[4,2,32,128]{3,2,1,0:T(8,128)(2,1)S(1)}, bf16[4,2,32,128]{3,2,1,0:T(8,128)(2,1)S(1)}, u32[]{:S(2)}, u32[]{:S(2)}) collective-permute-start(bf16[4,2,32,128]{3,2,1,0:T(8,128)(2,1)S(1)} %slice.15), channel_id=1, source_target_pairs={{0,4},{4,0},{8,12},{12,8},{16,20},{20,16},{24,28},{28,24},{1,5},{5... | collective-permute-start | bytes 196616 | tf_op jit(solution)/shard_map/ppermute | solution.py:179
  21.7 4.3 %collective-permute-start.4 = (bf16[4,2,32,128]{3,2,1,0:T(8,128)(2,1)S(1)}, bf16[4,2,32,128]{3,2,1,0:T(8,128)(2,1)S(1)}, u32[]{:S(2)}, u32[]{:S(2)}) collective-permute-start(bf16[4,2,32,128]{3,2,1,0:T(8,128)(2,1)S(1)} %slice.14), channel_id=1, source_target_pairs={{0,2},{1,3},{2,0},{3,1},{4,6},{5,7},{6,4},{7,5},{8,10},{9,11},{10,... | collective-permute-start | bytes 196616 | tf_op jit(solution)/shard_map/ppermute | solution.py:179
  25.9 1.3 %collective-permute-start.8 = (bf16[4,2,32,128]{3,2,1,0:T(8,128)(2,1)S(1)}, bf16[4,2,32,128]{3,2,1,0:T(8,128)(2,1)S(1)}, u32[]{:S(2)}, u32[]{:S(2)}) collective-permute-start(bf16[4,2,32,128]{3,2,1,0:T(8,128)(2,1)S(1)} %collective-permute-done.4.refs_1_), channel_id=1, source_target_pairs={{0,1},{1,0},{2,3},{3,2},{4,5},{5,4},{6,7},{7,6},{8,9},{9,8},{10,11... | collective-permute-start | bytes 196616 | tf_op jit(solution)/shard_map/ppermute | solution.py:179
  25.9 1.4 %collective-permute-start.9 = (bf16[4,2,32,128]{3,2,1,0:T(8,128)(2,1)S(1)}, bf16[4,2,32,128]{3,2,1,0:T(8,128)(2,1)S(1)}, u32[]{:S(2)}, u32[]{:S(2)}) collective-permute-start(bf16[4,2,32,128]{3,2,1,0:T(8,128)(2,1)S(1)} %collective-permute-done.5.refs_2_), channel_id=1, source_target_pairs={{0,1},{1,0},{2,3},{3,2},{4,5},{5,4},{6,7},{7,6},{8,9},{9,8},{10,11... | collective-permute-start | bytes 196616 | tf_op jit(solution)/shard_map/ppermute | solution.py:179

commit v10 on v8

--- a/solution.py
+++ b/solution.py
@@ -12,13 +12,13 @@
 STEP_BLOCKS = 8
 
 
-def attention_kernel(head_size, place, first, tail, last, pieces, *refs):
+def attention_kernel(head_size, place, first, tail, last, pieces, window, *refs):
     queries_ref, *refs = refs
     kv_refs, refs = refs[:pieces], refs[pieces:]
-    blocks, _, piece_rows, _ = kv_refs[0].shape
-    step_blocks = math.gcd(blocks, STEP_BLOCKS)
+    counts = [kv_ref.shape[0] for kv_ref in kv_refs]
+    piece_rows = kv_refs[0].shape[2]
     lengths_ref = None
-    if first or blocks > step_blocks:
+    if first or window > STEP_BLOCKS:
         lengths_ref, *refs = refs
     if first:
         stats_ref, sums_ref, starts_ref, turned_ref = refs
@@ -28,6 +28,7 @@
     else:
         old_stats_ref, old_sums_ref, starts_ref, stats_ref, sums_ref = refs
     own, piece = lax.axis_index("ctx"), lax.axis_index("head") ^ place
+    base = jnp.maximum(own - (window - 1), 0)
     heads, _, rows = old_sums_ref.shape
     slope = math.log2(math.e) / math.sqrt(head_size)
 
@@ -49,17 +50,25 @@
         queries_ref = turned_ref
     in_block = piece * piece_rows + lax.broadcasted_iota(jnp.int32, (piece_rows, rows), 0)
 
-    def step(index, count, old, emit):
-        start = index * step_blocks
+    def step(start, taken, old, emit):
         keys, values = (
             jnp.concatenate(
-                [kv_ref[pl.ds(start, count), i].reshape(count * piece_rows, head_size) for kv_ref in kv_refs], axis=0
+                [
+                    kv_ref[pl.ds(start, count), i].reshape(count * piece_rows, head_size)
+                    for kv_ref, count in zip(kv_refs, taken)
+                ],
+                axis=0,
             )
             for i in range(2)
         )
         values = values.T
         key_pos = jnp.concatenate(
-            [(i * blocks + start + j) * rows + in_block for i in range(pieces) for j in range(count)], axis=0
+            [
+                (base + sum(counts[:i]) + start + j) * rows + in_block
+                for i, count in enumerate(taken)
+                for j in range(count)
+            ],
+            axis=0,
         )
         valid = (key_pos >= starts) & (key_pos <= query_pos)
         scores = [
@@ -97,14 +106,15 @@
         result_ref[:, head * head_size : (head + 1) * head_size] = (sums * (1.0 / total)).astype(result_ref.dtype).T
         send(head).start()
 
-    if blocks == step_blocks:
+    if window <= STEP_BLOCKS:
         if first or not tail:
-            step(0, blocks, None if first else old_state, keep)
+            step(0, counts, None if first else old_state, keep)
         else:
             emit = finish if last else keep
             reach = 0
-            for count in sorted({max(blocks // 4, 1), max(blocks // 2, 1), blocks}):
-                pl.when((own >= reach) & (own < count))(functools.partial(step, 0, count, old_state, emit))
+            for count in sorted({min(max(STEP_BLOCKS // 4, 1), window), min(max(STEP_BLOCKS // 2, 1), window), window}):
+                here = (own >= reach) & (own < count) if count < window else own >= reach
+                pl.when(here)(functools.partial(step, 0, [count], old_state, emit))
                 reach = count
     else:
         if last:
@@ -119,12 +129,13 @@
         def new_state(head):
             return stats_ref[head : head + 1], stats_ref[heads + head : heads + head + 1], sums_ref[head]
 
-        low = first_key // rows // step_blocks if pieces == 1 else 0
-        high = jnp.minimum(own // step_blocks + 1, blocks // step_blocks)
+        step_blocks = math.gcd(counts[0], STEP_BLOCKS)
+        low = jnp.maximum(first_key // rows - base, 0) // step_blocks if pieces == 1 else 0
+        high = jnp.minimum((own - base) // step_blocks + 1, counts[0] // step_blocks)
 
         @pl.loop(low, high)
         def _(index):
-            step(index, step_blocks, new_state, keep)
+            step(index * step_blocks, [step_blocks] * pieces, new_state, keep)
 
         if last:
             for head in range(heads):
@@ -135,7 +146,7 @@
 
 
 def attend(place, first, tail, last, lengths, queries, kvs, state, heads):
-    blocks, _, piece_rows, head_size = kvs[0].shape
+    window, head_size = sum(kv.shape[0] for kv in kvs), kvs[0].shape[3]
     rows = queries.shape[0] if first else queries.shape[2]
     stats = jax.ShapeDtypeStruct((2 * heads, rows), jnp.float32)
     sums = jax.ShapeDtypeStruct((heads, head_size, rows), jnp.float32)
@@ -143,7 +154,7 @@
     turned = jax.ShapeDtypeStruct((heads, head_size, rows), queries.dtype)
     whole = pl.BlockSpec(memory_space=pltpu.VMEM)
     operands, in_specs = [queries, *kvs], [whole] * (1 + len(kvs))
-    if first or blocks > math.gcd(blocks, STEP_BLOCKS):
+    if first or window > STEP_BLOCKS:
         operands.append(lengths)
         in_specs.append(pl.BlockSpec(memory_space=pltpu.SMEM))
     scratch = []
@@ -151,13 +162,13 @@
         out_shape = jax.ShapeDtypeStruct((rows, heads * head_size), queries.dtype)
         out_specs = pl.BlockSpec(memory_space=pl.ANY)
         scratch = [pltpu.VMEM(out_shape.shape, out_shape.dtype), pltpu.SemaphoreType.DMA((heads,))]
-        if blocks > math.gcd(blocks, STEP_BLOCKS):
+        if window > STEP_BLOCKS:
             scratch += [pltpu.VMEM(stats.shape, stats.dtype), pltpu.VMEM(sums.shape, sums.dtype)]
     else:
         out_shape = (stats, sums, starts, turned) if first else (stats, sums)
         out_specs = (whole,) * len(out_shape)
     return pl.pallas_call(
-        functools.partial(attention_kernel, head_size, place, first, tail, last, len(kvs)),
+        functools.partial(attention_kernel, head_size, place, first, tail, last, len(kvs), window),
         out_shape=out_shape,
         in_specs=in_specs + [whole] * len(state),
         out_specs=out_specs,
@@ -170,6 +181,14 @@
 def all_blocks(block, axis):
     size = lax.axis_size(axis)
     return lax.all_to_all(jnp.broadcast_to(block, (size,) + block.shape), axis, 0, 0)
+
+
+def window_blocks(rows, blocks):
+    longest = 3 * rows * blocks // 4
+    window = -(-(longest - 1) // rows) + 1
+    if window > STEP_BLOCKS:
+        window = -(-window // STEP_BLOCKS) * STEP_BLOCKS
+    return min(window, blocks)
 
 
 def exchange(piece, axis, bits):
@@ -184,7 +203,10 @@
     for seq in range(seqs):
         lengths = document_lengths[seq : seq + 1]
         piece_0 = all_blocks(jnp.stack([key_rows[seq], value_rows[seq]]), "ctx")
-        half = piece_0.shape[0] // 2
+        window = window_blocks(rows, piece_0.shape[0])
+        base = jnp.maximum(lax.axis_index("ctx") - (window - 1), 0)
+        piece_0 = lax.dynamic_slice_in_dim(piece_0, base, window, 0)
+        half = (window + 1) // 2
         piece_2 = exchange(piece_0, "head", 2)
         piece_1 = [exchange(piece_0[:half], "head", 1), exchange(piece_0[half:], "head", 1)]
         *state, starts, turned = attend(0, True, False, False, lengths, queries[seq], [piece_0], (), heads)

time: 26.2 us -> 26.8 us (1.023)
  blocking collectives: 16 us -> 0 us
  waiting for transfers between devices: 2.34 us -> 11 us
  starting transfers between devices: 2.08 us -> 9.45 us
  local copies, waits for them, and re-layouts: 0.23 us -> 0.91 us
    all_to_all x1 -> x0, blocking collectives: 16 us -> none  [all_blocks(): lax.all_to_all(jnp.broadcast_to(block, (size,) + block.shape), axis, 0, 0)]
    all_to_all x0 -> x1, waiting for transfers between devices: none -> 8.92 us  [all_blocks(): lax.all_to_all(jnp.broadcast_to(block, (size,) + block.shape), axis, 0, 0)]
    all_to_all x0 -> x1, starting transfers between devices: none -> 7.25 us  [all_blocks(): lax.all_to_all(jnp.broadcast_to(block, (size,) + block.shape), axis, 0, 0)]
    broadcast_in_dim x1, local copies, waits for them, and re-layouts: 0.04 us -> 0.75 us  [all_blocks(): jnp.broadcast_to(block, (size,) + block.shape)]
  transfers between devices with their start and end apart: 4 -> 5, of which waited for: 2 -> 3; matrix products, arithmetic and copies ran while one was open for 0% -> 0% of each run, Pallas kernels for 13% -> 11%
where the time goes in v10:
time: 26.8 us; the launch traced here: 26.5 us
  waiting for transfers between devices  11 us (41%)
  starting transfers between devices  9.45 us (35%)
  Pallas kernels  4.27 us (16%)
  local copies, waits for them, and re-layouts  0.91 us (3%)
  other arithmetic  0.74 us (3%)
    all_to_all x1, waiting for transfers between devices, all_blocks(): lax.all_to_all(jnp.broadcast_to(block, (size,) + block.shape), axis, 0, 0)  8.92 us
    all_to_all x1, starting transfers between devices, all_blocks(): lax.all_to_all(jnp.broadcast_to(block, (size,) + block.shape), axis, 0, 0)  7.25 us
    pallas_call x4, Pallas kernels, attend(): pl.pallas_call(functools.partial(attention_kernel, head_size, place, firs...  4.27 us
    ppermute x4, starting transfers between devices, exchange(): lax.ppermute(piece, axis, [(i, i ^ bits) for i in range(lax.axis_size(axi...  2.2 us
    ppermute x4, waiting for transfers between devices, exchange(): lax.ppermute(piece, axis, [(i, i ^ bits) for i in range(lax.axis_size(axi...  2.13 us
    broadcast_in_dim x1, local copies, waits for them, and re-layouts, all_blocks(): jnp.broadcast_to(block, (size,) + block.shape)  0.75 us
    another operation x1, other arithmetic, body(): piece_0 = all_blocks(jnp.stack([key_rows[seq], value_rows[seq]]), 'ctx')  0.74 us
  transfers between devices with their start and end apart: 5, of which 3 were waited for; matrix products, arithmetic and copies ran while one was open for 0% of the time, Pallas kernels for 11%

profile of v10, /device:TPU:0, one launch (start us, length us, event | category | flops | bytes accessed | tf_op | source)
XLA Modules:
  0.0 26.5 jit_solution(1521791071239543981)
XLA Ops:
  0.0 0.7 %pad_maximum_fusion = bf16[2,64,128]{2,1,0:T(8,128)(2,1)S(1)} fusion(bf16[1,64,128]{2,1,0:T(8,128)(2,1)} %param.6, bf16[1,64,128]{2,1,0:T(8,128)(2,1)} %param.5), kind=kLoop, calls=%fused_computation | loop fusion | flops 16384 | bytes 65536 | tf_op jit(solution)/shard_map/stack | solution.py:205
  0.7 0.8 %broadcast_in_dim.3 = bf16[8,2,64,128]{3,2,1,0:T(8,128)(2,1)} broadcast(bf16[2,64,128]{2,1,0:T(8,128)(2,1)S(1)} %pad_maximum_fusion), dimensions={1,2,3} | broadcast | bytes 294912 | tf_op jit(solution)/shard_map/broadcast_in_dim | solution.py:183
  1.5 7.3 %all-to-all-start = ((bf16[8,2,64,128]{3,2,1,0:T(8,128)(2,1)}), bf16[8,2,64,128]{3,2,1,0:T(8,128)(2,1)S(1)}, u32[]{:S(2)}, u32[]{:S(2)}) async-start(bf16[8,2,64,128]{3,2,1,0:T(8,128)(2,1)} %broadcast_in_dim.3), calls=%async_computation | async-start | bytes 524288 | tf_op jit(solution)/shard_map/all_to_all | solution.py:183
  8.7 8.9 %all-to-all-done = bf16[8,2,64,128]{3,2,1,0:T(8,128)(2,1)S(1)} async-done(((bf16[8,2,64,128]{3,2,1,0:T(8,128)(2,1)}), bf16[8,2,64,128]{3,2,1,0:T(8,128)(2,1)S(1)}, u32[]{:S(2)}, u32[]{:S(2)}) %all-to-all-start) | async-done | bytes 262176 | tf_op jit(solution)/shard_map/all_to_all | solution.py:183
  17.7 0.0 copy-start
  17.7 1.6 %collective-permute-start = (bf16[7,2,64,128]{3,2,1,0:T(8,128)(2,1)S(1)}, bf16[7,2,64,128]{3,2,1,0:T(8,128)(2,1)S(1)}, u32[]{:S(2)}, u32[]{:S(2)}) collective-permute-start(bf16[7,2,64,128]{3,2,1,0:T(8,128)(2,1)S(1)} %constant_dynamic-slice_fusion.2.refs_1_), channel_id=1, source_target_pairs={{0,2},{1,3},{2,0},{3,1},{4,6},{5,7},{6,4},{7,5},{8,10},{9,11},{10,... | collective-permute-start | bytes 688136 | tf_op jit(solution)/shard_map/ppermute | solution.py:195
  19.3 0.1 collective-permute-start.1
  19.4 0.0 copy-start.1
  19.4 0.5 %collective-permute-start.2 = (bf16[3,2,64,128]{3,2,1,0:T(8,128)(2,1)S(1)}, bf16[3,2,64,128]{3,2,1,0:T(8,128)(2,1)S(1)}, u32[]{:S(2)}, u32[]{:S(2)}) collective-permute-start(bf16[3,2,64,128]{3,2,1,0:T(8,128)(2,1)S(1)} %constant_dynamic-slice_fusion), channel_id=1, source_target_pairs={{0,1},{1,0},{2,3},{3,2},{4,5},{5,4},{6,7},{7,6},{8,9},{9,8},{10,11... | collective-permute-start | bytes 294920 | tf_op jit(solution)/shard_map/ppermute | solution.py:195
  20.0 0.0 copy-done
  20.0 0.1 copy-done.1
  20.1 1.5 %shard_map.46 = (f32[8,256]{1,0:T(8,128)S(1)}, f32[4,128,256]{2,1,0:T(8,128)S(1)}, s32[1,256]{1,0:T(1,128)S(1)}, bf16[4,128,256]{2,1,0:T(8,128)(2,1)S(1)}) custom-call(bf16[256,512]{1,0:T(8,128)(2,1)S(1)} %bitcast.2, bf16[7,2,64,128]{3,2,1,0:T(8,128)(2,1)S(1)} %constant_dynamic-slice_fusion.2.refs_1_, s32[1,4]{1,0:T(1,128)S(1)} %copy-done.1), custom_call_target="tpu_custom_call" | custom-call | flops 1 | bytes 1 | tf_op jit(solution)/shard_map/pallas_call | solution.py:170
  21.6 0.0 collective-permute-done.2.refs_2_
  21.6 0.0 collective-permute-done.1.refs_1_
  21.6 1.0 %shard_map.47 = (f32[8,256]{1,0:T(8,128)S(1)}, f32[4,128,256]{2,1,0:T(8,128)S(1)}) custom-call(bf16[4,128,256]{2,1,0:T(8,128)(2,1)S(1)} %get-tuple-element.16.refs_0_, bf16[4,2,64,128]{3,2,1,0:T(8,128)(2,1)S(1)} %collective-permute-done.1.refs_1_, bf16[3,2,64,128]{3,2,1,0:T(8,128)(2,1)S(1)} %collective-permute-done.2.refs_2_, ...), custom_call_target="tpu_custom_call" | custom-call | flops 1 | bytes 1 | tf_op jit(solution)/shard_map/pallas_call | solution.py:170
  22.6 1.1 %collective-permute-done.refs_1_ = bf16[7,2,64,128]{3,2,1,0:T(8,128)(2,1)S(1)} collective-permute-done((bf16[7,2,64,128]{3,2,1,0:T(8,128)(2,1)S(1)}, bf16[7,2,64,128]{3,2,1,0:T(8,128)(2,1)S(1)}, u32[]{:S(2)}, u32[]{:S(2)}) %collective-permute-start) | collective-permute-done | bytes 229408 | tf_op jit(solution)/shard_map/ppermute | solution.py:195
  23.8 0.0 collective-permute-start.3
  23.8 0.5 %shard_map.48 = (f32[8,256]{1,0:T(8,128)S(1)}, f32[4,128,256]{2,1,0:T(8,128)S(1)}) custom-call(bf16[4,128,256]{2,1,0:T(8,128)(2,1)S(1)} %get-tuple-element.16.refs_0_, bf16[7,2,64,128]{3,2,1,0:T(8,128)(2,1)S(1)} %collective-permute-done.refs_1_, f32[8,256]{1,0:T(8,128)S(1)} %get-tuple-element.23.refs_2_, f32[4,128,256]{2,1,0:T(8,128)S(1)} %get-tuple-element.24.refs_3_, ...), custom_call_target="tpu_custom_call" | custom-call | flops 1 | bytes 1 | tf_op jit(solution)/shard_map/pallas_call | solution.py:170
  24.3 1.0 %collective-permute-done.3.refs_1_ = bf16[7,2,64,128]{3,2,1,0:T(8,128)(2,1)S(1)} collective-permute-done((bf16[7,2,64,128]{3,2,1,0:T(8,128)(2,1)S(1)}, bf16[7,2,64,128]{3,2,1,0:T(8,128)(2,1)S(1)}, u32[]{:S(2)}, u32[]{:S(2)}) %collective-permute-start.3) | collective-permute-done | bytes 229408 | tf_op jit(solution)/shard_map/ppermute | solution.py:195
  25.3 1.2 %shard_map.49 = bf16[256,512]{1,0:T(8,128)(2,1)} custom-call(bf16[4,128,256]{2,1,0:T(8,128)(2,1)S(1)} %get-tuple-element.16.refs_0_, bf16[7,2,64,128]{3,2,1,0:T(8,128)(2,1)S(1)} %collective-permute-done.3.refs_1_, f32[8,256]{1,0:T(8,128)S(1)} %get-tuple-element.25.refs_2_, f32[4,128,256]{2,1,0:T(8,128)S(1)} %get-tuple-element.26.refs_3_, ...), custom_call_target="tpu_custom_call" | custom-call | flops 1 | bytes 1 | tf_op jit(solution)/shard_map/pallas_call | solution.py:170
  (3 shorter events, 0.0 us)
Async XLA Ops:
  1.5 16.2 %all-to-all-start = ((bf16[8,2,64,128]{3,2,1,0:T(8,128)(2,1)}), bf16[8,2,64,128]{3,2,1,0:T(8,128)(2,1)S(1)}, u32[]{:S(2)}, u32[]{:S(2)}) async-start(bf16[8,2,64,128]{3,2,1,0:T(8,128)(2,1)} %broadcast_in_dim.3), calls=%async_computation | async-start | bytes 524288 | tf_op jit(solution)/shard_map/all_to_all | solution.py:183
  17.7 2.3 %copy-start = (bf16[1,256,512]{2,1,0:T(8,128)(2,1)S(1)}, bf16[1,256,512]{2,1,0:T(8,128)(2,1)}, u32[]{:S(2)}) copy-start(bf16[1,256,512]{2,1,0:T(8,128)(2,1)} %param.4) | copy-start | bytes 786436
  17.7 6.1 %collective-permute-start = (bf16[7,2,64,128]{3,2,1,0:T(8,128)(2,1)S(1)}, bf16[7,2,64,128]{3,2,1,0:T(8,128)(2,1)S(1)}, u32[]{:S(2)}, u32[]{:S(2)}) collective-permute-start(bf16[7,2,64,128]{3,2,1,0:T(8,128)(2,1)S(1)} %constant_dynamic-slice_fusion.2.refs_1_), channel_id=1, source_target_pairs={{0,2},{1,3},{2,0},{3,1},{4,6},{5,7},{6,4},{7,5},{8,10},{9,11},{10,... | collective-permute-start | bytes 688136 | tf_op jit(solution)/shard_map/ppermute | solution.py:195
  19.3 2.3 %collective-permute-start.1 = (bf16[4,2,64,128]{3,2,1,0:T(8,128)(2,1)S(1)}, bf16[4,2,64,128]{3,2,1,0:T(8,128)(2,1)S(1)}, u32[]{:S(2)}, u32[]{:S(2)}) collective-permute-start(bf16[4,2,64,128]{3,2,1,0:T(8,128)(2,1)S(1)} %constant_dynamic-slice_fusion.1), channel_id=1, source_target_pairs={{0,1},{1,0},{2,3},{3,2},{4,5},{5,4},{6,7},{7,6},{8,9},{9,8},{10,11... | collective-permute-start | bytes 393224 | tf_op jit(solution)/shard_map/ppermute | solution.py:195
  19.4 0.7 %copy-start.1 = (s32[1,4]{1,0:T(1,128)S(1)}, s32[1,4]{1,0:T(1,128)}, u32[]{:S(2)}) copy-start(s32[1,4]{1,0:T(1,128)} %refs_2_.1) | copy-start | bytes 52
  19.4 2.2 %collective-permute-start.2 = (bf16[3,2,64,128]{3,2,1,0:T(8,128)(2,1)S(1)}, bf16[3,2,64,128]{3,2,1,0:T(8,128)(2,1)S(1)}, u32[]{:S(2)}, u32[]{:S(2)}) collective-permute-start(bf16[3,2,64,128]{3,2,1,0:T(8,128)(2,1)S(1)} %constant_dynamic-slice_fusion), channel_id=1, source_target_pairs={{0,1},{1,0},{2,3},{3,2},{4,5},{5,4},{6,7},{7,6},{8,9},{9,8},{10,11... | collective-permute-start | bytes 294920 | tf_op jit(solution)/shard_map/ppermute | solution.py:195
  23.8 1.5 %collective-permute-start.3 = (bf16[7,2,64,128]{3,2,1,0:T(8,128)(2,1)S(1)}, bf16[7,2,64,128]{3,2,1,0:T(8,128)(2,1)S(1)}, u32[]{:S(2)}, u32[]{:S(2)}) collective-permute-start(bf16[7,2,64,128]{3,2,1,0:T(8,128)(2,1)S(1)} %collective-permute-done.refs_1_), channel_id=1, source_target_pairs={{0,1},{1,0},{2,3},{3,2},{4,5},{5,4},{6,7},{7,6},{8,9},{9,8},{10,11... | collective-permute-start | bytes 688136 | tf_op jit(solution)/shard_map/ppermute | solution.py:195

commit v11 on v9

--- a/solution.py
+++ b/solution.py
@@ -179,6 +179,11 @@
     return lax.ppermute(piece, axis, [(i, i ^ bits) for i in range(lax.axis_size(axis))])
 
 
+def halves_exchanged(piece):
+    half = piece.shape[2] // 2
+    return [exchange(piece[:, :, :half], "head", 1), exchange(piece[:, :, half:], "head", 1)]
+
+
 def body(queries, key_rows, value_rows, document_lengths):
     seqs, rows, width = queries.shape
     heads = width // key_rows.shape[2]
@@ -191,21 +196,21 @@
 
         across = exchange(own, "ctx", 1)
         far = exchange(own, "head", 2)
-        near = [exchange(own[:, :, :half], "head", 1), exchange(own[:, :, half:], "head", 1)]
+        corner = exchange(own, ("ctx", "head"), lax.axis_size("head") + 2)
+        near = halves_exchanged(own)
         stats, sums, starts, turned = run([(0, 0, 0)], "first", queries=queries[seq], kvs=[own], state=())
         run = functools.partial(run, queries=turned)
         stats, sums = run([(0, 1, 0), (0, 1, half)], "middle", kvs=near, state=(stats, sums, starts))
+
         across, far, stats, sums = lax.optimization_barrier((across, far, stats, sums))
-
-        corner = [exchange(across[:, :, :half], "head", 2), exchange(far[:, :, half:], "ctx", 1)]
-        near = [exchange(across, "head", 1), exchange(far, "head", 1)]
+        near = halves_exchanged(across) + halves_exchanged(far)
         stats, sums = run([(1, 0, 0), (0, 2, 0)], "middle", kvs=[across, far], state=(stats, sums, starts))
-        stats, sums = run([(1, 1, 0), (0, 3, 0)], "middle", kvs=near, state=(stats, sums, starts))
-        *corner, stats, sums = lax.optimization_barrier((*corner, stats, sums))
-
-        near = [exchange(part, "head", 1) for part in corner]
-        stats, sums = run([(1, 2, 0), (1, 2, half)], "middle", kvs=corner, state=(stats, sums, starts))
-        results.append(run([(1, 3, 0), (1, 3, half)], "last", kvs=near, state=(stats, sums, starts)))
+        parts = [(1, 1, 0), (1, 1, half), (0, 3, 0), (0, 3, half)]
+        stats, sums = run(parts, "middle", kvs=near, state=(stats, sums, starts))
+        corner, stats, sums = lax.optimization_barrier((corner, stats, sums))
+        near = exchange(corner, "head", 1)
+        stats, sums = run([(1, 2, 0)], "middle", kvs=[corner], state=(stats, sums, starts))
+        results.append(run([(1, 3, 0)], "last", kvs=[near], state=(stats, sums, starts)))
     return jnp.stack(results)
 
 

time: 28.9 us -> 27 us (0.934)
  starting transfers between devices: 6.65 us -> 5.6 us
  waiting for transfers between devices: 4.2 us -> 3.49 us
    ppermute x10, starting transfers between devices: 6.65 us -> 5.6 us  [exchange(): lax.ppermute(piece, axis, [(i, i ^ bits) for i in range(lax.axis_size(axi...]
    ppermute x10, waiting for transfers between devices: 4.2 us -> 3.49 us  [exchange(): lax.ppermute(piece, axis, [(i, i ^ bits) for i in range(lax.axis_size(axi...]
  transfers between devices with their start and end apart: 10 -> 10, of which waited for: 5 -> 4; matrix products, arithmetic and copies ran while one was open for 0% -> 0% of each run, Pallas kernels for 11% -> 12%
where the time goes in v11:
time: 27 us; the launch traced here: 26.6 us
  blocking collectives  12.3 us (46%)
  starting transfers between devices  5.6 us (21%)
  Pallas kernels  4.28 us (16%)
  waiting for transfers between devices  3.49 us (13%)
  other arithmetic  0.74 us (3%)
    all_to_all x1, blocking collectives, same_parity_blocks(): return lax.all_to_all(spread, axis, 0, 0, axis_index_groups=groups)  12.3 us
    ppermute x10, starting transfers between devices, exchange(): lax.ppermute(piece, axis, [(i, i ^ bits) for i in range(lax.axis_size(axi...  5.6 us
    pallas_call x6, Pallas kernels, attend(): pl.pallas_call(functools.partial(attention_kernel, head_size, parts, kind...  4.28 us
    ppermute x10, waiting for transfers between devices, exchange(): lax.ppermute(piece, axis, [(i, i ^ bits) for i in range(lax.axis_size(axi...  3.49 us
    another operation x1, other arithmetic, body(): own = same_parity_blocks(jnp.stack([key_rows[seq], value_rows[seq]]), 'ctx')  0.74 us
  transfers between devices with their start and end apart: 10, of which 4 were waited for; matrix products, arithmetic and copies ran while one was open for 0% of the time, Pallas kernels for 12%

profile of v11, /device:TPU:0, one launch (start us, length us, event | category | flops | bytes accessed | tf_op | source)
XLA Modules:
  0.0 26.6 jit_solution(9815239620908367942)
XLA Ops:
  0.0 0.7 %pad_maximum_fusion = bf16[2,64,128]{2,1,0:T(8,128)(2,1)S(1)} fusion(bf16[1,64,128]{2,1,0:T(8,128)(2,1)} %param.6, bf16[1,64,128]{2,1,0:T(8,128)(2,1)} %param.5), kind=kLoop, calls=%fused_computation | loop fusion | flops 16384 | bytes 65536 | tf_op jit(solution)/shard_map/stack | solution.py:194
  0.8 0.0 copy-start
  0.8 12.3 %all_to_all.5.refs_1_ = bf16[4,2,64,128]{3,2,1,0:T(8,128)(2,1)S(1)} all-to-all(bf16[4,2,64,128]{3,2,1,0:T(8,128)(2,1)S(1)} %broadcast_in_dim.3), channel_id=1, replica_groups={{0,8,16,24},{4,12,20,28},{1,9,17,25},{5,13,21,29},{2,10,18,26},{6,14,22..., dimensions={0} | all-to-all | bytes 262144 | tf_op jit(solution)/shard_map/all_to_all | solution.py:175
  13.1 1.5 %collective-permute-start.1 = (bf16[4,2,64,128]{3,2,1,0:T(8,128)(2,1)S(1)}, bf16[4,2,64,128]{3,2,1,0:T(8,128)(2,1)S(1)}, u32[]{:S(2)}, u32[]{:S(2)}) collective-permute-start(bf16[4,2,64,128]{3,2,1,0:T(8,128)(2,1)S(1)} %all_to_all.5.refs_1_), channel_id=1, source_target_pairs={{0,4},{4,0},{8,12},{12,8},{16,20},{20,16},{24,28},{28,24},{1,5},{5... | collective-permute-start | bytes 393224 | tf_op jit(solution)/shard_map/ppermute | solution.py:179
  14.6 1.5 %collective-permute-start.2 = (bf16[4,2,64,128]{3,2,1,0:T(8,128)(2,1)S(1)}, bf16[4,2,64,128]{3,2,1,0:T(8,128)(2,1)S(1)}, u32[]{:S(2)}, u32[]{:S(2)}) collective-permute-start(bf16[4,2,64,128]{3,2,1,0:T(8,128)(2,1)S(1)} %all_to_all.5.refs_1_), channel_id=1, source_target_pairs={{0,2},{1,3},{2,0},{3,1},{4,6},{5,7},{6,4},{7,5},{8,10},{9,11},{10,... | collective-permute-start | bytes 393224 | tf_op jit(solution)/shard_map/ppermute | solution.py:179
  16.1 0.1 collective-permute-start.3
  16.2 0.0 copy-start.1
  16.2 0.5 %collective-permute-start.4 = (bf16[4,2,32,128]{3,2,1,0:T(8,128)(2,1)S(1)}, bf16[4,2,32,128]{3,2,1,0:T(8,128)(2,1)S(1)}, u32[]{:S(2)}, u32[]{:S(2)}) collective-permute-start(bf16[4,2,32,128]{3,2,1,0:T(8,128)(2,1)S(1)} %get-tuple-element.47), channel_id=1, source_target_pairs={{0,1},{1,0},{2,3},{3,2},{4,5},{5,4},{6,7},{7,6},{8,9},{9,8},{10,11... | collective-permute-start | bytes 196616 | tf_op jit(solution)/shard_map/ppermute | solution.py:179
  16.7 0.5 %collective-permute-start = (bf16[4,2,64,128]{3,2,1,0:T(8,128)(2,1)S(1)}, bf16[4,2,64,128]{3,2,1,0:T(8,128)(2,1)S(1)}, u32[]{:S(2)}, u32[]{:S(2)}) collective-permute-start(bf16[4,2,64,128]{3,2,1,0:T(8,128)(2,1)S(1)} %all_to_all.5.refs_1_), channel_id=1, source_target_pairs={{0,6},{1,7},{2,4},{3,5},{4,2},{5,3},{6,0},{7,1},{8,14},{9,15},{10,... | collective-permute-start | bytes 393224 | tf_op jit(solution)/shard_map/ppermute | solution.py:179
  17.2 0.0 copy-done
  17.2 0.0 copy-done.1
  17.2 1.2 %shard_map.46 = (f32[8,256]{1,0:T(8,128)S(1)}, f32[4,128,256]{2,1,0:T(8,128)S(1)}, s32[1,256]{1,0:T(1,128)S(1)}, bf16[4,128,256]{2,1,0:T(8,128)(2,1)S(1)}) custom-call(bf16[256,512]{1,0:T(8,128)(2,1)S(1)} %bitcast.2, bf16[4,2,64,128]{3,2,1,0:T(8,128)(2,1)S(1)} %all_to_all.5.refs_1_, s32[1,4]{1,0:T(1,128)S(1)} %copy-done.1), custom_call_target="tpu_custom_call" | custom-call | flops 1 | bytes 1 | tf_op jit(solution)/shard_map/pallas_call | solution.py:160
  18.4 0.0 collective-permute-done.3.refs_1_
  18.4 0.0 collective-permute-done.4.refs_2_
  18.4 0.4 %shard_map.47 = (f32[8,256]{1,0:T(8,128)S(1)}, f32[4,128,256]{2,1,0:T(8,128)S(1)}) custom-call(bf16[4,128,256]{2,1,0:T(8,128)(2,1)S(1)} %get-tuple-element.24.refs_0_, bf16[4,2,32,128]{3,2,1,0:T(8,128)(2,1)S(1)} %collective-permute-done.3.refs_1_, bf16[4,2,32,128]{3,2,1,0:T(8,128)(2,1)S(1)} %collective-permute-done.4.refs_2_, ...), custom_call_target="tpu_custom_call" | custom-call | flops 1 | bytes 1 | tf_op jit(solution)/shard_map/pallas_call | solution.py:160
  18.9 0.0 collective-permute-done.1.refs_1_
  18.9 2.5 %collective-permute-done.2.refs_2_ = bf16[4,2,64,128]{3,2,1,0:T(8,128)(2,1)S(1)} collective-permute-done((bf16[4,2,64,128]{3,2,1,0:T(8,128)(2,1)S(1)}, bf16[4,2,64,128]{3,2,1,0:T(8,128)(2,1)S(1)}, u32[]{:S(2)}, u32[]{:S(2)}) %collective-permute-start.2) | collective-permute-done | bytes 131104 | tf_op jit(solution)/shard_map/ppermute | solution.py:179
  21.5 0.1 collective-permute-start.5
  21.5 0.5 %collective-permute-start.6 = (bf16[4,2,32,128]{3,2,1,0:T(8,128)(2,1)S(1)}, bf16[4,2,32,128]{3,2,1,0:T(8,128)(2,1)S(1)}, u32[]{:S(2)}, u32[]{:S(2)}) collective-permute-start(bf16[4,2,32,128]{3,2,1,0:T(8,128)(2,1)S(1)} %get-tuple-element.45), channel_id=1, source_target_pairs={{0,1},{1,0},{2,3},{3,2},{4,5},{5,4},{6,7},{7,6},{8,9},{9,8},{10,11... | collective-permute-start | bytes 196616 | tf_op jit(solution)/shard_map/ppermute | solution.py:179
  22.0 0.1 collective-permute-start.7
  22.2 0.4 %collective-permute-start.8 = (bf16[4,2,32,128]{3,2,1,0:T(8,128)(2,1)S(1)}, bf16[4,2,32,128]{3,2,1,0:T(8,128)(2,1)S(1)}, u32[]{:S(2)}, u32[]{:S(2)}) collective-permute-start(bf16[4,2,32,128]{3,2,1,0:T(8,128)(2,1)S(1)} %get-tuple-element.43), channel_id=1, source_target_pairs={{0,1},{1,0},{2,3},{3,2},{4,5},{5,4},{6,7},{7,6},{8,9},{9,8},{10,11... | collective-permute-start | bytes 196616 | tf_op jit(solution)/shard_map/ppermute | solution.py:179
  22.6 0.5 %shard_map.48 = (f32[8,256]{1,0:T(8,128)S(1)}, f32[4,128,256]{2,1,0:T(8,128)S(1)}) custom-call(bf16[4,128,256]{2,1,0:T(8,128)(2,1)S(1)} %get-tuple-element.24.refs_0_, bf16[4,2,64,128]{3,2,1,0:T(8,128)(2,1)S(1)} %collective-permute-done.1.refs_1_, bf16[4,2,64,128]{3,2,1,0:T(8,128)(2,1)S(1)} %collective-permute-done.2.refs_2_, ...), custom_call_target="tpu_custom_call" | custom-call | flops 1 | bytes 1 | tf_op jit(solution)/shard_map/pallas_call | solution.py:160
  23.1 0.0 collective-permute-done.5.refs_1_
  23.1 0.0 collective-permute-done.6.refs_2_
  23.1 0.2 collective-permute-done.7.refs_3_
  23.4 0.2 collective-permute-done.8.refs_4_
  23.5 0.5 %shard_map.49 = (f32[8,256]{1,0:T(8,128)S(1)}, f32[4,128,256]{2,1,0:T(8,128)S(1)}) custom-call(bf16[4,128,256]{2,1,0:T(8,128)(2,1)S(1)} %get-tuple-element.24.refs_0_, bf16[4,2,32,128]{3,2,1,0:T(8,128)(2,1)S(1)} %collective-permute-done.5.refs_1_, bf16[4,2,32,128]{3,2,1,0:T(8,128)(2,1)S(1)} %collective-permute-done.6.refs_2_, ...), custom_call_target="tpu_custom_call" | custom-call | flops 1 | bytes 1 | tf_op jit(solution)/shard_map/pallas_call | solution.py:160
  24.0 0.0 collective-permute-done.refs_1_
  24.0 0.4 %collective-permute-start.9 = (bf16[4,2,64,128]{3,2,1,0:T(8,128)(2,1)S(1)}, bf16[4,2,64,128]{3,2,1,0:T(8,128)(2,1)S(1)}, u32[]{:S(2)}, u32[]{:S(2)}) collective-permute-start(bf16[4,2,64,128]{3,2,1,0:T(8,128)(2,1)S(1)} %collective-permute-done.refs_1_), channel_id=1, source_target_pairs={{0,1},{1,0},{2,3},{3,2},{4,5},{5,4},{6,7},{7,6},{8,9},{9,8},{10,11... | collective-permute-start | bytes 393224 | tf_op jit(solution)/shard_map/ppermute | solution.py:179
  24.4 0.4 %shard_map.50 = (f32[8,256]{1,0:T(8,128)S(1)}, f32[4,128,256]{2,1,0:T(8,128)S(1)}) custom-call(bf16[4,128,256]{2,1,0:T(8,128)(2,1)S(1)} %get-tuple-element.24.refs_0_, bf16[4,2,64,128]{3,2,1,0:T(8,128)(2,1)S(1)} %collective-permute-done.refs_1_, f32[8,256]{1,0:T(8,128)S(1)} %get-tuple-element.39.refs_2_, f32[4,128,256]{2,1,0:T(8,128)S(1)} %get-tuple-element.40.refs_3_, ...), custom_call_target="tpu_custom_call" | custom-call | flops 1 | bytes 1 | tf_op jit(solution)/shard_map/pallas_call | solution.py:160
  24.9 0.6 %collective-permute-done.9.refs_1_ = bf16[4,2,64,128]{3,2,1,0:T(8,128)(2,1)S(1)} collective-permute-done((bf16[4,2,64,128]{3,2,1,0:T(8,128)(2,1)S(1)}, bf16[4,2,64,128]{3,2,1,0:T(8,128)(2,1)S(1)}, u32[]{:S(2)}, u32[]{:S(2)}) %collective-permute-start.9) | collective-permute-done | bytes 131104 | tf_op jit(solution)/shard_map/ppermute | solution.py:179
  25.4 1.2 %shard_map.51 = bf16[256,512]{1,0:T(8,128)(2,1)} custom-call(bf16[4,128,256]{2,1,0:T(8,128)(2,1)S(1)} %get-tuple-element.24.refs_0_, bf16[4,2,64,128]{3,2,1,0:T(8,128)(2,1)S(1)} %collective-permute-done.9.refs_1_, f32[8,256]{1,0:T(8,128)S(1)} %get-tuple-element.41.refs_2_, f32[4,128,256]{2,1,0:T(8,128)S(1)} %get-tuple-element.42.refs_3_, ...), custom_call_target="tpu_custom_call" | custom-call | flops 1 | bytes 1 | tf_op jit(solution)/shard_map/pallas_call | solution.py:160
  (4 shorter events, 0.0 us)
Async XLA Ops:
  0.8 16.4 %copy-start = (bf16[1,256,512]{2,1,0:T(8,128)(2,1)S(1)}, bf16[1,256,512]{2,1,0:T(8,128)(2,1)}, u32[]{:S(2)}) copy-start(bf16[1,256,512]{2,1,0:T(8,128)(2,1)} %param.4) | copy-start | bytes 786436
  13.1 5.8 %collective-permute-start.1 = (bf16[4,2,64,128]{3,2,1,0:T(8,128)(2,1)S(1)}, bf16[4,2,64,128]{3,2,1,0:T(8,128)(2,1)S(1)}, u32[]{:S(2)}, u32[]{:S(2)}) collective-permute-start(bf16[4,2,64,128]{3,2,1,0:T(8,128)(2,1)S(1)} %all_to_all.5.refs_1_), channel_id=1, source_target_pairs={{0,4},{4,0},{8,12},{12,8},{16,20},{20,16},{24,28},{28,24},{1,5},{5... | collective-permute-start | bytes 393224 | tf_op jit(solution)/shard_map/ppermute | solution.py:179
  14.6 6.8 %collective-permute-start.2 = (bf16[4,2,64,128]{3,2,1,0:T(8,128)(2,1)S(1)}, bf16[4,2,64,128]{3,2,1,0:T(8,128)(2,1)S(1)}, u32[]{:S(2)}, u32[]{:S(2)}) collective-permute-start(bf16[4,2,64,128]{3,2,1,0:T(8,128)(2,1)S(1)} %all_to_all.5.refs_1_), channel_id=1, source_target_pairs={{0,2},{1,3},{2,0},{3,1},{4,6},{5,7},{6,4},{7,5},{8,10},{9,11},{10,... | collective-permute-start | bytes 393224 | tf_op jit(solution)/shard_map/ppermute | solution.py:179
  16.1 2.3 %collective-permute-start.3 = (bf16[4,2,32,128]{3,2,1,0:T(8,128)(2,1)S(1)}, bf16[4,2,32,128]{3,2,1,0:T(8,128)(2,1)S(1)}, u32[]{:S(2)}, u32[]{:S(2)}) collective-permute-start(bf16[4,2,32,128]{3,2,1,0:T(8,128)(2,1)S(1)} %get-tuple-element.48), channel_id=1, source_target_pairs={{0,1},{1,0},{2,3},{3,2},{4,5},{5,4},{6,7},{7,6},{8,9},{9,8},{10,11... | collective-permute-start | bytes 196616 | tf_op jit(solution)/shard_map/ppermute | solution.py:179
  16.2 1.0 %copy-start.1 = (s32[1,4]{1,0:T(1,128)S(1)}, s32[1,4]{1,0:T(1,128)}, u32[]{:S(2)}) copy-start(s32[1,4]{1,0:T(1,128)} %refs_2_.1) | copy-start | bytes 52
  16.2 2.2 %collective-permute-start.4 = (bf16[4,2,32,128]{3,2,1,0:T(8,128)(2,1)S(1)}, bf16[4,2,32,128]{3,2,1,0:T(8,128)(2,1)S(1)}, u32[]{:S(2)}, u32[]{:S(2)}) collective-permute-start(bf16[4,2,32,128]{3,2,1,0:T(8,128)(2,1)S(1)} %get-tuple-element.47), channel_id=1, source_target_pairs={{0,1},{1,0},{2,3},{3,2},{4,5},{5,4},{6,7},{7,6},{8,9},{9,8},{10,11... | collective-permute-start | bytes 196616 | tf_op jit(solution)/shard_map/ppermute | solution.py:179
  16.7 7.3 %collective-permute-start = (bf16[4,2,64,128]{3,2,1,0:T(8,128)(2,1)S(1)}, bf16[4,2,64,128]{3,2,1,0:T(8,128)(2,1)S(1)}, u32[]{:S(2)}, u32[]{:S(2)}) collective-permute-start(bf16[4,2,64,128]{3,2,1,0:T(8,128)(2,1)S(1)} %all_to_all.5.refs_1_), channel_id=1, source_target_pairs={{0,6},{1,7},{2,4},{3,5},{4,2},{5,3},{6,0},{7,1},{8,14},{9,15},{10,... | collective-permute-start | bytes 393224 | tf_op jit(solution)/shard_map/ppermute | solution.py:179
  21.5 1.7 %collective-permute-start.5 = (bf16[4,2,32,128]{3,2,1,0:T(8,128)(2,1)S(1)}, bf16[4,2,32,128]{3,2,1,0:T(8,128)(2,1)S(1)}, u32[]{:S(2)}, u32[]{:S(2)}) collective-permute-start(bf16[4,2,32,128]{3,2,1,0:T(8,128)(2,1)S(1)} %get-tuple-element.46), channel_id=1, source_target_pairs={{0,1},{1,0},{2,3},{3,2},{4,5},{5,4},{6,7},{7,6},{8,9},{9,8},{10,11... | collective-permute-start | bytes 196616 | tf_op jit(solution)/shard_map/ppermute | solution.py:179
  21.5 1.6 %collective-permute-start.6 = (bf16[4,2,32,128]{3,2,1,0:T(8,128)(2,1)S(1)}, bf16[4,2,32,128]{3,2,1,0:T(8,128)(2,1)S(1)}, u32[]{:S(2)}, u32[]{:S(2)}) collective-permute-start(bf16[4,2,32,128]{3,2,1,0:T(8,128)(2,1)S(1)} %get-tuple-element.45), channel_id=1, source_target_pairs={{0,1},{1,0},{2,3},{3,2},{4,5},{5,4},{6,7},{7,6},{8,9},{9,8},{10,11... | collective-permute-start | bytes 196616 | tf_op jit(solution)/shard_map/ppermute | solution.py:179
  22.0 1.3 %collective-permute-start.7 = (bf16[4,2,32,128]{3,2,1,0:T(8,128)(2,1)S(1)}, bf16[4,2,32,128]{3,2,1,0:T(8,128)(2,1)S(1)}, u32[]{:S(2)}, u32[]{:S(2)}) collective-permute-start(bf16[4,2,32,128]{3,2,1,0:T(8,128)(2,1)S(1)} %get-tuple-element.44), channel_id=1, source_target_pairs={{0,1},{1,0},{2,3},{3,2},{4,5},{5,4},{6,7},{7,6},{8,9},{9,8},{10,11... | collective-permute-start | bytes 196616 | tf_op jit(solution)/shard_map/ppermute | solution.py:179
  22.2 1.3 %collective-permute-start.8 = (bf16[4,2,32,128]{3,2,1,0:T(8,128)(2,1)S(1)}, bf16[4,2,32,128]{3,2,1,0:T(8,128)(2,1)S(1)}, u32[]{:S(2)}, u32[]{:S(2)}) collective-permute-start(bf16[4,2,32,128]{3,2,1,0:T(8,128)(2,1)S(1)} %get-tuple-element.43), channel_id=1, source_target_pairs={{0,1},{1,0},{2,3},{3,2},{4,5},{5,4},{6,7},{7,6},{8,9},{9,8},{10,11... | collective-permute-start | bytes 196616 | tf_op jit(solution)/shard_map/ppermute | solution.py:179
  24.0 1.4 %collective-permute-start.9 = (bf16[4,2,64,128]{3,2,1,0:T(8,128)(2,1)S(1)}, bf16[4,2,64,128]{3,2,1,0:T(8,128)(2,1)S(1)}, u32[]{:S(2)}, u32[]{:S(2)}) collective-permute-start(bf16[4,2,64,128]{3,2,1,0:T(8,128)(2,1)S(1)} %collective-permute-done.refs_1_), channel_id=1, source_target_pairs={{0,1},{1,0},{2,3},{3,2},{4,5},{5,4},{6,7},{7,6},{8,9},{9,8},{10,11... | collective-permute-start | bytes 393224 | tf_op jit(solution)/shard_map/ppermute | solution.py:179

commit v12 on v9

--- a/solution.py
+++ b/solution.py
@@ -191,21 +191,20 @@
 
         across = exchange(own, "ctx", 1)
         far = exchange(own, "head", 2)
+        corner = exchange(own, ("ctx", "head"), lax.axis_size("head") + 2)
         near = [exchange(own[:, :, :half], "head", 1), exchange(own[:, :, half:], "head", 1)]
         stats, sums, starts, turned = run([(0, 0, 0)], "first", queries=queries[seq], kvs=[own], state=())
         run = functools.partial(run, queries=turned)
         stats, sums = run([(0, 1, 0), (0, 1, half)], "middle", kvs=near, state=(stats, sums, starts))
+
         across, far, stats, sums = lax.optimization_barrier((across, far, stats, sums))
-
-        corner = [exchange(across[:, :, :half], "head", 2), exchange(far[:, :, half:], "ctx", 1)]
         near = [exchange(across, "head", 1), exchange(far, "head", 1)]
         stats, sums = run([(1, 0, 0), (0, 2, 0)], "middle", kvs=[across, far], state=(stats, sums, starts))
-        stats, sums = run([(1, 1, 0), (0, 3, 0)], "middle", kvs=near, state=(stats, sums, starts))
-        *corner, stats, sums = lax.optimization_barrier((*corner, stats, sums))
-
-        near = [exchange(part, "head", 1) for part in corner]
-        stats, sums = run([(1, 2, 0), (1, 2, half)], "middle", kvs=corner, state=(stats, sums, starts))
-        results.append(run([(1, 3, 0), (1, 3, half)], "last", kvs=near, state=(stats, sums, starts)))
+        corner, stats, sums = lax.optimization_barrier((corner, stats, sums))
+        near_corner = exchange(corner, "head", 1)
+        parts = [(1, 1, 0), (0, 3, 0), (1, 2, 0)]
+        stats, sums = run(parts, "middle", kvs=[*near, corner], state=(stats, sums, starts))
+        results.append(run([(1, 3, 0)], "last", kvs=[near_corner], state=(stats, sums, starts)))
     return jnp.stack(results)
 
 

time: 28.9 us -> 24.8 us (0.86)
  starting transfers between devices: 6.65 us -> 4.56 us
  waiting for transfers between devices: 4.2 us -> 2.66 us
  Pallas kernels: 4.29 us -> 3.94 us
    ppermute x10 -> x8, starting transfers between devices: 6.65 us -> 4.56 us  [exchange(): lax.ppermute(piece, axis, [(i, i ^ bits) for i in range(lax.axis_size(axi...]
    ppermute x10 -> x8, waiting for transfers between devices: 4.2 us -> 2.66 us  [exchange(): lax.ppermute(piece, axis, [(i, i ^ bits) for i in range(lax.axis_size(axi...]
    pallas_call x6 -> x5, Pallas kernels: 4.29 us -> 3.94 us  [attend(): pl.pallas_call(functools.partial(attention_kernel, head_size, parts, kind...]
  transfers between devices with their start and end apart: 10 -> 8, of which waited for: 5 -> 4; matrix products, arithmetic and copies ran while one was open for 0% -> 0% of each run, Pallas kernels for 11% -> 11%
where the time goes in v12:
time: 24.8 us; the launch traced here: 24.5 us
  blocking collectives  12.3 us (50%)
  starting transfers between devices  4.56 us (18%)
  Pallas kernels  3.94 us (16%)
  waiting for transfers between devices  2.66 us (11%)
  other arithmetic  0.74 us (3%)
    all_to_all x1, blocking collectives, same_parity_blocks(): return lax.all_to_all(spread, axis, 0, 0, axis_index_groups=groups)  12.3 us
    ppermute x8, starting transfers between devices, exchange(): lax.ppermute(piece, axis, [(i, i ^ bits) for i in range(lax.axis_size(axi...  4.56 us
    pallas_call x5, Pallas kernels, attend(): pl.pallas_call(functools.partial(attention_kernel, head_size, parts, kind...  3.94 us
    ppermute x8, waiting for transfers between devices, exchange(): lax.ppermute(piece, axis, [(i, i ^ bits) for i in range(lax.axis_size(axi...  2.66 us
    another operation x1, other arithmetic, body(): own = same_parity_blocks(jnp.stack([key_rows[seq], value_rows[seq]]), 'ctx')  0.74 us
  transfers between devices with their start and end apart: 8, of which 4 were waited for; matrix products, arithmetic and copies ran while one was open for 0% of the time, Pallas kernels for 11%

profile of v12, /device:TPU:0, one launch (start us, length us, event | category | flops | bytes accessed | tf_op | source)
XLA Modules:
  0.0 24.5 jit_solution(4958189404767625635)
XLA Ops:
  0.0 0.7 %pad_maximum_fusion = bf16[2,64,128]{2,1,0:T(8,128)(2,1)S(1)} fusion(bf16[1,64,128]{2,1,0:T(8,128)(2,1)} %param.6, bf16[1,64,128]{2,1,0:T(8,128)(2,1)} %param.5), kind=kLoop, calls=%fused_computation | loop fusion | flops 16384 | bytes 65536 | tf_op jit(solution)/shard_map/stack | solution.py:189
  0.8 0.0 copy-start
  0.8 12.3 %all_to_all.5.refs_1_ = bf16[4,2,64,128]{3,2,1,0:T(8,128)(2,1)S(1)} all-to-all(bf16[4,2,64,128]{3,2,1,0:T(8,128)(2,1)S(1)} %broadcast_in_dim.3), channel_id=1, replica_groups={{0,8,16,24},{4,12,20,28},{1,9,17,25},{5,13,21,29},{2,10,18,26},{6,14,22..., dimensions={0} | all-to-all | bytes 262144 | tf_op jit(solution)/shard_map/all_to_all | solution.py:175
  13.1 1.5 %collective-permute-start.1 = (bf16[4,2,64,128]{3,2,1,0:T(8,128)(2,1)S(1)}, bf16[4,2,64,128]{3,2,1,0:T(8,128)(2,1)S(1)}, u32[]{:S(2)}, u32[]{:S(2)}) collective-permute-start(bf16[4,2,64,128]{3,2,1,0:T(8,128)(2,1)S(1)} %all_to_all.5.refs_1_), channel_id=1, source_target_pairs={{0,4},{4,0},{8,12},{12,8},{16,20},{20,16},{24,28},{28,24},{1,5},{5... | collective-permute-start | bytes 393224 | tf_op jit(solution)/shard_map/ppermute | solution.py:179
  14.6 1.5 %collective-permute-start.2 = (bf16[4,2,64,128]{3,2,1,0:T(8,128)(2,1)S(1)}, bf16[4,2,64,128]{3,2,1,0:T(8,128)(2,1)S(1)}, u32[]{:S(2)}, u32[]{:S(2)}) collective-permute-start(bf16[4,2,64,128]{3,2,1,0:T(8,128)(2,1)S(1)} %all_to_all.5.refs_1_), channel_id=1, source_target_pairs={{0,2},{1,3},{2,0},{3,1},{4,6},{5,7},{6,4},{7,5},{8,10},{9,11},{10,... | collective-permute-start | bytes 393224 | tf_op jit(solution)/shard_map/ppermute | solution.py:179
  16.1 0.5 %collective-permute-start = (bf16[4,2,64,128]{3,2,1,0:T(8,128)(2,1)S(1)}, bf16[4,2,64,128]{3,2,1,0:T(8,128)(2,1)S(1)}, u32[]{:S(2)}, u32[]{:S(2)}) collective-permute-start(bf16[4,2,64,128]{3,2,1,0:T(8,128)(2,1)S(1)} %all_to_all.5.refs_1_), channel_id=1, source_target_pairs={{0,6},{1,7},{2,4},{3,5},{4,2},{5,3},{6,0},{7,1},{8,14},{9,15},{10,... | collective-permute-start | bytes 393224 | tf_op jit(solution)/shard_map/ppermute | solution.py:179
  16.6 0.1 collective-permute-start.3
  16.7 0.0 copy-start.1
  16.7 0.5 %collective-permute-start.4 = (bf16[4,2,32,128]{3,2,1,0:T(8,128)(2,1)S(1)}, bf16[4,2,32,128]{3,2,1,0:T(8,128)(2,1)S(1)}, u32[]{:S(2)}, u32[]{:S(2)}) collective-permute-start(bf16[4,2,32,128]{3,2,1,0:T(8,128)(2,1)S(1)} %get-tuple-element.39), channel_id=1, source_target_pairs={{0,1},{1,0},{2,3},{3,2},{4,5},{5,4},{6,7},{7,6},{8,9},{9,8},{10,11... | collective-permute-start | bytes 196616 | tf_op jit(solution)/shard_map/ppermute | solution.py:179
  17.2 0.0 copy-done
  17.2 0.2 copy-done.1
  17.3 1.2 %shard_map.46 = (f32[8,256]{1,0:T(8,128)S(1)}, f32[4,128,256]{2,1,0:T(8,128)S(1)}, s32[1,256]{1,0:T(1,128)S(1)}, bf16[4,128,256]{2,1,0:T(8,128)(2,1)S(1)}) custom-call(bf16[256,512]{1,0:T(8,128)(2,1)S(1)} %bitcast.2, bf16[4,2,64,128]{3,2,1,0:T(8,128)(2,1)S(1)} %all_to_all.5.refs_1_, s32[1,4]{1,0:T(1,128)S(1)} %copy-done.1), custom_call_target="tpu_custom_call" | custom-call | flops 1 | bytes 1 | tf_op jit(solution)/shard_map/pallas_call | solution.py:160
  18.6 0.0 collective-permute-done.3.refs_1_
  18.6 0.0 collective-permute-done.4.refs_2_
  18.6 0.4 %shard_map.47 = (f32[8,256]{1,0:T(8,128)S(1)}, f32[4,128,256]{2,1,0:T(8,128)S(1)}) custom-call(bf16[4,128,256]{2,1,0:T(8,128)(2,1)S(1)} %get-tuple-element.22.refs_0_, bf16[4,2,32,128]{3,2,1,0:T(8,128)(2,1)S(1)} %collective-permute-done.3.refs_1_, bf16[4,2,32,128]{3,2,1,0:T(8,128)(2,1)S(1)} %collective-permute-done.4.refs_2_, ...), custom_call_target="tpu_custom_call" | custom-call | flops 1 | bytes 1 | tf_op jit(solution)/shard_map/pallas_call | solution.py:160
  19.1 0.1 collective-permute-done.1.refs_1_
  19.2 1.2 %collective-permute-done.2.refs_2_ = bf16[4,2,64,128]{3,2,1,0:T(8,128)(2,1)S(1)} collective-permute-done((bf16[4,2,64,128]{3,2,1,0:T(8,128)(2,1)S(1)}, bf16[4,2,64,128]{3,2,1,0:T(8,128)(2,1)S(1)}, u32[]{:S(2)}, u32[]{:S(2)}) %collective-permute-start.2) | collective-permute-done | bytes 131104 | tf_op jit(solution)/shard_map/ppermute | solution.py:179
  20.4 0.0 collective-permute-start.6
  20.4 0.5 %collective-permute-start.7 = (bf16[4,2,64,128]{3,2,1,0:T(8,128)(2,1)S(1)}, bf16[4,2,64,128]{3,2,1,0:T(8,128)(2,1)S(1)}, u32[]{:S(2)}, u32[]{:S(2)}) collective-permute-start(bf16[4,2,64,128]{3,2,1,0:T(8,128)(2,1)S(1)} %collective-permute-done.2.refs_2_), channel_id=1, source_target_pairs={{0,1},{1,0},{2,3},{3,2},{4,5},{5,4},{6,7},{7,6},{8,9},{9,8},{10,11... | collective-permute-start | bytes 393224 | tf_op jit(solution)/shard_map/ppermute | solution.py:179
  20.9 0.5 %shard_map.48 = (f32[8,256]{1,0:T(8,128)S(1)}, f32[4,128,256]{2,1,0:T(8,128)S(1)}) custom-call(bf16[4,128,256]{2,1,0:T(8,128)(2,1)S(1)} %get-tuple-element.22.refs_0_, bf16[4,2,64,128]{3,2,1,0:T(8,128)(2,1)S(1)} %collective-permute-done.1.refs_1_, bf16[4,2,64,128]{3,2,1,0:T(8,128)(2,1)S(1)} %collective-permute-done.2.refs_2_, ...), custom_call_target="tpu_custom_call" | custom-call | flops 1 | bytes 1 | tf_op jit(solution)/shard_map/pallas_call | solution.py:160
  21.4 0.6 %collective-permute-done.refs_3_ = bf16[4,2,64,128]{3,2,1,0:T(8,128)(2,1)S(1)} collective-permute-done((bf16[4,2,64,128]{3,2,1,0:T(8,128)(2,1)S(1)}, bf16[4,2,64,128]{3,2,1,0:T(8,128)(2,1)S(1)}, u32[]{:S(2)}, u32[]{:S(2)}) %collective-permute-start) | collective-permute-done | bytes 131104 | tf_op jit(solution)/shard_map/ppermute | solution.py:179
  22.0 0.0 collective-permute-start.5
  22.0 0.0 collective-permute-done.6.refs_1_
  22.0 0.0 collective-permute-done.7.refs_2_
  22.0 0.6 %shard_map.49 = (f32[8,256]{1,0:T(8,128)S(1)}, f32[4,128,256]{2,1,0:T(8,128)S(1)}) custom-call(bf16[4,128,256]{2,1,0:T(8,128)(2,1)S(1)} %get-tuple-element.22.refs_0_, bf16[4,2,64,128]{3,2,1,0:T(8,128)(2,1)S(1)} %collective-permute-done.6.refs_1_, bf16[4,2,64,128]{3,2,1,0:T(8,128)(2,1)S(1)} %collective-permute-done.7.refs_2_, ...), custom_call_target="tpu_custom_call" | custom-call | flops 1 | bytes 1 | tf_op jit(solution)/shard_map/pallas_call | solution.py:160
  22.6 0.7 %collective-permute-done.5.refs_1_ = bf16[4,2,64,128]{3,2,1,0:T(8,128)(2,1)S(1)} collective-permute-done((bf16[4,2,64,128]{3,2,1,0:T(8,128)(2,1)S(1)}, bf16[4,2,64,128]{3,2,1,0:T(8,128)(2,1)S(1)}, u32[]{:S(2)}, u32[]{:S(2)}) %collective-permute-start.5) | collective-permute-done | bytes 131104 | tf_op jit(solution)/shard_map/ppermute | solution.py:179
  23.3 1.2 %shard_map.50 = bf16[256,512]{1,0:T(8,128)(2,1)} custom-call(bf16[4,128,256]{2,1,0:T(8,128)(2,1)S(1)} %get-tuple-element.22.refs_0_, bf16[4,2,64,128]{3,2,1,0:T(8,128)(2,1)S(1)} %collective-permute-done.5.refs_1_, f32[8,256]{1,0:T(8,128)S(1)} %get-tuple-element.37.refs_2_, f32[4,128,256]{2,1,0:T(8,128)S(1)} %get-tuple-element.38.refs_3_, ...), custom_call_target="tpu_custom_call" | custom-call | flops 1 | bytes 1 | tf_op jit(solution)/shard_map/pallas_call | solution.py:160
  (2 shorter events, 0.0 us)
Async XLA Ops:
  0.8 16.4 %copy-start = (bf16[1,256,512]{2,1,0:T(8,128)(2,1)S(1)}, bf16[1,256,512]{2,1,0:T(8,128)(2,1)}, u32[]{:S(2)}) copy-start(bf16[1,256,512]{2,1,0:T(8,128)(2,1)} %param.4) | copy-start | bytes 786436
  13.1 6.1 %collective-permute-start.1 = (bf16[4,2,64,128]{3,2,1,0:T(8,128)(2,1)S(1)}, bf16[4,2,64,128]{3,2,1,0:T(8,128)(2,1)S(1)}, u32[]{:S(2)}, u32[]{:S(2)}) collective-permute-start(bf16[4,2,64,128]{3,2,1,0:T(8,128)(2,1)S(1)} %all_to_all.5.refs_1_), channel_id=1, source_target_pairs={{0,4},{4,0},{8,12},{12,8},{16,20},{20,16},{24,28},{28,24},{1,5},{5... | collective-permute-start | bytes 393224 | tf_op jit(solution)/shard_map/ppermute | solution.py:179
  14.6 5.8 %collective-permute-start.2 = (bf16[4,2,64,128]{3,2,1,0:T(8,128)(2,1)S(1)}, bf16[4,2,64,128]{3,2,1,0:T(8,128)(2,1)S(1)}, u32[]{:S(2)}, u32[]{:S(2)}) collective-permute-start(bf16[4,2,64,128]{3,2,1,0:T(8,128)(2,1)S(1)} %all_to_all.5.refs_1_), channel_id=1, source_target_pairs={{0,2},{1,3},{2,0},{3,1},{4,6},{5,7},{6,4},{7,5},{8,10},{9,11},{10,... | collective-permute-start | bytes 393224 | tf_op jit(solution)/shard_map/ppermute | solution.py:179
  16.1 5.9 %collective-permute-start = (bf16[4,2,64,128]{3,2,1,0:T(8,128)(2,1)S(1)}, bf16[4,2,64,128]{3,2,1,0:T(8,128)(2,1)S(1)}, u32[]{:S(2)}, u32[]{:S(2)}) collective-permute-start(bf16[4,2,64,128]{3,2,1,0:T(8,128)(2,1)S(1)} %all_to_all.5.refs_1_), channel_id=1, source_target_pairs={{0,6},{1,7},{2,4},{3,5},{4,2},{5,3},{6,0},{7,1},{8,14},{9,15},{10,... | collective-permute-start | bytes 393224 | tf_op jit(solution)/shard_map/ppermute | solution.py:179
  16.6 2.0 %collective-permute-start.3 = (bf16[4,2,32,128]{3,2,1,0:T(8,128)(2,1)S(1)}, bf16[4,2,32,128]{3,2,1,0:T(8,128)(2,1)S(1)}, u32[]{:S(2)}, u32[]{:S(2)}) collective-permute-start(bf16[4,2,32,128]{3,2,1,0:T(8,128)(2,1)S(1)} %get-tuple-element.40), channel_id=1, source_target_pairs={{0,1},{1,0},{2,3},{3,2},{4,5},{5,4},{6,7},{7,6},{8,9},{9,8},{10,11... | collective-permute-start | bytes 196616 | tf_op jit(solution)/shard_map/ppermute | solution.py:179
  16.7 0.7 %copy-start.1 = (s32[1,4]{1,0:T(1,128)S(1)}, s32[1,4]{1,0:T(1,128)}, u32[]{:S(2)}) copy-start(s32[1,4]{1,0:T(1,128)} %refs_2_.1) | copy-start | bytes 52
  16.7 1.9 %collective-permute-start.4 = (bf16[4,2,32,128]{3,2,1,0:T(8,128)(2,1)S(1)}, bf16[4,2,32,128]{3,2,1,0:T(8,128)(2,1)S(1)}, u32[]{:S(2)}, u32[]{:S(2)}) collective-permute-start(bf16[4,2,32,128]{3,2,1,0:T(8,128)(2,1)S(1)} %get-tuple-element.39), channel_id=1, source_target_pairs={{0,1},{1,0},{2,3},{3,2},{4,5},{5,4},{6,7},{7,6},{8,9},{9,8},{10,11... | collective-permute-start | bytes 196616 | tf_op jit(solution)/shard_map/ppermute | solution.py:179
  20.4 1.6 %collective-permute-start.6 = (bf16[4,2,64,128]{3,2,1,0:T(8,128)(2,1)S(1)}, bf16[4,2,64,128]{3,2,1,0:T(8,128)(2,1)S(1)}, u32[]{:S(2)}, u32[]{:S(2)}) collective-permute-start(bf16[4,2,64,128]{3,2,1,0:T(8,128)(2,1)S(1)} %collective-permute-done.1.refs_1_), channel_id=1, source_target_pairs={{0,1},{1,0},{2,3},{3,2},{4,5},{5,4},{6,7},{7,6},{8,9},{9,8},{10,11... | collective-permute-start | bytes 393224 | tf_op jit(solution)/shard_map/ppermute | solution.py:179
  20.4 1.6 %collective-permute-start.7 = (bf16[4,2,64,128]{3,2,1,0:T(8,128)(2,1)S(1)}, bf16[4,2,64,128]{3,2,1,0:T(8,128)(2,1)S(1)}, u32[]{:S(2)}, u32[]{:S(2)}) collective-permute-start(bf16[4,2,64,128]{3,2,1,0:T(8,128)(2,1)S(1)} %collective-permute-done.2.refs_2_), channel_id=1, source_target_pairs={{0,1},{1,0},{2,3},{3,2},{4,5},{5,4},{6,7},{7,6},{8,9},{9,8},{10,11... | collective-permute-start | bytes 393224 | tf_op jit(solution)/shard_map/ppermute | solution.py:179
  22.0 1.3 %collective-permute-start.5 = (bf16[4,2,64,128]{3,2,1,0:T(8,128)(2,1)S(1)}, bf16[4,2,64,128]{3,2,1,0:T(8,128)(2,1)S(1)}, u32[]{:S(2)}, u32[]{:S(2)}) collective-permute-start(bf16[4,2,64,128]{3,2,1,0:T(8,128)(2,1)S(1)} %collective-permute-done.refs_3_), channel_id=1, source_target_pairs={{0,1},{1,0},{2,3},{3,2},{4,5},{5,4},{6,7},{7,6},{8,9},{9,8},{10,11... | collective-permute-start | bytes 393224 | tf_op jit(solution)/shard_map/ppermute | solution.py:179

commit v13 on v12

--- a/solution.py
+++ b/solution.py
@@ -10,6 +10,7 @@
 
 NEG = -1e30
 STEP_BLOCKS = 8
+DIGIT = 4
 
 
 def attention_kernel(head_size, parts, kind, *refs):
@@ -60,7 +61,7 @@
         key_pos = []
         for kv_ref, (flip, place, skip) in zip(kv_refs, parts):
             for i in range(count):
-                block = 2 * (index * step_blocks + i) + (own ^ flip) % 2
+                block = 2 * ((own // 2) ^ (index * step_blocks + i)) + (own ^ flip) % 2
                 start = block * rows + (head_place ^ place) * piece_rows + skip
                 key_pos.append(start + in_piece[: kv_ref.shape[2]])
         key_pos = jnp.concatenate(key_pos, axis=0)
@@ -122,9 +123,11 @@
         def new_state(head):
             return stats_ref[head : head + 1], stats_ref[heads + head : heads + head + 1], sums_ref[head]
 
-        @pl.loop(first_key // rows // 2 // step_blocks, own // 2 // step_blocks + 1)
+        @pl.loop(0, blocks // step_blocks)
         def _(index):
-            step(index, step_blocks, new_state, keep)
+            group = (own // 2 // step_blocks) ^ index
+            needed = (group <= own // 2 // step_blocks) & (group >= first_key // rows // 2 // step_blocks)
+            pl.when(needed)(lambda: step(index, step_blocks, new_state, keep))
 
         if last:
             for head in range(heads):
@@ -168,15 +171,17 @@
     )(*operands, *state)
 
 
-def same_parity_blocks(block, axis):
-    size = lax.axis_size(axis)
-    groups = [list(range(parity, size, 2)) for parity in range(2)]
-    spread = jnp.broadcast_to(block, (size // 2,) + block.shape)
-    return lax.all_to_all(spread, axis, 0, 0, axis_index_groups=groups)
-
-
 def exchange(piece, axis, bits):
     return lax.ppermute(piece, axis, [(i, i ^ bits) for i in range(lax.axis_size(axis))])
+
+
+def same_parity_blocks(block, axis):
+    pairs = lax.axis_size(axis) // 2
+    held = block[None]
+    while (count := held.shape[0]) < pairs:
+        digits = range(1, min(DIGIT, pairs // count))
+        held = jnp.concatenate([held] + [exchange(held, axis, 2 * digit * count) for digit in digits])
+    return held
 
 
 def body(queries, key_rows, value_rows, document_lengths):

time: 24.8 us -> 23.9 us (0.964)
  blocking collectives: 12.3 us -> 0 us
  waiting for transfers between devices: 2.66 us -> 8.37 us
  starting transfers between devices: 4.56 us -> 10.2 us
    all_to_all x1 -> x0, blocking collectives: 12.3 us -> none  [same_parity_blocks(): return lax.all_to_all(spread, axis, 0, 0, axis_index_groups=groups)]
    ppermute x8 -> x11, waiting for transfers between devices: 2.66 us -> 8.37 us  [exchange(): lax.ppermute(piece, axis, [(i, i ^ bits) for i in range(lax.axis_size(axi...]
    ppermute x8 -> x11, starting transfers between devices: 4.56 us -> 10.2 us  [exchange(): lax.ppermute(piece, axis, [(i, i ^ bits) for i in range(lax.axis_size(axi...]
    broadcast_in_dim x0 -> x1, other arithmetic: none -> 0.74 us  [same_parity_blocks(): held = block[None]]
    another operation x1 -> x0, other arithmetic: 0.74 us -> none  [body(): own = same_parity_blocks(jnp.stack([key_rows[seq], value_rows[seq]]), 'ctx')]
  transfers between devices with their start and end apart: 8 -> 11, of which waited for: 4 -> 6; matrix products, arithmetic and copies ran while one was open for 0% -> 0% of each run, Pallas kernels for 11% -> 12%
where the time goes in v13:
time: 23.9 us; the launch traced here: 23.6 us
  starting transfers between devices  10.2 us (43%)
  waiting for transfers between devices  8.37 us (35%)
  Pallas kernels  3.93 us (16%)
  other arithmetic  0.76 us (3%)
    ppermute x11, starting transfers between devices, exchange(): lax.ppermute(piece, axis, [(i, i ^ bits) for i in range(lax.axis_size(axi...  10.2 us
    ppermute x11, waiting for transfers between devices, exchange(): lax.ppermute(piece, axis, [(i, i ^ bits) for i in range(lax.axis_size(axi...  8.37 us
    pallas_call x5, Pallas kernels, attend(): pl.pallas_call(functools.partial(attention_kernel, head_size, parts, kind...  3.93 us
    broadcast_in_dim x1, other arithmetic, same_parity_blocks(): held = block[None]  0.74 us
  transfers between devices with their start and end apart: 11, of which 6 were waited for; matrix products, arithmetic and copies ran while one was open for 0% of the time, Pallas kernels for 12%

profile of v13, /device:TPU:0, one launch (start us, length us, event | category | flops | bytes accessed | tf_op | source)
XLA Modules:
  0.0 23.6 jit_solution(11869814823480203854)
XLA Ops:
  0.0 0.7 %maximum_bitcast_fusion = bf16[1,2,64,128]{3,2,1,0:T(8,128)(2,1)S(1)} fusion(bf16[1,64,128]{2,1,0:T(8,128)(2,1)} %param.6, bf16[1,64,128]{2,1,0:T(8,128)(2,1)} %param.5), kind=kLoop, calls=%fused_computation.1 | loop fusion | flops 16384 | bytes 65536 | tf_op jit(solution)/shard_map/broadcast_in_dim | solution.py:180
  0.7 0.0 copy-start
  0.7 3.0 %collective-permute-start = (bf16[1,2,64,128]{3,2,1,0:T(8,128)(2,1)S(1)}, bf16[1,2,64,128]{3,2,1,0:T(8,128)(2,1)S(1)}, u32[]{:S(2)}, u32[]{:S(2)}) collective-permute-start(bf16[1,2,64,128]{3,2,1,0:T(8,128)(2,1)S(1)} %maximum_bitcast_fusion), channel_id=1, source_target_pairs={{0,8},{4,12},{8,0},{12,4},{16,24},{20,28},{24,16},{28,20},{1,9},{5... | collective-permute-start | bytes 98312 | tf_op jit(solution)/shard_map/ppermute | solution.py:175
  3.8 2.6 %collective-permute-start.1 = (bf16[1,2,64,128]{3,2,1,0:T(8,128)(2,1)S(1)}, bf16[1,2,64,128]{3,2,1,0:T(8,128)(2,1)S(1)}, u32[]{:S(2)}, u32[]{:S(2)}) collective-permute-start(bf16[1,2,64,128]{3,2,1,0:T(8,128)(2,1)S(1)} %maximum_bitcast_fusion), channel_id=1, source_target_pairs={{0,16},{4,20},{8,24},{12,28},{16,0},{20,4},{24,8},{28,12},{1,17},{... | collective-permute-start | bytes 98312 | tf_op jit(solution)/shard_map/ppermute | solution.py:175
  6.4 0.0 collective-permute-start.2
  6.4 0.0 collective-permute-done
  6.4 2.8 %collective-permute-done.1 = bf16[1,2,64,128]{3,2,1,0:T(8,128)(2,1)S(1)} collective-permute-done((bf16[1,2,64,128]{3,2,1,0:T(8,128)(2,1)S(1)}, bf16[1,2,64,128]{3,2,1,0:T(8,128)(2,1)S(1)}, u32[]{:S(2)}, u32[]{:S(2)}) %collective-permute-start.1) | collective-permute-done | bytes 32800 | tf_op jit(solution)/shard_map/ppermute | solution.py:175
  9.2 2.9 %collective-permute-done.2 = bf16[1,2,64,128]{3,2,1,0:T(8,128)(2,1)S(1)} collective-permute-done((bf16[1,2,64,128]{3,2,1,0:T(8,128)(2,1)S(1)}, bf16[1,2,64,128]{3,2,1,0:T(8,128)(2,1)S(1)}, u32[]{:S(2)}, u32[]{:S(2)}) %collective-permute-start.2) | collective-permute-done | bytes 32800 | tf_op jit(solution)/shard_map/ppermute | solution.py:175
  12.1 1.6 %collective-permute-start.4 = (bf16[4,2,64,128]{3,2,1,0:T(8,128)(2,1)S(1)}, bf16[4,2,64,128]{3,2,1,0:T(8,128)(2,1)S(1)}, u32[]{:S(2)}, u32[]{:S(2)}) collective-permute-start(bf16[4,2,64,128]{3,2,1,0:T(8,128)(2,1)S(1)} %pad_maximum_fusion.refs_1_), channel_id=1, source_target_pairs={{0,4},{4,0},{8,12},{12,8},{16,20},{20,16},{24,28},{28,24},{1,5},{5... | collective-permute-start | bytes 393224 | tf_op jit(solution)/shard_map/ppermute | solution.py:175
  13.6 1.5 %collective-permute-start.5 = (bf16[4,2,64,128]{3,2,1,0:T(8,128)(2,1)S(1)}, bf16[4,2,64,128]{3,2,1,0:T(8,128)(2,1)S(1)}, u32[]{:S(2)}, u32[]{:S(2)}) collective-permute-start(bf16[4,2,64,128]{3,2,1,0:T(8,128)(2,1)S(1)} %pad_maximum_fusion.refs_1_), channel_id=1, source_target_pairs={{0,2},{1,3},{2,0},{3,1},{4,6},{5,7},{6,4},{7,5},{8,10},{9,11},{10,... | collective-permute-start | bytes 393224 | tf_op jit(solution)/shard_map/ppermute | solution.py:175
  15.2 0.5 %collective-permute-start.3 = (bf16[4,2,64,128]{3,2,1,0:T(8,128)(2,1)S(1)}, bf16[4,2,64,128]{3,2,1,0:T(8,128)(2,1)S(1)}, u32[]{:S(2)}, u32[]{:S(2)}) collective-permute-start(bf16[4,2,64,128]{3,2,1,0:T(8,128)(2,1)S(1)} %pad_maximum_fusion.refs_1_), channel_id=1, source_target_pairs={{0,6},{1,7},{2,4},{3,5},{4,2},{5,3},{6,0},{7,1},{8,14},{9,15},{10,... | collective-permute-start | bytes 393224 | tf_op jit(solution)/shard_map/ppermute | solution.py:175
  15.7 0.1 collective-permute-start.6
  15.7 0.0 copy-start.1
  15.8 0.5 %collective-permute-start.7 = (bf16[4,2,32,128]{3,2,1,0:T(8,128)(2,1)S(1)}, bf16[4,2,32,128]{3,2,1,0:T(8,128)(2,1)S(1)}, u32[]{:S(2)}, u32[]{:S(2)}) collective-permute-start(bf16[4,2,32,128]{3,2,1,0:T(8,128)(2,1)S(1)} %get-tuple-element.39), channel_id=1, source_target_pairs={{0,1},{1,0},{2,3},{3,2},{4,5},{5,4},{6,7},{7,6},{8,9},{9,8},{10,11... | collective-permute-start | bytes 196616 | tf_op jit(solution)/shard_map/ppermute | solution.py:175
  16.2 0.0 copy-done
  16.2 0.2 copy-done.1
  16.4 1.2 %shard_map.46 = (f32[8,256]{1,0:T(8,128)S(1)}, f32[4,128,256]{2,1,0:T(8,128)S(1)}, s32[1,256]{1,0:T(1,128)S(1)}, bf16[4,128,256]{2,1,0:T(8,128)(2,1)S(1)}) custom-call(bf16[256,512]{1,0:T(8,128)(2,1)S(1)} %bitcast.4, bf16[4,2,64,128]{3,2,1,0:T(8,128)(2,1)S(1)} %pad_maximum_fusion.refs_1_, s32[1,4]{1,0:T(1,128)S(1)} %copy-done.1), custom_call_target="tpu_custom_call" | custom-call | flops 1 | bytes 1 | tf_op jit(solution)/shard_map/pallas_call | solution.py:163
  17.6 0.0 collective-permute-done.6.refs_1_
  17.6 0.0 collective-permute-done.7.refs_2_
  17.7 0.4 %shard_map.47 = (f32[8,256]{1,0:T(8,128)S(1)}, f32[4,128,256]{2,1,0:T(8,128)S(1)}) custom-call(bf16[4,128,256]{2,1,0:T(8,128)(2,1)S(1)} %get-tuple-element.22.refs_0_, bf16[4,2,32,128]{3,2,1,0:T(8,128)(2,1)S(1)} %collective-permute-done.6.refs_1_, bf16[4,2,32,128]{3,2,1,0:T(8,128)(2,1)S(1)} %collective-permute-done.7.refs_2_, ...), custom_call_target="tpu_custom_call" | custom-call | flops 1 | bytes 1 | tf_op jit(solution)/shard_map/pallas_call | solution.py:163
  18.1 0.1 collective-permute-done.4.refs_1_
  18.2 1.2 %collective-permute-done.5.refs_2_ = bf16[4,2,64,128]{3,2,1,0:T(8,128)(2,1)S(1)} collective-permute-done((bf16[4,2,64,128]{3,2,1,0:T(8,128)(2,1)S(1)}, bf16[4,2,64,128]{3,2,1,0:T(8,128)(2,1)S(1)}, u32[]{:S(2)}, u32[]{:S(2)}) %collective-permute-start.5) | collective-permute-done | bytes 131104 | tf_op jit(solution)/shard_map/ppermute | solution.py:175
  19.4 0.0 collective-permute-start.10
  19.4 0.5 %collective-permute-start.9 = (bf16[4,2,64,128]{3,2,1,0:T(8,128)(2,1)S(1)}, bf16[4,2,64,128]{3,2,1,0:T(8,128)(2,1)S(1)}, u32[]{:S(2)}, u32[]{:S(2)}) collective-permute-start(bf16[4,2,64,128]{3,2,1,0:T(8,128)(2,1)S(1)} %collective-permute-done.4.refs_1_), channel_id=1, source_target_pairs={{0,1},{1,0},{2,3},{3,2},{4,5},{5,4},{6,7},{7,6},{8,9},{9,8},{10,11... | collective-permute-start | bytes 393224 | tf_op jit(solution)/shard_map/ppermute | solution.py:175
  19.9 0.5 %shard_map.48 = (f32[8,256]{1,0:T(8,128)S(1)}, f32[4,128,256]{2,1,0:T(8,128)S(1)}) custom-call(bf16[4,128,256]{2,1,0:T(8,128)(2,1)S(1)} %get-tuple-element.22.refs_0_, bf16[4,2,64,128]{3,2,1,0:T(8,128)(2,1)S(1)} %collective-permute-done.4.refs_1_, bf16[4,2,64,128]{3,2,1,0:T(8,128)(2,1)S(1)} %collective-permute-done.5.refs_2_, ...), custom_call_target="tpu_custom_call" | custom-call | flops 1 | bytes 1 | tf_op jit(solution)/shard_map/pallas_call | solution.py:163
  20.4 0.6 %collective-permute-done.3.refs_3_ = bf16[4,2,64,128]{3,2,1,0:T(8,128)(2,1)S(1)} collective-permute-done((bf16[4,2,64,128]{3,2,1,0:T(8,128)(2,1)S(1)}, bf16[4,2,64,128]{3,2,1,0:T(8,128)(2,1)S(1)}, u32[]{:S(2)}, u32[]{:S(2)}) %collective-permute-start.3) | collective-permute-done | bytes 131104 | tf_op jit(solution)/shard_map/ppermute | solution.py:175
  21.0 0.0 collective-permute-start.8
  21.0 0.0 collective-permute-done.10.refs_2_
  21.0 0.0 collective-permute-done.9.refs_1_
  21.0 0.6 %shard_map.49 = (f32[8,256]{1,0:T(8,128)S(1)}, f32[4,128,256]{2,1,0:T(8,128)S(1)}) custom-call(bf16[4,128,256]{2,1,0:T(8,128)(2,1)S(1)} %get-tuple-element.22.refs_0_, bf16[4,2,64,128]{3,2,1,0:T(8,128)(2,1)S(1)} %collective-permute-done.9.refs_1_, bf16[4,2,64,128]{3,2,1,0:T(8,128)(2,1)S(1)} %collective-permute-done.10.refs_2_, ...), custom_call_target="tpu_custom_call" | custom-call | flops 1 | bytes 1 | tf_op jit(solution)/shard_map/pallas_call | solution.py:163
  21.6 0.7 %collective-permute-done.8.refs_1_ = bf16[4,2,64,128]{3,2,1,0:T(8,128)(2,1)S(1)} collective-permute-done((bf16[4,2,64,128]{3,2,1,0:T(8,128)(2,1)S(1)}, bf16[4,2,64,128]{3,2,1,0:T(8,128)(2,1)S(1)}, u32[]{:S(2)}, u32[]{:S(2)}) %collective-permute-start.8) | collective-permute-done | bytes 131104 | tf_op jit(solution)/shard_map/ppermute | solution.py:175
  22.4 1.2 %shard_map.50 = bf16[256,512]{1,0:T(8,128)(2,1)} custom-call(bf16[4,128,256]{2,1,0:T(8,128)(2,1)S(1)} %get-tuple-element.22.refs_0_, bf16[4,2,64,128]{3,2,1,0:T(8,128)(2,1)S(1)} %collective-permute-done.8.refs_1_, f32[8,256]{1,0:T(8,128)S(1)} %get-tuple-element.37.refs_2_, f32[4,128,256]{2,1,0:T(8,128)S(1)} %get-tuple-element.38.refs_3_, ...), custom_call_target="tpu_custom_call" | custom-call | flops 1 | bytes 1 | tf_op jit(solution)/shard_map/pallas_call | solution.py:163
  (2 shorter events, 0.0 us)
Async XLA Ops:
  0.7 15.5 %copy-start = (bf16[1,256,512]{2,1,0:T(8,128)(2,1)S(1)}, bf16[1,256,512]{2,1,0:T(8,128)(2,1)}, u32[]{:S(2)}) copy-start(bf16[1,256,512]{2,1,0:T(8,128)(2,1)} %param.4) | copy-start | bytes 786436
  0.7 5.6 %collective-permute-start = (bf16[1,2,64,128]{3,2,1,0:T(8,128)(2,1)S(1)}, bf16[1,2,64,128]{3,2,1,0:T(8,128)(2,1)S(1)}, u32[]{:S(2)}, u32[]{:S(2)}) collective-permute-start(bf16[1,2,64,128]{3,2,1,0:T(8,128)(2,1)S(1)} %maximum_bitcast_fusion), channel_id=1, source_target_pairs={{0,8},{4,12},{8,0},{12,4},{16,24},{20,28},{24,16},{28,20},{1,9},{5... | collective-permute-start | bytes 98312 | tf_op jit(solution)/shard_map/ppermute | solution.py:175
  3.8 5.4 %collective-permute-start.1 = (bf16[1,2,64,128]{3,2,1,0:T(8,128)(2,1)S(1)}, bf16[1,2,64,128]{3,2,1,0:T(8,128)(2,1)S(1)}, u32[]{:S(2)}, u32[]{:S(2)}) collective-permute-start(bf16[1,2,64,128]{3,2,1,0:T(8,128)(2,1)S(1)} %maximum_bitcast_fusion), channel_id=1, source_target_pairs={{0,16},{4,20},{8,24},{12,28},{16,0},{20,4},{24,8},{28,12},{1,17},{... | collective-permute-start | bytes 98312 | tf_op jit(solution)/shard_map/ppermute | solution.py:175
  6.4 5.7 %collective-permute-start.2 = (bf16[1,2,64,128]{3,2,1,0:T(8,128)(2,1)S(1)}, bf16[1,2,64,128]{3,2,1,0:T(8,128)(2,1)S(1)}, u32[]{:S(2)}, u32[]{:S(2)}) collective-permute-start(bf16[1,2,64,128]{3,2,1,0:T(8,128)(2,1)S(1)} %maximum_bitcast_fusion), channel_id=1, source_target_pairs={{0,24},{4,28},{8,16},{12,20},{16,8},{20,12},{24,0},{28,4},{1,25},{... | collective-permute-start | bytes 98312 | tf_op jit(solution)/shard_map/ppermute | solution.py:175
  12.1 6.1 %collective-permute-start.4 = (bf16[4,2,64,128]{3,2,1,0:T(8,128)(2,1)S(1)}, bf16[4,2,64,128]{3,2,1,0:T(8,128)(2,1)S(1)}, u32[]{:S(2)}, u32[]{:S(2)}) collective-permute-start(bf16[4,2,64,128]{3,2,1,0:T(8,128)(2,1)S(1)} %pad_maximum_fusion.refs_1_), channel_id=1, source_target_pairs={{0,4},{4,0},{8,12},{12,8},{16,20},{20,16},{24,28},{28,24},{1,5},{5... | collective-permute-start | bytes 393224 | tf_op jit(solution)/shard_map/ppermute | solution.py:175
  13.6 5.8 %collective-permute-start.5 = (bf16[4,2,64,128]{3,2,1,0:T(8,128)(2,1)S(1)}, bf16[4,2,64,128]{3,2,1,0:T(8,128)(2,1)S(1)}, u32[]{:S(2)}, u32[]{:S(2)}) collective-permute-start(bf16[4,2,64,128]{3,2,1,0:T(8,128)(2,1)S(1)} %pad_maximum_fusion.refs_1_), channel_id=1, source_target_pairs={{0,2},{1,3},{2,0},{3,1},{4,6},{5,7},{6,4},{7,5},{8,10},{9,11},{10,... | collective-permute-start | bytes 393224 | tf_op jit(solution)/shard_map/ppermute | solution.py:175
  15.2 5.9 %collective-permute-start.3 = (bf16[4,2,64,128]{3,2,1,0:T(8,128)(2,1)S(1)}, bf16[4,2,64,128]{3,2,1,0:T(8,128)(2,1)S(1)}, u32[]{:S(2)}, u32[]{:S(2)}) collective-permute-start(bf16[4,2,64,128]{3,2,1,0:T(8,128)(2,1)S(1)} %pad_maximum_fusion.refs_1_), channel_id=1, source_target_pairs={{0,6},{1,7},{2,4},{3,5},{4,2},{5,3},{6,0},{7,1},{8,14},{9,15},{10,... | collective-permute-start | bytes 393224 | tf_op jit(solution)/shard_map/ppermute | solution.py:175
  15.7 2.0 %collective-permute-start.6 = (bf16[4,2,32,128]{3,2,1,0:T(8,128)(2,1)S(1)}, bf16[4,2,32,128]{3,2,1,0:T(8,128)(2,1)S(1)}, u32[]{:S(2)}, u32[]{:S(2)}) collective-permute-start(bf16[4,2,32,128]{3,2,1,0:T(8,128)(2,1)S(1)} %get-tuple-element.40), channel_id=1, source_target_pairs={{0,1},{1,0},{2,3},{3,2},{4,5},{5,4},{6,7},{7,6},{8,9},{9,8},{10,11... | collective-permute-start | bytes 196616 | tf_op jit(solution)/shard_map/ppermute | solution.py:175
  15.7 0.7 %copy-start.1 = (s32[1,4]{1,0:T(1,128)S(1)}, s32[1,4]{1,0:T(1,128)}, u32[]{:S(2)}) copy-start(s32[1,4]{1,0:T(1,128)} %refs_2_.1) | copy-start | bytes 52
  15.8 1.9 %collective-permute-start.7 = (bf16[4,2,32,128]{3,2,1,0:T(8,128)(2,1)S(1)}, bf16[4,2,32,128]{3,2,1,0:T(8,128)(2,1)S(1)}, u32[]{:S(2)}, u32[]{:S(2)}) collective-permute-start(bf16[4,2,32,128]{3,2,1,0:T(8,128)(2,1)S(1)} %get-tuple-element.39), channel_id=1, source_target_pairs={{0,1},{1,0},{2,3},{3,2},{4,5},{5,4},{6,7},{7,6},{8,9},{9,8},{10,11... | collective-permute-start | bytes 196616 | tf_op jit(solution)/shard_map/ppermute | solution.py:175
  19.4 1.6 %collective-permute-start.10 = (bf16[4,2,64,128]{3,2,1,0:T(8,128)(2,1)S(1)}, bf16[4,2,64,128]{3,2,1,0:T(8,128)(2,1)S(1)}, u32[]{:S(2)}, u32[]{:S(2)}) collective-permute-start(bf16[4,2,64,128]{3,2,1,0:T(8,128)(2,1)S(1)} %collective-permute-done.5.refs_2_), channel_id=1, source_target_pairs={{0,1},{1,0},{2,3},{3,2},{4,5},{5,4},{6,7},{7,6},{8,9},{9,8},{10,11... | collective-permute-start | bytes 393224 | tf_op jit(solution)/shard_map/ppermute | solution.py:175
  19.4 1.6 %collective-permute-start.9 = (bf16[4,2,64,128]{3,2,1,0:T(8,128)(2,1)S(1)}, bf16[4,2,64,128]{3,2,1,0:T(8,128)(2,1)S(1)}, u32[]{:S(2)}, u32[]{:S(2)}) collective-permute-start(bf16[4,2,64,128]{3,2,1,0:T(8,128)(2,1)S(1)} %collective-permute-done.4.refs_1_), channel_id=1, source_target_pairs={{0,1},{1,0},{2,3},{3,2},{4,5},{5,4},{6,7},{7,6},{8,9},{9,8},{10,11... | collective-permute-start | bytes 393224 | tf_op jit(solution)/shard_map/ppermute | solution.py:175
  21.0 1.3 %collective-permute-start.8 = (bf16[4,2,64,128]{3,2,1,0:T(8,128)(2,1)S(1)}, bf16[4,2,64,128]{3,2,1,0:T(8,128)(2,1)S(1)}, u32[]{:S(2)}, u32[]{:S(2)}) collective-permute-start(bf16[4,2,64,128]{3,2,1,0:T(8,128)(2,1)S(1)} %collective-permute-done.3.refs_3_), channel_id=1, source_target_pairs={{0,1},{1,0},{2,3},{3,2},{4,5},{5,4},{6,7},{7,6},{8,9},{9,8},{10,11... | collective-permute-start | bytes 393224 | tf_op jit(solution)/shard_map/ppermute | solution.py:175

commit v14 on v13

--- a/solution.py
+++ b/solution.py
@@ -11,6 +11,7 @@
 NEG = -1e30
 STEP_BLOCKS = 8
 DIGIT = 4
+ORDER = (2, 3, 1)
 
 
 def attention_kernel(head_size, parts, kind, *refs):
@@ -179,8 +180,10 @@
     pairs = lax.axis_size(axis) // 2
     held = block[None]
     while (count := held.shape[0]) < pairs:
-        digits = range(1, min(DIGIT, pairs // count))
-        held = jnp.concatenate([held] + [exchange(held, axis, 2 * digit * count) for digit in digits])
+        digits = sorted(range(1, min(DIGIT, pairs // count)), key=lambda digit: ORDER.index(digit))
+        moved = lax.optimization_barrier([exchange(held, axis, 2 * digit * count) for digit in digits])
+        moved = dict(zip(digits, moved))
+        held = jnp.concatenate([held] + [moved[digit] for digit in sorted(digits)])
     return held
 
 

time: 23.9 us -> 22.5 us (0.941)
  the two profiles are of different devices: /device:TPU:0 before, /device:TPU:25 now
where the time goes in v14:
time: 22.5 us; the launch traced here: 22.1 us
  starting transfers between devices  11.5 us (51%)
  Pallas kernels  6.05 us (27%)
  waiting for transfers between devices  3.16 us (14%)
  other arithmetic  0.76 us (3%)
  local copies, waits for them, and re-layouts  0.58 us (3%)
    ppermute x11, starting transfers between devices, exchange(): lax.ppermute(piece, axis, [(i, i ^ bits) for i in range(lax.axis_size(axi...  11.5 us
    pallas_call x5, Pallas kernels, attend(): pl.pallas_call(functools.partial(attention_kernel, head_size, parts, kind...  6.05 us
    ppermute x11, waiting for transfers between devices, exchange(): lax.ppermute(piece, axis, [(i, i ^ bits) for i in range(lax.axis_size(axi...  3.16 us
    broadcast_in_dim x1, other arithmetic, same_parity_blocks(): held = block[None]  0.74 us
    unnamed x4, local copies, waits for them, and re-layouts  0.57 us
  transfers between devices with their start and end apart: 11, of which 3 were waited for; matrix products, arithmetic and copies ran while one was open for 0% of the time, Pallas kernels for 21%

profile of v14, /device:TPU:25, one launch (start us, length us, event | category | flops | bytes accessed | tf_op | source)
XLA Modules:
  0.0 22.1 jit_solution(2106317573602962797)
XLA Ops:
  0.0 0.7 %maximum_bitcast_fusion = bf16[1,2,64,128]{3,2,1,0:T(8,128)(2,1)S(1)} fusion(bf16[1,64,128]{2,1,0:T(8,128)(2,1)} %param.6, bf16[1,64,128]{2,1,0:T(8,128)(2,1)} %param.5), kind=kLoop, calls=%fused_computation.1 | loop fusion | flops 16384 | bytes 65536 | tf_op jit(solution)/shard_map/broadcast_in_dim | solution.py:181
  0.7 0.0 copy-start
  0.7 0.1 collective-permute-start
  0.8 2.2 %collective-permute-start.1 = (bf16[1,2,64,128]{3,2,1,0:T(8,128)(2,1)S(1)}, bf16[1,2,64,128]{3,2,1,0:T(8,128)(2,1)S(1)}, u32[]{:S(2)}, u32[]{:S(2)}) collective-permute-start(bf16[1,2,64,128]{3,2,1,0:T(8,128)(2,1)S(1)} %maximum_bitcast_fusion), channel_id=1, source_target_pairs={{0,24},{4,28},{8,16},{12,20},{16,8},{20,12},{24,0},{28,4},{1,25},{... | collective-permute-start | bytes 98312 | tf_op jit(solution)/shard_map/ppermute | solution.py:176
  3.0 0.4 %collective-permute-start.2 = (bf16[1,2,64,128]{3,2,1,0:T(8,128)(2,1)S(1)}, bf16[1,2,64,128]{3,2,1,0:T(8,128)(2,1)S(1)}, u32[]{:S(2)}, u32[]{:S(2)}) collective-permute-start(bf16[1,2,64,128]{3,2,1,0:T(8,128)(2,1)S(1)} %maximum_bitcast_fusion), channel_id=1, source_target_pairs={{0,8},{4,12},{8,0},{12,4},{16,24},{20,28},{24,16},{28,20},{1,9},{5... | collective-permute-start | bytes 98312 | tf_op jit(solution)/shard_map/ppermute | solution.py:176
  3.4 1.3 %collective-permute-done = bf16[1,2,64,128]{3,2,1,0:T(8,128)(2,1)S(1)} collective-permute-done((bf16[1,2,64,128]{3,2,1,0:T(8,128)(2,1)S(1)}, bf16[1,2,64,128]{3,2,1,0:T(8,128)(2,1)S(1)}, u32[]{:S(2)}, u32[]{:S(2)}) %collective-permute-start) | collective-permute-done | bytes 32800 | tf_op jit(solution)/shard_map/ppermute | solution.py:176
  4.6 1.1 %collective-permute-done.1 = bf16[1,2,64,128]{3,2,1,0:T(8,128)(2,1)S(1)} collective-permute-done((bf16[1,2,64,128]{3,2,1,0:T(8,128)(2,1)S(1)}, bf16[1,2,64,128]{3,2,1,0:T(8,128)(2,1)S(1)}, u32[]{:S(2)}, u32[]{:S(2)}) %collective-permute-start.1) | collective-permute-done | bytes 32800 | tf_op jit(solution)/shard_map/ppermute | solution.py:176
  5.7 0.8 %collective-permute-done.2 = bf16[1,2,64,128]{3,2,1,0:T(8,128)(2,1)S(1)} collective-permute-done((bf16[1,2,64,128]{3,2,1,0:T(8,128)(2,1)S(1)}, bf16[1,2,64,128]{3,2,1,0:T(8,128)(2,1)S(1)}, u32[]{:S(2)}, u32[]{:S(2)}) %collective-permute-start.2) | collective-permute-done | bytes 32800 | tf_op jit(solution)/shard_map/ppermute | solution.py:176
  6.6 1.3 %collective-permute-start.4 = (bf16[4,2,64,128]{3,2,1,0:T(8,128)(2,1)S(1)}, bf16[4,2,64,128]{3,2,1,0:T(8,128)(2,1)S(1)}, u32[]{:S(2)}, u32[]{:S(2)}) collective-permute-start(bf16[4,2,64,128]{3,2,1,0:T(8,128)(2,1)S(1)} %pad_maximum_fusion.refs_1_), channel_id=1, source_target_pairs={{0,4},{4,0},{8,12},{12,8},{16,20},{20,16},{24,28},{28,24},{1,5},{5... | collective-permute-start | bytes 393224 | tf_op jit(solution)/shard_map/ppermute | solution.py:176
  7.8 1.2 %collective-permute-start.5 = (bf16[4,2,64,128]{3,2,1,0:T(8,128)(2,1)S(1)}, bf16[4,2,64,128]{3,2,1,0:T(8,128)(2,1)S(1)}, u32[]{:S(2)}, u32[]{:S(2)}) collective-permute-start(bf16[4,2,64,128]{3,2,1,0:T(8,128)(2,1)S(1)} %pad_maximum_fusion.refs_1_), channel_id=1, source_target_pairs={{0,2},{1,3},{2,0},{3,1},{4,6},{5,7},{6,4},{7,5},{8,10},{9,11},{10,... | collective-permute-start | bytes 393224 | tf_op jit(solution)/shard_map/ppermute | solution.py:176
  9.1 0.2 collective-permute-start.3
  9.3 2.5 %collective-permute-start.6 = (bf16[4,2,32,128]{3,2,1,0:T(8,128)(2,1)S(1)}, bf16[4,2,32,128]{3,2,1,0:T(8,128)(2,1)S(1)}, u32[]{:S(2)}, u32[]{:S(2)}) collective-permute-start(bf16[4,2,32,128]{3,2,1,0:T(8,128)(2,1)S(1)} %get-tuple-element.46), channel_id=1, source_target_pairs={{0,1},{1,0},{2,3},{3,2},{4,5},{5,4},{6,7},{7,6},{8,9},{9,8},{10,11... | collective-permute-start | bytes 196616 | tf_op jit(solution)/shard_map/ppermute | solution.py:176
  11.8 0.0 copy-start.1
  11.8 0.1 collective-permute-start.7
  11.9 0.0 copy-done
  11.9 0.6 %copy-done.1 = s32[1,4]{1,0:T(1,128)S(1)} copy-done((s32[1,4]{1,0:T(1,128)S(1)}, s32[1,4]{1,0:T(1,128)}, u32[]{:S(2)}) %copy-start.1) | copy-done | bytes 40
  12.5 1.2 %shard_map.46 = (f32[8,256]{1,0:T(8,128)S(1)}, f32[4,128,256]{2,1,0:T(8,128)S(1)}, s32[1,256]{1,0:T(1,128)S(1)}, bf16[4,128,256]{2,1,0:T(8,128)(2,1)S(1)}) custom-call(bf16[256,512]{1,0:T(8,128)(2,1)S(1)} %bitcast.4, bf16[4,2,64,128]{3,2,1,0:T(8,128)(2,1)S(1)} %pad_maximum_fusion.refs_1_, s32[1,4]{1,0:T(1,128)S(1)} %copy-done.1), custom_call_target="tpu_custom_call" | custom-call | flops 1 | bytes 1 | tf_op jit(solution)/shard_map/pallas_call | solution.py:164
  13.7 0.0 collective-permute-done.6.refs_1_
  13.7 0.0 collective-permute-done.7.refs_2_
  13.7 0.7 %shard_map.47 = (f32[8,256]{1,0:T(8,128)S(1)}, f32[4,128,256]{2,1,0:T(8,128)S(1)}) custom-call(bf16[4,128,256]{2,1,0:T(8,128)(2,1)S(1)} %get-tuple-element.28.refs_0_, bf16[4,2,32,128]{3,2,1,0:T(8,128)(2,1)S(1)} %collective-permute-done.6.refs_1_, bf16[4,2,32,128]{3,2,1,0:T(8,128)(2,1)S(1)} %collective-permute-done.7.refs_2_, ...), custom_call_target="tpu_custom_call" | custom-call | flops 1 | bytes 1 | tf_op jit(solution)/shard_map/pallas_call | solution.py:164
  14.4 0.0 collective-permute-done.4.refs_1_
  14.4 0.0 collective-permute-done.5.refs_2_
  14.4 3.0 %collective-permute-start.10 = (bf16[4,2,64,128]{3,2,1,0:T(8,128)(2,1)S(1)}, bf16[4,2,64,128]{3,2,1,0:T(8,128)(2,1)S(1)}, u32[]{:S(2)}, u32[]{:S(2)}) collective-permute-start(bf16[4,2,64,128]{3,2,1,0:T(8,128)(2,1)S(1)} %collective-permute-done.5.refs_2_), channel_id=1, source_target_pairs={{0,1},{1,0},{2,3},{3,2},{4,5},{5,4},{6,7},{7,6},{8,9},{9,8},{10,11... | collective-permute-start | bytes 393224 | tf_op jit(solution)/shard_map/ppermute | solution.py:176
  17.4 0.0 collective-permute-start.9
  17.4 1.1 %shard_map.48 = (f32[8,256]{1,0:T(8,128)S(1)}, f32[4,128,256]{2,1,0:T(8,128)S(1)}) custom-call(bf16[4,128,256]{2,1,0:T(8,128)(2,1)S(1)} %get-tuple-element.28.refs_0_, bf16[4,2,64,128]{3,2,1,0:T(8,128)(2,1)S(1)} %collective-permute-done.4.refs_1_, bf16[4,2,64,128]{3,2,1,0:T(8,128)(2,1)S(1)} %collective-permute-done.5.refs_2_, ...), custom_call_target="tpu_custom_call" | custom-call | flops 1 | bytes 1 | tf_op jit(solution)/shard_map/pallas_call | solution.py:164
  18.5 0.0 collective-permute-done.3.refs_3_
  18.5 0.6 %collective-permute-start.8 = (bf16[4,2,64,128]{3,2,1,0:T(8,128)(2,1)S(1)}, bf16[4,2,64,128]{3,2,1,0:T(8,128)(2,1)S(1)}, u32[]{:S(2)}, u32[]{:S(2)}) collective-permute-start(bf16[4,2,64,128]{3,2,1,0:T(8,128)(2,1)S(1)} %collective-permute-done.3.refs_3_), channel_id=1, source_target_pairs={{0,1},{1,0},{2,3},{3,2},{4,5},{5,4},{6,7},{7,6},{8,9},{9,8},{10,11... | collective-permute-start | bytes 393224 | tf_op jit(solution)/shard_map/ppermute | solution.py:176
  19.1 0.0 collective-permute-done.10.refs_2_
  19.1 0.0 collective-permute-done.9.refs_1_
  19.1 1.6 %shard_map.49 = (f32[8,256]{1,0:T(8,128)S(1)}, f32[4,128,256]{2,1,0:T(8,128)S(1)}) custom-call(bf16[4,128,256]{2,1,0:T(8,128)(2,1)S(1)} %get-tuple-element.28.refs_0_, bf16[4,2,64,128]{3,2,1,0:T(8,128)(2,1)S(1)} %collective-permute-done.9.refs_1_, bf16[4,2,64,128]{3,2,1,0:T(8,128)(2,1)S(1)} %collective-permute-done.10.refs_2_, ...), custom_call_target="tpu_custom_call" | custom-call | flops 1 | bytes 1 | tf_op jit(solution)/shard_map/pallas_call | solution.py:164
  20.7 0.0 collective-permute-done.8.refs_1_
  20.7 1.4 %shard_map.50 = bf16[256,512]{1,0:T(8,128)(2,1)} custom-call(bf16[4,128,256]{2,1,0:T(8,128)(2,1)S(1)} %get-tuple-element.28.refs_0_, bf16[4,2,64,128]{3,2,1,0:T(8,128)(2,1)S(1)} %collective-permute-done.8.refs_1_, f32[8,256]{1,0:T(8,128)S(1)} %get-tuple-element.43.refs_2_, f32[4,128,256]{2,1,0:T(8,128)S(1)} %get-tuple-element.44.refs_3_, ...), custom_call_target="tpu_custom_call" | custom-call | flops 1 | bytes 1 | tf_op jit(solution)/shard_map/pallas_call | solution.py:164
  (2 shorter events, 0.0 us)
Async XLA Ops:
  0.7 11.2 %copy-start = (bf16[1,256,512]{2,1,0:T(8,128)(2,1)S(1)}, bf16[1,256,512]{2,1,0:T(8,128)(2,1)}, u32[]{:S(2)}) copy-start(bf16[1,256,512]{2,1,0:T(8,128)(2,1)} %param.4) | copy-start | bytes 786436
  0.7 3.9 %collective-permute-start = (bf16[1,2,64,128]{3,2,1,0:T(8,128)(2,1)S(1)}, bf16[1,2,64,128]{3,2,1,0:T(8,128)(2,1)S(1)}, u32[]{:S(2)}, u32[]{:S(2)}) collective-permute-start(bf16[1,2,64,128]{3,2,1,0:T(8,128)(2,1)S(1)} %maximum_bitcast_fusion), channel_id=1, source_target_pairs={{0,16},{4,20},{8,24},{12,28},{16,0},{20,4},{24,8},{28,12},{1,17},{... | collective-permute-start | bytes 98312 | tf_op jit(solution)/shard_map/ppermute | solution.py:176
  0.8 4.9 %collective-permute-start.1 = (bf16[1,2,64,128]{3,2,1,0:T(8,128)(2,1)S(1)}, bf16[1,2,64,128]{3,2,1,0:T(8,128)(2,1)S(1)}, u32[]{:S(2)}, u32[]{:S(2)}) collective-permute-start(bf16[1,2,64,128]{3,2,1,0:T(8,128)(2,1)S(1)} %maximum_bitcast_fusion), channel_id=1, source_target_pairs={{0,24},{4,28},{8,16},{12,20},{16,8},{20,12},{24,0},{28,4},{1,25},{... | collective-permute-start | bytes 98312 | tf_op jit(solution)/shard_map/ppermute | solution.py:176
  3.0 3.5 %collective-permute-start.2 = (bf16[1,2,64,128]{3,2,1,0:T(8,128)(2,1)S(1)}, bf16[1,2,64,128]{3,2,1,0:T(8,128)(2,1)S(1)}, u32[]{:S(2)}, u32[]{:S(2)}) collective-permute-start(bf16[1,2,64,128]{3,2,1,0:T(8,128)(2,1)S(1)} %maximum_bitcast_fusion), channel_id=1, source_target_pairs={{0,8},{4,12},{8,0},{12,4},{16,24},{20,28},{24,16},{28,20},{1,9},{5... | collective-permute-start | bytes 98312 | tf_op jit(solution)/shard_map/ppermute | solution.py:176
  6.6 7.9 %collective-permute-start.4 = (bf16[4,2,64,128]{3,2,1,0:T(8,128)(2,1)S(1)}, bf16[4,2,64,128]{3,2,1,0:T(8,128)(2,1)S(1)}, u32[]{:S(2)}, u32[]{:S(2)}) collective-permute-start(bf16[4,2,64,128]{3,2,1,0:T(8,128)(2,1)S(1)} %pad_maximum_fusion.refs_1_), channel_id=1, source_target_pairs={{0,4},{4,0},{8,12},{12,8},{16,20},{20,16},{24,28},{28,24},{1,5},{5... | collective-permute-start | bytes 393224 | tf_op jit(solution)/shard_map/ppermute | solution.py:176
  7.8 6.6 %collective-permute-start.5 = (bf16[4,2,64,128]{3,2,1,0:T(8,128)(2,1)S(1)}, bf16[4,2,64,128]{3,2,1,0:T(8,128)(2,1)S(1)}, u32[]{:S(2)}, u32[]{:S(2)}) collective-permute-start(bf16[4,2,64,128]{3,2,1,0:T(8,128)(2,1)S(1)} %pad_maximum_fusion.refs_1_), channel_id=1, source_target_pairs={{0,2},{1,3},{2,0},{3,1},{4,6},{5,7},{6,4},{7,5},{8,10},{9,11},{10,... | collective-permute-start | bytes 393224 | tf_op jit(solution)/shard_map/ppermute | solution.py:176
  9.1 9.4 %collective-permute-start.3 = (bf16[4,2,64,128]{3,2,1,0:T(8,128)(2,1)S(1)}, bf16[4,2,64,128]{3,2,1,0:T(8,128)(2,1)S(1)}, u32[]{:S(2)}, u32[]{:S(2)}) collective-permute-start(bf16[4,2,64,128]{3,2,1,0:T(8,128)(2,1)S(1)} %pad_maximum_fusion.refs_1_), channel_id=1, source_target_pairs={{0,6},{1,7},{2,4},{3,5},{4,2},{5,3},{6,0},{7,1},{8,14},{9,15},{10,... | collective-permute-start | bytes 393224 | tf_op jit(solution)/shard_map/ppermute | solution.py:176
  9.3 4.4 %collective-permute-start.6 = (bf16[4,2,32,128]{3,2,1,0:T(8,128)(2,1)S(1)}, bf16[4,2,32,128]{3,2,1,0:T(8,128)(2,1)S(1)}, u32[]{:S(2)}, u32[]{:S(2)}) collective-permute-start(bf16[4,2,32,128]{3,2,1,0:T(8,128)(2,1)S(1)} %get-tuple-element.46), channel_id=1, source_target_pairs={{0,1},{1,0},{2,3},{3,2},{4,5},{5,4},{6,7},{7,6},{8,9},{9,8},{10,11... | collective-permute-start | bytes 196616 | tf_op jit(solution)/shard_map/ppermute | solution.py:176
  11.8 0.7 %copy-start.1 = (s32[1,4]{1,0:T(1,128)S(1)}, s32[1,4]{1,0:T(1,128)}, u32[]{:S(2)}) copy-start(s32[1,4]{1,0:T(1,128)} %refs_2_.1) | copy-start | bytes 52
  11.8 1.9 %collective-permute-start.7 = (bf16[4,2,32,128]{3,2,1,0:T(8,128)(2,1)S(1)}, bf16[4,2,32,128]{3,2,1,0:T(8,128)(2,1)S(1)}, u32[]{:S(2)}, u32[]{:S(2)}) collective-permute-start(bf16[4,2,32,128]{3,2,1,0:T(8,128)(2,1)S(1)} %get-tuple-element.45), channel_id=1, source_target_pairs={{0,1},{1,0},{2,3},{3,2},{4,5},{5,4},{6,7},{7,6},{8,9},{9,8},{10,11... | collective-permute-start | bytes 196616 | tf_op jit(solution)/shard_map/ppermute | solution.py:176
  14.4 4.6 %collective-permute-start.10 = (bf16[4,2,64,128]{3,2,1,0:T(8,128)(2,1)S(1)}, bf16[4,2,64,128]{3,2,1,0:T(8,128)(2,1)S(1)}, u32[]{:S(2)}, u32[]{:S(2)}) collective-permute-start(bf16[4,2,64,128]{3,2,1,0:T(8,128)(2,1)S(1)} %collective-permute-done.5.refs_2_), channel_id=1, source_target_pairs={{0,1},{1,0},{2,3},{3,2},{4,5},{5,4},{6,7},{7,6},{8,9},{9,8},{10,11... | collective-permute-start | bytes 393224 | tf_op jit(solution)/shard_map/ppermute | solution.py:176
  17.4 1.7 %collective-permute-start.9 = (bf16[4,2,64,128]{3,2,1,0:T(8,128)(2,1)S(1)}, bf16[4,2,64,128]{3,2,1,0:T(8,128)(2,1)S(1)}, u32[]{:S(2)}, u32[]{:S(2)}) collective-permute-start(bf16[4,2,64,128]{3,2,1,0:T(8,128)(2,1)S(1)} %collective-permute-done.4.refs_1_), channel_id=1, source_target_pairs={{0,1},{1,0},{2,3},{3,2},{4,5},{5,4},{6,7},{7,6},{8,9},{9,8},{10,11... | collective-permute-start | bytes 393224 | tf_op jit(solution)/shard_map/ppermute | solution.py:176
  18.5 2.2 %collective-permute-start.8 = (bf16[4,2,64,128]{3,2,1,0:T(8,128)(2,1)S(1)}, bf16[4,2,64,128]{3,2,1,0:T(8,128)(2,1)S(1)}, u32[]{:S(2)}, u32[]{:S(2)}) collective-permute-start(bf16[4,2,64,128]{3,2,1,0:T(8,128)(2,1)S(1)} %collective-permute-done.3.refs_3_), channel_id=1, source_target_pairs={{0,1},{1,0},{2,3},{3,2},{4,5},{5,4},{6,7},{7,6},{8,9},{9,8},{10,11... | collective-permute-start | bytes 393224 | tf_op jit(solution)/shard_map/ppermute | solution.py:176

commit v15 on v14

--- a/solution.py
+++ b/solution.py
@@ -181,8 +181,12 @@
     held = block[None]
     while (count := held.shape[0]) < pairs:
         digits = sorted(range(1, min(DIGIT, pairs // count)), key=lambda digit: ORDER.index(digit))
-        moved = lax.optimization_barrier([exchange(held, axis, 2 * digit * count) for digit in digits])
-        moved = dict(zip(digits, moved))
+        moved = []
+        for digit in digits:
+            targets = [(i, i ^ (2 * digit * count)) for i in range(lax.axis_size(axis))]
+            targets = [(i, j) for i, j in targets if j // (2 * count) % DIGIT]
+            moved.append(lax.ppermute(held, axis, targets))
+        moved = dict(zip(digits, lax.optimization_barrier(moved)))
         held = jnp.concatenate([held] + [moved[digit] for digit in sorted(digits)])
     return held
 

time: 22.5 us -> 27.5 us (1.22)
  the two profiles are of different devices: /device:TPU:25 before, /device:TPU:21 now
where the time goes in v15:
time: 27.5 us; the launch traced here: 27.1 us
  starting transfers between devices  16.9 us (61%)
  Pallas kernels  6.07 us (22%)
  waiting for transfers between devices  2.74 us (10%)
  other arithmetic  0.76 us (3%)
  local copies, waits for them, and re-layouts  0.58 us (2%)
    ppermute x8, starting transfers between devices, exchange(): lax.ppermute(piece, axis, [(i, i ^ bits) for i in range(lax.axis_size(axi...  8.54 us
    ppermute x3, starting transfers between devices, same_parity_blocks(): moved.append(lax.ppermute(held, axis, targets))  8.34 us
    pallas_call x5, Pallas kernels, attend(): pl.pallas_call(functools.partial(attention_kernel, head_size, parts, kind...  6.07 us
    ppermute x3, waiting for transfers between devices, same_parity_blocks(): moved.append(lax.ppermute(held, axis, targets))  2.71 us
    broadcast_in_dim x1, other arithmetic, same_parity_blocks(): held = block[None]  0.74 us
    unnamed x4, local copies, waits for them, and re-layouts  0.57 us
  transfers between devices with their start and end apart: 11, of which 1 were waited for; matrix products, arithmetic and copies ran while one was open for 0% of the time, Pallas kernels for 17%

profile of v15, /device:TPU:21, one launch (start us, length us, event | category | flops | bytes accessed | tf_op | source)
XLA Modules:
  0.0 27.1 jit_solution(1276147544638511156)
XLA Ops:
  0.0 0.7 %maximum_bitcast_fusion = bf16[1,2,64,128]{3,2,1,0:T(8,128)(2,1)S(1)} fusion(bf16[1,64,128]{2,1,0:T(8,128)(2,1)} %param.6, bf16[1,64,128]{2,1,0:T(8,128)(2,1)} %param.5), kind=kLoop, calls=%fused_computation.1 | loop fusion | flops 16384 | bytes 65536 | tf_op jit(solution)/shard_map/broadcast_in_dim | solution.py:181
  0.7 0.0 copy-start
  0.7 1.4 %collective-permute-start = (bf16[1,2,64,128]{3,2,1,0:T(8,128)(2,1)S(1)}, bf16[1,2,64,128]{3,2,1,0:T(8,128)(2,1)S(1)}, u32[]{:S(2)}, u32[]{:S(2)}) collective-permute-start(bf16[1,2,64,128]{3,2,1,0:T(8,128)(2,1)S(1)} %maximum_bitcast_fusion), channel_id=1, source_target_pairs={{0,16},{4,20},{8,24},{12,28},{24,8},{28,12},{1,17},{5,21},{9,25},{... | collective-permute-start | bytes 98312 | tf_op jit(solution)/shard_map/ppermute | solution.py:188
  2.2 5.0 %collective-permute-start.1 = (bf16[1,2,64,128]{3,2,1,0:T(8,128)(2,1)S(1)}, bf16[1,2,64,128]{3,2,1,0:T(8,128)(2,1)S(1)}, u32[]{:S(2)}, u32[]{:S(2)}) collective-permute-start(bf16[1,2,64,128]{3,2,1,0:T(8,128)(2,1)S(1)} %maximum_bitcast_fusion), channel_id=1, source_target_pairs={{0,24},{4,28},{8,16},{12,20},{16,8},{20,12},{1,25},{5,29},{9,17},{... | collective-permute-start | bytes 98312 | tf_op jit(solution)/shard_map/ppermute | solution.py:188
  7.2 1.9 %collective-permute-start.2 = (bf16[1,2,64,128]{3,2,1,0:T(8,128)(2,1)S(1)}, bf16[1,2,64,128]{3,2,1,0:T(8,128)(2,1)S(1)}, u32[]{:S(2)}, u32[]{:S(2)}) collective-permute-start(bf16[1,2,64,128]{3,2,1,0:T(8,128)(2,1)S(1)} %maximum_bitcast_fusion), channel_id=1, source_target_pairs={{0,8},{4,12},{16,24},{20,28},{24,16},{28,20},{1,9},{5,13},{17,25},... | collective-permute-start | bytes 98312 | tf_op jit(solution)/shard_map/ppermute | solution.py:188
  9.1 0.0 collective-permute-done
  9.1 0.0 collective-permute-done.1
  9.1 2.7 %collective-permute-done.2 = bf16[1,2,64,128]{3,2,1,0:T(8,128)(2,1)S(1)} collective-permute-done((bf16[1,2,64,128]{3,2,1,0:T(8,128)(2,1)S(1)}, bf16[1,2,64,128]{3,2,1,0:T(8,128)(2,1)S(1)}, u32[]{:S(2)}, u32[]{:S(2)}) %collective-permute-start.2) | collective-permute-done | bytes 32800 | tf_op jit(solution)/shard_map/ppermute | solution.py:188
  11.9 1.3 %collective-permute-start.4 = (bf16[4,2,64,128]{3,2,1,0:T(8,128)(2,1)S(1)}, bf16[4,2,64,128]{3,2,1,0:T(8,128)(2,1)S(1)}, u32[]{:S(2)}, u32[]{:S(2)}) collective-permute-start(bf16[4,2,64,128]{3,2,1,0:T(8,128)(2,1)S(1)} %pad_maximum_fusion.refs_1_), channel_id=1, source_target_pairs={{0,4},{4,0},{8,12},{12,8},{16,20},{20,16},{24,28},{28,24},{1,5},{5... | collective-permute-start | bytes 393224 | tf_op jit(solution)/shard_map/ppermute | solution.py:176
  13.1 0.2 collective-permute-start.5
  13.4 1.2 %collective-permute-start.3 = (bf16[4,2,64,128]{3,2,1,0:T(8,128)(2,1)S(1)}, bf16[4,2,64,128]{3,2,1,0:T(8,128)(2,1)S(1)}, u32[]{:S(2)}, u32[]{:S(2)}) collective-permute-start(bf16[4,2,64,128]{3,2,1,0:T(8,128)(2,1)S(1)} %pad_maximum_fusion.refs_1_), channel_id=1, source_target_pairs={{0,6},{1,7},{2,4},{3,5},{4,2},{5,3},{6,0},{7,1},{8,14},{9,15},{10,... | collective-permute-start | bytes 393224 | tf_op jit(solution)/shard_map/ppermute | solution.py:176
  14.6 3.3 %collective-permute-start.6 = (bf16[4,2,32,128]{3,2,1,0:T(8,128)(2,1)S(1)}, bf16[4,2,32,128]{3,2,1,0:T(8,128)(2,1)S(1)}, u32[]{:S(2)}, u32[]{:S(2)}) collective-permute-start(bf16[4,2,32,128]{3,2,1,0:T(8,128)(2,1)S(1)} %get-tuple-element.46), channel_id=1, source_target_pairs={{0,1},{1,0},{2,3},{3,2},{4,5},{5,4},{6,7},{7,6},{8,9},{9,8},{10,11... | collective-permute-start | bytes 196616 | tf_op jit(solution)/shard_map/ppermute | solution.py:176
  17.9 0.0 copy-start.1
  17.9 0.1 collective-permute-start.7
  18.0 0.0 copy-done
  18.0 0.6 %copy-done.1 = s32[1,4]{1,0:T(1,128)S(1)} copy-done((s32[1,4]{1,0:T(1,128)S(1)}, s32[1,4]{1,0:T(1,128)}, u32[]{:S(2)}) %copy-start.1) | copy-done | bytes 40
  18.5 1.2 %shard_map.46 = (f32[8,256]{1,0:T(8,128)S(1)}, f32[4,128,256]{2,1,0:T(8,128)S(1)}, s32[1,256]{1,0:T(1,128)S(1)}, bf16[4,128,256]{2,1,0:T(8,128)(2,1)S(1)}) custom-call(bf16[256,512]{1,0:T(8,128)(2,1)S(1)} %bitcast.4, bf16[4,2,64,128]{3,2,1,0:T(8,128)(2,1)S(1)} %pad_maximum_fusion.refs_1_, s32[1,4]{1,0:T(1,128)S(1)} %copy-done.1), custom_call_target="tpu_custom_call" | custom-call | flops 1 | bytes 1 | tf_op jit(solution)/shard_map/pallas_call | solution.py:164
  19.8 0.0 collective-permute-done.6.refs_1_
  19.8 0.0 collective-permute-done.7.refs_2_
  19.8 0.7 %shard_map.47 = (f32[8,256]{1,0:T(8,128)S(1)}, f32[4,128,256]{2,1,0:T(8,128)S(1)}) custom-call(bf16[4,128,256]{2,1,0:T(8,128)(2,1)S(1)} %get-tuple-element.28.refs_0_, bf16[4,2,32,128]{3,2,1,0:T(8,128)(2,1)S(1)} %collective-permute-done.6.refs_1_, bf16[4,2,32,128]{3,2,1,0:T(8,128)(2,1)S(1)} %collective-permute-done.7.refs_2_, ...), custom_call_target="tpu_custom_call" | custom-call | flops 1 | bytes 1 | tf_op jit(solution)/shard_map/pallas_call | solution.py:164
  20.5 0.0 collective-permute-done.4.refs_1_
  20.5 0.0 collective-permute-done.5.refs_2_
  20.5 1.9 %collective-permute-start.10 = (bf16[4,2,64,128]{3,2,1,0:T(8,128)(2,1)S(1)}, bf16[4,2,64,128]{3,2,1,0:T(8,128)(2,1)S(1)}, u32[]{:S(2)}, u32[]{:S(2)}) collective-permute-start(bf16[4,2,64,128]{3,2,1,0:T(8,128)(2,1)S(1)} %collective-permute-done.5.refs_2_), channel_id=1, source_target_pairs={{0,1},{1,0},{2,3},{3,2},{4,5},{5,4},{6,7},{7,6},{8,9},{9,8},{10,11... | collective-permute-start | bytes 393224 | tf_op jit(solution)/shard_map/ppermute | solution.py:176
  22.4 0.0 collective-permute-start.9
  22.4 1.1 %shard_map.48 = (f32[8,256]{1,0:T(8,128)S(1)}, f32[4,128,256]{2,1,0:T(8,128)S(1)}) custom-call(bf16[4,128,256]{2,1,0:T(8,128)(2,1)S(1)} %get-tuple-element.28.refs_0_, bf16[4,2,64,128]{3,2,1,0:T(8,128)(2,1)S(1)} %collective-permute-done.4.refs_1_, bf16[4,2,64,128]{3,2,1,0:T(8,128)(2,1)S(1)} %collective-permute-done.5.refs_2_, ...), custom_call_target="tpu_custom_call" | custom-call | flops 1 | bytes 1 | tf_op jit(solution)/shard_map/pallas_call | solution.py:164
  23.5 0.0 collective-permute-done.3.refs_3_
  23.5 0.6 %collective-permute-start.8 = (bf16[4,2,64,128]{3,2,1,0:T(8,128)(2,1)S(1)}, bf16[4,2,64,128]{3,2,1,0:T(8,128)(2,1)S(1)}, u32[]{:S(2)}, u32[]{:S(2)}) collective-permute-start(bf16[4,2,64,128]{3,2,1,0:T(8,128)(2,1)S(1)} %collective-permute-done.3.refs_3_), channel_id=1, source_target_pairs={{0,1},{1,0},{2,3},{3,2},{4,5},{5,4},{6,7},{7,6},{8,9},{9,8},{10,11... | collective-permute-start | bytes 393224 | tf_op jit(solution)/shard_map/ppermute | solution.py:176
  24.1 0.0 collective-permute-done.10.refs_2_
  24.1 0.0 collective-permute-done.9.refs_1_
  24.1 1.6 %shard_map.49 = (f32[8,256]{1,0:T(8,128)S(1)}, f32[4,128,256]{2,1,0:T(8,128)S(1)}) custom-call(bf16[4,128,256]{2,1,0:T(8,128)(2,1)S(1)} %get-tuple-element.28.refs_0_, bf16[4,2,64,128]{3,2,1,0:T(8,128)(2,1)S(1)} %collective-permute-done.9.refs_1_, bf16[4,2,64,128]{3,2,1,0:T(8,128)(2,1)S(1)} %collective-permute-done.10.refs_2_, ...), custom_call_target="tpu_custom_call" | custom-call | flops 1 | bytes 1 | tf_op jit(solution)/shard_map/pallas_call | solution.py:164
  25.7 0.0 collective-permute-done.8.refs_1_
  25.7 1.4 %shard_map.50 = bf16[256,512]{1,0:T(8,128)(2,1)} custom-call(bf16[4,128,256]{2,1,0:T(8,128)(2,1)S(1)} %get-tuple-element.28.refs_0_, bf16[4,2,64,128]{3,2,1,0:T(8,128)(2,1)S(1)} %collective-permute-done.8.refs_1_, f32[8,256]{1,0:T(8,128)S(1)} %get-tuple-element.43.refs_2_, f32[4,128,256]{2,1,0:T(8,128)S(1)} %get-tuple-element.44.refs_3_, ...), custom_call_target="tpu_custom_call" | custom-call | flops 1 | bytes 1 | tf_op jit(solution)/shard_map/pallas_call | solution.py:164
  (2 shorter events, 0.0 us)
Async XLA Ops:
  0.7 17.2 %copy-start = (bf16[1,256,512]{2,1,0:T(8,128)(2,1)S(1)}, bf16[1,256,512]{2,1,0:T(8,128)(2,1)}, u32[]{:S(2)}) copy-start(bf16[1,256,512]{2,1,0:T(8,128)(2,1)} %param.4) | copy-start | bytes 786436
  0.7 8.4 %collective-permute-start = (bf16[1,2,64,128]{3,2,1,0:T(8,128)(2,1)S(1)}, bf16[1,2,64,128]{3,2,1,0:T(8,128)(2,1)S(1)}, u32[]{:S(2)}, u32[]{:S(2)}) collective-permute-start(bf16[1,2,64,128]{3,2,1,0:T(8,128)(2,1)S(1)} %maximum_bitcast_fusion), channel_id=1, source_target_pairs={{0,16},{4,20},{8,24},{12,28},{24,8},{28,12},{1,17},{5,21},{9,25},{... | collective-permute-start | bytes 98312 | tf_op jit(solution)/shard_map/ppermute | solution.py:188
  2.2 7.0 %collective-permute-start.1 = (bf16[1,2,64,128]{3,2,1,0:T(8,128)(2,1)S(1)}, bf16[1,2,64,128]{3,2,1,0:T(8,128)(2,1)S(1)}, u32[]{:S(2)}, u32[]{:S(2)}) collective-permute-start(bf16[1,2,64,128]{3,2,1,0:T(8,128)(2,1)S(1)} %maximum_bitcast_fusion), channel_id=1, source_target_pairs={{0,24},{4,28},{8,16},{12,20},{16,8},{20,12},{1,25},{5,29},{9,17},{... | collective-permute-start | bytes 98312 | tf_op jit(solution)/shard_map/ppermute | solution.py:188
  7.2 4.7 %collective-permute-start.2 = (bf16[1,2,64,128]{3,2,1,0:T(8,128)(2,1)S(1)}, bf16[1,2,64,128]{3,2,1,0:T(8,128)(2,1)S(1)}, u32[]{:S(2)}, u32[]{:S(2)}) collective-permute-start(bf16[1,2,64,128]{3,2,1,0:T(8,128)(2,1)S(1)} %maximum_bitcast_fusion), channel_id=1, source_target_pairs={{0,8},{4,12},{16,24},{20,28},{24,16},{28,20},{1,9},{5,13},{17,25},... | collective-permute-start | bytes 98312 | tf_op jit(solution)/shard_map/ppermute | solution.py:188
  11.9 8.6 %collective-permute-start.4 = (bf16[4,2,64,128]{3,2,1,0:T(8,128)(2,1)S(1)}, bf16[4,2,64,128]{3,2,1,0:T(8,128)(2,1)S(1)}, u32[]{:S(2)}, u32[]{:S(2)}) collective-permute-start(bf16[4,2,64,128]{3,2,1,0:T(8,128)(2,1)S(1)} %pad_maximum_fusion.refs_1_), channel_id=1, source_target_pairs={{0,4},{4,0},{8,12},{12,8},{16,20},{20,16},{24,28},{28,24},{1,5},{5... | collective-permute-start | bytes 393224 | tf_op jit(solution)/shard_map/ppermute | solution.py:176
  13.1 7.4 %collective-permute-start.5 = (bf16[4,2,64,128]{3,2,1,0:T(8,128)(2,1)S(1)}, bf16[4,2,64,128]{3,2,1,0:T(8,128)(2,1)S(1)}, u32[]{:S(2)}, u32[]{:S(2)}) collective-permute-start(bf16[4,2,64,128]{3,2,1,0:T(8,128)(2,1)S(1)} %pad_maximum_fusion.refs_1_), channel_id=1, source_target_pairs={{0,2},{1,3},{2,0},{3,1},{4,6},{5,7},{6,4},{7,5},{8,10},{9,11},{10,... | collective-permute-start | bytes 393224 | tf_op jit(solution)/shard_map/ppermute | solution.py:176
  13.4 10.1 %collective-permute-start.3 = (bf16[4,2,64,128]{3,2,1,0:T(8,128)(2,1)S(1)}, bf16[4,2,64,128]{3,2,1,0:T(8,128)(2,1)S(1)}, u32[]{:S(2)}, u32[]{:S(2)}) collective-permute-start(bf16[4,2,64,128]{3,2,1,0:T(8,128)(2,1)S(1)} %pad_maximum_fusion.refs_1_), channel_id=1, source_target_pairs={{0,6},{1,7},{2,4},{3,5},{4,2},{5,3},{6,0},{7,1},{8,14},{9,15},{10,... | collective-permute-start | bytes 393224 | tf_op jit(solution)/shard_map/ppermute | solution.py:176
  14.6 5.2 %collective-permute-start.6 = (bf16[4,2,32,128]{3,2,1,0:T(8,128)(2,1)S(1)}, bf16[4,2,32,128]{3,2,1,0:T(8,128)(2,1)S(1)}, u32[]{:S(2)}, u32[]{:S(2)}) collective-permute-start(bf16[4,2,32,128]{3,2,1,0:T(8,128)(2,1)S(1)} %get-tuple-element.46), channel_id=1, source_target_pairs={{0,1},{1,0},{2,3},{3,2},{4,5},{5,4},{6,7},{7,6},{8,9},{9,8},{10,11... | collective-permute-start | bytes 196616 | tf_op jit(solution)/shard_map/ppermute | solution.py:176
  17.9 0.7 %copy-start.1 = (s32[1,4]{1,0:T(1,128)S(1)}, s32[1,4]{1,0:T(1,128)}, u32[]{:S(2)}) copy-start(s32[1,4]{1,0:T(1,128)} %refs_2_.1) | copy-start | bytes 52
  17.9 1.9 %collective-permute-start.7 = (bf16[4,2,32,128]{3,2,1,0:T(8,128)(2,1)S(1)}, bf16[4,2,32,128]{3,2,1,0:T(8,128)(2,1)S(1)}, u32[]{:S(2)}, u32[]{:S(2)}) collective-permute-start(bf16[4,2,32,128]{3,2,1,0:T(8,128)(2,1)S(1)} %get-tuple-element.45), channel_id=1, source_target_pairs={{0,1},{1,0},{2,3},{3,2},{4,5},{5,4},{6,7},{7,6},{8,9},{9,8},{10,11... | collective-permute-start | bytes 196616 | tf_op jit(solution)/shard_map/ppermute | solution.py:176
  20.5 3.6 %collective-permute-start.10 = (bf16[4,2,64,128]{3,2,1,0:T(8,128)(2,1)S(1)}, bf16[4,2,64,128]{3,2,1,0:T(8,128)(2,1)S(1)}, u32[]{:S(2)}, u32[]{:S(2)}) collective-permute-start(bf16[4,2,64,128]{3,2,1,0:T(8,128)(2,1)S(1)} %collective-permute-done.5.refs_2_), channel_id=1, source_target_pairs={{0,1},{1,0},{2,3},{3,2},{4,5},{5,4},{6,7},{7,6},{8,9},{9,8},{10,11... | collective-permute-start | bytes 393224 | tf_op jit(solution)/shard_map/ppermute | solution.py:176
  22.4 1.7 %collective-permute-start.9 = (bf16[4,2,64,128]{3,2,1,0:T(8,128)(2,1)S(1)}, bf16[4,2,64,128]{3,2,1,0:T(8,128)(2,1)S(1)}, u32[]{:S(2)}, u32[]{:S(2)}) collective-permute-start(bf16[4,2,64,128]{3,2,1,0:T(8,128)(2,1)S(1)} %collective-permute-done.4.refs_1_), channel_id=1, source_target_pairs={{0,1},{1,0},{2,3},{3,2},{4,5},{5,4},{6,7},{7,6},{8,9},{9,8},{10,11... | collective-permute-start | bytes 393224 | tf_op jit(solution)/shard_map/ppermute | solution.py:176
  23.5 2.2 %collective-permute-start.8 = (bf16[4,2,64,128]{3,2,1,0:T(8,128)(2,1)S(1)}, bf16[4,2,64,128]{3,2,1,0:T(8,128)(2,1)S(1)}, u32[]{:S(2)}, u32[]{:S(2)}) collective-permute-start(bf16[4,2,64,128]{3,2,1,0:T(8,128)(2,1)S(1)} %collective-permute-done.3.refs_3_), channel_id=1, source_target_pairs={{0,1},{1,0},{2,3},{3,2},{4,5},{5,4},{6,7},{7,6},{8,9},{9,8},{10,11... | collective-permute-start | bytes 393224 | tf_op jit(solution)/shard_map/ppermute | solution.py:176

commit v16 on v14

--- a/solution.py
+++ b/solution.py
@@ -198,21 +198,21 @@
         half = own.shape[2] // 2
 
         across = exchange(own, "ctx", 1)
+        corner = exchange(own, ("ctx", "head"), lax.axis_size("head") + 2)
         far = exchange(own, "head", 2)
-        corner = exchange(own, ("ctx", "head"), lax.axis_size("head") + 2)
         near = [exchange(own[:, :, :half], "head", 1), exchange(own[:, :, half:], "head", 1)]
         stats, sums, starts, turned = run([(0, 0, 0)], "first", queries=queries[seq], kvs=[own], state=())
         run = functools.partial(run, queries=turned)
         stats, sums = run([(0, 1, 0), (0, 1, half)], "middle", kvs=near, state=(stats, sums, starts))
 
-        across, far, stats, sums = lax.optimization_barrier((across, far, stats, sums))
-        near = [exchange(across, "head", 1), exchange(far, "head", 1)]
-        stats, sums = run([(1, 0, 0), (0, 2, 0)], "middle", kvs=[across, far], state=(stats, sums, starts))
-        corner, stats, sums = lax.optimization_barrier((corner, stats, sums))
-        near_corner = exchange(corner, "head", 1)
-        parts = [(1, 1, 0), (0, 3, 0), (1, 2, 0)]
-        stats, sums = run(parts, "middle", kvs=[*near, corner], state=(stats, sums, starts))
-        results.append(run([(1, 3, 0)], "last", kvs=[near_corner], state=(stats, sums, starts)))
+        across, corner, stats, sums = lax.optimization_barrier((across, corner, stats, sums))
+        near = [exchange(across, "head", 1), exchange(corner, "head", 1)]
+        stats, sums = run([(1, 0, 0), (1, 2, 0)], "middle", kvs=[across, corner], state=(stats, sums, starts))
+        far, stats, sums = lax.optimization_barrier((far, stats, sums))
+        near_far = exchange(far, "head", 1)
+        parts = [(1, 1, 0), (1, 3, 0), (0, 2, 0)]
+        stats, sums = run(parts, "middle", kvs=[*near, far], state=(stats, sums, starts))
+        results.append(run([(0, 3, 0)], "last", kvs=[near_far], state=(stats, sums, starts)))
     return jnp.stack(results)
 
 

time: 22.5 us -> 22.4 us (level)
  the two profiles are of different devices: /device:TPU:25 before, /device:TPU:0 now
where the time goes in v16:
time: 22.4 us; the launch traced here: 22.1 us
  starting transfers between devices  10.2 us (46%)
  waiting for transfers between devices  6.92 us (31%)
  Pallas kernels  3.92 us (18%)
  other arithmetic  0.76 us (3%)
    ppermute x11, starting transfers between devices, exchange(): lax.ppermute(piece, axis, [(i, i ^ bits) for i in range(lax.axis_size(axi...  10.2 us
    ppermute x11, waiting for transfers between devices, exchange(): lax.ppermute(piece, axis, [(i, i ^ bits) for i in range(lax.axis_size(axi...  6.92 us
    pallas_call x5, Pallas kernels, attend(): pl.pallas_call(functools.partial(attention_kernel, head_size, parts, kind...  3.92 us
    broadcast_in_dim x1, other arithmetic, same_parity_blocks(): held = block[None]  0.74 us
  transfers between devices with their start and end apart: 11, of which 6 were waited for; matrix products, arithmetic and copies ran while one was open for 0% of the time, Pallas kernels for 12%

profile of v16, /device:TPU:0, one launch (start us, length us, event | category | flops | bytes accessed | tf_op | source)
XLA Modules:
  0.0 22.1 jit_solution(17890319662690665194)
XLA Ops:
  0.0 0.7 %maximum_bitcast_fusion = bf16[1,2,64,128]{3,2,1,0:T(8,128)(2,1)S(1)} fusion(bf16[1,64,128]{2,1,0:T(8,128)(2,1)} %param.6, bf16[1,64,128]{2,1,0:T(8,128)(2,1)} %param.5), kind=kLoop, calls=%fused_computation.1 | loop fusion | flops 16384 | bytes 65536 | tf_op jit(solution)/shard_map/broadcast_in_dim | solution.py:181
  0.7 0.0 copy-start
  0.7 4.0 %collective-permute-start = (bf16[1,2,64,128]{3,2,1,0:T(8,128)(2,1)S(1)}, bf16[1,2,64,128]{3,2,1,0:T(8,128)(2,1)S(1)}, u32[]{:S(2)}, u32[]{:S(2)}) collective-permute-start(bf16[1,2,64,128]{3,2,1,0:T(8,128)(2,1)S(1)} %maximum_bitcast_fusion), channel_id=1, source_target_pairs={{0,16},{4,20},{8,24},{12,28},{16,0},{20,4},{24,8},{28,12},{1,17},{... | collective-permute-start | bytes 98312 | tf_op jit(solution)/shard_map/ppermute | solution.py:176
  4.8 1.3 %collective-permute-start.1 = (bf16[1,2,64,128]{3,2,1,0:T(8,128)(2,1)S(1)}, bf16[1,2,64,128]{3,2,1,0:T(8,128)(2,1)S(1)}, u32[]{:S(2)}, u32[]{:S(2)}) collective-permute-start(bf16[1,2,64,128]{3,2,1,0:T(8,128)(2,1)S(1)} %maximum_bitcast_fusion), channel_id=1, source_target_pairs={{0,24},{4,28},{8,16},{12,20},{16,8},{20,12},{24,0},{28,4},{1,25},{... | collective-permute-start | bytes 98312 | tf_op jit(solution)/shard_map/ppermute | solution.py:176
  6.1 0.2 %collective-permute-start.2 = (bf16[1,2,64,128]{3,2,1,0:T(8,128)(2,1)S(1)}, bf16[1,2,64,128]{3,2,1,0:T(8,128)(2,1)S(1)}, u32[]{:S(2)}, u32[]{:S(2)}) collective-permute-start(bf16[1,2,64,128]{3,2,1,0:T(8,128)(2,1)S(1)} %maximum_bitcast_fusion), channel_id=1, source_target_pairs={{0,8},{4,12},{8,0},{12,4},{16,24},{20,28},{24,16},{28,20},{1,9},{5... | collective-permute-start | bytes 98312 | tf_op jit(solution)/shard_map/ppermute | solution.py:176
  6.4 0.7 %collective-permute-done = bf16[1,2,64,128]{3,2,1,0:T(8,128)(2,1)S(1)} collective-permute-done((bf16[1,2,64,128]{3,2,1,0:T(8,128)(2,1)S(1)}, bf16[1,2,64,128]{3,2,1,0:T(8,128)(2,1)S(1)}, u32[]{:S(2)}, u32[]{:S(2)}) %collective-permute-start) | collective-permute-done | bytes 32800 | tf_op jit(solution)/shard_map/ppermute | solution.py:176
  7.0 3.5 %collective-permute-done.1 = bf16[1,2,64,128]{3,2,1,0:T(8,128)(2,1)S(1)} collective-permute-done((bf16[1,2,64,128]{3,2,1,0:T(8,128)(2,1)S(1)}, bf16[1,2,64,128]{3,2,1,0:T(8,128)(2,1)S(1)}, u32[]{:S(2)}, u32[]{:S(2)}) %collective-permute-start.1) | collective-permute-done | bytes 32800 | tf_op jit(solution)/shard_map/ppermute | solution.py:176
  10.5 0.0 collective-permute-done.2
  10.5 1.6 %collective-permute-start.4 = (bf16[4,2,64,128]{3,2,1,0:T(8,128)(2,1)S(1)}, bf16[4,2,64,128]{3,2,1,0:T(8,128)(2,1)S(1)}, u32[]{:S(2)}, u32[]{:S(2)}) collective-permute-start(bf16[4,2,64,128]{3,2,1,0:T(8,128)(2,1)S(1)} %pad_maximum_fusion.refs_1_), channel_id=1, source_target_pairs={{0,4},{4,0},{8,12},{12,8},{16,20},{20,16},{24,28},{28,24},{1,5},{5... | collective-permute-start | bytes 393224 | tf_op jit(solution)/shard_map/ppermute | solution.py:176
  12.1 1.5 %collective-permute-start.5 = (bf16[4,2,64,128]{3,2,1,0:T(8,128)(2,1)S(1)}, bf16[4,2,64,128]{3,2,1,0:T(8,128)(2,1)S(1)}, u32[]{:S(2)}, u32[]{:S(2)}) collective-permute-start(bf16[4,2,64,128]{3,2,1,0:T(8,128)(2,1)S(1)} %pad_maximum_fusion.refs_1_), channel_id=1, source_target_pairs={{0,6},{1,7},{2,4},{3,5},{4,2},{5,3},{6,0},{7,1},{8,14},{9,15},{10,... | collective-permute-start | bytes 393224 | tf_op jit(solution)/shard_map/ppermute | solution.py:176
  13.6 0.5 %collective-permute-start.3 = (bf16[4,2,64,128]{3,2,1,0:T(8,128)(2,1)S(1)}, bf16[4,2,64,128]{3,2,1,0:T(8,128)(2,1)S(1)}, u32[]{:S(2)}, u32[]{:S(2)}) collective-permute-start(bf16[4,2,64,128]{3,2,1,0:T(8,128)(2,1)S(1)} %pad_maximum_fusion.refs_1_), channel_id=1, source_target_pairs={{0,2},{1,3},{2,0},{3,1},{4,6},{5,7},{6,4},{7,5},{8,10},{9,11},{10,... | collective-permute-start | bytes 393224 | tf_op jit(solution)/shard_map/ppermute | solution.py:176
  14.1 0.1 collective-permute-start.6
  14.2 0.0 copy-start.1
  14.2 0.5 %collective-permute-start.7 = (bf16[4,2,32,128]{3,2,1,0:T(8,128)(2,1)S(1)}, bf16[4,2,32,128]{3,2,1,0:T(8,128)(2,1)S(1)}, u32[]{:S(2)}, u32[]{:S(2)}) collective-permute-start(bf16[4,2,32,128]{3,2,1,0:T(8,128)(2,1)S(1)} %get-tuple-element.45), channel_id=1, source_target_pairs={{0,1},{1,0},{2,3},{3,2},{4,5},{5,4},{6,7},{7,6},{8,9},{9,8},{10,11... | collective-permute-start | bytes 196616 | tf_op jit(solution)/shard_map/ppermute | solution.py:176
  14.7 0.0 copy-done
  14.7 0.2 copy-done.1
  14.8 1.2 %shard_map.46 = (f32[8,256]{1,0:T(8,128)S(1)}, f32[4,128,256]{2,1,0:T(8,128)S(1)}, s32[1,256]{1,0:T(1,128)S(1)}, bf16[4,128,256]{2,1,0:T(8,128)(2,1)S(1)}) custom-call(bf16[256,512]{1,0:T(8,128)(2,1)S(1)} %bitcast.4, bf16[4,2,64,128]{3,2,1,0:T(8,128)(2,1)S(1)} %pad_maximum_fusion.refs_1_, s32[1,4]{1,0:T(1,128)S(1)} %copy-done.1), custom_call_target="tpu_custom_call" | custom-call | flops 1 | bytes 1 | tf_op jit(solution)/shard_map/pallas_call | solution.py:164
  16.1 0.0 collective-permute-done.6.refs_1_
  16.1 0.0 collective-permute-done.7.refs_2_
  16.1 0.4 %shard_map.47 = (f32[8,256]{1,0:T(8,128)S(1)}, f32[4,128,256]{2,1,0:T(8,128)S(1)}) custom-call(bf16[4,128,256]{2,1,0:T(8,128)(2,1)S(1)} %get-tuple-element.28.refs_0_, bf16[4,2,32,128]{3,2,1,0:T(8,128)(2,1)S(1)} %collective-permute-done.6.refs_1_, bf16[4,2,32,128]{3,2,1,0:T(8,128)(2,1)S(1)} %collective-permute-done.7.refs_2_, ...), custom_call_target="tpu_custom_call" | custom-call | flops 1 | bytes 1 | tf_op jit(solution)/shard_map/pallas_call | solution.py:164
  16.5 0.0 collective-permute-done.4.refs_1_
  16.6 1.7 %collective-permute-done.5.refs_2_ = bf16[4,2,64,128]{3,2,1,0:T(8,128)(2,1)S(1)} collective-permute-done((bf16[4,2,64,128]{3,2,1,0:T(8,128)(2,1)S(1)}, bf16[4,2,64,128]{3,2,1,0:T(8,128)(2,1)S(1)}, u32[]{:S(2)}, u32[]{:S(2)}) %collective-permute-start.5) | collective-permute-done | bytes 131104 | tf_op jit(solution)/shard_map/ppermute | solution.py:176
  18.3 0.0 collective-permute-start.10
  18.3 0.5 %collective-permute-start.9 = (bf16[4,2,64,128]{3,2,1,0:T(8,128)(2,1)S(1)}, bf16[4,2,64,128]{3,2,1,0:T(8,128)(2,1)S(1)}, u32[]{:S(2)}, u32[]{:S(2)}) collective-permute-start(bf16[4,2,64,128]{3,2,1,0:T(8,128)(2,1)S(1)} %collective-permute-done.4.refs_1_), channel_id=1, source_target_pairs={{0,1},{1,0},{2,3},{3,2},{4,5},{5,4},{6,7},{7,6},{8,9},{9,8},{10,11... | collective-permute-start | bytes 393224 | tf_op jit(solution)/shard_map/ppermute | solution.py:176
  18.8 0.5 %shard_map.48 = (f32[8,256]{1,0:T(8,128)S(1)}, f32[4,128,256]{2,1,0:T(8,128)S(1)}) custom-call(bf16[4,128,256]{2,1,0:T(8,128)(2,1)S(1)} %get-tuple-element.28.refs_0_, bf16[4,2,64,128]{3,2,1,0:T(8,128)(2,1)S(1)} %collective-permute-done.4.refs_1_, bf16[4,2,64,128]{3,2,1,0:T(8,128)(2,1)S(1)} %collective-permute-done.5.refs_2_, ...), custom_call_target="tpu_custom_call" | custom-call | flops 1 | bytes 1 | tf_op jit(solution)/shard_map/pallas_call | solution.py:164
  19.3 0.3 %collective-permute-done.3.refs_3_ = bf16[4,2,64,128]{3,2,1,0:T(8,128)(2,1)S(1)} collective-permute-done((bf16[4,2,64,128]{3,2,1,0:T(8,128)(2,1)S(1)}, bf16[4,2,64,128]{3,2,1,0:T(8,128)(2,1)S(1)}, u32[]{:S(2)}, u32[]{:S(2)}) %collective-permute-start.3) | collective-permute-done | bytes 131104 | tf_op jit(solution)/shard_map/ppermute | solution.py:176
  19.6 0.0 collective-permute-start.8
  19.6 0.0 collective-permute-done.10.refs_2_
  19.6 0.2 collective-permute-done.9.refs_1_
  19.8 0.6 %shard_map.49 = (f32[8,256]{1,0:T(8,128)S(1)}, f32[4,128,256]{2,1,0:T(8,128)S(1)}) custom-call(bf16[4,128,256]{2,1,0:T(8,128)(2,1)S(1)} %get-tuple-element.28.refs_0_, bf16[4,2,64,128]{3,2,1,0:T(8,128)(2,1)S(1)} %collective-permute-done.9.refs_1_, bf16[4,2,64,128]{3,2,1,0:T(8,128)(2,1)S(1)} %collective-permute-done.10.refs_2_, ...), custom_call_target="tpu_custom_call" | custom-call | flops 1 | bytes 1 | tf_op jit(solution)/shard_map/pallas_call | solution.py:164
  20.4 0.5 %collective-permute-done.8.refs_1_ = bf16[4,2,64,128]{3,2,1,0:T(8,128)(2,1)S(1)} collective-permute-done((bf16[4,2,64,128]{3,2,1,0:T(8,128)(2,1)S(1)}, bf16[4,2,64,128]{3,2,1,0:T(8,128)(2,1)S(1)}, u32[]{:S(2)}, u32[]{:S(2)}) %collective-permute-start.8) | collective-permute-done | bytes 131104 | tf_op jit(solution)/shard_map/ppermute | solution.py:176
  20.9 1.2 %shard_map.50 = bf16[256,512]{1,0:T(8,128)(2,1)} custom-call(bf16[4,128,256]{2,1,0:T(8,128)(2,1)S(1)} %get-tuple-element.28.refs_0_, bf16[4,2,64,128]{3,2,1,0:T(8,128)(2,1)S(1)} %collective-permute-done.8.refs_1_, f32[8,256]{1,0:T(8,128)S(1)} %get-tuple-element.43.refs_2_, f32[4,128,256]{2,1,0:T(8,128)S(1)} %get-tuple-element.44.refs_3_, ...), custom_call_target="tpu_custom_call" | custom-call | flops 1 | bytes 1 | tf_op jit(solution)/shard_map/pallas_call | solution.py:164
  (2 shorter events, 0.0 us)
Async XLA Ops:
  0.7 13.9 %copy-start = (bf16[1,256,512]{2,1,0:T(8,128)(2,1)S(1)}, bf16[1,256,512]{2,1,0:T(8,128)(2,1)}, u32[]{:S(2)}) copy-start(bf16[1,256,512]{2,1,0:T(8,128)(2,1)} %param.4) | copy-start | bytes 786436
  0.7 6.3 %collective-permute-start = (bf16[1,2,64,128]{3,2,1,0:T(8,128)(2,1)S(1)}, bf16[1,2,64,128]{3,2,1,0:T(8,128)(2,1)S(1)}, u32[]{:S(2)}, u32[]{:S(2)}) collective-permute-start(bf16[1,2,64,128]{3,2,1,0:T(8,128)(2,1)S(1)} %maximum_bitcast_fusion), channel_id=1, source_target_pairs={{0,16},{4,20},{8,24},{12,28},{16,0},{20,4},{24,8},{28,12},{1,17},{... | collective-permute-start | bytes 98312 | tf_op jit(solution)/shard_map/ppermute | solution.py:176
  4.8 5.7 %collective-permute-start.1 = (bf16[1,2,64,128]{3,2,1,0:T(8,128)(2,1)S(1)}, bf16[1,2,64,128]{3,2,1,0:T(8,128)(2,1)S(1)}, u32[]{:S(2)}, u32[]{:S(2)}) collective-permute-start(bf16[1,2,64,128]{3,2,1,0:T(8,128)(2,1)S(1)} %maximum_bitcast_fusion), channel_id=1, source_target_pairs={{0,24},{4,28},{8,16},{12,20},{16,8},{20,12},{24,0},{28,4},{1,25},{... | collective-permute-start | bytes 98312 | tf_op jit(solution)/shard_map/ppermute | solution.py:176
  6.1 4.4 %collective-permute-start.2 = (bf16[1,2,64,128]{3,2,1,0:T(8,128)(2,1)S(1)}, bf16[1,2,64,128]{3,2,1,0:T(8,128)(2,1)S(1)}, u32[]{:S(2)}, u32[]{:S(2)}) collective-permute-start(bf16[1,2,64,128]{3,2,1,0:T(8,128)(2,1)S(1)} %maximum_bitcast_fusion), channel_id=1, source_target_pairs={{0,8},{4,12},{8,0},{12,4},{16,24},{20,28},{24,16},{28,20},{1,9},{5... | collective-permute-start | bytes 98312 | tf_op jit(solution)/shard_map/ppermute | solution.py:176
  10.5 6.0 %collective-permute-start.4 = (bf16[4,2,64,128]{3,2,1,0:T(8,128)(2,1)S(1)}, bf16[4,2,64,128]{3,2,1,0:T(8,128)(2,1)S(1)}, u32[]{:S(2)}, u32[]{:S(2)}) collective-permute-start(bf16[4,2,64,128]{3,2,1,0:T(8,128)(2,1)S(1)} %pad_maximum_fusion.refs_1_), channel_id=1, source_target_pairs={{0,4},{4,0},{8,12},{12,8},{16,20},{20,16},{24,28},{28,24},{1,5},{5... | collective-permute-start | bytes 393224 | tf_op jit(solution)/shard_map/ppermute | solution.py:176
  12.1 6.2 %collective-permute-start.5 = (bf16[4,2,64,128]{3,2,1,0:T(8,128)(2,1)S(1)}, bf16[4,2,64,128]{3,2,1,0:T(8,128)(2,1)S(1)}, u32[]{:S(2)}, u32[]{:S(2)}) collective-permute-start(bf16[4,2,64,128]{3,2,1,0:T(8,128)(2,1)S(1)} %pad_maximum_fusion.refs_1_), channel_id=1, source_target_pairs={{0,6},{1,7},{2,4},{3,5},{4,2},{5,3},{6,0},{7,1},{8,14},{9,15},{10,... | collective-permute-start | bytes 393224 | tf_op jit(solution)/shard_map/ppermute | solution.py:176
  13.6 6.0 %collective-permute-start.3 = (bf16[4,2,64,128]{3,2,1,0:T(8,128)(2,1)S(1)}, bf16[4,2,64,128]{3,2,1,0:T(8,128)(2,1)S(1)}, u32[]{:S(2)}, u32[]{:S(2)}) collective-permute-start(bf16[4,2,64,128]{3,2,1,0:T(8,128)(2,1)S(1)} %pad_maximum_fusion.refs_1_), channel_id=1, source_target_pairs={{0,2},{1,3},{2,0},{3,1},{4,6},{5,7},{6,4},{7,5},{8,10},{9,11},{10,... | collective-permute-start | bytes 393224 | tf_op jit(solution)/shard_map/ppermute | solution.py:176
  14.1 2.0 %collective-permute-start.6 = (bf16[4,2,32,128]{3,2,1,0:T(8,128)(2,1)S(1)}, bf16[4,2,32,128]{3,2,1,0:T(8,128)(2,1)S(1)}, u32[]{:S(2)}, u32[]{:S(2)}) collective-permute-start(bf16[4,2,32,128]{3,2,1,0:T(8,128)(2,1)S(1)} %get-tuple-element.46), channel_id=1, source_target_pairs={{0,1},{1,0},{2,3},{3,2},{4,5},{5,4},{6,7},{7,6},{8,9},{9,8},{10,11... | collective-permute-start | bytes 196616 | tf_op jit(solution)/shard_map/ppermute | solution.py:176
  14.2 0.7 %copy-start.1 = (s32[1,4]{1,0:T(1,128)S(1)}, s32[1,4]{1,0:T(1,128)}, u32[]{:S(2)}) copy-start(s32[1,4]{1,0:T(1,128)} %refs_2_.1) | copy-start | bytes 52
  14.2 1.9 %collective-permute-start.7 = (bf16[4,2,32,128]{3,2,1,0:T(8,128)(2,1)S(1)}, bf16[4,2,32,128]{3,2,1,0:T(8,128)(2,1)S(1)}, u32[]{:S(2)}, u32[]{:S(2)}) collective-permute-start(bf16[4,2,32,128]{3,2,1,0:T(8,128)(2,1)S(1)} %get-tuple-element.45), channel_id=1, source_target_pairs={{0,1},{1,0},{2,3},{3,2},{4,5},{5,4},{6,7},{7,6},{8,9},{9,8},{10,11... | collective-permute-start | bytes 196616 | tf_op jit(solution)/shard_map/ppermute | solution.py:176
  18.3 1.3 %collective-permute-start.10 = (bf16[4,2,64,128]{3,2,1,0:T(8,128)(2,1)S(1)}, bf16[4,2,64,128]{3,2,1,0:T(8,128)(2,1)S(1)}, u32[]{:S(2)}, u32[]{:S(2)}) collective-permute-start(bf16[4,2,64,128]{3,2,1,0:T(8,128)(2,1)S(1)} %collective-permute-done.5.refs_2_), channel_id=1, source_target_pairs={{0,1},{1,0},{2,3},{3,2},{4,5},{5,4},{6,7},{7,6},{8,9},{9,8},{10,11... | collective-permute-start | bytes 393224 | tf_op jit(solution)/shard_map/ppermute | solution.py:176
  18.3 1.5 %collective-permute-start.9 = (bf16[4,2,64,128]{3,2,1,0:T(8,128)(2,1)S(1)}, bf16[4,2,64,128]{3,2,1,0:T(8,128)(2,1)S(1)}, u32[]{:S(2)}, u32[]{:S(2)}) collective-permute-start(bf16[4,2,64,128]{3,2,1,0:T(8,128)(2,1)S(1)} %collective-permute-done.4.refs_1_), channel_id=1, source_target_pairs={{0,1},{1,0},{2,3},{3,2},{4,5},{5,4},{6,7},{7,6},{8,9},{9,8},{10,11... | collective-permute-start | bytes 393224 | tf_op jit(solution)/shard_map/ppermute | solution.py:176
  19.6 1.3 %collective-permute-start.8 = (bf16[4,2,64,128]{3,2,1,0:T(8,128)(2,1)S(1)}, bf16[4,2,64,128]{3,2,1,0:T(8,128)(2,1)S(1)}, u32[]{:S(2)}, u32[]{:S(2)}) collective-permute-start(bf16[4,2,64,128]{3,2,1,0:T(8,128)(2,1)S(1)} %collective-permute-done.3.refs_3_), channel_id=1, source_target_pairs={{0,1},{1,0},{2,3},{3,2},{4,5},{5,4},{6,7},{7,6},{8,9},{9,8},{10,11... | collective-permute-start | bytes 393224 | tf_op jit(solution)/shard_map/ppermute | solution.py:176

commit v17 on v14

--- a/solution.py
+++ b/solution.py
@@ -205,9 +205,11 @@
         run = functools.partial(run, queries=turned)
         stats, sums = run([(0, 1, 0), (0, 1, half)], "middle", kvs=near, state=(stats, sums, starts))
 
+        across, stats, sums = lax.optimization_barrier((across, stats, sums))
+        stats, sums = run([(1, 0, 0)], "middle", kvs=[across], state=(stats, sums, starts))
         across, far, stats, sums = lax.optimization_barrier((across, far, stats, sums))
         near = [exchange(across, "head", 1), exchange(far, "head", 1)]
-        stats, sums = run([(1, 0, 0), (0, 2, 0)], "middle", kvs=[across, far], state=(stats, sums, starts))
+        stats, sums = run([(0, 2, 0)], "middle", kvs=[far], state=(stats, sums, starts))
         corner, stats, sums = lax.optimization_barrier((corner, stats, sums))
         near_corner = exchange(corner, "head", 1)
         parts = [(1, 1, 0), (0, 3, 0), (1, 2, 0)]

time: 22.5 us -> 22.3 us (level)
  the two profiles are of different devices: /device:TPU:25 before, /device:TPU:0 now
where the time goes in v17:
time: 22.3 us; the launch traced here: 22 us
  starting transfers between devices  10.2 us (46%)
  waiting for transfers between devices  6.45 us (29%)
  Pallas kernels  4.28 us (19%)
  other arithmetic  0.76 us (3%)
    ppermute x11, starting transfers between devices, exchange(): lax.ppermute(piece, axis, [(i, i ^ bits) for i in range(lax.axis_size(axi...  10.2 us
    ppermute x11, waiting for transfers between devices, exchange(): lax.ppermute(piece, axis, [(i, i ^ bits) for i in range(lax.axis_size(axi...  6.45 us
    pallas_call x6, Pallas kernels, attend(): pl.pallas_call(functools.partial(attention_kernel, head_size, parts, kind...  4.28 us
    broadcast_in_dim x1, other arithmetic, same_parity_blocks(): held = block[None]  0.74 us
  transfers between devices with their start and end apart: 11, of which 7 were waited for; matrix products, arithmetic and copies ran while one was open for 0% of the time, Pallas kernels for 14%

profile of v17, /device:TPU:0, one launch (start us, length us, event | category | flops | bytes accessed | tf_op | source)
XLA Modules:
  0.0 22.0 jit_solution(11259525813318074898)
XLA Ops:
  0.0 0.7 %maximum_bitcast_fusion = bf16[1,2,64,128]{3,2,1,0:T(8,128)(2,1)S(1)} fusion(bf16[1,64,128]{2,1,0:T(8,128)(2,1)} %param.6, bf16[1,64,128]{2,1,0:T(8,128)(2,1)} %param.5), kind=kLoop, calls=%fused_computation.1 | loop fusion | flops 16384 | bytes 65536 | tf_op jit(solution)/shard_map/broadcast_in_dim | solution.py:181
  0.7 0.0 copy-start
  0.7 4.0 %collective-permute-start = (bf16[1,2,64,128]{3,2,1,0:T(8,128)(2,1)S(1)}, bf16[1,2,64,128]{3,2,1,0:T(8,128)(2,1)S(1)}, u32[]{:S(2)}, u32[]{:S(2)}) collective-permute-start(bf16[1,2,64,128]{3,2,1,0:T(8,128)(2,1)S(1)} %maximum_bitcast_fusion), channel_id=1, source_target_pairs={{0,16},{4,20},{8,24},{12,28},{16,0},{20,4},{24,8},{28,12},{1,17},{... | collective-permute-start | bytes 98312 | tf_op jit(solution)/shard_map/ppermute | solution.py:176
  4.8 1.3 %collective-permute-start.1 = (bf16[1,2,64,128]{3,2,1,0:T(8,128)(2,1)S(1)}, bf16[1,2,64,128]{3,2,1,0:T(8,128)(2,1)S(1)}, u32[]{:S(2)}, u32[]{:S(2)}) collective-permute-start(bf16[1,2,64,128]{3,2,1,0:T(8,128)(2,1)S(1)} %maximum_bitcast_fusion), channel_id=1, source_target_pairs={{0,24},{4,28},{8,16},{12,20},{16,8},{20,12},{24,0},{28,4},{1,25},{... | collective-permute-start | bytes 98312 | tf_op jit(solution)/shard_map/ppermute | solution.py:176
  6.1 0.2 %collective-permute-start.2 = (bf16[1,2,64,128]{3,2,1,0:T(8,128)(2,1)S(1)}, bf16[1,2,64,128]{3,2,1,0:T(8,128)(2,1)S(1)}, u32[]{:S(2)}, u32[]{:S(2)}) collective-permute-start(bf16[1,2,64,128]{3,2,1,0:T(8,128)(2,1)S(1)} %maximum_bitcast_fusion), channel_id=1, source_target_pairs={{0,8},{4,12},{8,0},{12,4},{16,24},{20,28},{24,16},{28,20},{1,9},{5... | collective-permute-start | bytes 98312 | tf_op jit(solution)/shard_map/ppermute | solution.py:176
  6.4 0.7 %collective-permute-done = bf16[1,2,64,128]{3,2,1,0:T(8,128)(2,1)S(1)} collective-permute-done((bf16[1,2,64,128]{3,2,1,0:T(8,128)(2,1)S(1)}, bf16[1,2,64,128]{3,2,1,0:T(8,128)(2,1)S(1)}, u32[]{:S(2)}, u32[]{:S(2)}) %collective-permute-start) | collective-permute-done | bytes 32800 | tf_op jit(solution)/shard_map/ppermute | solution.py:176
  7.0 3.5 %collective-permute-done.1 = bf16[1,2,64,128]{3,2,1,0:T(8,128)(2,1)S(1)} collective-permute-done((bf16[1,2,64,128]{3,2,1,0:T(8,128)(2,1)S(1)}, bf16[1,2,64,128]{3,2,1,0:T(8,128)(2,1)S(1)}, u32[]{:S(2)}, u32[]{:S(2)}) %collective-permute-start.1) | collective-permute-done | bytes 32800 | tf_op jit(solution)/shard_map/ppermute | solution.py:176
  10.5 0.0 collective-permute-done.2
  10.5 1.6 %collective-permute-start.4 = (bf16[4,2,64,128]{3,2,1,0:T(8,128)(2,1)S(1)}, bf16[4,2,64,128]{3,2,1,0:T(8,128)(2,1)S(1)}, u32[]{:S(2)}, u32[]{:S(2)}) collective-permute-start(bf16[4,2,64,128]{3,2,1,0:T(8,128)(2,1)S(1)} %pad_maximum_fusion.refs_1_), channel_id=1, source_target_pairs={{0,4},{4,0},{8,12},{12,8},{16,20},{20,16},{24,28},{28,24},{1,5},{5... | collective-permute-start | bytes 393224 | tf_op jit(solution)/shard_map/ppermute | solution.py:176
  12.1 1.5 %collective-permute-start.7 = (bf16[4,2,64,128]{3,2,1,0:T(8,128)(2,1)S(1)}, bf16[4,2,64,128]{3,2,1,0:T(8,128)(2,1)S(1)}, u32[]{:S(2)}, u32[]{:S(2)}) collective-permute-start(bf16[4,2,64,128]{3,2,1,0:T(8,128)(2,1)S(1)} %pad_maximum_fusion.refs_1_), channel_id=1, source_target_pairs={{0,2},{1,3},{2,0},{3,1},{4,6},{5,7},{6,4},{7,5},{8,10},{9,11},{10,... | collective-permute-start | bytes 393224 | tf_op jit(solution)/shard_map/ppermute | solution.py:176
  13.6 0.5 %collective-permute-start.3 = (bf16[4,2,64,128]{3,2,1,0:T(8,128)(2,1)S(1)}, bf16[4,2,64,128]{3,2,1,0:T(8,128)(2,1)S(1)}, u32[]{:S(2)}, u32[]{:S(2)}) collective-permute-start(bf16[4,2,64,128]{3,2,1,0:T(8,128)(2,1)S(1)} %pad_maximum_fusion.refs_1_), channel_id=1, source_target_pairs={{0,6},{1,7},{2,4},{3,5},{4,2},{5,3},{6,0},{7,1},{8,14},{9,15},{10,... | collective-permute-start | bytes 393224 | tf_op jit(solution)/shard_map/ppermute | solution.py:176
  14.1 0.1 collective-permute-start.5
  14.2 0.0 copy-start.1
  14.2 0.5 %collective-permute-start.6 = (bf16[4,2,32,128]{3,2,1,0:T(8,128)(2,1)S(1)}, bf16[4,2,32,128]{3,2,1,0:T(8,128)(2,1)S(1)}, u32[]{:S(2)}, u32[]{:S(2)}) collective-permute-start(bf16[4,2,32,128]{3,2,1,0:T(8,128)(2,1)S(1)} %get-tuple-element.55), channel_id=1, source_target_pairs={{0,1},{1,0},{2,3},{3,2},{4,5},{5,4},{6,7},{7,6},{8,9},{9,8},{10,11... | collective-permute-start | bytes 196616 | tf_op jit(solution)/shard_map/ppermute | solution.py:176
  14.7 0.0 copy-done
  14.7 0.2 copy-done.1
  14.8 1.2 %shard_map.46 = (f32[8,256]{1,0:T(8,128)S(1)}, f32[4,128,256]{2,1,0:T(8,128)S(1)}, s32[1,256]{1,0:T(1,128)S(1)}, bf16[4,128,256]{2,1,0:T(8,128)(2,1)S(1)}) custom-call(bf16[256,512]{1,0:T(8,128)(2,1)S(1)} %bitcast.4, bf16[4,2,64,128]{3,2,1,0:T(8,128)(2,1)S(1)} %pad_maximum_fusion.refs_1_, s32[1,4]{1,0:T(1,128)S(1)} %copy-done.1), custom_call_target="tpu_custom_call" | custom-call | flops 1 | bytes 1 | tf_op jit(solution)/shard_map/pallas_call | solution.py:164
  16.1 0.0 collective-permute-done.5.refs_1_
  16.1 0.0 collective-permute-done.6.refs_2_
  16.1 0.4 %shard_map.47 = (f32[8,256]{1,0:T(8,128)S(1)}, f32[4,128,256]{2,1,0:T(8,128)S(1)}) custom-call(bf16[4,128,256]{2,1,0:T(8,128)(2,1)S(1)} %get-tuple-element.33.refs_0_, bf16[4,2,32,128]{3,2,1,0:T(8,128)(2,1)S(1)} %collective-permute-done.5.refs_1_, bf16[4,2,32,128]{3,2,1,0:T(8,128)(2,1)S(1)} %collective-permute-done.6.refs_2_, ...), custom_call_target="tpu_custom_call" | custom-call | flops 1 | bytes 1 | tf_op jit(solution)/shard_map/pallas_call | solution.py:164
  16.5 0.3 %collective-permute-done.4.refs_1_ = bf16[4,2,64,128]{3,2,1,0:T(8,128)(2,1)S(1)} collective-permute-done((bf16[4,2,64,128]{3,2,1,0:T(8,128)(2,1)S(1)}, bf16[4,2,64,128]{3,2,1,0:T(8,128)(2,1)S(1)}, u32[]{:S(2)}, u32[]{:S(2)}) %collective-permute-start.4) | collective-permute-done | bytes 131104 | tf_op jit(solution)/shard_map/ppermute | solution.py:176
  16.8 0.4 %shard_map.48 = (f32[8,256]{1,0:T(8,128)S(1)}, f32[4,128,256]{2,1,0:T(8,128)S(1)}) custom-call(bf16[4,128,256]{2,1,0:T(8,128)(2,1)S(1)} %get-tuple-element.33.refs_0_, bf16[4,2,64,128]{3,2,1,0:T(8,128)(2,1)S(1)} %collective-permute-done.4.refs_1_, f32[8,256]{1,0:T(8,128)S(1)} %get-tuple-element.40.refs_2_, f32[4,128,256]{2,1,0:T(8,128)S(1)} %get-tuple-element.41.refs_3_, ...), custom_call_target="tpu_custom_call" | custom-call | flops 1 | bytes 1 | tf_op jit(solution)/shard_map/pallas_call | solution.py:164
  17.2 0.8 %collective-permute-done.7.refs_1_ = bf16[4,2,64,128]{3,2,1,0:T(8,128)(2,1)S(1)} collective-permute-done((bf16[4,2,64,128]{3,2,1,0:T(8,128)(2,1)S(1)}, bf16[4,2,64,128]{3,2,1,0:T(8,128)(2,1)S(1)}, u32[]{:S(2)}, u32[]{:S(2)}) %collective-permute-start.7) | collective-permute-done | bytes 131104 | tf_op jit(solution)/shard_map/ppermute | solution.py:176
  18.0 0.0 collective-permute-start.10
  18.0 0.5 %collective-permute-start.9 = (bf16[4,2,64,128]{3,2,1,0:T(8,128)(2,1)S(1)}, bf16[4,2,64,128]{3,2,1,0:T(8,128)(2,1)S(1)}, u32[]{:S(2)}, u32[]{:S(2)}) collective-permute-start(bf16[4,2,64,128]{3,2,1,0:T(8,128)(2,1)S(1)} %collective-permute-done.4.refs_1_), channel_id=1, source_target_pairs={{0,1},{1,0},{2,3},{3,2},{4,5},{5,4},{6,7},{7,6},{8,9},{9,8},{10,11... | collective-permute-start | bytes 393224 | tf_op jit(solution)/shard_map/ppermute | solution.py:176
  18.5 0.4 %shard_map.49 = (f32[8,256]{1,0:T(8,128)S(1)}, f32[4,128,256]{2,1,0:T(8,128)S(1)}) custom-call(bf16[4,128,256]{2,1,0:T(8,128)(2,1)S(1)} %get-tuple-element.33.refs_0_, bf16[4,2,64,128]{3,2,1,0:T(8,128)(2,1)S(1)} %collective-permute-done.7.refs_1_, f32[8,256]{1,0:T(8,128)S(1)} %get-tuple-element.45.refs_2_, f32[4,128,256]{2,1,0:T(8,128)S(1)} %get-tuple-element.46.refs_3_, ...), custom_call_target="tpu_custom_call" | custom-call | flops 1 | bytes 1 | tf_op jit(solution)/shard_map/pallas_call | solution.py:164
  19.0 0.5 %collective-permute-done.3.refs_3_ = bf16[4,2,64,128]{3,2,1,0:T(8,128)(2,1)S(1)} collective-permute-done((bf16[4,2,64,128]{3,2,1,0:T(8,128)(2,1)S(1)}, bf16[4,2,64,128]{3,2,1,0:T(8,128)(2,1)S(1)}, u32[]{:S(2)}, u32[]{:S(2)}) %collective-permute-start.3) | collective-permute-done | bytes 131104 | tf_op jit(solution)/shard_map/ppermute | solution.py:176
  19.5 0.0 collective-permute-start.8
  19.5 0.0 collective-permute-done.10.refs_2_
  19.5 0.1 collective-permute-done.9.refs_1_
  19.5 0.6 %shard_map.50 = (f32[8,256]{1,0:T(8,128)S(1)}, f32[4,128,256]{2,1,0:T(8,128)S(1)}) custom-call(bf16[4,128,256]{2,1,0:T(8,128)(2,1)S(1)} %get-tuple-element.33.refs_0_, bf16[4,2,64,128]{3,2,1,0:T(8,128)(2,1)S(1)} %collective-permute-done.9.refs_1_, bf16[4,2,64,128]{3,2,1,0:T(8,128)(2,1)S(1)} %collective-permute-done.10.refs_2_, ...), custom_call_target="tpu_custom_call" | custom-call | flops 1 | bytes 1 | tf_op jit(solution)/shard_map/pallas_call | solution.py:164
  20.1 0.7 %collective-permute-done.8.refs_1_ = bf16[4,2,64,128]{3,2,1,0:T(8,128)(2,1)S(1)} collective-permute-done((bf16[4,2,64,128]{3,2,1,0:T(8,128)(2,1)S(1)}, bf16[4,2,64,128]{3,2,1,0:T(8,128)(2,1)S(1)}, u32[]{:S(2)}, u32[]{:S(2)}) %collective-permute-start.8) | collective-permute-done | bytes 131104 | tf_op jit(solution)/shard_map/ppermute | solution.py:176
  20.8 1.2 %shard_map.51 = bf16[256,512]{1,0:T(8,128)(2,1)} custom-call(bf16[4,128,256]{2,1,0:T(8,128)(2,1)S(1)} %get-tuple-element.33.refs_0_, bf16[4,2,64,128]{3,2,1,0:T(8,128)(2,1)S(1)} %collective-permute-done.8.refs_1_, f32[8,256]{1,0:T(8,128)S(1)} %get-tuple-element.53.refs_2_, f32[4,128,256]{2,1,0:T(8,128)S(1)} %get-tuple-element.54.refs_3_, ...), custom_call_target="tpu_custom_call" | custom-call | flops 1 | bytes 1 | tf_op jit(solution)/shard_map/pallas_call | solution.py:164
  (2 shorter events, 0.0 us)
Async XLA Ops:
  0.7 13.9 %copy-start = (bf16[1,256,512]{2,1,0:T(8,128)(2,1)S(1)}, bf16[1,256,512]{2,1,0:T(8,128)(2,1)}, u32[]{:S(2)}) copy-start(bf16[1,256,512]{2,1,0:T(8,128)(2,1)} %param.4) | copy-start | bytes 786436
  0.7 6.3 %collective-permute-start = (bf16[1,2,64,128]{3,2,1,0:T(8,128)(2,1)S(1)}, bf16[1,2,64,128]{3,2,1,0:T(8,128)(2,1)S(1)}, u32[]{:S(2)}, u32[]{:S(2)}) collective-permute-start(bf16[1,2,64,128]{3,2,1,0:T(8,128)(2,1)S(1)} %maximum_bitcast_fusion), channel_id=1, source_target_pairs={{0,16},{4,20},{8,24},{12,28},{16,0},{20,4},{24,8},{28,12},{1,17},{... | collective-permute-start | bytes 98312 | tf_op jit(solution)/shard_map/ppermute | solution.py:176
  4.8 5.7 %collective-permute-start.1 = (bf16[1,2,64,128]{3,2,1,0:T(8,128)(2,1)S(1)}, bf16[1,2,64,128]{3,2,1,0:T(8,128)(2,1)S(1)}, u32[]{:S(2)}, u32[]{:S(2)}) collective-permute-start(bf16[1,2,64,128]{3,2,1,0:T(8,128)(2,1)S(1)} %maximum_bitcast_fusion), channel_id=1, source_target_pairs={{0,24},{4,28},{8,16},{12,20},{16,8},{20,12},{24,0},{28,4},{1,25},{... | collective-permute-start | bytes 98312 | tf_op jit(solution)/shard_map/ppermute | solution.py:176
  6.1 4.4 %collective-permute-start.2 = (bf16[1,2,64,128]{3,2,1,0:T(8,128)(2,1)S(1)}, bf16[1,2,64,128]{3,2,1,0:T(8,128)(2,1)S(1)}, u32[]{:S(2)}, u32[]{:S(2)}) collective-permute-start(bf16[1,2,64,128]{3,2,1,0:T(8,128)(2,1)S(1)} %maximum_bitcast_fusion), channel_id=1, source_target_pairs={{0,8},{4,12},{8,0},{12,4},{16,24},{20,28},{24,16},{28,20},{1,9},{5... | collective-permute-start | bytes 98312 | tf_op jit(solution)/shard_map/ppermute | solution.py:176
  10.5 6.3 %collective-permute-start.4 = (bf16[4,2,64,128]{3,2,1,0:T(8,128)(2,1)S(1)}, bf16[4,2,64,128]{3,2,1,0:T(8,128)(2,1)S(1)}, u32[]{:S(2)}, u32[]{:S(2)}) collective-permute-start(bf16[4,2,64,128]{3,2,1,0:T(8,128)(2,1)S(1)} %pad_maximum_fusion.refs_1_), channel_id=1, source_target_pairs={{0,4},{4,0},{8,12},{12,8},{16,20},{20,16},{24,28},{28,24},{1,5},{5... | collective-permute-start | bytes 393224 | tf_op jit(solution)/shard_map/ppermute | solution.py:176
  12.1 5.9 %collective-permute-start.7 = (bf16[4,2,64,128]{3,2,1,0:T(8,128)(2,1)S(1)}, bf16[4,2,64,128]{3,2,1,0:T(8,128)(2,1)S(1)}, u32[]{:S(2)}, u32[]{:S(2)}) collective-permute-start(bf16[4,2,64,128]{3,2,1,0:T(8,128)(2,1)S(1)} %pad_maximum_fusion.refs_1_), channel_id=1, source_target_pairs={{0,2},{1,3},{2,0},{3,1},{4,6},{5,7},{6,4},{7,5},{8,10},{9,11},{10,... | collective-permute-start | bytes 393224 | tf_op jit(solution)/shard_map/ppermute | solution.py:176
  13.6 5.9 %collective-permute-start.3 = (bf16[4,2,64,128]{3,2,1,0:T(8,128)(2,1)S(1)}, bf16[4,2,64,128]{3,2,1,0:T(8,128)(2,1)S(1)}, u32[]{:S(2)}, u32[]{:S(2)}) collective-permute-start(bf16[4,2,64,128]{3,2,1,0:T(8,128)(2,1)S(1)} %pad_maximum_fusion.refs_1_), channel_id=1, source_target_pairs={{0,6},{1,7},{2,4},{3,5},{4,2},{5,3},{6,0},{7,1},{8,14},{9,15},{10,... | collective-permute-start | bytes 393224 | tf_op jit(solution)/shard_map/ppermute | solution.py:176
  14.1 2.0 %collective-permute-start.5 = (bf16[4,2,32,128]{3,2,1,0:T(8,128)(2,1)S(1)}, bf16[4,2,32,128]{3,2,1,0:T(8,128)(2,1)S(1)}, u32[]{:S(2)}, u32[]{:S(2)}) collective-permute-start(bf16[4,2,32,128]{3,2,1,0:T(8,128)(2,1)S(1)} %get-tuple-element.56), channel_id=1, source_target_pairs={{0,1},{1,0},{2,3},{3,2},{4,5},{5,4},{6,7},{7,6},{8,9},{9,8},{10,11... | collective-permute-start | bytes 196616 | tf_op jit(solution)/shard_map/ppermute | solution.py:176
  14.2 0.7 %copy-start.1 = (s32[1,4]{1,0:T(1,128)S(1)}, s32[1,4]{1,0:T(1,128)}, u32[]{:S(2)}) copy-start(s32[1,4]{1,0:T(1,128)} %refs_2_.1) | copy-start | bytes 52
  14.2 1.9 %collective-permute-start.6 = (bf16[4,2,32,128]{3,2,1,0:T(8,128)(2,1)S(1)}, bf16[4,2,32,128]{3,2,1,0:T(8,128)(2,1)S(1)}, u32[]{:S(2)}, u32[]{:S(2)}) collective-permute-start(bf16[4,2,32,128]{3,2,1,0:T(8,128)(2,1)S(1)} %get-tuple-element.55), channel_id=1, source_target_pairs={{0,1},{1,0},{2,3},{3,2},{4,5},{5,4},{6,7},{7,6},{8,9},{9,8},{10,11... | collective-permute-start | bytes 196616 | tf_op jit(solution)/shard_map/ppermute | solution.py:176
  18.0 1.5 %collective-permute-start.10 = (bf16[4,2,64,128]{3,2,1,0:T(8,128)(2,1)S(1)}, bf16[4,2,64,128]{3,2,1,0:T(8,128)(2,1)S(1)}, u32[]{:S(2)}, u32[]{:S(2)}) collective-permute-start(bf16[4,2,64,128]{3,2,1,0:T(8,128)(2,1)S(1)} %collective-permute-done.7.refs_1_), channel_id=1, source_target_pairs={{0,1},{1,0},{2,3},{3,2},{4,5},{5,4},{6,7},{7,6},{8,9},{9,8},{10,11... | collective-permute-start | bytes 393224 | tf_op jit(solution)/shard_map/ppermute | solution.py:176
  18.0 1.5 %collective-permute-start.9 = (bf16[4,2,64,128]{3,2,1,0:T(8,128)(2,1)S(1)}, bf16[4,2,64,128]{3,2,1,0:T(8,128)(2,1)S(1)}, u32[]{:S(2)}, u32[]{:S(2)}) collective-permute-start(bf16[4,2,64,128]{3,2,1,0:T(8,128)(2,1)S(1)} %collective-permute-done.4.refs_1_), channel_id=1, source_target_pairs={{0,1},{1,0},{2,3},{3,2},{4,5},{5,4},{6,7},{7,6},{8,9},{9,8},{10,11... | collective-permute-start | bytes 393224 | tf_op jit(solution)/shard_map/ppermute | solution.py:176
  19.5 1.3 %collective-permute-start.8 = (bf16[4,2,64,128]{3,2,1,0:T(8,128)(2,1)S(1)}, bf16[4,2,64,128]{3,2,1,0:T(8,128)(2,1)S(1)}, u32[]{:S(2)}, u32[]{:S(2)}) collective-permute-start(bf16[4,2,64,128]{3,2,1,0:T(8,128)(2,1)S(1)} %collective-permute-done.3.refs_3_), channel_id=1, source_target_pairs={{0,1},{1,0},{2,3},{3,2},{4,5},{5,4},{6,7},{7,6},{8,9},{9,8},{10,11... | collective-permute-start | bytes 393224 | tf_op jit(solution)/shard_map/ppermute | solution.py:176

commit v18 on v17

--- a/solution.py
+++ b/solution.py
@@ -181,7 +181,16 @@
     held = block[None]
     while (count := held.shape[0]) < pairs:
         digits = sorted(range(1, min(DIGIT, pairs // count)), key=lambda digit: ORDER.index(digit))
-        moved = lax.optimization_barrier([exchange(held, axis, 2 * digit * count) for digit in digits])
+        moved = []
+        for digit in digits:
+            to = [source ^ digit for source in range(DIGIT)]
+            if digit == 3 and count * DIGIT == pairs:
+                to = [3, 2, 0, 1]
+            sources = range(lax.axis_size(axis))
+            place = [i // (2 * count) % DIGIT for i in sources]
+            targets = [(i, i ^ (2 * count * (place[i] ^ to[place[i]]))) for i in sources]
+            moved.append(lax.ppermute(held, axis, targets))
+        moved = lax.optimization_barrier(moved)
         moved = dict(zip(digits, moved))
         held = jnp.concatenate([held] + [moved[digit] for digit in sorted(digits)])
     return held

time: 22.3 us -> 22.2 us (level)
  the two profiles are of different devices: /device:TPU:0 before, /device:TPU:25 now
where the time goes in v18:
time: 22.2 us; the launch traced here: 21.9 us
  starting transfers between devices  10.7 us (48%)
  Pallas kernels  6.33 us (29%)
  waiting for transfers between devices  3.39 us (15%)
  other arithmetic  0.76 us (3%)
  local copies, waits for them, and re-layouts  0.58 us (3%)
    ppermute x8, starting transfers between devices, exchange(): lax.ppermute(piece, axis, [(i, i ^ bits) for i in range(lax.axis_size(axi...  8.19 us
    pallas_call x6, Pallas kernels, attend(): pl.pallas_call(functools.partial(attention_kernel, head_size, parts, kind...  6.33 us
    ppermute x3, waiting for transfers between devices, same_parity_blocks(): moved.append(lax.ppermute(held, axis, targets))  3.29 us
    ppermute x3, starting transfers between devices, same_parity_blocks(): moved.append(lax.ppermute(held, axis, targets))  2.53 us
    broadcast_in_dim x1, other arithmetic, same_parity_blocks(): held = block[None]  0.74 us
    unnamed x4, local copies, waits for them, and re-layouts  0.57 us
  transfers between devices with their start and end apart: 11, of which 4 were waited for; matrix products, arithmetic and copies ran while one was open for 0% of the time, Pallas kernels for 22%

profile of v18, /device:TPU:25, one launch (start us, length us, event | category | flops | bytes accessed | tf_op | source)
XLA Modules:
  0.0 21.9 jit_solution(11673988712726268390)
XLA Ops:
  0.0 0.7 %maximum_bitcast_fusion = bf16[1,2,64,128]{3,2,1,0:T(8,128)(2,1)S(1)} fusion(bf16[1,64,128]{2,1,0:T(8,128)(2,1)} %param.6, bf16[1,64,128]{2,1,0:T(8,128)(2,1)} %param.5), kind=kLoop, calls=%fused_computation.1 | loop fusion | flops 16384 | bytes 65536 | tf_op jit(solution)/shard_map/broadcast_in_dim | solution.py:181
  0.7 0.0 copy-start
  0.7 0.1 collective-permute-start
  0.8 2.3 %collective-permute-start.1 = (bf16[1,2,64,128]{3,2,1,0:T(8,128)(2,1)S(1)}, bf16[1,2,64,128]{3,2,1,0:T(8,128)(2,1)S(1)}, u32[]{:S(2)}, u32[]{:S(2)}) collective-permute-start(bf16[1,2,64,128]{3,2,1,0:T(8,128)(2,1)S(1)} %maximum_bitcast_fusion), channel_id=1, source_target_pairs={{0,24},{4,28},{8,16},{12,20},{16,0},{20,4},{24,8},{28,12},{1,25},{... | collective-permute-start | bytes 98312 | tf_op jit(solution)/shard_map/ppermute | solution.py:192
  3.1 0.2 collective-permute-start.2
  3.3 1.4 %collective-permute-done = bf16[1,2,64,128]{3,2,1,0:T(8,128)(2,1)S(1)} collective-permute-done((bf16[1,2,64,128]{3,2,1,0:T(8,128)(2,1)S(1)}, bf16[1,2,64,128]{3,2,1,0:T(8,128)(2,1)S(1)}, u32[]{:S(2)}, u32[]{:S(2)}) %collective-permute-start) | collective-permute-done | bytes 32800 | tf_op jit(solution)/shard_map/ppermute | solution.py:192
  4.6 1.1 %collective-permute-done.1 = bf16[1,2,64,128]{3,2,1,0:T(8,128)(2,1)S(1)} collective-permute-done((bf16[1,2,64,128]{3,2,1,0:T(8,128)(2,1)S(1)}, bf16[1,2,64,128]{3,2,1,0:T(8,128)(2,1)S(1)}, u32[]{:S(2)}, u32[]{:S(2)}) %collective-permute-start.1) | collective-permute-done | bytes 32800 | tf_op jit(solution)/shard_map/ppermute | solution.py:192
  5.8 0.8 %collective-permute-done.2 = bf16[1,2,64,128]{3,2,1,0:T(8,128)(2,1)S(1)} collective-permute-done((bf16[1,2,64,128]{3,2,1,0:T(8,128)(2,1)S(1)}, bf16[1,2,64,128]{3,2,1,0:T(8,128)(2,1)S(1)}, u32[]{:S(2)}, u32[]{:S(2)}) %collective-permute-start.2) | collective-permute-done | bytes 32800 | tf_op jit(solution)/shard_map/ppermute | solution.py:192
  6.6 1.3 %collective-permute-start.4 = (bf16[4,2,64,128]{3,2,1,0:T(8,128)(2,1)S(1)}, bf16[4,2,64,128]{3,2,1,0:T(8,128)(2,1)S(1)}, u32[]{:S(2)}, u32[]{:S(2)}) collective-permute-start(bf16[4,2,64,128]{3,2,1,0:T(8,128)(2,1)S(1)} %pad_maximum_fusion.refs_1_), channel_id=1, source_target_pairs={{0,4},{4,0},{8,12},{12,8},{16,20},{20,16},{24,28},{28,24},{1,5},{5... | collective-permute-start | bytes 393224 | tf_op jit(solution)/shard_map/ppermute | solution.py:176
  7.9 1.2 %collective-permute-start.7 = (bf16[4,2,64,128]{3,2,1,0:T(8,128)(2,1)S(1)}, bf16[4,2,64,128]{3,2,1,0:T(8,128)(2,1)S(1)}, u32[]{:S(2)}, u32[]{:S(2)}) collective-permute-start(bf16[4,2,64,128]{3,2,1,0:T(8,128)(2,1)S(1)} %pad_maximum_fusion.refs_1_), channel_id=1, source_target_pairs={{0,2},{1,3},{2,0},{3,1},{4,6},{5,7},{6,4},{7,5},{8,10},{9,11},{10,... | collective-permute-start | bytes 393224 | tf_op jit(solution)/shard_map/ppermute | solution.py:176
  9.1 0.2 collective-permute-start.3
  9.3 2.6 %collective-permute-start.5 = (bf16[4,2,32,128]{3,2,1,0:T(8,128)(2,1)S(1)}, bf16[4,2,32,128]{3,2,1,0:T(8,128)(2,1)S(1)}, u32[]{:S(2)}, u32[]{:S(2)}) collective-permute-start(bf16[4,2,32,128]{3,2,1,0:T(8,128)(2,1)S(1)} %get-tuple-element.56), channel_id=1, source_target_pairs={{0,1},{1,0},{2,3},{3,2},{4,5},{5,4},{6,7},{7,6},{8,9},{9,8},{10,11... | collective-permute-start | bytes 196616 | tf_op jit(solution)/shard_map/ppermute | solution.py:176
  11.9 0.0 copy-start.1
  11.9 0.1 collective-permute-start.6
  12.0 0.0 copy-done
  12.0 0.6 %copy-done.1 = s32[1,4]{1,0:T(1,128)S(1)} copy-done((s32[1,4]{1,0:T(1,128)S(1)}, s32[1,4]{1,0:T(1,128)}, u32[]{:S(2)}) %copy-start.1) | copy-done | bytes 40
  12.6 1.2 %shard_map.46 = (f32[8,256]{1,0:T(8,128)S(1)}, f32[4,128,256]{2,1,0:T(8,128)S(1)}, s32[1,256]{1,0:T(1,128)S(1)}, bf16[4,128,256]{2,1,0:T(8,128)(2,1)S(1)}) custom-call(bf16[256,512]{1,0:T(8,128)(2,1)S(1)} %bitcast.4, bf16[4,2,64,128]{3,2,1,0:T(8,128)(2,1)S(1)} %pad_maximum_fusion.refs_1_, s32[1,4]{1,0:T(1,128)S(1)} %copy-done.1), custom_call_target="tpu_custom_call" | custom-call | flops 1 | bytes 1 | tf_op jit(solution)/shard_map/pallas_call | solution.py:164
  13.8 0.0 collective-permute-done.5.refs_1_
  13.8 0.0 collective-permute-done.6.refs_2_
  13.8 0.7 %shard_map.47 = (f32[8,256]{1,0:T(8,128)S(1)}, f32[4,128,256]{2,1,0:T(8,128)S(1)}) custom-call(bf16[4,128,256]{2,1,0:T(8,128)(2,1)S(1)} %get-tuple-element.33.refs_0_, bf16[4,2,32,128]{3,2,1,0:T(8,128)(2,1)S(1)} %collective-permute-done.5.refs_1_, bf16[4,2,32,128]{3,2,1,0:T(8,128)(2,1)S(1)} %collective-permute-done.6.refs_2_, ...), custom_call_target="tpu_custom_call" | custom-call | flops 1 | bytes 1 | tf_op jit(solution)/shard_map/pallas_call | solution.py:164
  14.5 0.0 collective-permute-done.4.refs_1_
  14.5 0.7 %shard_map.48 = (f32[8,256]{1,0:T(8,128)S(1)}, f32[4,128,256]{2,1,0:T(8,128)S(1)}) custom-call(bf16[4,128,256]{2,1,0:T(8,128)(2,1)S(1)} %get-tuple-element.33.refs_0_, bf16[4,2,64,128]{3,2,1,0:T(8,128)(2,1)S(1)} %collective-permute-done.4.refs_1_, f32[8,256]{1,0:T(8,128)S(1)} %get-tuple-element.40.refs_2_, f32[4,128,256]{2,1,0:T(8,128)S(1)} %get-tuple-element.41.refs_3_, ...), custom_call_target="tpu_custom_call" | custom-call | flops 1 | bytes 1 | tf_op jit(solution)/shard_map/pallas_call | solution.py:164
  15.3 0.0 collective-permute-done.7.refs_1_
  15.3 2.2 %collective-permute-start.10 = (bf16[4,2,64,128]{3,2,1,0:T(8,128)(2,1)S(1)}, bf16[4,2,64,128]{3,2,1,0:T(8,128)(2,1)S(1)}, u32[]{:S(2)}, u32[]{:S(2)}) collective-permute-start(bf16[4,2,64,128]{3,2,1,0:T(8,128)(2,1)S(1)} %collective-permute-done.7.refs_1_), channel_id=1, source_target_pairs={{0,1},{1,0},{2,3},{3,2},{4,5},{5,4},{6,7},{7,6},{8,9},{9,8},{10,11... | collective-permute-start | bytes 393224 | tf_op jit(solution)/shard_map/ppermute | solution.py:176
  17.5 0.0 collective-permute-start.9
  17.5 0.7 %shard_map.49 = (f32[8,256]{1,0:T(8,128)S(1)}, f32[4,128,256]{2,1,0:T(8,128)S(1)}) custom-call(bf16[4,128,256]{2,1,0:T(8,128)(2,1)S(1)} %get-tuple-element.33.refs_0_, bf16[4,2,64,128]{3,2,1,0:T(8,128)(2,1)S(1)} %collective-permute-done.7.refs_1_, f32[8,256]{1,0:T(8,128)S(1)} %get-tuple-element.45.refs_2_, f32[4,128,256]{2,1,0:T(8,128)S(1)} %get-tuple-element.46.refs_3_, ...), custom_call_target="tpu_custom_call" | custom-call | flops 1 | bytes 1 | tf_op jit(solution)/shard_map/pallas_call | solution.py:164
  18.2 0.0 collective-permute-done.3.refs_3_
  18.2 0.6 %collective-permute-start.8 = (bf16[4,2,64,128]{3,2,1,0:T(8,128)(2,1)S(1)}, bf16[4,2,64,128]{3,2,1,0:T(8,128)(2,1)S(1)}, u32[]{:S(2)}, u32[]{:S(2)}) collective-permute-start(bf16[4,2,64,128]{3,2,1,0:T(8,128)(2,1)S(1)} %collective-permute-done.3.refs_3_), channel_id=1, source_target_pairs={{0,1},{1,0},{2,3},{3,2},{4,5},{5,4},{6,7},{7,6},{8,9},{9,8},{10,11... | collective-permute-start | bytes 393224 | tf_op jit(solution)/shard_map/ppermute | solution.py:176
  18.7 0.0 collective-permute-done.10.refs_2_
  18.7 0.1 collective-permute-done.9.refs_1_
  18.8 1.6 %shard_map.50 = (f32[8,256]{1,0:T(8,128)S(1)}, f32[4,128,256]{2,1,0:T(8,128)S(1)}) custom-call(bf16[4,128,256]{2,1,0:T(8,128)(2,1)S(1)} %get-tuple-element.33.refs_0_, bf16[4,2,64,128]{3,2,1,0:T(8,128)(2,1)S(1)} %collective-permute-done.9.refs_1_, bf16[4,2,64,128]{3,2,1,0:T(8,128)(2,1)S(1)} %collective-permute-done.10.refs_2_, ...), custom_call_target="tpu_custom_call" | custom-call | flops 1 | bytes 1 | tf_op jit(solution)/shard_map/pallas_call | solution.py:164
  20.4 0.0 collective-permute-done.8.refs_1_
  20.4 1.4 %shard_map.51 = bf16[256,512]{1,0:T(8,128)(2,1)} custom-call(bf16[4,128,256]{2,1,0:T(8,128)(2,1)S(1)} %get-tuple-element.33.refs_0_, bf16[4,2,64,128]{3,2,1,0:T(8,128)(2,1)S(1)} %collective-permute-done.8.refs_1_, f32[8,256]{1,0:T(8,128)S(1)} %get-tuple-element.53.refs_2_, f32[4,128,256]{2,1,0:T(8,128)S(1)} %get-tuple-element.54.refs_3_, ...), custom_call_target="tpu_custom_call" | custom-call | flops 1 | bytes 1 | tf_op jit(solution)/shard_map/pallas_call | solution.py:164
  (2 shorter events, 0.0 us)
Async XLA Ops:
  0.7 11.3 %copy-start = (bf16[1,256,512]{2,1,0:T(8,128)(2,1)S(1)}, bf16[1,256,512]{2,1,0:T(8,128)(2,1)}, u32[]{:S(2)}) copy-start(bf16[1,256,512]{2,1,0:T(8,128)(2,1)} %param.4) | copy-start | bytes 786436
  0.7 3.9 %collective-permute-start = (bf16[1,2,64,128]{3,2,1,0:T(8,128)(2,1)S(1)}, bf16[1,2,64,128]{3,2,1,0:T(8,128)(2,1)S(1)}, u32[]{:S(2)}, u32[]{:S(2)}) collective-permute-start(bf16[1,2,64,128]{3,2,1,0:T(8,128)(2,1)S(1)} %maximum_bitcast_fusion), channel_id=1, source_target_pairs={{0,16},{4,20},{8,24},{12,28},{16,0},{20,4},{24,8},{28,12},{1,17},{... | collective-permute-start | bytes 98312 | tf_op jit(solution)/shard_map/ppermute | solution.py:192
  0.8 5.0 %collective-permute-start.1 = (bf16[1,2,64,128]{3,2,1,0:T(8,128)(2,1)S(1)}, bf16[1,2,64,128]{3,2,1,0:T(8,128)(2,1)S(1)}, u32[]{:S(2)}, u32[]{:S(2)}) collective-permute-start(bf16[1,2,64,128]{3,2,1,0:T(8,128)(2,1)S(1)} %maximum_bitcast_fusion), channel_id=1, source_target_pairs={{0,24},{4,28},{8,16},{12,20},{16,0},{20,4},{24,8},{28,12},{1,25},{... | collective-permute-start | bytes 98312 | tf_op jit(solution)/shard_map/ppermute | solution.py:192
  3.1 3.5 %collective-permute-start.2 = (bf16[1,2,64,128]{3,2,1,0:T(8,128)(2,1)S(1)}, bf16[1,2,64,128]{3,2,1,0:T(8,128)(2,1)S(1)}, u32[]{:S(2)}, u32[]{:S(2)}) collective-permute-start(bf16[1,2,64,128]{3,2,1,0:T(8,128)(2,1)S(1)} %maximum_bitcast_fusion), channel_id=1, source_target_pairs={{0,8},{4,12},{8,0},{12,4},{16,24},{20,28},{24,16},{28,20},{1,9},{5... | collective-permute-start | bytes 98312 | tf_op jit(solution)/shard_map/ppermute | solution.py:192
  6.6 7.9 %collective-permute-start.4 = (bf16[4,2,64,128]{3,2,1,0:T(8,128)(2,1)S(1)}, bf16[4,2,64,128]{3,2,1,0:T(8,128)(2,1)S(1)}, u32[]{:S(2)}, u32[]{:S(2)}) collective-permute-start(bf16[4,2,64,128]{3,2,1,0:T(8,128)(2,1)S(1)} %pad_maximum_fusion.refs_1_), channel_id=1, source_target_pairs={{0,4},{4,0},{8,12},{12,8},{16,20},{20,16},{24,28},{28,24},{1,5},{5... | collective-permute-start | bytes 393224 | tf_op jit(solution)/shard_map/ppermute | solution.py:176
  7.9 7.4 %collective-permute-start.7 = (bf16[4,2,64,128]{3,2,1,0:T(8,128)(2,1)S(1)}, bf16[4,2,64,128]{3,2,1,0:T(8,128)(2,1)S(1)}, u32[]{:S(2)}, u32[]{:S(2)}) collective-permute-start(bf16[4,2,64,128]{3,2,1,0:T(8,128)(2,1)S(1)} %pad_maximum_fusion.refs_1_), channel_id=1, source_target_pairs={{0,2},{1,3},{2,0},{3,1},{4,6},{5,7},{6,4},{7,5},{8,10},{9,11},{10,... | collective-permute-start | bytes 393224 | tf_op jit(solution)/shard_map/ppermute | solution.py:176
  9.1 9.0 %collective-permute-start.3 = (bf16[4,2,64,128]{3,2,1,0:T(8,128)(2,1)S(1)}, bf16[4,2,64,128]{3,2,1,0:T(8,128)(2,1)S(1)}, u32[]{:S(2)}, u32[]{:S(2)}) collective-permute-start(bf16[4,2,64,128]{3,2,1,0:T(8,128)(2,1)S(1)} %pad_maximum_fusion.refs_1_), channel_id=1, source_target_pairs={{0,6},{1,7},{2,4},{3,5},{4,2},{5,3},{6,0},{7,1},{8,14},{9,15},{10,... | collective-permute-start | bytes 393224 | tf_op jit(solution)/shard_map/ppermute | solution.py:176
  9.3 4.5 %collective-permute-start.5 = (bf16[4,2,32,128]{3,2,1,0:T(8,128)(2,1)S(1)}, bf16[4,2,32,128]{3,2,1,0:T(8,128)(2,1)S(1)}, u32[]{:S(2)}, u32[]{:S(2)}) collective-permute-start(bf16[4,2,32,128]{3,2,1,0:T(8,128)(2,1)S(1)} %get-tuple-element.56), channel_id=1, source_target_pairs={{0,1},{1,0},{2,3},{3,2},{4,5},{5,4},{6,7},{7,6},{8,9},{9,8},{10,11... | collective-permute-start | bytes 196616 | tf_op jit(solution)/shard_map/ppermute | solution.py:176
  11.9 0.7 %copy-start.1 = (s32[1,4]{1,0:T(1,128)S(1)}, s32[1,4]{1,0:T(1,128)}, u32[]{:S(2)}) copy-start(s32[1,4]{1,0:T(1,128)} %refs_2_.1) | copy-start | bytes 52
  11.9 1.9 %collective-permute-start.6 = (bf16[4,2,32,128]{3,2,1,0:T(8,128)(2,1)S(1)}, bf16[4,2,32,128]{3,2,1,0:T(8,128)(2,1)S(1)}, u32[]{:S(2)}, u32[]{:S(2)}) collective-permute-start(bf16[4,2,32,128]{3,2,1,0:T(8,128)(2,1)S(1)} %get-tuple-element.55), channel_id=1, source_target_pairs={{0,1},{1,0},{2,3},{3,2},{4,5},{5,4},{6,7},{7,6},{8,9},{9,8},{10,11... | collective-permute-start | bytes 196616 | tf_op jit(solution)/shard_map/ppermute | solution.py:176
  15.3 3.5 %collective-permute-start.10 = (bf16[4,2,64,128]{3,2,1,0:T(8,128)(2,1)S(1)}, bf16[4,2,64,128]{3,2,1,0:T(8,128)(2,1)S(1)}, u32[]{:S(2)}, u32[]{:S(2)}) collective-permute-start(bf16[4,2,64,128]{3,2,1,0:T(8,128)(2,1)S(1)} %collective-permute-done.7.refs_1_), channel_id=1, source_target_pairs={{0,1},{1,0},{2,3},{3,2},{4,5},{5,4},{6,7},{7,6},{8,9},{9,8},{10,11... | collective-permute-start | bytes 393224 | tf_op jit(solution)/shard_map/ppermute | solution.py:176
  17.5 1.3 %collective-permute-start.9 = (bf16[4,2,64,128]{3,2,1,0:T(8,128)(2,1)S(1)}, bf16[4,2,64,128]{3,2,1,0:T(8,128)(2,1)S(1)}, u32[]{:S(2)}, u32[]{:S(2)}) collective-permute-start(bf16[4,2,64,128]{3,2,1,0:T(8,128)(2,1)S(1)} %collective-permute-done.4.refs_1_), channel_id=1, source_target_pairs={{0,1},{1,0},{2,3},{3,2},{4,5},{5,4},{6,7},{7,6},{8,9},{9,8},{10,11... | collective-permute-start | bytes 393224 | tf_op jit(solution)/shard_map/ppermute | solution.py:176
  18.2 2.3 %collective-permute-start.8 = (bf16[4,2,64,128]{3,2,1,0:T(8,128)(2,1)S(1)}, bf16[4,2,64,128]{3,2,1,0:T(8,128)(2,1)S(1)}, u32[]{:S(2)}, u32[]{:S(2)}) collective-permute-start(bf16[4,2,64,128]{3,2,1,0:T(8,128)(2,1)S(1)} %collective-permute-done.3.refs_3_), channel_id=1, source_target_pairs={{0,1},{1,0},{2,3},{3,2},{4,5},{5,4},{6,7},{7,6},{8,9},{9,8},{10,11... | collective-permute-start | bytes 393224 | tf_op jit(solution)/shard_map/ppermute | solution.py:176

commit v19 on v18

--- a/solution.py
+++ b/solution.py
@@ -209,20 +209,20 @@
         across = exchange(own, "ctx", 1)
         far = exchange(own, "head", 2)
         corner = exchange(own, ("ctx", "head"), lax.axis_size("head") + 2)
-        near = [exchange(own[:, :, :half], "head", 1), exchange(own[:, :, half:], "head", 1)]
         stats, sums, starts, turned = run([(0, 0, 0)], "first", queries=queries[seq], kvs=[own], state=())
         run = functools.partial(run, queries=turned)
-        stats, sums = run([(0, 1, 0), (0, 1, half)], "middle", kvs=near, state=(stats, sums, starts))
-
-        across, stats, sums = lax.optimization_barrier((across, stats, sums))
+
+        across, stats, sums, held = lax.optimization_barrier((across, stats, sums, own))
+        near = [exchange(piece[:, :, rows], "head", 1) for piece in (held, across) for rows in (slice(half), slice(half, None))]
         stats, sums = run([(1, 0, 0)], "middle", kvs=[across], state=(stats, sums, starts))
-        across, far, stats, sums = lax.optimization_barrier((across, far, stats, sums))
-        near = [exchange(across, "head", 1), exchange(far, "head", 1)]
+        parts = [(0, 1, 0), (0, 1, half), (1, 1, 0), (1, 1, half)]
+        stats, sums = run(parts, "middle", kvs=near, state=(stats, sums, starts))
+        far, stats, sums = lax.optimization_barrier((far, stats, sums))
+        near_far = exchange(far, "head", 1)
         stats, sums = run([(0, 2, 0)], "middle", kvs=[far], state=(stats, sums, starts))
         corner, stats, sums = lax.optimization_barrier((corner, stats, sums))
         near_corner = exchange(corner, "head", 1)
-        parts = [(1, 1, 0), (0, 3, 0), (1, 2, 0)]
-        stats, sums = run(parts, "middle", kvs=[*near, corner], state=(stats, sums, starts))
+        stats, sums = run([(0, 3, 0), (1, 2, 0)], "middle", kvs=[near_far, corner], state=(stats, sums, starts))
         results.append(run([(1, 3, 0)], "last", kvs=[near_corner], state=(stats, sums, starts)))
     return jnp.stack(results)
 

time: 22.2 us -> 23 us (1.036)
  the two profiles are of different devices: /device:TPU:25 before, /device:TPU:0 now
where the time goes in v19:
time: 23 us; the launch traced here: 22.8 us
  starting transfers between devices  10.7 us (47%)
  waiting for transfers between devices  6.93 us (30%)
  Pallas kernels  4.26 us (19%)
  other arithmetic  0.8 us (3%)
    ppermute x3, starting transfers between devices, same_parity_blocks(): moved.append(lax.ppermute(held, axis, targets))  5.62 us
    ppermute x9, starting transfers between devices, exchange(): lax.ppermute(piece, axis, [(i, i ^ bits) for i in range(lax.axis_size(axi...  5.06 us
    pallas_call x6, Pallas kernels, attend(): pl.pallas_call(functools.partial(attention_kernel, head_size, parts, kind...  4.26 us
    ppermute x3, waiting for transfers between devices, same_parity_blocks(): moved.append(lax.ppermute(held, axis, targets))  3.68 us
    ppermute x9, waiting for transfers between devices, exchange(): lax.ppermute(piece, axis, [(i, i ^ bits) for i in range(lax.axis_size(axi...  3.25 us
    broadcast_in_dim x1, other arithmetic, same_parity_blocks(): held = block[None]  0.78 us
  transfers between devices with their start and end apart: 12, of which 8 were waited for; matrix products, arithmetic and copies ran while one was open for 0% of the time, Pallas kernels for 14%

profile of v19, /device:TPU:0, one launch (start us, length us, event | category | flops | bytes accessed | tf_op | source)
XLA Modules:
  0.0 22.8 jit_solution(11730774931126832477)
XLA Ops:
  0.0 0.0 copy-start
  0.0 0.8 %maximum_bitcast_fusion = bf16[1,2,64,128]{3,2,1,0:T(8,128)(2,1)S(1)} fusion(bf16[1,64,128]{2,1,0:T(8,128)(2,1)} %param.6, bf16[1,64,128]{2,1,0:T(8,128)(2,1)} %param.5), kind=kLoop, calls=%fused_computation.1 | loop fusion | flops 16384 | bytes 65536 | tf_op jit(solution)/shard_map/broadcast_in_dim | solution.py:181
  0.8 4.0 %collective-permute-start = (bf16[1,2,64,128]{3,2,1,0:T(8,128)(2,1)S(1)}, bf16[1,2,64,128]{3,2,1,0:T(8,128)(2,1)S(1)}, u32[]{:S(2)}, u32[]{:S(2)}) collective-permute-start(bf16[1,2,64,128]{3,2,1,0:T(8,128)(2,1)S(1)} %maximum_bitcast_fusion), channel_id=1, source_target_pairs={{0,16},{4,20},{8,24},{12,28},{16,0},{20,4},{24,8},{28,12},{1,17},{... | collective-permute-start | bytes 98312 | tf_op jit(solution)/shard_map/ppermute | solution.py:192
  4.8 1.3 %collective-permute-start.1 = (bf16[1,2,64,128]{3,2,1,0:T(8,128)(2,1)S(1)}, bf16[1,2,64,128]{3,2,1,0:T(8,128)(2,1)S(1)}, u32[]{:S(2)}, u32[]{:S(2)}) collective-permute-start(bf16[1,2,64,128]{3,2,1,0:T(8,128)(2,1)S(1)} %maximum_bitcast_fusion), channel_id=1, source_target_pairs={{0,24},{4,28},{8,16},{12,20},{16,0},{20,4},{24,8},{28,12},{1,25},{... | collective-permute-start | bytes 98312 | tf_op jit(solution)/shard_map/ppermute | solution.py:192
  6.2 0.2 %collective-permute-start.2 = (bf16[1,2,64,128]{3,2,1,0:T(8,128)(2,1)S(1)}, bf16[1,2,64,128]{3,2,1,0:T(8,128)(2,1)S(1)}, u32[]{:S(2)}, u32[]{:S(2)}) collective-permute-start(bf16[1,2,64,128]{3,2,1,0:T(8,128)(2,1)S(1)} %maximum_bitcast_fusion), channel_id=1, source_target_pairs={{0,8},{4,12},{8,0},{12,4},{16,24},{20,28},{24,16},{28,20},{1,9},{5... | collective-permute-start | bytes 98312 | tf_op jit(solution)/shard_map/ppermute | solution.py:192
  6.4 0.7 %collective-permute-done = bf16[1,2,64,128]{3,2,1,0:T(8,128)(2,1)S(1)} collective-permute-done((bf16[1,2,64,128]{3,2,1,0:T(8,128)(2,1)S(1)}, bf16[1,2,64,128]{3,2,1,0:T(8,128)(2,1)S(1)}, u32[]{:S(2)}, u32[]{:S(2)}) %collective-permute-start) | collective-permute-done | bytes 32800 | tf_op jit(solution)/shard_map/ppermute | solution.py:192
  7.1 2.6 %collective-permute-done.1 = bf16[1,2,64,128]{3,2,1,0:T(8,128)(2,1)S(1)} collective-permute-done((bf16[1,2,64,128]{3,2,1,0:T(8,128)(2,1)S(1)}, bf16[1,2,64,128]{3,2,1,0:T(8,128)(2,1)S(1)}, u32[]{:S(2)}, u32[]{:S(2)}) %collective-permute-start.1) | collective-permute-done | bytes 32800 | tf_op jit(solution)/shard_map/ppermute | solution.py:192
  9.6 0.4 %collective-permute-done.2 = bf16[1,2,64,128]{3,2,1,0:T(8,128)(2,1)S(1)} collective-permute-done((bf16[1,2,64,128]{3,2,1,0:T(8,128)(2,1)S(1)}, bf16[1,2,64,128]{3,2,1,0:T(8,128)(2,1)S(1)}, u32[]{:S(2)}, u32[]{:S(2)}) %collective-permute-start.2) | collective-permute-done | bytes 32800 | tf_op jit(solution)/shard_map/ppermute | solution.py:192
  10.1 0.0 copy-start.1
  10.1 1.6 %collective-permute-start.5 = (bf16[4,2,64,128]{3,2,1,0:T(8,128)(2,1)S(1)}, bf16[4,2,64,128]{3,2,1,0:T(8,128)(2,1)S(1)}, u32[]{:S(2)}, u32[]{:S(2)}) collective-permute-start(bf16[4,2,64,128]{3,2,1,0:T(8,128)(2,1)S(1)} %pad_maximum_fusion.refs_1_), channel_id=1, source_target_pairs={{0,4},{4,0},{8,12},{12,8},{16,20},{20,16},{24,28},{28,24},{1,5},{5... | collective-permute-start | bytes 393224 | tf_op jit(solution)/shard_map/ppermute | solution.py:176
  11.7 1.5 %collective-permute-start.4 = (bf16[4,2,64,128]{3,2,1,0:T(8,128)(2,1)S(1)}, bf16[4,2,64,128]{3,2,1,0:T(8,128)(2,1)S(1)}, u32[]{:S(2)}, u32[]{:S(2)}) collective-permute-start(bf16[4,2,64,128]{3,2,1,0:T(8,128)(2,1)S(1)} %pad_maximum_fusion.refs_1_), channel_id=1, source_target_pairs={{0,2},{1,3},{2,0},{3,1},{4,6},{5,7},{6,4},{7,5},{8,10},{9,11},{10,... | collective-permute-start | bytes 393224 | tf_op jit(solution)/shard_map/ppermute | solution.py:176
  13.2 0.5 %collective-permute-start.3 = (bf16[4,2,64,128]{3,2,1,0:T(8,128)(2,1)S(1)}, bf16[4,2,64,128]{3,2,1,0:T(8,128)(2,1)S(1)}, u32[]{:S(2)}, u32[]{:S(2)}) collective-permute-start(bf16[4,2,64,128]{3,2,1,0:T(8,128)(2,1)S(1)} %pad_maximum_fusion.refs_1_), channel_id=1, source_target_pairs={{0,6},{1,7},{2,4},{3,5},{4,2},{5,3},{6,0},{7,1},{8,14},{9,15},{10,... | collective-permute-start | bytes 393224 | tf_op jit(solution)/shard_map/ppermute | solution.py:176
  13.7 0.0 copy-done
  13.7 0.0 copy-done.1
  13.7 1.2 %shard_map.46 = (f32[8,256]{1,0:T(8,128)S(1)}, f32[4,128,256]{2,1,0:T(8,128)S(1)}, s32[1,256]{1,0:T(1,128)S(1)}, bf16[4,128,256]{2,1,0:T(8,128)(2,1)S(1)}) custom-call(bf16[256,512]{1,0:T(8,128)(2,1)S(1)} %bitcast.4, bf16[4,2,64,128]{3,2,1,0:T(8,128)(2,1)S(1)} %pad_maximum_fusion.refs_1_, s32[1,4]{1,0:T(1,128)S(1)} %copy-done.1), custom_call_target="tpu_custom_call" | custom-call | flops 1 | bytes 1 | tf_op jit(solution)/shard_map/pallas_call | solution.py:164
  14.9 1.5 %collective-permute-done.5.refs_1_ = bf16[4,2,64,128]{3,2,1,0:T(8,128)(2,1)S(1)} collective-permute-done((bf16[4,2,64,128]{3,2,1,0:T(8,128)(2,1)S(1)}, bf16[4,2,64,128]{3,2,1,0:T(8,128)(2,1)S(1)}, u32[]{:S(2)}, u32[]{:S(2)}) %collective-permute-start.5) | collective-permute-done | bytes 131104 | tf_op jit(solution)/shard_map/ppermute | solution.py:176
  16.5 0.1 collective-permute-start.6
  16.5 0.5 %collective-permute-start.7 = (bf16[4,2,32,128]{3,2,1,0:T(8,128)(2,1)S(1)}, bf16[4,2,32,128]{3,2,1,0:T(8,128)(2,1)S(1)}, u32[]{:S(2)}, u32[]{:S(2)}) collective-permute-start(bf16[4,2,32,128]{3,2,1,0:T(8,128)(2,1)S(1)} %get-tuple-element.57), channel_id=1, source_target_pairs={{0,1},{1,0},{2,3},{3,2},{4,5},{5,4},{6,7},{7,6},{8,9},{9,8},{10,11... | collective-permute-start | bytes 196616 | tf_op jit(solution)/shard_map/ppermute | solution.py:176
  17.0 0.1 collective-permute-start.8
  17.2 0.6 %collective-permute-done.6.refs_1_ = bf16[4,2,32,128]{3,2,1,0:T(8,128)(2,1)S(1)} collective-permute-done((bf16[4,2,32,128]{3,2,1,0:T(8,128)(2,1)S(1)}, bf16[4,2,32,128]{3,2,1,0:T(8,128)(2,1)S(1)}, u32[]{:S(2)}, u32[]{:S(2)}) %collective-permute-start.6) | collective-permute-done | bytes 65568 | tf_op jit(solution)/shard_map/ppermute | solution.py:176
  17.8 0.2 collective-permute-start.9
  17.9 0.4 %shard_map.47 = (f32[8,256]{1,0:T(8,128)S(1)}, f32[4,128,256]{2,1,0:T(8,128)S(1)}) custom-call(bf16[4,128,256]{2,1,0:T(8,128)(2,1)S(1)} %get-tuple-element.33.refs_0_, bf16[4,2,64,128]{3,2,1,0:T(8,128)(2,1)S(1)} %collective-permute-done.5.refs_1_, f32[8,256]{1,0:T(8,128)S(1)} %get-tuple-element.38.refs_2_, f32[4,128,256]{2,1,0:T(8,128)S(1)} %get-tuple-element.39.refs_3_, ...), custom_call_target="tpu_custom_call" | custom-call | flops 1 | bytes 1 | tf_op jit(solution)/shard_map/pallas_call | solution.py:164
  18.4 0.0 collective-permute-done.7.refs_2_
  18.4 0.0 collective-permute-done.8.refs_3_
  18.4 0.6 %collective-permute-done.9.refs_4_ = bf16[4,2,32,128]{3,2,1,0:T(8,128)(2,1)S(1)} collective-permute-done((bf16[4,2,32,128]{3,2,1,0:T(8,128)(2,1)S(1)}, bf16[4,2,32,128]{3,2,1,0:T(8,128)(2,1)S(1)}, u32[]{:S(2)}, u32[]{:S(2)}) %collective-permute-start.9) | collective-permute-done | bytes 65568 | tf_op jit(solution)/shard_map/ppermute | solution.py:176
  19.0 0.5 %shard_map.48 = (f32[8,256]{1,0:T(8,128)S(1)}, f32[4,128,256]{2,1,0:T(8,128)S(1)}) custom-call(bf16[4,128,256]{2,1,0:T(8,128)(2,1)S(1)} %get-tuple-element.33.refs_0_, bf16[4,2,32,128]{3,2,1,0:T(8,128)(2,1)S(1)} %collective-permute-done.6.refs_1_, bf16[4,2,32,128]{3,2,1,0:T(8,128)(2,1)S(1)} %collective-permute-done.7.refs_2_, ...), custom_call_target="tpu_custom_call" | custom-call | flops 1 | bytes 1 | tf_op jit(solution)/shard_map/pallas_call | solution.py:164
  19.5 0.0 collective-permute-done.4.refs_1_
  19.5 0.2 collective-permute-start.11
  19.8 0.4 %shard_map.49 = (f32[8,256]{1,0:T(8,128)S(1)}, f32[4,128,256]{2,1,0:T(8,128)S(1)}) custom-call(bf16[4,128,256]{2,1,0:T(8,128)(2,1)S(1)} %get-tuple-element.33.refs_0_, bf16[4,2,64,128]{3,2,1,0:T(8,128)(2,1)S(1)} %collective-permute-done.4.refs_1_, f32[8,256]{1,0:T(8,128)S(1)} %get-tuple-element.46.refs_2_, f32[4,128,256]{2,1,0:T(8,128)S(1)} %get-tuple-element.47.refs_3_, ...), custom_call_target="tpu_custom_call" | custom-call | flops 1 | bytes 1 | tf_op jit(solution)/shard_map/pallas_call | solution.py:164
  20.2 0.0 collective-permute-done.3.refs_2_
  20.2 0.4 %collective-permute-start.10 = (bf16[4,2,64,128]{3,2,1,0:T(8,128)(2,1)S(1)}, bf16[4,2,64,128]{3,2,1,0:T(8,128)(2,1)S(1)}, u32[]{:S(2)}, u32[]{:S(2)}) collective-permute-start(bf16[4,2,64,128]{3,2,1,0:T(8,128)(2,1)S(1)} %collective-permute-done.3.refs_2_), channel_id=1, source_target_pairs={{0,1},{1,0},{2,3},{3,2},{4,5},{5,4},{6,7},{7,6},{8,9},{9,8},{10,11... | collective-permute-start | bytes 393224 | tf_op jit(solution)/shard_map/ppermute | solution.py:176
  20.6 0.3 %collective-permute-done.11.refs_1_ = bf16[4,2,64,128]{3,2,1,0:T(8,128)(2,1)S(1)} collective-permute-done((bf16[4,2,64,128]{3,2,1,0:T(8,128)(2,1)S(1)}, bf16[4,2,64,128]{3,2,1,0:T(8,128)(2,1)S(1)}, u32[]{:S(2)}, u32[]{:S(2)}) %collective-permute-start.11) | collective-permute-done | bytes 131104 | tf_op jit(solution)/shard_map/ppermute | solution.py:176
  21.0 0.5 %shard_map.50 = (f32[8,256]{1,0:T(8,128)S(1)}, f32[4,128,256]{2,1,0:T(8,128)S(1)}) custom-call(bf16[4,128,256]{2,1,0:T(8,128)(2,1)S(1)} %get-tuple-element.33.refs_0_, bf16[4,2,64,128]{3,2,1,0:T(8,128)(2,1)S(1)} %collective-permute-done.11.refs_1_, bf16[4,2,64,128]{3,2,1,0:T(8,128)(2,1)S(1)} %collective-permute-done.3.refs_2_, ...), custom_call_target="tpu_custom_call" | custom-call | flops 1 | bytes 1 | tf_op jit(solution)/shard_map/pallas_call | solution.py:164
  21.5 0.2 collective-permute-done.10.refs_1_
  21.6 1.2 %shard_map.51 = bf16[256,512]{1,0:T(8,128)(2,1)} custom-call(bf16[4,128,256]{2,1,0:T(8,128)(2,1)S(1)} %get-tuple-element.33.refs_0_, bf16[4,2,64,128]{3,2,1,0:T(8,128)(2,1)S(1)} %collective-permute-done.10.refs_1_, f32[8,256]{1,0:T(8,128)S(1)} %get-tuple-element.53.refs_2_, f32[4,128,256]{2,1,0:T(8,128)S(1)} %get-tuple-element.54.refs_3_, ...), custom_call_target="tpu_custom_call" | custom-call | flops 1 | bytes 1 | tf_op jit(solution)/shard_map/pallas_call | solution.py:164
  (3 shorter events, 0.0 us)
Async XLA Ops:
  0.0 13.7 %copy-start = (bf16[1,256,512]{2,1,0:T(8,128)(2,1)S(1)}, bf16[1,256,512]{2,1,0:T(8,128)(2,1)}, u32[]{:S(2)}) copy-start(bf16[1,256,512]{2,1,0:T(8,128)(2,1)} %param.4) | copy-start | bytes 786436
  0.8 6.3 %collective-permute-start = (bf16[1,2,64,128]{3,2,1,0:T(8,128)(2,1)S(1)}, bf16[1,2,64,128]{3,2,1,0:T(8,128)(2,1)S(1)}, u32[]{:S(2)}, u32[]{:S(2)}) collective-permute-start(bf16[1,2,64,128]{3,2,1,0:T(8,128)(2,1)S(1)} %maximum_bitcast_fusion), channel_id=1, source_target_pairs={{0,16},{4,20},{8,24},{12,28},{16,0},{20,4},{24,8},{28,12},{1,17},{... | collective-permute-start | bytes 98312 | tf_op jit(solution)/shard_map/ppermute | solution.py:192
  4.8 4.8 %collective-permute-start.1 = (bf16[1,2,64,128]{3,2,1,0:T(8,128)(2,1)S(1)}, bf16[1,2,64,128]{3,2,1,0:T(8,128)(2,1)S(1)}, u32[]{:S(2)}, u32[]{:S(2)}) collective-permute-start(bf16[1,2,64,128]{3,2,1,0:T(8,128)(2,1)S(1)} %maximum_bitcast_fusion), channel_id=1, source_target_pairs={{0,24},{4,28},{8,16},{12,20},{16,0},{20,4},{24,8},{28,12},{1,25},{... | collective-permute-start | bytes 98312 | tf_op jit(solution)/shard_map/ppermute | solution.py:192
  6.2 3.9 %collective-permute-start.2 = (bf16[1,2,64,128]{3,2,1,0:T(8,128)(2,1)S(1)}, bf16[1,2,64,128]{3,2,1,0:T(8,128)(2,1)S(1)}, u32[]{:S(2)}, u32[]{:S(2)}) collective-permute-start(bf16[1,2,64,128]{3,2,1,0:T(8,128)(2,1)S(1)} %maximum_bitcast_fusion), channel_id=1, source_target_pairs={{0,8},{4,12},{8,0},{12,4},{16,24},{20,28},{24,16},{28,20},{1,9},{5... | collective-permute-start | bytes 98312 | tf_op jit(solution)/shard_map/ppermute | solution.py:192
  10.1 3.6 %copy-start.1 = (s32[1,4]{1,0:T(1,128)S(1)}, s32[1,4]{1,0:T(1,128)}, u32[]{:S(2)}) copy-start(s32[1,4]{1,0:T(1,128)} %refs_2_.1) | copy-start | bytes 52
  10.1 6.3 %collective-permute-start.5 = (bf16[4,2,64,128]{3,2,1,0:T(8,128)(2,1)S(1)}, bf16[4,2,64,128]{3,2,1,0:T(8,128)(2,1)S(1)}, u32[]{:S(2)}, u32[]{:S(2)}) collective-permute-start(bf16[4,2,64,128]{3,2,1,0:T(8,128)(2,1)S(1)} %pad_maximum_fusion.refs_1_), channel_id=1, source_target_pairs={{0,4},{4,0},{8,12},{12,8},{16,20},{20,16},{24,28},{28,24},{1,5},{5... | collective-permute-start | bytes 393224 | tf_op jit(solution)/shard_map/ppermute | solution.py:176
  11.7 7.9 %collective-permute-start.4 = (bf16[4,2,64,128]{3,2,1,0:T(8,128)(2,1)S(1)}, bf16[4,2,64,128]{3,2,1,0:T(8,128)(2,1)S(1)}, u32[]{:S(2)}, u32[]{:S(2)}) collective-permute-start(bf16[4,2,64,128]{3,2,1,0:T(8,128)(2,1)S(1)} %pad_maximum_fusion.refs_1_), channel_id=1, source_target_pairs={{0,2},{1,3},{2,0},{3,1},{4,6},{5,7},{6,4},{7,5},{8,10},{9,11},{10,... | collective-permute-start | bytes 393224 | tf_op jit(solution)/shard_map/ppermute | solution.py:176
  13.2 7.0 %collective-permute-start.3 = (bf16[4,2,64,128]{3,2,1,0:T(8,128)(2,1)S(1)}, bf16[4,2,64,128]{3,2,1,0:T(8,128)(2,1)S(1)}, u32[]{:S(2)}, u32[]{:S(2)}) collective-permute-start(bf16[4,2,64,128]{3,2,1,0:T(8,128)(2,1)S(1)} %pad_maximum_fusion.refs_1_), channel_id=1, source_target_pairs={{0,6},{1,7},{2,4},{3,5},{4,2},{5,3},{6,0},{7,1},{8,14},{9,15},{10,... | collective-permute-start | bytes 393224 | tf_op jit(solution)/shard_map/ppermute | solution.py:176
  16.5 1.3 %collective-permute-start.6 = (bf16[4,2,32,128]{3,2,1,0:T(8,128)(2,1)S(1)}, bf16[4,2,32,128]{3,2,1,0:T(8,128)(2,1)S(1)}, u32[]{:S(2)}, u32[]{:S(2)}) collective-permute-start(bf16[4,2,32,128]{3,2,1,0:T(8,128)(2,1)S(1)} %get-tuple-element.58), channel_id=1, source_target_pairs={{0,1},{1,0},{2,3},{3,2},{4,5},{5,4},{6,7},{7,6},{8,9},{9,8},{10,11... | collective-permute-start | bytes 196616 | tf_op jit(solution)/shard_map/ppermute | solution.py:176
  16.5 1.8 %collective-permute-start.7 = (bf16[4,2,32,128]{3,2,1,0:T(8,128)(2,1)S(1)}, bf16[4,2,32,128]{3,2,1,0:T(8,128)(2,1)S(1)}, u32[]{:S(2)}, u32[]{:S(2)}) collective-permute-start(bf16[4,2,32,128]{3,2,1,0:T(8,128)(2,1)S(1)} %get-tuple-element.57), channel_id=1, source_target_pairs={{0,1},{1,0},{2,3},{3,2},{4,5},{5,4},{6,7},{7,6},{8,9},{9,8},{10,11... | collective-permute-start | bytes 196616 | tf_op jit(solution)/shard_map/ppermute | solution.py:176
  17.0 1.3 %collective-permute-start.8 = (bf16[4,2,32,128]{3,2,1,0:T(8,128)(2,1)S(1)}, bf16[4,2,32,128]{3,2,1,0:T(8,128)(2,1)S(1)}, u32[]{:S(2)}, u32[]{:S(2)}) collective-permute-start(bf16[4,2,32,128]{3,2,1,0:T(8,128)(2,1)S(1)} %get-tuple-element.56), channel_id=1, source_target_pairs={{0,1},{1,0},{2,3},{3,2},{4,5},{5,4},{6,7},{7,6},{8,9},{9,8},{10,11... | collective-permute-start | bytes 196616 | tf_op jit(solution)/shard_map/ppermute | solution.py:176
  17.8 1.3 %collective-permute-start.9 = (bf16[4,2,32,128]{3,2,1,0:T(8,128)(2,1)S(1)}, bf16[4,2,32,128]{3,2,1,0:T(8,128)(2,1)S(1)}, u32[]{:S(2)}, u32[]{:S(2)}) collective-permute-start(bf16[4,2,32,128]{3,2,1,0:T(8,128)(2,1)S(1)} %get-tuple-element.55), channel_id=1, source_target_pairs={{0,1},{1,0},{2,3},{3,2},{4,5},{5,4},{6,7},{7,6},{8,9},{9,8},{10,11... | collective-permute-start | bytes 196616 | tf_op jit(solution)/shard_map/ppermute | solution.py:176
  19.5 1.4 %collective-permute-start.11 = (bf16[4,2,64,128]{3,2,1,0:T(8,128)(2,1)S(1)}, bf16[4,2,64,128]{3,2,1,0:T(8,128)(2,1)S(1)}, u32[]{:S(2)}, u32[]{:S(2)}) collective-permute-start(bf16[4,2,64,128]{3,2,1,0:T(8,128)(2,1)S(1)} %collective-permute-done.4.refs_1_), channel_id=1, source_target_pairs={{0,1},{1,0},{2,3},{3,2},{4,5},{5,4},{6,7},{7,6},{8,9},{9,8},{10,11... | collective-permute-start | bytes 393224 | tf_op jit(solution)/shard_map/ppermute | solution.py:176
  20.2 1.4 %collective-permute-start.10 = (bf16[4,2,64,128]{3,2,1,0:T(8,128)(2,1)S(1)}, bf16[4,2,64,128]{3,2,1,0:T(8,128)(2,1)S(1)}, u32[]{:S(2)}, u32[]{:S(2)}) collective-permute-start(bf16[4,2,64,128]{3,2,1,0:T(8,128)(2,1)S(1)} %collective-permute-done.3.refs_2_), channel_id=1, source_target_pairs={{0,1},{1,0},{2,3},{3,2},{4,5},{5,4},{6,7},{7,6},{8,9},{9,8},{10,11... | collective-permute-start | bytes 393224 | tf_op jit(solution)/shard_map/ppermute | solution.py:176

commit v20 on v16

--- a/solution.py
+++ b/solution.py
@@ -181,7 +181,16 @@
     held = block[None]
     while (count := held.shape[0]) < pairs:
         digits = sorted(range(1, min(DIGIT, pairs // count)), key=lambda digit: ORDER.index(digit))
-        moved = lax.optimization_barrier([exchange(held, axis, 2 * digit * count) for digit in digits])
+        moved = []
+        for digit in digits:
+            to = [source ^ digit for source in range(DIGIT)]
+            if digit == 3 and count * DIGIT == pairs:
+                to = [3, 2, 0, 1]
+            sources = range(lax.axis_size(axis))
+            place = [i // (2 * count) % DIGIT for i in sources]
+            targets = [(i, i ^ (2 * count * (place[i] ^ to[place[i]]))) for i in sources]
+            moved.append(lax.ppermute(held, axis, targets))
+        moved = lax.optimization_barrier(moved)
         moved = dict(zip(digits, moved))
         held = jnp.concatenate([held] + [moved[digit] for digit in sorted(digits)])
     return held
@@ -205,9 +214,11 @@
         run = functools.partial(run, queries=turned)
         stats, sums = run([(0, 1, 0), (0, 1, half)], "middle", kvs=near, state=(stats, sums, starts))
 
+        across, stats, sums = lax.optimization_barrier((across, stats, sums))
+        stats, sums = run([(1, 0, 0)], "middle", kvs=[across], state=(stats, sums, starts))
         across, corner, stats, sums = lax.optimization_barrier((across, corner, stats, sums))
         near = [exchange(across, "head", 1), exchange(corner, "head", 1)]
-        stats, sums = run([(1, 0, 0), (1, 2, 0)], "middle", kvs=[across, corner], state=(stats, sums, starts))
+        stats, sums = run([(1, 2, 0)], "middle", kvs=[corner], state=(stats, sums, starts))
         far, stats, sums = lax.optimization_barrier((far, stats, sums))
         near_far = exchange(far, "head", 1)
         parts = [(1, 1, 0), (1, 3, 0), (0, 2, 0)]

time: 22.4 us -> 22 us (0.982)
  waiting for transfers between devices: 6.92 us -> 6.15 us
  Pallas kernels: 3.92 us -> 4.29 us
    ppermute x0 -> x3, starting transfers between devices: none -> 5.62 us  [same_parity_blocks(): moved.append(lax.ppermute(held, axis, targets))]
    ppermute x11 -> x8, starting transfers between devices: 10.2 us -> 4.62 us  [exchange(): lax.ppermute(piece, axis, [(i, i ^ bits) for i in range(lax.axis_size(axi...]
    ppermute x11 -> x8, waiting for transfers between devices: 6.92 us -> 2.47 us  [exchange(): lax.ppermute(piece, axis, [(i, i ^ bits) for i in range(lax.axis_size(axi...]
    ppermute x0 -> x3, waiting for transfers between devices: none -> 3.68 us  [same_parity_blocks(): moved.append(lax.ppermute(held, axis, targets))]
    pallas_call x5 -> x6, Pallas kernels: 3.92 us -> 4.29 us  [attend(): pl.pallas_call(functools.partial(attention_kernel, head_size, parts, kind...]
  transfers between devices with their start and end apart: 11 -> 11, of which waited for: 6 -> 8; matrix products, arithmetic and copies ran while one was open for 0% -> 0% of each run, Pallas kernels for 12% -> 14%
where the time goes in v20:
time: 22 us; the launch traced here: 21.7 us
  starting transfers between devices  10.2 us (46%)
  waiting for transfers between devices  6.15 us (28%)
  Pallas kernels  4.29 us (20%)
  other arithmetic  0.76 us (3%)
    ppermute x3, starting transfers between devices, same_parity_blocks(): moved.append(lax.ppermute(held, axis, targets))  5.62 us
    ppermute x8, starting transfers between devices, exchange(): lax.ppermute(piece, axis, [(i, i ^ bits) for i in range(lax.axis_size(axi...  4.62 us
    pallas_call x6, Pallas kernels, attend(): pl.pallas_call(functools.partial(attention_kernel, head_size, parts, kind...  4.29 us
    ppermute x3, waiting for transfers between devices, same_parity_blocks(): moved.append(lax.ppermute(held, axis, targets))  3.68 us
    ppermute x8, waiting for transfers between devices, exchange(): lax.ppermute(piece, axis, [(i, i ^ bits) for i in range(lax.axis_size(axi...  2.47 us
    broadcast_in_dim x1, other arithmetic, same_parity_blocks(): held = block[None]  0.74 us
  transfers between devices with their start and end apart: 11, of which 8 were waited for; matrix products, arithmetic and copies ran while one was open for 0% of the time, Pallas kernels for 14%

profile of v20, /device:TPU:0, one launch (start us, length us, event | category | flops | bytes accessed | tf_op | source)
XLA Modules:
  0.0 21.7 jit_solution(5703825681472053393)
XLA Ops:
  0.0 0.7 %maximum_bitcast_fusion = bf16[1,2,64,128]{3,2,1,0:T(8,128)(2,1)S(1)} fusion(bf16[1,64,128]{2,1,0:T(8,128)(2,1)} %param.6, bf16[1,64,128]{2,1,0:T(8,128)(2,1)} %param.5), kind=kLoop, calls=%fused_computation.1 | loop fusion | flops 16384 | bytes 65536 | tf_op jit(solution)/shard_map/broadcast_in_dim | solution.py:181
  0.7 0.0 copy-start
  0.7 4.0 %collective-permute-start = (bf16[1,2,64,128]{3,2,1,0:T(8,128)(2,1)S(1)}, bf16[1,2,64,128]{3,2,1,0:T(8,128)(2,1)S(1)}, u32[]{:S(2)}, u32[]{:S(2)}) collective-permute-start(bf16[1,2,64,128]{3,2,1,0:T(8,128)(2,1)S(1)} %maximum_bitcast_fusion), channel_id=1, source_target_pairs={{0,16},{4,20},{8,24},{12,28},{16,0},{20,4},{24,8},{28,12},{1,17},{... | collective-permute-start | bytes 98312 | tf_op jit(solution)/shard_map/ppermute | solution.py:192
  4.8 1.3 %collective-permute-start.1 = (bf16[1,2,64,128]{3,2,1,0:T(8,128)(2,1)S(1)}, bf16[1,2,64,128]{3,2,1,0:T(8,128)(2,1)S(1)}, u32[]{:S(2)}, u32[]{:S(2)}) collective-permute-start(bf16[1,2,64,128]{3,2,1,0:T(8,128)(2,1)S(1)} %maximum_bitcast_fusion), channel_id=1, source_target_pairs={{0,24},{4,28},{8,16},{12,20},{16,0},{20,4},{24,8},{28,12},{1,25},{... | collective-permute-start | bytes 98312 | tf_op jit(solution)/shard_map/ppermute | solution.py:192
  6.1 0.2 %collective-permute-start.2 = (bf16[1,2,64,128]{3,2,1,0:T(8,128)(2,1)S(1)}, bf16[1,2,64,128]{3,2,1,0:T(8,128)(2,1)S(1)}, u32[]{:S(2)}, u32[]{:S(2)}) collective-permute-start(bf16[1,2,64,128]{3,2,1,0:T(8,128)(2,1)S(1)} %maximum_bitcast_fusion), channel_id=1, source_target_pairs={{0,8},{4,12},{8,0},{12,4},{16,24},{20,28},{24,16},{28,20},{1,9},{5... | collective-permute-start | bytes 98312 | tf_op jit(solution)/shard_map/ppermute | solution.py:192
  6.4 0.7 %collective-permute-done = bf16[1,2,64,128]{3,2,1,0:T(8,128)(2,1)S(1)} collective-permute-done((bf16[1,2,64,128]{3,2,1,0:T(8,128)(2,1)S(1)}, bf16[1,2,64,128]{3,2,1,0:T(8,128)(2,1)S(1)}, u32[]{:S(2)}, u32[]{:S(2)}) %collective-permute-start) | collective-permute-done | bytes 32800 | tf_op jit(solution)/shard_map/ppermute | solution.py:192
  7.0 2.6 %collective-permute-done.1 = bf16[1,2,64,128]{3,2,1,0:T(8,128)(2,1)S(1)} collective-permute-done((bf16[1,2,64,128]{3,2,1,0:T(8,128)(2,1)S(1)}, bf16[1,2,64,128]{3,2,1,0:T(8,128)(2,1)S(1)}, u32[]{:S(2)}, u32[]{:S(2)}) %collective-permute-start.1) | collective-permute-done | bytes 32800 | tf_op jit(solution)/shard_map/ppermute | solution.py:192
  9.6 0.4 %collective-permute-done.2 = bf16[1,2,64,128]{3,2,1,0:T(8,128)(2,1)S(1)} collective-permute-done((bf16[1,2,64,128]{3,2,1,0:T(8,128)(2,1)S(1)}, bf16[1,2,64,128]{3,2,1,0:T(8,128)(2,1)S(1)}, u32[]{:S(2)}, u32[]{:S(2)}) %collective-permute-start.2) | collective-permute-done | bytes 32800 | tf_op jit(solution)/shard_map/ppermute | solution.py:192
  10.1 1.6 %collective-permute-start.4 = (bf16[4,2,64,128]{3,2,1,0:T(8,128)(2,1)S(1)}, bf16[4,2,64,128]{3,2,1,0:T(8,128)(2,1)S(1)}, u32[]{:S(2)}, u32[]{:S(2)}) collective-permute-start(bf16[4,2,64,128]{3,2,1,0:T(8,128)(2,1)S(1)} %pad_maximum_fusion.refs_1_), channel_id=1, source_target_pairs={{0,4},{4,0},{8,12},{12,8},{16,20},{20,16},{24,28},{28,24},{1,5},{5... | collective-permute-start | bytes 393224 | tf_op jit(solution)/shard_map/ppermute | solution.py:176
  11.6 1.5 %collective-permute-start.7 = (bf16[4,2,64,128]{3,2,1,0:T(8,128)(2,1)S(1)}, bf16[4,2,64,128]{3,2,1,0:T(8,128)(2,1)S(1)}, u32[]{:S(2)}, u32[]{:S(2)}) collective-permute-start(bf16[4,2,64,128]{3,2,1,0:T(8,128)(2,1)S(1)} %pad_maximum_fusion.refs_1_), channel_id=1, source_target_pairs={{0,6},{1,7},{2,4},{3,5},{4,2},{5,3},{6,0},{7,1},{8,14},{9,15},{10,... | collective-permute-start | bytes 393224 | tf_op jit(solution)/shard_map/ppermute | solution.py:176
  13.1 0.5 %collective-permute-start.3 = (bf16[4,2,64,128]{3,2,1,0:T(8,128)(2,1)S(1)}, bf16[4,2,64,128]{3,2,1,0:T(8,128)(2,1)S(1)}, u32[]{:S(2)}, u32[]{:S(2)}) collective-permute-start(bf16[4,2,64,128]{3,2,1,0:T(8,128)(2,1)S(1)} %pad_maximum_fusion.refs_1_), channel_id=1, source_target_pairs={{0,2},{1,3},{2,0},{3,1},{4,6},{5,7},{6,4},{7,5},{8,10},{9,11},{10,... | collective-permute-start | bytes 393224 | tf_op jit(solution)/shard_map/ppermute | solution.py:176
  13.6 0.1 collective-permute-start.5
  13.7 0.0 copy-start.1
  13.7 0.5 %collective-permute-start.6 = (bf16[4,2,32,128]{3,2,1,0:T(8,128)(2,1)S(1)}, bf16[4,2,32,128]{3,2,1,0:T(8,128)(2,1)S(1)}, u32[]{:S(2)}, u32[]{:S(2)}) collective-permute-start(bf16[4,2,32,128]{3,2,1,0:T(8,128)(2,1)S(1)} %get-tuple-element.55), channel_id=1, source_target_pairs={{0,1},{1,0},{2,3},{3,2},{4,5},{5,4},{6,7},{7,6},{8,9},{9,8},{10,11... | collective-permute-start | bytes 196616 | tf_op jit(solution)/shard_map/ppermute | solution.py:176
  14.2 0.0 copy-done
  14.2 0.2 copy-done.1
  14.4 1.2 %shard_map.46 = (f32[8,256]{1,0:T(8,128)S(1)}, f32[4,128,256]{2,1,0:T(8,128)S(1)}, s32[1,256]{1,0:T(1,128)S(1)}, bf16[4,128,256]{2,1,0:T(8,128)(2,1)S(1)}) custom-call(bf16[256,512]{1,0:T(8,128)(2,1)S(1)} %bitcast.4, bf16[4,2,64,128]{3,2,1,0:T(8,128)(2,1)S(1)} %pad_maximum_fusion.refs_1_, s32[1,4]{1,0:T(1,128)S(1)} %copy-done.1), custom_call_target="tpu_custom_call" | custom-call | flops 1 | bytes 1 | tf_op jit(solution)/shard_map/pallas_call | solution.py:164
  15.6 0.0 collective-permute-done.5.refs_1_
  15.6 0.0 collective-permute-done.6.refs_2_
  15.6 0.4 %shard_map.47 = (f32[8,256]{1,0:T(8,128)S(1)}, f32[4,128,256]{2,1,0:T(8,128)S(1)}) custom-call(bf16[4,128,256]{2,1,0:T(8,128)(2,1)S(1)} %get-tuple-element.33.refs_0_, bf16[4,2,32,128]{3,2,1,0:T(8,128)(2,1)S(1)} %collective-permute-done.5.refs_1_, bf16[4,2,32,128]{3,2,1,0:T(8,128)(2,1)S(1)} %collective-permute-done.6.refs_2_, ...), custom_call_target="tpu_custom_call" | custom-call | flops 1 | bytes 1 | tf_op jit(solution)/shard_map/pallas_call | solution.py:164
  16.1 0.1 collective-permute-done.4.refs_1_
  16.2 0.4 %shard_map.48 = (f32[8,256]{1,0:T(8,128)S(1)}, f32[4,128,256]{2,1,0:T(8,128)S(1)}) custom-call(bf16[4,128,256]{2,1,0:T(8,128)(2,1)S(1)} %get-tuple-element.33.refs_0_, bf16[4,2,64,128]{3,2,1,0:T(8,128)(2,1)S(1)} %collective-permute-done.4.refs_1_, f32[8,256]{1,0:T(8,128)S(1)} %get-tuple-element.40.refs_2_, f32[4,128,256]{2,1,0:T(8,128)S(1)} %get-tuple-element.41.refs_3_, ...), custom_call_target="tpu_custom_call" | custom-call | flops 1 | bytes 1 | tf_op jit(solution)/shard_map/pallas_call | solution.py:164
  16.6 1.3 %collective-permute-done.7.refs_1_ = bf16[4,2,64,128]{3,2,1,0:T(8,128)(2,1)S(1)} collective-permute-done((bf16[4,2,64,128]{3,2,1,0:T(8,128)(2,1)S(1)}, bf16[4,2,64,128]{3,2,1,0:T(8,128)(2,1)S(1)}, u32[]{:S(2)}, u32[]{:S(2)}) %collective-permute-start.7) | collective-permute-done | bytes 131104 | tf_op jit(solution)/shard_map/ppermute | solution.py:176
  17.9 0.0 collective-permute-start.10
  17.9 0.5 %collective-permute-start.9 = (bf16[4,2,64,128]{3,2,1,0:T(8,128)(2,1)S(1)}, bf16[4,2,64,128]{3,2,1,0:T(8,128)(2,1)S(1)}, u32[]{:S(2)}, u32[]{:S(2)}) collective-permute-start(bf16[4,2,64,128]{3,2,1,0:T(8,128)(2,1)S(1)} %collective-permute-done.4.refs_1_), channel_id=1, source_target_pairs={{0,1},{1,0},{2,3},{3,2},{4,5},{5,4},{6,7},{7,6},{8,9},{9,8},{10,11... | collective-permute-start | bytes 393224 | tf_op jit(solution)/shard_map/ppermute | solution.py:176
  18.4 0.4 %shard_map.49 = (f32[8,256]{1,0:T(8,128)S(1)}, f32[4,128,256]{2,1,0:T(8,128)S(1)}) custom-call(bf16[4,128,256]{2,1,0:T(8,128)(2,1)S(1)} %get-tuple-element.33.refs_0_, bf16[4,2,64,128]{3,2,1,0:T(8,128)(2,1)S(1)} %collective-permute-done.7.refs_1_, f32[8,256]{1,0:T(8,128)S(1)} %get-tuple-element.45.refs_2_, f32[4,128,256]{2,1,0:T(8,128)S(1)} %get-tuple-element.46.refs_3_, ...), custom_call_target="tpu_custom_call" | custom-call | flops 1 | bytes 1 | tf_op jit(solution)/shard_map/pallas_call | solution.py:164
  18.8 0.3 %collective-permute-done.3.refs_3_ = bf16[4,2,64,128]{3,2,1,0:T(8,128)(2,1)S(1)} collective-permute-done((bf16[4,2,64,128]{3,2,1,0:T(8,128)(2,1)S(1)}, bf16[4,2,64,128]{3,2,1,0:T(8,128)(2,1)S(1)}, u32[]{:S(2)}, u32[]{:S(2)}) %collective-permute-start.3) | collective-permute-done | bytes 131104 | tf_op jit(solution)/shard_map/ppermute | solution.py:176
  19.2 0.0 collective-permute-start.8
  19.2 0.0 collective-permute-done.10.refs_2_
  19.2 0.2 collective-permute-done.9.refs_1_
  19.4 0.6 %shard_map.50 = (f32[8,256]{1,0:T(8,128)S(1)}, f32[4,128,256]{2,1,0:T(8,128)S(1)}) custom-call(bf16[4,128,256]{2,1,0:T(8,128)(2,1)S(1)} %get-tuple-element.33.refs_0_, bf16[4,2,64,128]{3,2,1,0:T(8,128)(2,1)S(1)} %collective-permute-done.9.refs_1_, bf16[4,2,64,128]{3,2,1,0:T(8,128)(2,1)S(1)} %collective-permute-done.10.refs_2_, ...), custom_call_target="tpu_custom_call" | custom-call | flops 1 | bytes 1 | tf_op jit(solution)/shard_map/pallas_call | solution.py:164
  20.0 0.5 %collective-permute-done.8.refs_1_ = bf16[4,2,64,128]{3,2,1,0:T(8,128)(2,1)S(1)} collective-permute-done((bf16[4,2,64,128]{3,2,1,0:T(8,128)(2,1)S(1)}, bf16[4,2,64,128]{3,2,1,0:T(8,128)(2,1)S(1)}, u32[]{:S(2)}, u32[]{:S(2)}) %collective-permute-start.8) | collective-permute-done | bytes 131104 | tf_op jit(solution)/shard_map/ppermute | solution.py:176
  20.5 1.2 %shard_map.51 = bf16[256,512]{1,0:T(8,128)(2,1)} custom-call(bf16[4,128,256]{2,1,0:T(8,128)(2,1)S(1)} %get-tuple-element.33.refs_0_, bf16[4,2,64,128]{3,2,1,0:T(8,128)(2,1)S(1)} %collective-permute-done.8.refs_1_, f32[8,256]{1,0:T(8,128)S(1)} %get-tuple-element.53.refs_2_, f32[4,128,256]{2,1,0:T(8,128)S(1)} %get-tuple-element.54.refs_3_, ...), custom_call_target="tpu_custom_call" | custom-call | flops 1 | bytes 1 | tf_op jit(solution)/shard_map/pallas_call | solution.py:164
  (2 shorter events, 0.0 us)
Async XLA Ops:
  0.7 13.5 %copy-start = (bf16[1,256,512]{2,1,0:T(8,128)(2,1)S(1)}, bf16[1,256,512]{2,1,0:T(8,128)(2,1)}, u32[]{:S(2)}) copy-start(bf16[1,256,512]{2,1,0:T(8,128)(2,1)} %param.4) | copy-start | bytes 786436
  0.7 6.3 %collective-permute-start = (bf16[1,2,64,128]{3,2,1,0:T(8,128)(2,1)S(1)}, bf16[1,2,64,128]{3,2,1,0:T(8,128)(2,1)S(1)}, u32[]{:S(2)}, u32[]{:S(2)}) collective-permute-start(bf16[1,2,64,128]{3,2,1,0:T(8,128)(2,1)S(1)} %maximum_bitcast_fusion), channel_id=1, source_target_pairs={{0,16},{4,20},{8,24},{12,28},{16,0},{20,4},{24,8},{28,12},{1,17},{... | collective-permute-start | bytes 98312 | tf_op jit(solution)/shard_map/ppermute | solution.py:192
  4.8 4.8 %collective-permute-start.1 = (bf16[1,2,64,128]{3,2,1,0:T(8,128)(2,1)S(1)}, bf16[1,2,64,128]{3,2,1,0:T(8,128)(2,1)S(1)}, u32[]{:S(2)}, u32[]{:S(2)}) collective-permute-start(bf16[1,2,64,128]{3,2,1,0:T(8,128)(2,1)S(1)} %maximum_bitcast_fusion), channel_id=1, source_target_pairs={{0,24},{4,28},{8,16},{12,20},{16,0},{20,4},{24,8},{28,12},{1,25},{... | collective-permute-start | bytes 98312 | tf_op jit(solution)/shard_map/ppermute | solution.py:192
  6.1 3.9 %collective-permute-start.2 = (bf16[1,2,64,128]{3,2,1,0:T(8,128)(2,1)S(1)}, bf16[1,2,64,128]{3,2,1,0:T(8,128)(2,1)S(1)}, u32[]{:S(2)}, u32[]{:S(2)}) collective-permute-start(bf16[1,2,64,128]{3,2,1,0:T(8,128)(2,1)S(1)} %maximum_bitcast_fusion), channel_id=1, source_target_pairs={{0,8},{4,12},{8,0},{12,4},{16,24},{20,28},{24,16},{28,20},{1,9},{5... | collective-permute-start | bytes 98312 | tf_op jit(solution)/shard_map/ppermute | solution.py:192
  10.1 6.1 %collective-permute-start.4 = (bf16[4,2,64,128]{3,2,1,0:T(8,128)(2,1)S(1)}, bf16[4,2,64,128]{3,2,1,0:T(8,128)(2,1)S(1)}, u32[]{:S(2)}, u32[]{:S(2)}) collective-permute-start(bf16[4,2,64,128]{3,2,1,0:T(8,128)(2,1)S(1)} %pad_maximum_fusion.refs_1_), channel_id=1, source_target_pairs={{0,4},{4,0},{8,12},{12,8},{16,20},{20,16},{24,28},{28,24},{1,5},{5... | collective-permute-start | bytes 393224 | tf_op jit(solution)/shard_map/ppermute | solution.py:176
  11.6 6.2 %collective-permute-start.7 = (bf16[4,2,64,128]{3,2,1,0:T(8,128)(2,1)S(1)}, bf16[4,2,64,128]{3,2,1,0:T(8,128)(2,1)S(1)}, u32[]{:S(2)}, u32[]{:S(2)}) collective-permute-start(bf16[4,2,64,128]{3,2,1,0:T(8,128)(2,1)S(1)} %pad_maximum_fusion.refs_1_), channel_id=1, source_target_pairs={{0,6},{1,7},{2,4},{3,5},{4,2},{5,3},{6,0},{7,1},{8,14},{9,15},{10,... | collective-permute-start | bytes 393224 | tf_op jit(solution)/shard_map/ppermute | solution.py:176
  13.1 6.1 %collective-permute-start.3 = (bf16[4,2,64,128]{3,2,1,0:T(8,128)(2,1)S(1)}, bf16[4,2,64,128]{3,2,1,0:T(8,128)(2,1)S(1)}, u32[]{:S(2)}, u32[]{:S(2)}) collective-permute-start(bf16[4,2,64,128]{3,2,1,0:T(8,128)(2,1)S(1)} %pad_maximum_fusion.refs_1_), channel_id=1, source_target_pairs={{0,2},{1,3},{2,0},{3,1},{4,6},{5,7},{6,4},{7,5},{8,10},{9,11},{10,... | collective-permute-start | bytes 393224 | tf_op jit(solution)/shard_map/ppermute | solution.py:176
  13.6 2.0 %collective-permute-start.5 = (bf16[4,2,32,128]{3,2,1,0:T(8,128)(2,1)S(1)}, bf16[4,2,32,128]{3,2,1,0:T(8,128)(2,1)S(1)}, u32[]{:S(2)}, u32[]{:S(2)}) collective-permute-start(bf16[4,2,32,128]{3,2,1,0:T(8,128)(2,1)S(1)} %get-tuple-element.56), channel_id=1, source_target_pairs={{0,1},{1,0},{2,3},{3,2},{4,5},{5,4},{6,7},{7,6},{8,9},{9,8},{10,11... | collective-permute-start | bytes 196616 | tf_op jit(solution)/shard_map/ppermute | solution.py:176
  13.7 0.7 %copy-start.1 = (s32[1,4]{1,0:T(1,128)S(1)}, s32[1,4]{1,0:T(1,128)}, u32[]{:S(2)}) copy-start(s32[1,4]{1,0:T(1,128)} %refs_2_.1) | copy-start | bytes 52
  13.7 1.9 %collective-permute-start.6 = (bf16[4,2,32,128]{3,2,1,0:T(8,128)(2,1)S(1)}, bf16[4,2,32,128]{3,2,1,0:T(8,128)(2,1)S(1)}, u32[]{:S(2)}, u32[]{:S(2)}) collective-permute-start(bf16[4,2,32,128]{3,2,1,0:T(8,128)(2,1)S(1)} %get-tuple-element.55), channel_id=1, source_target_pairs={{0,1},{1,0},{2,3},{3,2},{4,5},{5,4},{6,7},{7,6},{8,9},{9,8},{10,11... | collective-permute-start | bytes 196616 | tf_op jit(solution)/shard_map/ppermute | solution.py:176
  17.9 1.3 %collective-permute-start.10 = (bf16[4,2,64,128]{3,2,1,0:T(8,128)(2,1)S(1)}, bf16[4,2,64,128]{3,2,1,0:T(8,128)(2,1)S(1)}, u32[]{:S(2)}, u32[]{:S(2)}) collective-permute-start(bf16[4,2,64,128]{3,2,1,0:T(8,128)(2,1)S(1)} %collective-permute-done.7.refs_1_), channel_id=1, source_target_pairs={{0,1},{1,0},{2,3},{3,2},{4,5},{5,4},{6,7},{7,6},{8,9},{9,8},{10,11... | collective-permute-start | bytes 393224 | tf_op jit(solution)/shard_map/ppermute | solution.py:176
  17.9 1.5 %collective-permute-start.9 = (bf16[4,2,64,128]{3,2,1,0:T(8,128)(2,1)S(1)}, bf16[4,2,64,128]{3,2,1,0:T(8,128)(2,1)S(1)}, u32[]{:S(2)}, u32[]{:S(2)}) collective-permute-start(bf16[4,2,64,128]{3,2,1,0:T(8,128)(2,1)S(1)} %collective-permute-done.4.refs_1_), channel_id=1, source_target_pairs={{0,1},{1,0},{2,3},{3,2},{4,5},{5,4},{6,7},{7,6},{8,9},{9,8},{10,11... | collective-permute-start | bytes 393224 | tf_op jit(solution)/shard_map/ppermute | solution.py:176
  19.2 1.3 %collective-permute-start.8 = (bf16[4,2,64,128]{3,2,1,0:T(8,128)(2,1)S(1)}, bf16[4,2,64,128]{3,2,1,0:T(8,128)(2,1)S(1)}, u32[]{:S(2)}, u32[]{:S(2)}) collective-permute-start(bf16[4,2,64,128]{3,2,1,0:T(8,128)(2,1)S(1)} %collective-permute-done.3.refs_3_), channel_id=1, source_target_pairs={{0,1},{1,0},{2,3},{3,2},{4,5},{5,4},{6,7},{7,6},{8,9},{9,8},{10,11... | collective-permute-start | bytes 393224 | tf_op jit(solution)/shard_map/ppermute | solution.py:176

commit v21 on v20

--- a/solution.py
+++ b/solution.py
@@ -206,8 +206,8 @@
         own = same_parity_blocks(jnp.stack([key_rows[seq], value_rows[seq]]), "ctx")
         half = own.shape[2] // 2
 
+        corner = exchange(own, ("ctx", "head"), lax.axis_size("head") + 2)
         across = exchange(own, "ctx", 1)
-        corner = exchange(own, ("ctx", "head"), lax.axis_size("head") + 2)
         far = exchange(own, "head", 2)
         near = [exchange(own[:, :, :half], "head", 1), exchange(own[:, :, half:], "head", 1)]
         stats, sums, starts, turned = run([(0, 0, 0)], "first", queries=queries[seq], kvs=[own], state=())
@@ -216,7 +216,7 @@
 
         across, stats, sums = lax.optimization_barrier((across, stats, sums))
         stats, sums = run([(1, 0, 0)], "middle", kvs=[across], state=(stats, sums, starts))
-        across, corner, stats, sums = lax.optimization_barrier((across, corner, stats, sums))
+        corner, across, stats, sums = lax.optimization_barrier((corner, across, stats, sums))
         near = [exchange(across, "head", 1), exchange(corner, "head", 1)]
         stats, sums = run([(1, 2, 0)], "middle", kvs=[corner], state=(stats, sums, starts))
         far, stats, sums = lax.optimization_barrier((far, stats, sums))

time: 22 us -> 22 us (level)
  no operation moved by 1% of the time
where the time goes in v21:
time: 22 us; the launch traced here: 21.7 us
  starting transfers between devices  10.2 us (46%)
  waiting for transfers between devices  6.15 us (28%)
  Pallas kernels  4.29 us (20%)
  other arithmetic  0.76 us (3%)
    ppermute x3, starting transfers between devices, same_parity_blocks(): moved.append(lax.ppermute(held, axis, targets))  5.62 us
    ppermute x8, starting transfers between devices, exchange(): lax.ppermute(piece, axis, [(i, i ^ bits) for i in range(lax.axis_size(axi...  4.62 us
    pallas_call x6, Pallas kernels, attend(): pl.pallas_call(functools.partial(attention_kernel, head_size, parts, kind...  4.29 us
    ppermute x3, waiting for transfers between devices, same_parity_blocks(): moved.append(lax.ppermute(held, axis, targets))  3.68 us
    ppermute x8, waiting for transfers between devices, exchange(): lax.ppermute(piece, axis, [(i, i ^ bits) for i in range(lax.axis_size(axi...  2.47 us
    broadcast_in_dim x1, other arithmetic, same_parity_blocks(): held = block[None]  0.74 us
  transfers between devices with their start and end apart: 11, of which 8 were waited for; matrix products, arithmetic and copies ran while one was open for 0% of the time, Pallas kernels for 14%

profile of v21, /device:TPU:0, one launch (start us, length us, event | category | flops | bytes accessed | tf_op | source)
XLA Modules:
  0.0 21.7 jit_solution(5703825681472053393)
XLA Ops:
  0.0 0.7 %maximum_bitcast_fusion = bf16[1,2,64,128]{3,2,1,0:T(8,128)(2,1)S(1)} fusion(bf16[1,64,128]{2,1,0:T(8,128)(2,1)} %param.6, bf16[1,64,128]{2,1,0:T(8,128)(2,1)} %param.5), kind=kLoop, calls=%fused_computation.1 | loop fusion | flops 16384 | bytes 65536 | tf_op jit(solution)/shard_map/broadcast_in_dim | solution.py:181
  0.7 0.0 copy-start
  0.7 4.0 %collective-permute-start = (bf16[1,2,64,128]{3,2,1,0:T(8,128)(2,1)S(1)}, bf16[1,2,64,128]{3,2,1,0:T(8,128)(2,1)S(1)}, u32[]{:S(2)}, u32[]{:S(2)}) collective-permute-start(bf16[1,2,64,128]{3,2,1,0:T(8,128)(2,1)S(1)} %maximum_bitcast_fusion), channel_id=1, source_target_pairs={{0,16},{4,20},{8,24},{12,28},{16,0},{20,4},{24,8},{28,12},{1,17},{... | collective-permute-start | bytes 98312 | tf_op jit(solution)/shard_map/ppermute | solution.py:192
  4.8 1.3 %collective-permute-start.1 = (bf16[1,2,64,128]{3,2,1,0:T(8,128)(2,1)S(1)}, bf16[1,2,64,128]{3,2,1,0:T(8,128)(2,1)S(1)}, u32[]{:S(2)}, u32[]{:S(2)}) collective-permute-start(bf16[1,2,64,128]{3,2,1,0:T(8,128)(2,1)S(1)} %maximum_bitcast_fusion), channel_id=1, source_target_pairs={{0,24},{4,28},{8,16},{12,20},{16,0},{20,4},{24,8},{28,12},{1,25},{... | collective-permute-start | bytes 98312 | tf_op jit(solution)/shard_map/ppermute | solution.py:192
  6.1 0.2 %collective-permute-start.2 = (bf16[1,2,64,128]{3,2,1,0:T(8,128)(2,1)S(1)}, bf16[1,2,64,128]{3,2,1,0:T(8,128)(2,1)S(1)}, u32[]{:S(2)}, u32[]{:S(2)}) collective-permute-start(bf16[1,2,64,128]{3,2,1,0:T(8,128)(2,1)S(1)} %maximum_bitcast_fusion), channel_id=1, source_target_pairs={{0,8},{4,12},{8,0},{12,4},{16,24},{20,28},{24,16},{28,20},{1,9},{5... | collective-permute-start | bytes 98312 | tf_op jit(solution)/shard_map/ppermute | solution.py:192
  6.4 0.7 %collective-permute-done = bf16[1,2,64,128]{3,2,1,0:T(8,128)(2,1)S(1)} collective-permute-done((bf16[1,2,64,128]{3,2,1,0:T(8,128)(2,1)S(1)}, bf16[1,2,64,128]{3,2,1,0:T(8,128)(2,1)S(1)}, u32[]{:S(2)}, u32[]{:S(2)}) %collective-permute-start) | collective-permute-done | bytes 32800 | tf_op jit(solution)/shard_map/ppermute | solution.py:192
  7.0 2.6 %collective-permute-done.1 = bf16[1,2,64,128]{3,2,1,0:T(8,128)(2,1)S(1)} collective-permute-done((bf16[1,2,64,128]{3,2,1,0:T(8,128)(2,1)S(1)}, bf16[1,2,64,128]{3,2,1,0:T(8,128)(2,1)S(1)}, u32[]{:S(2)}, u32[]{:S(2)}) %collective-permute-start.1) | collective-permute-done | bytes 32800 | tf_op jit(solution)/shard_map/ppermute | solution.py:192
  9.6 0.4 %collective-permute-done.2 = bf16[1,2,64,128]{3,2,1,0:T(8,128)(2,1)S(1)} collective-permute-done((bf16[1,2,64,128]{3,2,1,0:T(8,128)(2,1)S(1)}, bf16[1,2,64,128]{3,2,1,0:T(8,128)(2,1)S(1)}, u32[]{:S(2)}, u32[]{:S(2)}) %collective-permute-start.2) | collective-permute-done | bytes 32800 | tf_op jit(solution)/shard_map/ppermute | solution.py:192
  10.1 1.6 %collective-permute-start.5 = (bf16[4,2,64,128]{3,2,1,0:T(8,128)(2,1)S(1)}, bf16[4,2,64,128]{3,2,1,0:T(8,128)(2,1)S(1)}, u32[]{:S(2)}, u32[]{:S(2)}) collective-permute-start(bf16[4,2,64,128]{3,2,1,0:T(8,128)(2,1)S(1)} %pad_maximum_fusion.refs_1_), channel_id=1, source_target_pairs={{0,4},{4,0},{8,12},{12,8},{16,20},{20,16},{24,28},{28,24},{1,5},{5... | collective-permute-start | bytes 393224 | tf_op jit(solution)/shard_map/ppermute | solution.py:176
  11.6 1.5 %collective-permute-start.4 = (bf16[4,2,64,128]{3,2,1,0:T(8,128)(2,1)S(1)}, bf16[4,2,64,128]{3,2,1,0:T(8,128)(2,1)S(1)}, u32[]{:S(2)}, u32[]{:S(2)}) collective-permute-start(bf16[4,2,64,128]{3,2,1,0:T(8,128)(2,1)S(1)} %pad_maximum_fusion.refs_1_), channel_id=1, source_target_pairs={{0,6},{1,7},{2,4},{3,5},{4,2},{5,3},{6,0},{7,1},{8,14},{9,15},{10,... | collective-permute-start | bytes 393224 | tf_op jit(solution)/shard_map/ppermute | solution.py:176
  13.1 0.5 %collective-permute-start.3 = (bf16[4,2,64,128]{3,2,1,0:T(8,128)(2,1)S(1)}, bf16[4,2,64,128]{3,2,1,0:T(8,128)(2,1)S(1)}, u32[]{:S(2)}, u32[]{:S(2)}) collective-permute-start(bf16[4,2,64,128]{3,2,1,0:T(8,128)(2,1)S(1)} %pad_maximum_fusion.refs_1_), channel_id=1, source_target_pairs={{0,2},{1,3},{2,0},{3,1},{4,6},{5,7},{6,4},{7,5},{8,10},{9,11},{10,... | collective-permute-start | bytes 393224 | tf_op jit(solution)/shard_map/ppermute | solution.py:176
  13.6 0.1 collective-permute-start.6
  13.7 0.0 copy-start.1
  13.7 0.5 %collective-permute-start.7 = (bf16[4,2,32,128]{3,2,1,0:T(8,128)(2,1)S(1)}, bf16[4,2,32,128]{3,2,1,0:T(8,128)(2,1)S(1)}, u32[]{:S(2)}, u32[]{:S(2)}) collective-permute-start(bf16[4,2,32,128]{3,2,1,0:T(8,128)(2,1)S(1)} %get-tuple-element.55), channel_id=1, source_target_pairs={{0,1},{1,0},{2,3},{3,2},{4,5},{5,4},{6,7},{7,6},{8,9},{9,8},{10,11... | collective-permute-start | bytes 196616 | tf_op jit(solution)/shard_map/ppermute | solution.py:176
  14.2 0.0 copy-done
  14.2 0.2 copy-done.1
  14.4 1.2 %shard_map.46 = (f32[8,256]{1,0:T(8,128)S(1)}, f32[4,128,256]{2,1,0:T(8,128)S(1)}, s32[1,256]{1,0:T(1,128)S(1)}, bf16[4,128,256]{2,1,0:T(8,128)(2,1)S(1)}) custom-call(bf16[256,512]{1,0:T(8,128)(2,1)S(1)} %bitcast.4, bf16[4,2,64,128]{3,2,1,0:T(8,128)(2,1)S(1)} %pad_maximum_fusion.refs_1_, s32[1,4]{1,0:T(1,128)S(1)} %copy-done.1), custom_call_target="tpu_custom_call" | custom-call | flops 1 | bytes 1 | tf_op jit(solution)/shard_map/pallas_call | solution.py:164
  15.6 0.0 collective-permute-done.6.refs_1_
  15.6 0.0 collective-permute-done.7.refs_2_
  15.6 0.4 %shard_map.47 = (f32[8,256]{1,0:T(8,128)S(1)}, f32[4,128,256]{2,1,0:T(8,128)S(1)}) custom-call(bf16[4,128,256]{2,1,0:T(8,128)(2,1)S(1)} %get-tuple-element.33.refs_0_, bf16[4,2,32,128]{3,2,1,0:T(8,128)(2,1)S(1)} %collective-permute-done.6.refs_1_, bf16[4,2,32,128]{3,2,1,0:T(8,128)(2,1)S(1)} %collective-permute-done.7.refs_2_, ...), custom_call_target="tpu_custom_call" | custom-call | flops 1 | bytes 1 | tf_op jit(solution)/shard_map/pallas_call | solution.py:164
  16.1 0.1 collective-permute-done.5.refs_1_
  16.2 0.4 %shard_map.48 = (f32[8,256]{1,0:T(8,128)S(1)}, f32[4,128,256]{2,1,0:T(8,128)S(1)}) custom-call(bf16[4,128,256]{2,1,0:T(8,128)(2,1)S(1)} %get-tuple-element.33.refs_0_, bf16[4,2,64,128]{3,2,1,0:T(8,128)(2,1)S(1)} %collective-permute-done.5.refs_1_, f32[8,256]{1,0:T(8,128)S(1)} %get-tuple-element.40.refs_2_, f32[4,128,256]{2,1,0:T(8,128)S(1)} %get-tuple-element.41.refs_3_, ...), custom_call_target="tpu_custom_call" | custom-call | flops 1 | bytes 1 | tf_op jit(solution)/shard_map/pallas_call | solution.py:164
  16.6 1.3 %collective-permute-done.4.refs_1_ = bf16[4,2,64,128]{3,2,1,0:T(8,128)(2,1)S(1)} collective-permute-done((bf16[4,2,64,128]{3,2,1,0:T(8,128)(2,1)S(1)}, bf16[4,2,64,128]{3,2,1,0:T(8,128)(2,1)S(1)}, u32[]{:S(2)}, u32[]{:S(2)}) %collective-permute-start.4) | collective-permute-done | bytes 131104 | tf_op jit(solution)/shard_map/ppermute | solution.py:176
  17.9 0.0 collective-permute-start.10
  17.9 0.5 %collective-permute-start.9 = (bf16[4,2,64,128]{3,2,1,0:T(8,128)(2,1)S(1)}, bf16[4,2,64,128]{3,2,1,0:T(8,128)(2,1)S(1)}, u32[]{:S(2)}, u32[]{:S(2)}) collective-permute-start(bf16[4,2,64,128]{3,2,1,0:T(8,128)(2,1)S(1)} %collective-permute-done.5.refs_1_), channel_id=1, source_target_pairs={{0,1},{1,0},{2,3},{3,2},{4,5},{5,4},{6,7},{7,6},{8,9},{9,8},{10,11... | collective-permute-start | bytes 393224 | tf_op jit(solution)/shard_map/ppermute | solution.py:176
  18.4 0.4 %shard_map.49 = (f32[8,256]{1,0:T(8,128)S(1)}, f32[4,128,256]{2,1,0:T(8,128)S(1)}) custom-call(bf16[4,128,256]{2,1,0:T(8,128)(2,1)S(1)} %get-tuple-element.33.refs_0_, bf16[4,2,64,128]{3,2,1,0:T(8,128)(2,1)S(1)} %collective-permute-done.4.refs_1_, f32[8,256]{1,0:T(8,128)S(1)} %get-tuple-element.45.refs_2_, f32[4,128,256]{2,1,0:T(8,128)S(1)} %get-tuple-element.46.refs_3_, ...), custom_call_target="tpu_custom_call" | custom-call | flops 1 | bytes 1 | tf_op jit(solution)/shard_map/pallas_call | solution.py:164
  18.8 0.3 %collective-permute-done.3.refs_3_ = bf16[4,2,64,128]{3,2,1,0:T(8,128)(2,1)S(1)} collective-permute-done((bf16[4,2,64,128]{3,2,1,0:T(8,128)(2,1)S(1)}, bf16[4,2,64,128]{3,2,1,0:T(8,128)(2,1)S(1)}, u32[]{:S(2)}, u32[]{:S(2)}) %collective-permute-start.3) | collective-permute-done | bytes 131104 | tf_op jit(solution)/shard_map/ppermute | solution.py:176
  19.2 0.0 collective-permute-start.8
  19.2 0.0 collective-permute-done.10.refs_2_
  19.2 0.2 collective-permute-done.9.refs_1_
  19.4 0.6 %shard_map.50 = (f32[8,256]{1,0:T(8,128)S(1)}, f32[4,128,256]{2,1,0:T(8,128)S(1)}) custom-call(bf16[4,128,256]{2,1,0:T(8,128)(2,1)S(1)} %get-tuple-element.33.refs_0_, bf16[4,2,64,128]{3,2,1,0:T(8,128)(2,1)S(1)} %collective-permute-done.9.refs_1_, bf16[4,2,64,128]{3,2,1,0:T(8,128)(2,1)S(1)} %collective-permute-done.10.refs_2_, ...), custom_call_target="tpu_custom_call" | custom-call | flops 1 | bytes 1 | tf_op jit(solution)/shard_map/pallas_call | solution.py:164
  20.0 0.5 %collective-permute-done.8.refs_1_ = bf16[4,2,64,128]{3,2,1,0:T(8,128)(2,1)S(1)} collective-permute-done((bf16[4,2,64,128]{3,2,1,0:T(8,128)(2,1)S(1)}, bf16[4,2,64,128]{3,2,1,0:T(8,128)(2,1)S(1)}, u32[]{:S(2)}, u32[]{:S(2)}) %collective-permute-start.8) | collective-permute-done | bytes 131104 | tf_op jit(solution)/shard_map/ppermute | solution.py:176
  20.5 1.2 %shard_map.51 = bf16[256,512]{1,0:T(8,128)(2,1)} custom-call(bf16[4,128,256]{2,1,0:T(8,128)(2,1)S(1)} %get-tuple-element.33.refs_0_, bf16[4,2,64,128]{3,2,1,0:T(8,128)(2,1)S(1)} %collective-permute-done.8.refs_1_, f32[8,256]{1,0:T(8,128)S(1)} %get-tuple-element.53.refs_2_, f32[4,128,256]{2,1,0:T(8,128)S(1)} %get-tuple-element.54.refs_3_, ...), custom_call_target="tpu_custom_call" | custom-call | flops 1 | bytes 1 | tf_op jit(solution)/shard_map/pallas_call | solution.py:164
  (2 shorter events, 0.0 us)
Async XLA Ops:
  0.7 13.5 %copy-start = (bf16[1,256,512]{2,1,0:T(8,128)(2,1)S(1)}, bf16[1,256,512]{2,1,0:T(8,128)(2,1)}, u32[]{:S(2)}) copy-start(bf16[1,256,512]{2,1,0:T(8,128)(2,1)} %param.4) | copy-start | bytes 786436
  0.7 6.3 %collective-permute-start = (bf16[1,2,64,128]{3,2,1,0:T(8,128)(2,1)S(1)}, bf16[1,2,64,128]{3,2,1,0:T(8,128)(2,1)S(1)}, u32[]{:S(2)}, u32[]{:S(2)}) collective-permute-start(bf16[1,2,64,128]{3,2,1,0:T(8,128)(2,1)S(1)} %maximum_bitcast_fusion), channel_id=1, source_target_pairs={{0,16},{4,20},{8,24},{12,28},{16,0},{20,4},{24,8},{28,12},{1,17},{... | collective-permute-start | bytes 98312 | tf_op jit(solution)/shard_map/ppermute | solution.py:192
  4.8 4.8 %collective-permute-start.1 = (bf16[1,2,64,128]{3,2,1,0:T(8,128)(2,1)S(1)}, bf16[1,2,64,128]{3,2,1,0:T(8,128)(2,1)S(1)}, u32[]{:S(2)}, u32[]{:S(2)}) collective-permute-start(bf16[1,2,64,128]{3,2,1,0:T(8,128)(2,1)S(1)} %maximum_bitcast_fusion), channel_id=1, source_target_pairs={{0,24},{4,28},{8,16},{12,20},{16,0},{20,4},{24,8},{28,12},{1,25},{... | collective-permute-start | bytes 98312 | tf_op jit(solution)/shard_map/ppermute | solution.py:192
  6.1 3.9 %collective-permute-start.2 = (bf16[1,2,64,128]{3,2,1,0:T(8,128)(2,1)S(1)}, bf16[1,2,64,128]{3,2,1,0:T(8,128)(2,1)S(1)}, u32[]{:S(2)}, u32[]{:S(2)}) collective-permute-start(bf16[1,2,64,128]{3,2,1,0:T(8,128)(2,1)S(1)} %maximum_bitcast_fusion), channel_id=1, source_target_pairs={{0,8},{4,12},{8,0},{12,4},{16,24},{20,28},{24,16},{28,20},{1,9},{5... | collective-permute-start | bytes 98312 | tf_op jit(solution)/shard_map/ppermute | solution.py:192
  10.1 6.1 %collective-permute-start.5 = (bf16[4,2,64,128]{3,2,1,0:T(8,128)(2,1)S(1)}, bf16[4,2,64,128]{3,2,1,0:T(8,128)(2,1)S(1)}, u32[]{:S(2)}, u32[]{:S(2)}) collective-permute-start(bf16[4,2,64,128]{3,2,1,0:T(8,128)(2,1)S(1)} %pad_maximum_fusion.refs_1_), channel_id=1, source_target_pairs={{0,4},{4,0},{8,12},{12,8},{16,20},{20,16},{24,28},{28,24},{1,5},{5... | collective-permute-start | bytes 393224 | tf_op jit(solution)/shard_map/ppermute | solution.py:176
  11.6 6.2 %collective-permute-start.4 = (bf16[4,2,64,128]{3,2,1,0:T(8,128)(2,1)S(1)}, bf16[4,2,64,128]{3,2,1,0:T(8,128)(2,1)S(1)}, u32[]{:S(2)}, u32[]{:S(2)}) collective-permute-start(bf16[4,2,64,128]{3,2,1,0:T(8,128)(2,1)S(1)} %pad_maximum_fusion.refs_1_), channel_id=1, source_target_pairs={{0,6},{1,7},{2,4},{3,5},{4,2},{5,3},{6,0},{7,1},{8,14},{9,15},{10,... | collective-permute-start | bytes 393224 | tf_op jit(solution)/shard_map/ppermute | solution.py:176
  13.1 6.1 %collective-permute-start.3 = (bf16[4,2,64,128]{3,2,1,0:T(8,128)(2,1)S(1)}, bf16[4,2,64,128]{3,2,1,0:T(8,128)(2,1)S(1)}, u32[]{:S(2)}, u32[]{:S(2)}) collective-permute-start(bf16[4,2,64,128]{3,2,1,0:T(8,128)(2,1)S(1)} %pad_maximum_fusion.refs_1_), channel_id=1, source_target_pairs={{0,2},{1,3},{2,0},{3,1},{4,6},{5,7},{6,4},{7,5},{8,10},{9,11},{10,... | collective-permute-start | bytes 393224 | tf_op jit(solution)/shard_map/ppermute | solution.py:176
  13.6 2.0 %collective-permute-start.6 = (bf16[4,2,32,128]{3,2,1,0:T(8,128)(2,1)S(1)}, bf16[4,2,32,128]{3,2,1,0:T(8,128)(2,1)S(1)}, u32[]{:S(2)}, u32[]{:S(2)}) collective-permute-start(bf16[4,2,32,128]{3,2,1,0:T(8,128)(2,1)S(1)} %get-tuple-element.56), channel_id=1, source_target_pairs={{0,1},{1,0},{2,3},{3,2},{4,5},{5,4},{6,7},{7,6},{8,9},{9,8},{10,11... | collective-permute-start | bytes 196616 | tf_op jit(solution)/shard_map/ppermute | solution.py:176
  13.7 0.7 %copy-start.1 = (s32[1,4]{1,0:T(1,128)S(1)}, s32[1,4]{1,0:T(1,128)}, u32[]{:S(2)}) copy-start(s32[1,4]{1,0:T(1,128)} %refs_2_.1) | copy-start | bytes 52
  13.7 1.9 %collective-permute-start.7 = (bf16[4,2,32,128]{3,2,1,0:T(8,128)(2,1)S(1)}, bf16[4,2,32,128]{3,2,1,0:T(8,128)(2,1)S(1)}, u32[]{:S(2)}, u32[]{:S(2)}) collective-permute-start(bf16[4,2,32,128]{3,2,1,0:T(8,128)(2,1)S(1)} %get-tuple-element.55), channel_id=1, source_target_pairs={{0,1},{1,0},{2,3},{3,2},{4,5},{5,4},{6,7},{7,6},{8,9},{9,8},{10,11... | collective-permute-start | bytes 196616 | tf_op jit(solution)/shard_map/ppermute | solution.py:176
  17.9 1.3 %collective-permute-start.10 = (bf16[4,2,64,128]{3,2,1,0:T(8,128)(2,1)S(1)}, bf16[4,2,64,128]{3,2,1,0:T(8,128)(2,1)S(1)}, u32[]{:S(2)}, u32[]{:S(2)}) collective-permute-start(bf16[4,2,64,128]{3,2,1,0:T(8,128)(2,1)S(1)} %collective-permute-done.4.refs_1_), channel_id=1, source_target_pairs={{0,1},{1,0},{2,3},{3,2},{4,5},{5,4},{6,7},{7,6},{8,9},{9,8},{10,11... | collective-permute-start | bytes 393224 | tf_op jit(solution)/shard_map/ppermute | solution.py:176
  17.9 1.5 %collective-permute-start.9 = (bf16[4,2,64,128]{3,2,1,0:T(8,128)(2,1)S(1)}, bf16[4,2,64,128]{3,2,1,0:T(8,128)(2,1)S(1)}, u32[]{:S(2)}, u32[]{:S(2)}) collective-permute-start(bf16[4,2,64,128]{3,2,1,0:T(8,128)(2,1)S(1)} %collective-permute-done.5.refs_1_), channel_id=1, source_target_pairs={{0,1},{1,0},{2,3},{3,2},{4,5},{5,4},{6,7},{7,6},{8,9},{9,8},{10,11... | collective-permute-start | bytes 393224 | tf_op jit(solution)/shard_map/ppermute | solution.py:176
  19.2 1.3 %collective-permute-start.8 = (bf16[4,2,64,128]{3,2,1,0:T(8,128)(2,1)S(1)}, bf16[4,2,64,128]{3,2,1,0:T(8,128)(2,1)S(1)}, u32[]{:S(2)}, u32[]{:S(2)}) collective-permute-start(bf16[4,2,64,128]{3,2,1,0:T(8,128)(2,1)S(1)} %collective-permute-done.3.refs_3_), channel_id=1, source_target_pairs={{0,1},{1,0},{2,3},{3,2},{4,5},{5,4},{6,7},{7,6},{8,9},{9,8},{10,11... | collective-permute-start | bytes 393224 | tf_op jit(solution)/shard_map/ppermute | solution.py:176
